TPU v7x, 32 devices: a whole 2x2x4 slice. The times are simulated.
32 devices in a mesh: rep: 4 (over y, x), ep: 8 (over z, core).
Axes of the slice: x: 2, y: 2, z: 4, core: 2. Of those that a mesh axis runs over, the one named last changes fastest.
Arguments:
- tokens: bfloat16 [4096, 3584], P(('rep', 'ep')), may hold values from -6 to 6
- out_grad: bfloat16 [4096, 3584], P(('rep', 'ep')), may hold values from -3 to 3
- expert_ids: int32 [4096, 8], P(('rep', 'ep')), may hold values from 0 to 127, all different within a row; in each aligned block of 128 rows (0 to 127, 128 to 255, ...) at most 16 rows name the same one
- route_weight: bfloat16 [4096, 8], P(('rep', 'ep')), may hold values from 0.049804688 to 0.59765625
- live_count: int32 [4], replicated, may hold values from 96 to 128
- cap_blocks: int32 [4, 1], replicated, may hold values from 1 to 3
- w_gate: bfloat16 [3584, 1024], P('rep', 'ep'), may hold values from -0.09375 to 0.09375
- w_up: bfloat16 [3584, 1024], P('rep', 'ep'), may hold values from -0.09375 to 0.09375
- w_down_t: bfloat16 [3584, 1024], P('rep', 'ep'), may hold values from -0.1875 to 0.1875
Outputs:
- grad_tokens: bfloat16 [4096, 3584], P(('rep', 'ep'))
- grad_weight: float32 [4096, 8], P(('rep', 'ep'))
- grad_gate: bfloat16 [3584, 1024], P('rep', 'ep')
- grad_up: bfloat16 [3584, 1024], P('rep', 'ep')
- grad_down_t: bfloat16 [3584, 1024], P('rep', 'ep')
Inputs may be any that keep to these rules, and one draw needn't show every extreme that they name: `expert_ids`: among the 128 rows of one device, no expert is named by more than 16 rows; each row names 8 different experts.
All inputs are finite; a program needn't handle non-finite values.
Results may differ from a plain program's by a relative error of at most 0.019.
Values may be sent and summed in bfloat16 or wider, within the bound.
No kernel may reach another device: no remote copies, remote signals or barrier semaphores. Data moves between devices by JAX's collectives and lax.ppermute only.
A program may use at most 128 MiB of HBM per device.

v0:
```python
import jax
import jax.numpy as jnp
from jax import lax
from jax.sharding import PartitionSpec as P

EXPERTS = 128
SLOT = 16
BLOCK = 128
SPLIT = 8


def expert_rows(token_rows, grad_rows, row_rate, kept_rows, gate_full, up_full, down_full):
    pre_gate = jnp.dot(token_rows, gate_full, preferred_element_type=jnp.float32)
    pre_up = jnp.dot(token_rows, up_full, preferred_element_type=jnp.float32)
    back_hidden = jnp.dot(grad_rows, down_full, preferred_element_type=jnp.float32)
    sigmoid_gate = jax.nn.sigmoid(pre_gate)
    activated = pre_gate * sigmoid_gate
    hidden = activated * pre_up
    dot_score = (jnp.sum(hidden * back_hidden, axis=1) * kept_rows).astype(jnp.bfloat16)
    scaled = back_hidden * row_rate[:, None]
    weighted_hidden = (hidden * row_rate[:, None]).astype(jnp.bfloat16)
    gate_grad = (scaled * pre_up * sigmoid_gate * (1.0 + pre_gate * (1.0 - sigmoid_gate))).astype(
        jnp.bfloat16
    )
    up_grad = (scaled * activated).astype(jnp.bfloat16)
    contract_units = (((1,), (1,)), ((), ()))
    partial_x = lax.dot_general(
        gate_grad, gate_full, contract_units, preferred_element_type=jnp.float32
    )
    partial_x = partial_x + lax.dot_general(
        up_grad, up_full, contract_units, preferred_element_type=jnp.float32
    )
    return (partial_x.astype(jnp.bfloat16), dot_score, gate_grad, up_grad, weighted_hidden)


def local(
    tokens, out_grad, expert_ids, route_weight, live_count, cap_blocks, w_gate, w_up, w_down_t
):
    ep_count = lax.axis_size("ep")
    flight = ep_count // SPLIT
    spacing = EXPERTS // flight
    tok_count = tokens.shape[0]
    model_dim = tokens.shape[1]
    rep_index = lax.axis_index("rep")
    ep_index = lax.axis_index("ep")
    gate_full, up_full, down_full = (
        lax.all_gather(w_gate, "rep", axis=0, tiled=True),
        lax.all_gather(w_up, "rep", axis=0, tiled=True),
        lax.all_gather(w_down_t, "rep", axis=0, tiled=True),
    )
    live_here = live_count[rep_index]
    targets = jnp.arange(flight, dtype=jnp.int32) * spacing
    matches = expert_ids[:, :, None] == targets[None, None, :]
    token_index = jnp.arange(tok_count, dtype=jnp.int32)
    routed = jnp.any(matches, axis=1) & (token_index[:, None] < live_here)
    weight_of = jnp.sum(
        jnp.where(matches, route_weight[:, :, None].astype(jnp.float32), 0.0), axis=1
    )
    slot_rank = jnp.cumsum(routed.astype(jnp.int32), axis=0, dtype=jnp.int32) - 1
    slot_ids = jnp.arange(SLOT, dtype=jnp.int32)
    placed = routed[:, :, None] & (slot_rank[:, :, None] == slot_ids[None, None, :])
    filled = jnp.any(placed, axis=0)
    token_of = jnp.sum(jnp.where(placed, token_index[:, None, None], 0), axis=0)
    send_x = jnp.where(filled[:, :, None], tokens[token_of], jnp.zeros((), jnp.bfloat16))
    send_dy = jnp.where(filled[:, :, None], out_grad[token_of], jnp.zeros((), jnp.bfloat16))
    send_weight = jnp.where(filled, jnp.take_along_axis(weight_of.T, token_of, axis=1), 0.0).astype(
        jnp.bfloat16
    )
    got_x, got_dy, got_weight = (
        lax.all_to_all(
            jnp.repeat(send_x, SPLIT, axis=0), "ep", split_axis=0, concat_axis=0, tiled=True
        ),
        lax.all_to_all(
            jnp.repeat(send_dy, SPLIT, axis=0), "ep", split_axis=0, concat_axis=0, tiled=True
        ),
        lax.all_to_all(
            jnp.repeat(send_weight, SPLIT, axis=0), "ep", split_axis=0, concat_axis=0, tiled=True
        ),
    )
    my_expert = ep_index // SPLIT
    capacity = BLOCK * cap_blocks[rep_index, my_expert]
    present = got_weight > 0
    counts = jnp.sum(present.astype(jnp.int32), axis=1)
    starts = jnp.cumsum(counts, dtype=jnp.int32) - counts
    arrival_rank = starts[:, None] + slot_ids[None, :]
    kept_mask = present & (arrival_rank < capacity)
    flat_x = got_x.reshape(ep_count * SLOT, model_dim)
    flat_dy = got_dy.reshape(ep_count * SLOT, model_dim)
    flat_rate = jnp.where(kept_mask, got_weight.astype(jnp.float32), 0.0).reshape(-1)
    partial_x, dot_score, gate_grad, up_grad, weighted_hidden = expert_rows(
        flat_x,
        flat_dy,
        flat_rate,
        kept_mask.reshape(-1).astype(jnp.float32),
        gate_full,
        up_full,
        down_full,
    )
    slot_x = partial_x.reshape(ep_count, SLOT, model_dim)
    slot_score = dot_score.reshape(ep_count, SLOT)
    contract_rows = (((0,), (0,)), ((), ()))
    term_gate = lax.dot_general(
        flat_x, gate_grad, contract_rows, preferred_element_type=jnp.float32
    )
    term_up = lax.dot_general(flat_x, up_grad, contract_rows, preferred_element_type=jnp.float32)
    term_down = lax.dot_general(
        flat_dy, weighted_hidden, contract_rows, preferred_element_type=jnp.float32
    )
    summed = lax.psum_scatter(
        jnp.concatenate([term_gate, term_up, term_down], axis=1).astype(jnp.bfloat16),
        "rep",
        scatter_dimension=0,
        tiled=True,
    ).astype(jnp.float32)
    unit_count = w_gate.shape[1]
    grad_gate = summed[:, :unit_count].astype(jnp.bfloat16)
    grad_up = summed[:, unit_count : 2 * unit_count].astype(jnp.bfloat16)
    grad_down = summed[:, 2 * unit_count :].astype(jnp.bfloat16)
    back_x, back_score = (
        lax.all_to_all(slot_x, "ep", split_axis=0, concat_axis=0, tiled=True),
        lax.all_to_all(slot_score, "ep", split_axis=0, concat_axis=0, tiled=True),
    )
    summed_x = jnp.sum(back_x.reshape(flight, SPLIT, SLOT, model_dim), axis=1, dtype=jnp.float32)
    summed_score = jnp.sum(back_score.reshape(flight, SPLIT, SLOT), axis=1, dtype=jnp.float32)
    contrib = jnp.where(filled[:, :, None], summed_x, 0.0).reshape(flight * SLOT, model_dim)
    grad_tokens = (
        jnp.zeros((tok_count, model_dim), jnp.float32)
        .at[token_of.reshape(-1)]
        .add(contrib)
        .astype(jnp.bfloat16)
    )
    slot_of = jnp.clip(slot_rank, 0, SLOT - 1)
    token_score = jnp.where(routed, jnp.take_along_axis(summed_score, slot_of.T, axis=1).T, 0.0)
    grad_weight = jnp.sum(jnp.where(matches, token_score[:, None, :], 0.0), axis=2)
    return (grad_tokens, grad_weight, grad_gate, grad_up, grad_down)


def solution(mesh):
    return jax.shard_map(
        local,
        mesh=mesh,
        in_specs=(
            P(("rep", "ep"), None),
            P(("rep", "ep"), None),
            P(("rep", "ep"), None),
            P(("rep", "ep"), None),
            P(),
            P(),
            P("rep", "ep"),
            P("rep", "ep"),
            P("rep", "ep"),
        ),
        out_specs=(
            P(("rep", "ep"), None),
            P(("rep", "ep"), None),
            P("rep", "ep"),
            P("rep", "ep"),
            P("rep", "ep"),
        ),
        check_vma=False,
    )
```

profile of v0, /device:TPU:0, one launch (start us, length us, event | category | flops | bytes accessed | tf_op | source)
XLA Modules:
  0.0 144.0 jit_solution(893043684888486238)
XLA Ops:
  7.2 0.9 select_reduce_fusion.2
  8.1 1.2 dynamic_slice.7
  10.0 0.7 compare_and_fusion
  11.3 0.7 gather_fusion.1
  12.6 6.3 %all-to-all-start.1 = ((bf16[8,1,16]{2,1,0:T(2,128)(2,1)}), bf16[8,1,16]{2,1,0:T(2,128)(2,1)S(1)}, u32[]{:S(2)}, u32[]{:S(2)}) async-start(bf16[8,1,16]{2,1,0:T(2,128)(2,1)} %reshape.487), calls=%async_computation.1 | async-start | bytes 8192 | tf_op jit(solution)/shard_map/all_to_all | solution.py:76
  20.3 4.1 %all-to-all-done.1 = bf16[8,1,16]{2,1,0:T(2,128)(2,1)S(1)} async-done(((bf16[8,1,16]{2,1,0:T(2,128)(2,1)}), bf16[8,1,16]{2,1,0:T(2,128)(2,1)S(1)}, u32[]{:S(2)}, u32[]{:S(2)}) %all-to-all-start.1) | async-done | bytes 288 | tf_op jit(solution)/shard_map/all_to_all | solution.py:76
  24.4 1.0 reshape.490
  25.4 3.6 %all-to-all-start.2 = ((bf16[8,16,3584]{2,1,0:T(8,128)(2,1)}), bf16[8,16,3584]{2,1,0:T(8,128)(2,1)S(1)}, u32[]{:S(2)}, u32[]{:S(2)}) async-start(bf16[8,16,3584]{2,1,0:T(8,128)(2,1)} %reshape.490), calls=%async_computation.2 | async-start | bytes 1835008 | tf_op jit(solution)/shard_map/all_to_all | solution.py:70
  28.9 13.6 %all_gather.10 = bf16[3584,128]{1,0:T(8,128)(2,1)S(1)} all-gather(bf16[896,128]{1,0:T(8,128)(2,1)S(1)} %copy-done.5), channel_id=1, replica_groups=mesh['rep'=4,'ep'=8] {'rep'}, dimensions={0}, use_global_device_ids=true | all-gather | bytes 1146880 | tf_op jit(solution)/shard_map/all_gather | solution.py:48
  42.5 12.4 %all_gather.11 = bf16[3584,128]{1,0:T(8,128)(2,1)} all-gather(bf16[896,128]{1,0:T(8,128)(2,1)S(1)} %copy-done.6), channel_id=1, replica_groups=mesh['rep'=4,'ep'=8] {'rep'}, dimensions={0}, use_global_device_ids=true | all-gather | bytes 1146880 | tf_op jit(solution)/shard_map/all_gather | solution.py:47
  55.0 1.0 reshape.485
  56.0 4.8 %all-to-all-start = ((bf16[8,16,3584]{2,1,0:T(8,128)(2,1)}), bf16[8,16,3584]{2,1,0:T(8,128)(2,1)}, u32[]{:S(2)}, u32[]{:S(2)}) async-start(bf16[8,16,3584]{2,1,0:T(8,128)(2,1)} %reshape.485), calls=%async_computation | async-start | bytes 1835008 | tf_op jit(solution)/shard_map/all_to_all | solution.py:73
  60.9 14.1 %all_gather.9 = bf16[3584,128]{1,0:T(8,128)(2,1)} all-gather(bf16[896,128]{1,0:T(8,128)(2,1)S(1)} %copy-done.7), channel_id=1, replica_groups=mesh['rep'=4,'ep'=8] {'rep'}, dimensions={0}, use_global_device_ids=true | all-gather | bytes 1146880 | tf_op jit(solution)/shard_map/all_gather | solution.py:49
  76.0 0.7 add_compare_fusion.1
  77.3 0.7 copy-done.1
  78.5 6.2 %all-to-all-done = bf16[8,16,3584]{2,1,0:T(8,128)(2,1)} async-done(((bf16[8,16,3584]{2,1,0:T(8,128)(2,1)}), bf16[8,16,3584]{2,1,0:T(8,128)(2,1)}, u32[]{:S(2)}, u32[]{:S(2)}) %all-to-all-start) | async-done | bytes 917536 | tf_op jit(solution)/shard_map/all_to_all | solution.py:73
  84.7 1.7 %convolution_convert_fusion = bf16[3584,128]{0,1:T(8,128)(2,1)S(1)} fusion(bf16[128,3584]{1,0:T(8,128)(2,1)} %bitcast.6, f32[128]{0:T(128)S(1)} %and_select_fusion.1, f32[128,128]{0,1:T(8,128)S(1)} %fusion.22, f32[128,128]{0,1:T(8,128)S(1)} %fusion.23), kind=kOutput, calls=%fused_computation.6 | convolution fusion | flops 118013952 | bytes 1966592 | tf_op jit(solution)/shard_map/dot_general | solution.py:106
  86.4 1.7 %multiply_reduce_fusion = (bf16[128]{0:T(256)(128)(2,1)S(1)}, bf16[128,128]{0,1:T(8,128)(2,1)S(1)}, bf16[128,128]{0,1:T(8,128)(2,1)S(1)}) fusion(f32[128,128]{0,1:T(8,128)S(1)} %fusion.22, f32[128,128]{0,1:T(8,128)S(1)} %fusion.23, f32[128]{0:T(128)S(1)} %and_select_fusion.1, bf16[128,3584]{1,0:T(8,128)(2,1)} %bitcast.6, bf16[3584,128]{1,0:T(8,128)(2,1)S(1)} %copy-done.3), kind=kOutput, calls=%fused_computation.21 | convolution fusion | flops 117718912 | bytes 2032384 | tf_op jit(solution)/shard_map/dot_general | solution.py:15
  88.8 1.7 %pad_maximum_fusion = bf16[3584,384]{0,1:T(8,128)(2,1)} fusion(bf16[3584,128]{0,1:T(8,128)(2,1)S(1)} %convolution_convert_fusion, bf16[3584,128]{0,1:T(8,128)(2,1)S(1)} %convolution_convert_fusion.1, bf16[3584,128]{0,1:T(8,128)(2,1)S(1)} %convolution_convert_fusion.2), kind=kLoop, calls=%fused_computation.9 | loop fusion | flops 8257536 | bytes 5505024 | tf_op jit(solution)/shard_map/concatenate | solution.py:110
  90.5 4.5 %copy.34 = bf16[3584,384]{1,0:T(8,128)(2,1)} copy(bf16[3584,384]{0,1:T(8,128)(2,1)} %pad_maximum_fusion) | data formatting | bytes 5505024
  95.2 0.8 select_convert_fusion
  96.5 3.3 %all-to-all-start.4 = ((bf16[8,1,16]{2,1,0:T(2,128)(2,1)}), bf16[8,1,16]{2,1,0:T(2,128)(2,1)S(1)}, u32[]{:S(2)}, u32[]{:S(2)}) async-start(bf16[8,1,16]{2,1,0:T(2,128)(2,1)} %copy.30), calls=%async_computation.4 | async-start | bytes 8192 | tf_op jit(solution)/shard_map/all_to_all | solution.py:121
  100.3 1.4 fusion
  101.7 3.6 %all-to-all-done.4 = bf16[8,1,16]{2,1,0:T(2,128)(2,1)S(1)} async-done(((bf16[8,1,16]{2,1,0:T(2,128)(2,1)}), bf16[8,1,16]{2,1,0:T(2,128)(2,1)S(1)}, u32[]{:S(2)}, u32[]{:S(2)}) %all-to-all-start.4) | async-done | bytes 288 | tf_op jit(solution)/shard_map/all_to_all | solution.py:121
  105.3 3.6 %all-to-all-start.3 = ((bf16[8,16,3584]{2,1,0:T(8,128)(2,1)}), bf16[8,16,3584]{2,1,0:T(8,128)(2,1)S(1)}, u32[]{:S(2)}, u32[]{:S(2)}) async-start(bf16[8,16,3584]{2,1,0:T(8,128)(2,1)} %bitcast.11), calls=%async_computation.3 | async-start | bytes 1835008 | tf_op jit(solution)/shard_map/all_to_all | solution.py:120
  109.1 0.7 fusion.20
  109.8 4.3 %select_reduce_fusion = f32[128]{0:T(128)S(1)} fusion(f32[]{:T(128)} %bitcast.21, f32[]{:T(128)} %bitcast.22, f32[]{:T(128)} %bitcast.23, f32[]{:T(128)} %bitcast.24, f32[]{:T(128)} %bitcast.25, f32[]{:T(128)} %bitcast.27, f32[]{:T(128)} %bitcast.26, s32[128,1]{1,0:T(8,128)S(1)} %reduce_window_sum.18), kind=kLoop, calls=%fused_computation.19 | loop fusion | flops 2176 | bytes 1052 | tf_op jit(solution)/shard_map/jit(take_along_axis)/gather | solution.py:133
  114.1 6.4 %fusion.14 = f32[128]{0:T(128)S(1)} fusion(pred[128]{0:T(512)(128)(4,1)S(1)} %get-tuple-element.33, pred[128]{0:T(512)(128)(4,1)S(1)} %get-tuple-element.26, pred[128]{0:T(512)(128)(4,1)S(1)} %get-tuple-element.31, pred[128]{0:T(512)(128)(4,1)S(1)} %get-tuple-element.30, pred[128]{0:T(512)(128)(4,1)S(1)} %get-tuple-element.29, ...), kind=kLoop, calls=%fused_computation.66 | loop fusion | flops 2560 | bytes 2856 | tf_op jit(solution)/shard_map/jit(_where)/select_n | solution.py:133
  121.1 11.4 %all-to-all-done.3 = bf16[8,16,3584]{2,1,0:T(8,128)(2,1)S(1)} async-done(((bf16[8,16,3584]{2,1,0:T(8,128)(2,1)}), bf16[8,16,3584]{2,1,0:T(8,128)(2,1)S(1)}, u32[]{:S(2)}, u32[]{:S(2)}) %all-to-all-start.3) | async-done | bytes 917536 | tf_op jit(solution)/shard_map/all_to_all | solution.py:120
  132.7 1.4 scatter_custom_fusion
  134.1 1.0 convert_element_type.87
  135.1 2.0 %fusion.19 = (bf16[896,128]{1,0:T(8,128)(2,1)}, bf16[896,128]{1,0:T(8,128)(2,1)}, bf16[896,128]{1,0:T(8,128)(2,1)}) fusion(bf16[896,384]{1,0:T(8,128)(2,1)} %reduce-scatter.4.cloned.1.call-done), kind=kLoop, calls=%fused_computation.72 | loop fusion | bytes 1376256 | tf_op jit(solution)/shard_map/slice | solution.py:118
  (57 shorter events, 8.4 us)
Async XLA Ops:
  7.2 11.7 %copy-start = (bf16[128,3584]{1,0:T(8,128)(2,1)S(1)}, bf16[128,3584]{1,0:T(8,128)(2,1)}, u32[]{:S(2)}) copy-start(bf16[128,3584]{1,0:T(8,128)(2,1)} %param.10) | copy-start | bytes 2752516
  7.2 12.4 %copy-start.4 = (bf16[128,3584]{1,0:T(8,128)(2,1)S(1)}, bf16[128,3584]{1,0:T(8,128)(2,1)}, u32[]{:S(2)}) copy-start(bf16[128,3584]{1,0:T(8,128)(2,1)} %param.9) | copy-start | bytes 2752516
  12.6 11.8 %all-to-all-start.1 = ((bf16[8,1,16]{2,1,0:T(2,128)(2,1)}), bf16[8,1,16]{2,1,0:T(2,128)(2,1)S(1)}, u32[]{:S(2)}, u32[]{:S(2)}) async-start(bf16[8,1,16]{2,1,0:T(2,128)(2,1)} %reshape.487), calls=%async_computation.1 | async-start | bytes 8192 | tf_op jit(solution)/shard_map/all_to_all | solution.py:76
  20.2 8.7 %copy-start.5 = (bf16[896,128]{1,0:T(8,128)(2,1)S(1)}, bf16[896,128]{1,0:T(8,128)(2,1)}, u32[]{:S(2)}) copy-start(bf16[896,128]{1,0:T(8,128)(2,1)} %param.16) | copy-start | bytes 688132
  24.4 18.2 %copy-start.6 = (bf16[896,128]{1,0:T(8,128)(2,1)S(1)}, bf16[896,128]{1,0:T(8,128)(2,1)}, u32[]{:S(2)}) copy-start(bf16[896,128]{1,0:T(8,128)(2,1)} %param.15) | copy-start | bytes 688132
  25.4 29.6 %all-to-all-start.2 = ((bf16[8,16,3584]{2,1,0:T(8,128)(2,1)}), bf16[8,16,3584]{2,1,0:T(8,128)(2,1)S(1)}, u32[]{:S(2)}, u32[]{:S(2)}) async-start(bf16[8,16,3584]{2,1,0:T(8,128)(2,1)} %reshape.490), calls=%async_computation.2 | async-start | bytes 1835008 | tf_op jit(solution)/shard_map/all_to_all | solution.py:70
  42.5 18.3 %copy-start.7 = (bf16[896,128]{1,0:T(8,128)(2,1)S(1)}, bf16[896,128]{1,0:T(8,128)(2,1)}, u32[]{:S(2)}) copy-start(bf16[896,128]{1,0:T(8,128)(2,1)} %param.17) | copy-start | bytes 688132
  55.0 20.0 %copy-start.8 = (s32[4,1]{0,1:T(1,128)S(1)}, s32[4,1]{0,1:T(1,128)}, u32[]{:S(2)}) copy-start(s32[4,1]{0,1:T(1,128)} %param.14) | copy-start | bytes 52
  56.0 28.7 %all-to-all-start = ((bf16[8,16,3584]{2,1,0:T(8,128)(2,1)}), bf16[8,16,3584]{2,1,0:T(8,128)(2,1)}, u32[]{:S(2)}, u32[]{:S(2)}) async-start(bf16[8,16,3584]{2,1,0:T(8,128)(2,1)} %reshape.485), calls=%async_computation | async-start | bytes 1835008 | tf_op jit(solution)/shard_map/all_to_all | solution.py:73
  60.8 74.3 %reduce-scatter.4.cloned.1.call-start = ((), (), s32[]{:S(2)}) async-start(), calls=%async_computation.6 | async-start | bytes 3440640
  76.8 1.2 copy-start.1
  84.7 1.7 %copy-start.3 = (bf16[3584,128]{1,0:T(8,128)(2,1)S(1)}, bf16[3584,128]{1,0:T(8,128)(2,1)}, u32[]{:S(2)}) copy-start(bf16[3584,128]{1,0:T(8,128)(2,1)} %all_gather.9) | copy-start | bytes 2752516
  95.0 4.8 %copy-start.2 = (bf16[3584,128]{1,0:T(8,128)(2,1)S(1)}, bf16[3584,128]{1,0:T(8,128)(2,1)}, u32[]{:S(2)}) copy-start(bf16[3584,128]{1,0:T(8,128)(2,1)} %all_gather.11) | copy-start | bytes 2752516
  96.5 8.7 %all-to-all-start.4 = ((bf16[8,1,16]{2,1,0:T(2,128)(2,1)}), bf16[8,1,16]{2,1,0:T(2,128)(2,1)S(1)}, u32[]{:S(2)}, u32[]{:S(2)}) async-start(bf16[8,1,16]{2,1,0:T(2,128)(2,1)} %copy.30), calls=%async_computation.4 | async-start | bytes 8192 | tf_op jit(solution)/shard_map/all_to_all | solution.py:121
  105.3 27.3 %all-to-all-start.3 = ((bf16[8,16,3584]{2,1,0:T(8,128)(2,1)}), bf16[8,16,3584]{2,1,0:T(8,128)(2,1)S(1)}, u32[]{:S(2)}, u32[]{:S(2)}) async-start(bf16[8,16,3584]{2,1,0:T(8,128)(2,1)} %bitcast.11), calls=%async_computation.3 | async-start | bytes 1835008 | tf_op jit(solution)/shard_map/all_to_all | solution.py:120
Sparse Core Ops, SparseCore 0:
  95.2 38.6 reduce-scatter.3
where the time goes:
time: 145 us; the launch traced here: 144 us
  blocking collectives  40.1 us (28%)
  waiting for transfers between devices  25.4 us (18%)
  starting transfers between devices  21.6 us (15%)
  other arithmetic  21.1 us (15%)
  local copies, waits for them, and re-layouts  14.7 us (10%)
  between operations  14.3 us (10%)
  matrix products  6.82 us (5%)
    all_gather x1, blocking collectives, local(): lax.all_gather(w_down_t, 'rep', axis=0, tiled=True)  14.1 us
    all_gather x1, blocking collectives, local(): lax.all_gather(w_up, 'rep', axis=0, tiled=True)  13.6 us
    all_gather x1, blocking collectives, local(): lax.all_gather(w_gate, 'rep', axis=0, tiled=True)  12.4 us
    all_to_all x1, waiting for transfers between devices, local(): lax.all_to_all(slot_x, 'ep', split_axis=0, concat_axis=0, tiled=True)  11.4 us
    select_n x1, other arithmetic, local(): jnp.where(routed, jnp.take_along_axis(summed_score, slot_of.T, axis=1).T,...  6.36 us
    all_to_all x1, starting transfers between devices, local(): lax.all_to_all(jnp.repeat(send_weight, SPLIT, axis=0), 'ep', split_axis=0...  6.33 us
    all_to_all x1, waiting for transfers between devices, local(): lax.all_to_all(jnp.repeat(send_dy, SPLIT, axis=0), 'ep', split_axis=0, co...  6.2 us
    unnamed x19, local copies, waits for them, and re-layouts  5.21 us
  transfers between devices with their start and end apart: 6, of which 4 were waited for; matrix products, arithmetic and copies ran while one was open for 15% of the time, Pallas kernels for 0%

commit v1 on v0

v1 whole, which is shorter than its diff:
```python
import jax
import jax.numpy as jnp
from jax import lax
from jax.sharding import PartitionSpec as P

EXPERTS = 128
SLOT = 16
BLOCK = 128
SPLIT = 8


def local(
    tokens, out_grad, expert_ids, route_weight, live_count, cap_blocks, w_gate, w_up, w_down_t
):
    rep_count = lax.axis_size("rep")
    ep_count = lax.axis_size("ep")
    flight = ep_count // SPLIT
    spacing = EXPERTS // flight
    tok_count, model_dim = tokens.shape
    width, units = w_gate.shape
    rep_index = lax.axis_index("rep")
    ep_index = lax.axis_index("ep")
    my_expert = ep_index // SPLIT
    same_split = [[w * SPLIT + s for w in range(flight)] for s in range(SPLIT)]
    same_expert = [[w * SPLIT + s for s in range(SPLIT)] for w in range(flight)]

    live_here = live_count[rep_index]
    targets = jnp.arange(flight, dtype=jnp.int32) * spacing
    matches = expert_ids[:, :, None] == targets[None, None, :]
    token_index = jnp.arange(tok_count, dtype=jnp.int32)
    routed = jnp.any(matches, axis=1) & (token_index[:, None] < live_here)
    weight_of = jnp.sum(
        jnp.where(matches, route_weight[:, :, None].astype(jnp.float32), 0.0), axis=1
    )
    slot_rank = jnp.cumsum(routed.astype(jnp.int32), axis=0, dtype=jnp.int32) - 1
    slot_ids = jnp.arange(SLOT, dtype=jnp.int32)
    placed = routed[:, :, None] & (slot_rank[:, :, None] == slot_ids[None, None, :])
    placed = placed.reshape(tok_count, flight * SLOT).astype(jnp.bfloat16)

    def pick(rows):
        chosen = lax.dot_general(
            placed, rows, (((0,), (0,)), ((), ())), preferred_element_type=jnp.float32
        ).astype(jnp.bfloat16)
        return chosen.reshape(flight, SLOT, rep_count, width).transpose(2, 0, 1, 3)

    send = jnp.stack([pick(tokens), pick(out_grad)], axis=1)
    send_weight = jnp.sum(
        placed.reshape(tok_count, flight, SLOT).astype(jnp.float32) * weight_of[:, :, None], axis=0
    ).astype(jnp.bfloat16)
    got = lax.all_to_all(send, "rep", split_axis=0, concat_axis=0, tiled=True)
    if flight > 1:
        got = lax.all_to_all(
            got, "ep", split_axis=2, concat_axis=2, tiled=True, axis_index_groups=same_split
        )
    rows = lax.all_gather(got, "ep", axis=0, axis_index_groups=same_expert)
    rows = rows.transpose(2, 1, 3, 0, 4, 5).reshape(2, rep_count * ep_count * SLOT, width)
    flat_x, flat_dy = rows[0], rows[1]
    all_weight = lax.all_gather(send_weight, "ep", axis=0)
    got_weight = lax.dynamic_index_in_dim(all_weight, my_expert, axis=1, keepdims=False)

    capacity = BLOCK * cap_blocks[rep_index, my_expert]
    present = got_weight > 0
    counts = jnp.sum(present.astype(jnp.int32), axis=1)
    starts = jnp.cumsum(counts, dtype=jnp.int32) - counts
    arrival_rank = starts[:, None] + slot_ids[None, :]
    kept_mask = present & (arrival_rank < capacity)
    rate = jnp.where(kept_mask, got_weight.astype(jnp.float32), 0.0).reshape(-1)[:, None]
    kept = kept_mask.reshape(-1).astype(jnp.float32)

    pre = jnp.concatenate(
        [
            jnp.dot(flat_x, w_gate, preferred_element_type=jnp.float32),
            jnp.dot(flat_x, w_up, preferred_element_type=jnp.float32),
            jnp.dot(flat_dy, w_down_t, preferred_element_type=jnp.float32),
        ],
        axis=1,
    )
    pre = lax.all_to_all(
        pre.reshape(rep_count, ep_count * SLOT, 3 * units), "rep", split_axis=0, concat_axis=0, tiled=True
    )
    pre = jnp.sum(pre, axis=0)
    pre_gate, pre_up, back_hidden = pre[:, :units], pre[:, units : 2 * units], pre[:, 2 * units :]
    sigmoid_gate = jax.nn.sigmoid(pre_gate)
    activated = pre_gate * sigmoid_gate
    hidden = activated * pre_up
    score = (jnp.sum(hidden * back_hidden, axis=1) * kept).astype(jnp.bfloat16)
    scaled = back_hidden * rate
    grads = jnp.concatenate(
        [
            scaled * pre_up * sigmoid_gate * (1.0 + pre_gate * (1.0 - sigmoid_gate)),
            scaled * activated,
            hidden * rate,
        ],
        axis=1,
    ).astype(jnp.bfloat16)
    grads = lax.all_gather(grads, "rep", axis=0, tiled=True)
    gate_grad, up_grad, weighted = grads[:, :units], grads[:, units : 2 * units], grads[:, 2 * units :]

    contract_units = (((1,), (1,)), ((), ()))
    partial_x = lax.dot_general(
        gate_grad, w_gate, contract_units, preferred_element_type=jnp.float32
    ) + lax.dot_general(up_grad, w_up, contract_units, preferred_element_type=jnp.float32)
    partial_x = partial_x.astype(jnp.bfloat16).reshape(rep_count, flight, SPLIT, SLOT, width)
    back = lax.all_to_all(
        partial_x, "ep", split_axis=2, concat_axis=2, tiled=True, axis_index_groups=same_expert
    )
    back = jnp.sum(back, axis=2, dtype=jnp.float32).astype(jnp.bfloat16)
    if flight > 1:
        back = lax.all_to_all(
            back, "ep", split_axis=1, concat_axis=1, tiled=True, axis_index_groups=same_split
        )
    back = lax.all_to_all(back, "rep", split_axis=0, concat_axis=0, tiled=True)
    back = back.transpose(1, 2, 0, 3).reshape(flight * SLOT, model_dim)
    grad_tokens = jnp.dot(placed, back, preferred_element_type=jnp.float32).astype(jnp.bfloat16)

    all_score = lax.all_to_all(
        score.reshape(ep_count, SLOT), "ep", split_axis=0, concat_axis=0, tiled=True
    )
    slot_score = jnp.sum(
        all_score.reshape(flight, SPLIT, SLOT), axis=1, dtype=jnp.float32
    )
    token_score = jnp.sum(
        placed.reshape(tok_count, flight, SLOT).astype(jnp.float32) * slot_score[None], axis=2
    )
    grad_weight = jnp.sum(jnp.where(matches, token_score[:, None, :], 0.0), axis=2)

    contract_rows = (((0,), (0,)), ((), ()))

    def weight_grad(inputs, hidden_grad):
        return lax.dot_general(
            inputs, hidden_grad, contract_rows, preferred_element_type=jnp.float32
        ).astype(jnp.bfloat16)

    return (
        grad_tokens,
        grad_weight,
        weight_grad(flat_x, gate_grad),
        weight_grad(flat_x, up_grad),
        weight_grad(flat_dy, weighted),
    )


def solution(mesh):
    return jax.shard_map(
        local,
        mesh=mesh,
        in_specs=(
            P(("rep", "ep"), None),
            P(("rep", "ep"), None),
            P(("rep", "ep"), None),
            P(("rep", "ep"), None),
            P(),
            P(),
            P("rep", "ep"),
            P("rep", "ep"),
            P("rep", "ep"),
        ),
        out_specs=(
            P(("rep", "ep"), None),
            P(("rep", "ep"), None),
            P("rep", "ep"),
            P("rep", "ep"),
            P("rep", "ep"),
        ),
        check_vma=False,
    )
```

time: 145 us -> 139 us (0.959)
  waiting for transfers between devices: 25.4 us -> 39.2 us
  other arithmetic: 21.1 us -> 13.9 us
  starting transfers between devices: 21.6 us -> 15.2 us
  local copies, waits for them, and re-layouts: 14.7 us -> 9.07 us
  blocking collectives: 40.1 us -> 35.9 us
  matrix products: 6.82 us -> 9.75 us
    all_gather x3 -> x1, blocking collectives: 40.1 us -> 9.47 us  [local(): grads = lax.all_gather(grads, 'rep', axis=0, tiled=True)]
    unnamed x0 -> x1, blocking collectives: none -> 15.7 us
    all_to_all x0 -> x1, blocking collectives: none -> 10.7 us  [local(): got = lax.all_to_all(send, 'rep', split_axis=0, concat_axis=0, tiled=True)]
    all_gather x0 -> x1, waiting for transfers between devices: none -> 7.48 us  [local(): rows = lax.all_gather(got, 'ep', axis=0, axis_index_groups=same_expert)]
    select_n x4 -> x0, other arithmetic: 6.46 us -> none  [the longest x1 6.36 us: local(): jnp.where(routed, jnp.take_along_axis(summed_score, slot_of.T, axis=1).T,...]
    all_to_all x5 -> x4, starting transfers between devices: 21.6 us -> 15.2 us  [the longest x1 5.02 us: local(): lax.all_to_all(partial_x, 'ep', split_axis=2, concat_axis=2, tiled=True,...]
    all_to_all x5 -> x4, waiting for transfers between devices: 25.3 us -> 31.7 us  [the longest x1 20.4 us: local(): lax.all_to_all(partial_x, 'ep', split_axis=2, concat_axis=2, tiled=True,...]
    gather x4 -> x0, other arithmetic: 4.58 us -> none  [the longest x2 4.57 us: local(): jnp.take_along_axis(summed_score, slot_of.T, axis=1)]
  transfers between devices with their start and end apart: 6 -> 5, of which waited for: 4 -> 4; matrix products, arithmetic and copies ran while one was open for 15% -> 10% of each run, Pallas kernels for 0% -> 0%
where the time goes in v1:
time: 139 us; the launch traced here: 138 us
  waiting for transfers between devices  39.2 us (28%)
  blocking collectives  35.9 us (26%)
  starting transfers between devices  15.2 us (11%)
  between operations  15 us (11%)
  other arithmetic  13.9 us (10%)
  matrix products  9.75 us (7%)
  local copies, waits for them, and re-layouts  9.07 us (7%)
    all_to_all x1, waiting for transfers between devices, local(): lax.all_to_all(partial_x, 'ep', split_axis=2, concat_axis=2, tiled=True,...  20.4 us
    unnamed x1, blocking collectives  15.7 us
    all_to_all x1, blocking collectives, local(): got = lax.all_to_all(send, 'rep', split_axis=0, concat_axis=0, tiled=True)  10.7 us
    all_gather x1, blocking collectives, local(): grads = lax.all_gather(grads, 'rep', axis=0, tiled=True)  9.47 us
    all_gather x1, waiting for transfers between devices, local(): rows = lax.all_gather(got, 'ep', axis=0, axis_index_groups=same_expert)  7.48 us
    all_to_all x1, waiting for transfers between devices, local(): lax.all_to_all(pre.reshape(rep_count, ep_count * SLOT, 3 * units), 'rep',...  6.96 us
    all_to_all x1, starting transfers between devices, local(): lax.all_to_all(partial_x, 'ep', split_axis=2, concat_axis=2, tiled=True,...  5.02 us
    all_to_all x1, waiting for transfers between devices, local(): back = lax.all_to_all(back, 'rep', split_axis=0, concat_axis=0, tiled=True)  4.35 us
  transfers between devices with their start and end apart: 5, of which 4 were waited for; matrix products, arithmetic and copies ran while one was open for 10% of the time, Pallas kernels for 0%

profile of v1, /device:TPU:0, one launch (start us, length us, event | category | flops | bytes accessed | tf_op | source)
XLA Modules:
  0.0 137.9 jit_solution(4943658859723932201)
XLA Ops:
  7.2 0.8 fusion.25
  8.0 1.2 dynamic_slice.9
  11.4 1.5 %convolution_convert_fusion.2 = bf16[16,3584]{1,0:T(8,128)(2,1)S(1)} fusion(bf16[128,3584]{1,0:T(8,128)(2,1)} %param.9, s32[128]{0:T(128)S(1)} %add_reduce_fusion, pred[128]{0:T(512)(128)(4,1)S(1)} %compare_and_fusion), kind=kOutput, calls=%fused_computation.2 | convolution fusion | flops 14741504 | bytes 1032832 | tf_op jit(solution)/shard_map/dot_general | solution.py:41
  13.0 10.7 %all_to_all.26 = bf16[4,2,1,16,896]{4,3,1,2,0:T(8,128)(2,1)} all-to-all(bf16[4,2,1,16,896]{4,3,1,2,0:T(8,128)(2,1)S(1)} %pad_maximum_fusion), channel_id=1, replica_groups=mesh['rep'=4,'ep'=8] {'rep'}, dimensions={0} | all-to-all | bytes 458752 | tf_op jit(solution)/shard_map/all_to_all | solution.py:50
  26.0 15.7 %all-reduce = bf16[128]{0:T(256)(128)(2,1)S(1)} all-reduce(bf16[128]{0:T(256)(128)(2,1)S(1)} %dynamic-update-slice), channel_id=3, replica_groups=mesh['rep'=4,'ep'=8] {'ep'}, use_global_device_ids=true, to_apply=%add | all-reduce | flops 128 | bytes 512
  42.5 0.7 reduce-window.16
  43.2 7.5 %all-gather.4.cloned.1.call-done = bf16[32,2,1,16,896]{4,3,2,1,0:T(8,128)(2,1)} async-done(((bf16[4,2,1,16,896]{4,3,2,1,0:T(8,128)(2,1)}), bf16[32,2,1,16,896]{4,3,2,1,0:T(8,128)(2,1)}) %all-gather.4.cloned.1.call-update) | async-done | bytes 1835024 | tf_op jit(solution)/shard_map/all_gather | solution.py:55
  50.7 1.6 %fusion.26 = (bf16[1,4,1,8,16,896]{5,4,0,1,3,2:T(8,128)(2,1)S(1)}, bf16[1,4,1,8,16,896]{5,4,0,1,3,2:T(8,128)(2,1)S(1)}) fusion(bf16[2,4,1,8,16,896]{5,4,0,1,3,2:T(8,128)(2,1)} %bitcast.61), kind=kLoop, calls=%fused_computation.63 | loop fusion | bytes 3670016 | tf_op jit(solution)/shard_map/slice | solution.py:57
  52.5 0.8 copy-done.2
  55.1 0.9 copy_bitcast_fusion
  56.1 3.5 %all-to-all-start.1 = ((f32[4,128,384]{1,2,0:T(8,128)}), f32[4,128,384]{1,2,0:T(8,128)S(1)}, u32[]{:S(2)}, u32[]{:S(2)}) async-start(f32[4,128,384]{1,2,0:T(8,128)} %copy_bitcast_fusion), calls=%async_computation.1 | async-start | bytes 1572864 | tf_op jit(solution)/shard_map/all_to_all | solution.py:78
  59.6 0.7 bitcast_subtract_fusion
  60.2 1.3 add_compare_fusion.1
  61.5 1.3 lt.65
  62.8 1.3 and_select_fusion
  64.1 7.0 %all-to-all-done.1 = f32[4,128,384]{1,2,0:T(8,128)S(1)} async-done(((f32[4,128,384]{1,2,0:T(8,128)}), f32[4,128,384]{1,2,0:T(8,128)S(1)}, u32[]{:S(2)}, u32[]{:S(2)}) %all-to-all-start.1) | async-done | bytes 786464 | tf_op jit(solution)/shard_map/all_to_all | solution.py:78
  71.0 0.7 reduce_sum.83
  71.7 1.0 multiply_convert_fusion.2
  72.8 1.4 %select_convert_fusion = bf16[8,1,16]{2,0,1:T(8,128)(2,1)S(1)} fusion(bf16[8,1,16]{2,0,1:T(8,128)(2,1)S(1)} %reduce_sum.90, pred[8,1,16]{2,0,1:T(8,128)(4,1)} %copy-done.6, s32[]{:T(128)} %bitcast.16, s32[8]{0:T(128)S(1)} %bitcast_subtract_fusion), kind=kLoop, calls=%fused_computation.45 | loop fusion | flops 512 | bytes 676 | tf_op jit(solution)/shard_map/convert_element_type | solution.py:86
  74.9 3.3 %all-to-all-start.4 = ((bf16[8,1,16]{2,1,0:T(2,128)(2,1)}), bf16[8,1,16]{2,1,0:T(2,128)(2,1)S(1)}, u32[]{:S(2)}, u32[]{:S(2)}) async-start(bf16[8,1,16]{2,1,0:T(2,128)(2,1)} %copy.46), calls=%async_computation.4 | async-start | bytes 8192 | tf_op jit(solution)/shard_map/all_to_all | solution.py:116
  78.2 9.5 %all_gather.16 = bf16[512,384]{0,1:T(8,128)(2,1)S(1)} all-gather(bf16[128,384]{0,1:T(8,128)(2,1)S(1)} %pad_maximum_fusion.1), channel_id=1, replica_groups=mesh['rep'=4,'ep'=8] {'rep'}, dimensions={0}, use_global_device_ids=true | all-gather | bytes 491520 | tf_op jit(solution)/shard_map/all_gather | solution.py:96
  87.7 1.4 fusion.4
  89.5 1.0 copy.42
  90.5 5.0 %all-to-all-start.2 = ((bf16[4,1,8,16,896]{4,3,0,1,2:T(8,128)(2,1)}), bf16[4,1,8,16,896]{4,3,0,1,2:T(8,128)(2,1)}, u32[]{:S(2)}, u32[]{:S(2)}) async-start(bf16[4,1,8,16,896]{4,3,0,1,2:T(8,128)(2,1)} %copy.42), calls=%async_computation.2 | async-start | bytes 1835008 | tf_op jit(solution)/shard_map/all_to_all | solution.py:104
  95.5 1.1 convolution_convert_fusion.3
  96.7 1.1 convolution_convert_fusion.5
  97.8 1.1 convolution_convert_fusion.4
  99.0 20.4 %all-to-all-done.2 = bf16[4,1,8,16,896]{4,3,0,1,2:T(8,128)(2,1)} async-done(((bf16[4,1,8,16,896]{4,3,0,1,2:T(8,128)(2,1)}), bf16[4,1,8,16,896]{4,3,0,1,2:T(8,128)(2,1)}, u32[]{:S(2)}, u32[]{:S(2)}) %all-to-all-start.2) | async-done | bytes 917536 | tf_op jit(solution)/shard_map/all_to_all | solution.py:104
  119.4 2.0 %reduce_sum.87 = bf16[4,16,896]{2,1,0:T(8,128)(2,1)} reduce(bf16[4,1,8,16,896]{4,3,0,1,2:T(8,128)(2,1)} %all-to-all-done.2, bf16[]{:T(256)} %constant.46.clone.1), dimensions={1,2}, to_apply=%region_7.8 | reduce | flops 401408 | bytes 1032194 | tf_op jit(solution)/shard_map/reduce_sum | solution.py:107
  121.4 3.3 %all-to-all-start.3 = ((bf16[4,1,16,896]{3,2,1,0:T(8,128)(2,1)}), bf16[4,1,16,896]{3,2,1,0:T(8,128)(2,1)S(1)}, u32[]{:S(2)}, u32[]{:S(2)}) async-start(bf16[4,1,16,896]{3,2,1,0:T(8,128)(2,1)} %bitcast.19), calls=%async_computation.3 | async-start | bytes 229376 | tf_op jit(solution)/shard_map/all_to_all | solution.py:112
  125.3 4.3 %all-to-all-done.3 = bf16[4,1,16,896]{3,2,1,0:T(8,128)(2,1)S(1)} async-done(((bf16[4,1,16,896]{3,2,1,0:T(8,128)(2,1)}), bf16[4,1,16,896]{3,2,1,0:T(8,128)(2,1)S(1)}, u32[]{:S(2)}, u32[]{:S(2)}) %all-to-all-start.3) | async-done | bytes 114720 | tf_op jit(solution)/shard_map/all_to_all | solution.py:112
  129.7 1.4 convolution_convert_fusion
  (57 shorter events, 8.4 us)
Async XLA Ops:
  7.2 3.8 %copy-start = (bf16[128,3584]{1,0:T(8,128)(2,1)S(1)}, bf16[128,3584]{1,0:T(8,128)(2,1)}, u32[]{:S(2)}) copy-start(bf16[128,3584]{1,0:T(8,128)(2,1)} %param.10) | copy-start | bytes 2752516
  7.2 43.5 %all-gather.4.cloned.1.call-start = ((), (), s32[]{:S(2)}) async-start(), calls=%async_computation.5 | async-start | bytes 2064384 | tf_op jit(solution)/shard_map/all_gather | solution.py:55
  11.0 12.8 %copy-start.7 = (s32[4,1]{0,1:T(1,128)S(1)}, s32[4,1]{0,1:T(1,128)}, u32[]{:S(2)}) copy-start(s32[4,1]{0,1:T(1,128)} %param.14) | copy-start | bytes 52
  11.0 13.4 %copy-start.8 = (u32[32]{0:T(128)S(1)}, u32[32]{0:T(128)}, u32[]{:S(2)}) copy-start(u32[32]{0:T(128)} %constant.51) | copy-start | bytes 388
  11.0 14.6 %copy-start.5 = (bf16[128,8]{0,1:T(8,128)(2,1)S(1)}, bf16[128,8]{0,1:T(8,128)(2,1)}, u32[]{:S(2)}) copy-start(bf16[128,8]{0,1:T(8,128)(2,1)} %param.12) | copy-start | bytes 6148
  41.7 0.6 copy-start.9
  42.4 9.9 %copy-start.6 = (pred[8,1,16]{2,0,1:T(8,128)(4,1)}, pred[8,1,16]{2,0,1:T(8,128)(4,1)S(1)}, u32[]{:S(2)}) copy-start(pred[8,1,16]{2,0,1:T(8,128)(4,1)S(1)} %reshape.440) | copy-start | bytes 388
  42.5 9.8 %copy-start.10 = (s32[8]{0:T(128)}, s32[8]{0:T(128)S(1)}, u32[]{:S(2)}) copy-start(s32[8]{0:T(128)S(1)} %convert_reduce_fusion.1) | copy-start | bytes 100
  52.3 0.9 copy-start.2
  52.4 1.4 copy-start.1
  53.7 0.9 copy-start.4
  56.1 15.0 %all-to-all-start.1 = ((f32[4,128,384]{1,2,0:T(8,128)}), f32[4,128,384]{1,2,0:T(8,128)S(1)}, u32[]{:S(2)}, u32[]{:S(2)}) async-start(f32[4,128,384]{1,2,0:T(8,128)} %copy_bitcast_fusion), calls=%async_computation.1 | async-start | bytes 1572864 | tf_op jit(solution)/shard_map/all_to_all | solution.py:78
  71.7 17.3 %copy-start.3 = (bf16[896,128]{1,0:T(8,128)(2,1)S(1)}, bf16[896,128]{1,0:T(8,128)(2,1)}, u32[]{:S(2)}) copy-start(bf16[896,128]{1,0:T(8,128)(2,1)} %param.16) | copy-start | bytes 688132
  74.9 15.6 %all-to-all-start.4 = ((bf16[8,1,16]{2,1,0:T(2,128)(2,1)}), bf16[8,1,16]{2,1,0:T(2,128)(2,1)S(1)}, u32[]{:S(2)}, u32[]{:S(2)}) async-start(bf16[8,1,16]{2,1,0:T(2,128)(2,1)} %copy.46), calls=%async_computation.4 | async-start | bytes 8192 | tf_op jit(solution)/shard_map/all_to_all | solution.py:116
  90.5 28.9 %all-to-all-start.2 = ((bf16[4,1,8,16,896]{4,3,0,1,2:T(8,128)(2,1)}), bf16[4,1,8,16,896]{4,3,0,1,2:T(8,128)(2,1)}, u32[]{:S(2)}, u32[]{:S(2)}) async-start(bf16[4,1,8,16,896]{4,3,0,1,2:T(8,128)(2,1)} %copy.42), calls=%async_computation.2 | async-start | bytes 1835008 | tf_op jit(solution)/shard_map/all_to_all | solution.py:104
  121.4 8.3 %all-to-all-start.3 = ((bf16[4,1,16,896]{3,2,1,0:T(8,128)(2,1)}), bf16[4,1,16,896]{3,2,1,0:T(8,128)(2,1)S(1)}, u32[]{:S(2)}, u32[]{:S(2)}) async-start(bf16[4,1,16,896]{3,2,1,0:T(8,128)(2,1)} %bitcast.19), calls=%async_computation.3 | async-start | bytes 229376 | tf_op jit(solution)/shard_map/all_to_all | solution.py:112
Sparse Core Ops, SparseCore 0:
  23.9 26.7 all-gather.3

commit v2 on v1

v2 whole, which is shorter than its diff:
```python
import functools

import jax
import jax.numpy as jnp
from jax import lax
from jax.experimental import pallas as pl
from jax.experimental.pallas import tpu as pltpu
from jax.sharding import PartitionSpec as P

EXPERTS = 128
SLOT = 16
BLOCK = 128
SPLIT = 8
CORES = 2
CHIPS = SPLIT // CORES
LANES = 128
F32 = jnp.float32
BF16 = jnp.bfloat16
SMEM = pl.BlockSpec(memory_space=pltpu.SMEM)
VMEM = pl.BlockSpec(memory_space=pltpu.VMEM)


def shape(dims, kind=BF16):
    return jax.ShapeDtypeStruct(dims, kind)


def call(kernel, outs, args, scalars=0, scratch=(), flops=0):
    size = sum(a.size * a.dtype.itemsize for a in args) + sum(
        o.size * o.dtype.itemsize for o in outs
    )
    return pl.pallas_call(
        kernel,
        out_shape=tuple(outs),
        in_specs=[SMEM] * scalars + [VMEM] * (len(args) - scalars),
        out_specs=tuple([VMEM] * len(outs)),
        scratch_shapes=scratch,
        compiler_params=pltpu.CompilerParams(vmem_limit_bytes=40 * 1024 * 1024),
        cost_estimate=pl.CostEstimate(flops=flops, bytes_accessed=size, transcendentals=0),
    )(*args)


def dot(a, b, dims=((1,), (0,))):
    return lax.dot_general(a, b, (dims, ((), ())), preferred_element_type=F32)


def iota(dims, axis):
    return lax.broadcasted_iota(jnp.int32, dims, axis)


def pack_kernel(rep, flight, live_ref, tok_ref, grad_ref, ids_ref, rw_ref, *refs):
    pays, hdr_ref, placed_ref, rows = refs[:rep], refs[rep], refs[rep + 1], refs[rep + 2]
    r = lax.axis_index("rep")
    mine = lax.axis_index("ep") // SPLIT
    count = tok_ref.shape[0]
    width = tok_ref.shape[1] // rep
    spacing = EXPERTS // flight
    token = iota((count, 1), 0)
    lower = (iota((count, count), 1) <= iota((count, count), 0)).astype(BF16)
    lane = iota((count, LANES), 1)
    weights = rw_ref[...].astype(F32)
    header = jnp.zeros((SLOT, LANES), F32)
    for w in range(flight):
        expert = jnp.bitwise_xor(mine, w)
        match = ids_ref[...] == expert * spacing
        routed = jnp.any(match, axis=1, keepdims=True) & (token < live_ref[r])
        weight = jnp.sum(jnp.where(match, weights, 0.0), axis=1, keepdims=True)
        routed_f = jnp.broadcast_to(jnp.where(routed, 1.0, 0.0), (count, LANES))
        rank = dot(lower, routed_f.astype(BF16)) - 1.0
        placed = jnp.where((rank == (lane % SLOT).astype(F32)), routed_f, 0.0).astype(BF16)
        placed_ref[w] = placed
        first = placed[:, :SLOT]
        header += dot(first, jnp.where(lane == expert, weight, 0.0).astype(BF16), ((0,), (0,)))
        for part, ref in enumerate((tok_ref, grad_ref)):
            chosen = dot(first, ref[...], ((0,), (0,))).astype(BF16)
            for b in range(rep):
                rows[b, w, part] = chosen[:, b * width : (b + 1) * width]
    hdr_ref[0] = header
    for k in range(rep):
        pays[k][...] = rows[jnp.bitwise_xor(r, k)]


def join_kernel(rep, flight, *refs):
    pays, xs, dys = refs[:rep], refs[rep : rep + flight], refs[rep + flight :]
    for w in range(flight):
        for k in range(rep):
            xs[w][k] = pays[k][w, 0]
            dys[w][k] = pays[k][w, 1]


def forward_kernel(rep, count, *refs):
    blocks, own_w, other_w = refs[:count], refs[count], refs[count + 1]
    sums, rows_ref = refs[count + 2 : count + 2 + rep], refs[count + 2 + rep]
    width = own_w.shape[0]
    units = own_w.shape[1]
    for k in range(rep):
        rows = jnp.concatenate([b[k] for b in blocks], axis=0)
        rows_ref[k] = rows
        sums[k][:, :units] = dot(rows, own_w[...]).astype(sums[k].dtype)
        sums[k][:, units:] = dot(rows, other_w[...]).astype(sums[k].dtype)


def hidden_kernel(rep, count, units, cap_ref, hdr_ref, *refs):
    sums_x, sums_d = refs[:rep], refs[rep : 2 * rep]
    weights = refs[2 * rep : 4 * rep]
    back_refs, grad_refs = refs[4 * rep : 4 * rep + count], refs[4 * rep + count :]
    r = lax.axis_index("rep")
    e = lax.axis_index("ep")
    mine = e // SPLIT
    width = weights[0].shape[0]
    ep = hdr_ref.shape[0]
    rates = jnp.where(iota(hdr_ref.shape, 2) == mine, hdr_ref[...], 0.0)
    rates = jnp.sum(rates, axis=2, keepdims=True)
    present = rates > 0.0
    counts = jnp.sum(jnp.where(present, 1.0, 0.0), axis=1, keepdims=True)
    order = jnp.bitwise_xor(iota((ep, 1, 1), 0), e)
    capacity = (BLOCK * cap_ref[r, mine]).astype(F32)
    slot = iota((SLOT, 1), 0).astype(F32)
    rate_rows, kept_rows = [], []
    for j in range(count):
        source = CORES * j
        before = jnp.where(order < jnp.bitwise_xor(e, source), counts, 0.0)
        start = jnp.sum(before, axis=0)
        kept = jnp.where(present[source] & (start + slot < capacity), 1.0, 0.0)
        kept_rows.append(kept)
        rate_rows.append(rates[source] * kept)
    rate = jnp.concatenate(rate_rows, axis=0)
    kept = jnp.concatenate(kept_rows, axis=0)

    total_x = sums_x[0][...]
    total_d = sums_d[0][...]
    for k in range(1, rep):
        total_x = total_x + sums_x[k][...].astype(F32)
        total_d = total_d + sums_d[k][...].astype(F32)
    lane = iota((count * SLOT, LANES), 1)
    scores = jnp.zeros((count * SLOT, LANES), F32)
    pairs = []
    for i in range(CORES):
        pre_gate = total_x[:, 2 * i * units : (2 * i + 1) * units]
        pre_up = total_x[:, (2 * i + 1) * units : (2 * i + 2) * units]
        back_hidden = total_d[:, i * units : (i + 1) * units]
        sig = 1.0 / (1.0 + jnp.exp(-pre_gate))
        activated = pre_gate * sig
        hidden = activated * pre_up
        score = jnp.sum(hidden * back_hidden, axis=1, keepdims=True) * kept
        scores = jnp.where(lane == i, score, scores)
        scaled = back_hidden * rate
        gate_grad = (scaled * pre_up * sig * (1.0 + pre_gate * (1.0 - sig))).astype(BF16)
        up_grad = (scaled * activated).astype(BF16)
        grad_refs[i][:, :units] = gate_grad
        grad_refs[i][:, units : 2 * units] = up_grad
        grad_refs[i][:, 2 * units :] = (hidden * rate).astype(BF16)
        pairs.append(jnp.concatenate([gate_grad, up_grad], axis=1))
    for k in range(rep):
        back = dot(pairs[0], weights[2 * k][...], ((1,), (1,)))
        back = back + dot(pairs[1], weights[2 * k + 1][...], ((1,), (1,)))
        back = back.astype(BF16)
        for j in range(count):
            back_refs[j][:, k * width : (k + 1) * width] = back[j * SLOT : (j + 1) * SLOT]
    scores = scores.astype(BF16)
    for j in range(count):
        back_refs[j][:, rep * width :] = scores[j * SLOT : (j + 1) * SLOT]


def weight_kernel(rep, units, x_own, x_other, d_own, d_other, *refs):
    grads, outs = refs[: 2 * rep], refs[2 * rep :]
    width = x_own.shape[2]
    gate_up = jnp.zeros((width, 2 * units), F32)
    down = jnp.zeros((width, units), F32)
    for i, (x_ref, d_ref) in enumerate(((x_own, d_own), (x_other, d_other))):
        got = jnp.concatenate([grads[2 * k + i][...] for k in range(rep)], axis=0)
        rows = x_ref[...].reshape(got.shape[0], width)
        gate_up = gate_up + dot(rows, got[:, : 2 * units], ((0,), (0,)))
        rows = d_ref[...].reshape(got.shape[0], width)
        down = down + dot(rows, got[:, 2 * units :], ((0,), (0,)))
    outs[0][...] = gate_up[:, :units].astype(BF16)
    outs[1][...] = gate_up[:, units:].astype(BF16)
    outs[2][...] = down.astype(BF16)


def token_kernel(rep, flight, placed_ref, ids_ref, *refs):
    backs, out_ref, weight_ref, blocks = refs[:-3], refs[-3], refs[-2], refs[-1]
    r = lax.axis_index("rep")
    mine = lax.axis_index("ep") // SPLIT
    spacing = EXPERTS // flight
    width = out_ref.shape[1] // rep
    depth = CHIPS * SLOT
    joined = [
        jnp.concatenate([b[...] for b in backs[w * CHIPS : (w + 1) * CHIPS]], axis=0)
        for w in range(flight)
    ]
    for k in range(rep):
        total = jnp.zeros((out_ref.shape[0], width), F32)
        for w in range(flight):
            total = total + dot(placed_ref[w][:, :depth], joined[w][:, k * width : (k + 1) * width])
        blocks[jnp.bitwise_xor(r, k)] = total.astype(BF16)
    for b in range(rep):
        out_ref[:, b * width : (b + 1) * width] = blocks[b]
    result = jnp.zeros(weight_ref.shape, F32)
    for w in range(flight):
        score = dot(placed_ref[w][:, :depth], joined[w][:, rep * width :])
        score = jnp.sum(score, axis=1, keepdims=True)
        match = ids_ref[...] == jnp.bitwise_xor(mine, w) * spacing
        result = result + jnp.where(match, score, 0.0)
    weight_ref[...] = result


def local(
    tokens, out_grad, expert_ids, route_weight, live_count, cap_blocks, w_gate, w_up, w_down_t
):
    rep = lax.axis_size("rep")
    ep = lax.axis_size("ep")
    flight = ep // SPLIT
    count = ep // CORES
    tok_count, model_dim = tokens.shape
    width, units = w_gate.shape
    rows = count * SLOT

    def send(array, rep_bits, ep_bits):
        mask = rep_bits * ep + ep_bits
        pairs = [(a, a ^ mask) for a in range(rep * ep)]
        return lax.ppermute(array, ("rep", "ep"), pairs)

    packed = call(
        functools.partial(pack_kernel, rep, flight),
        [shape((flight, 2, SLOT, width))] * rep
        + [shape((1, SLOT, LANES), F32), shape((flight, tok_count, LANES))],
        [live_count, tokens, out_grad, expert_ids, route_weight],
        scalars=1,
        scratch=[pltpu.VMEM((rep, flight, 2, SLOT, width), BF16)],
    )
    pays, header, placed = packed[:rep], packed[rep], packed[rep + 1]
    pays = [pays[0]] + [send(pays[k], k, 0) for k in range(1, rep)]
    gate_up = jnp.concatenate([w_gate, w_up], axis=1)
    gate_up_other, down_other = send(gate_up, 0, 1), send(w_down_t, 0, 1)
    bit = 1
    while bit < ep:
        header = jnp.concatenate([header, send(header, 0, bit)], axis=0)
        bit *= 2

    joined = call(
        functools.partial(join_kernel, rep, flight),
        [shape((rep, SLOT, width))] * (2 * flight),
        pays,
    )
    gate_up_late, joined = lax.optimization_barrier((gate_up, joined))
    xs, dys = joined[:flight], joined[flight:]
    x_blocks = [xs[0]] + [send(xs[j // CHIPS], 0, CORES * j) for j in range(1, count)]
    dy_blocks = [dys[0]] + [send(dys[j // CHIPS], 0, CORES * j) for j in range(1, count)]
    stored = [gate_up, gate_up_other]
    for k in range(1, rep):
        moved = send(gate_up_late, k, 0)
        stored += [moved, send(moved, 0, 1)]

    def forward(blocks, own, other):
        columns = 2 * own.shape[1]
        results = call(
            functools.partial(forward_kernel, rep, count),
            [shape((rows, columns), F32)]
            + [shape((rows, columns))] * (rep - 1)
            + [shape((rep, rows, width))],
            blocks + [own, other],
            flops=2 * rep * rows * width * columns,
        )
        sums, all_rows = results[:rep], results[rep]
        return [sums[0]] + [send(sums[k], k, 0) for k in range(1, rep)], all_rows

    sums_x, x_rows = forward(x_blocks, gate_up, gate_up_other)
    sums_d, dy_rows = forward(dy_blocks, w_down_t, down_other)
    x_rows_other, dy_rows_other = send(x_rows, 0, 1), send(dy_rows, 0, 1)

    results = call(
        functools.partial(hidden_kernel, rep, count, units),
        [shape((SLOT, model_dim + LANES))] * count + [shape((rows, 3 * units))] * CORES,
        [cap_blocks, header] + sums_x + sums_d + stored,
        scalars=1,
        flops=2 * rows * model_dim * 4 * units,
    )
    backs, grads = results[:count], results[count:]
    backs = [backs[0]] + [send(backs[j], 0, CORES * j) for j in range(1, count)]
    grads = [
        grads[i] if k + i == 0 else send(grads[i], k, i) for k in range(rep) for i in range(CORES)
    ]

    grad_gate, grad_up, grad_down = call(
        functools.partial(weight_kernel, rep, units),
        [shape((width, units))] * 3,
        [x_rows, x_rows_other, dy_rows, dy_rows_other] + grads,
        flops=2 * 2 * rep * rows * width * 3 * units,
    )
    grad_tokens, grad_weight = call(
        functools.partial(token_kernel, rep, flight),
        [shape((tok_count, model_dim)), shape(expert_ids.shape, F32)],
        [placed, expert_ids] + backs,
        scratch=[pltpu.VMEM((rep, tok_count, width), BF16)],
        flops=2 * tok_count * CHIPS * SLOT * model_dim,
    )
    return grad_tokens, grad_weight, grad_gate, grad_up, grad_down


def solution(mesh):
    return jax.shard_map(
        local,
        mesh=mesh,
        in_specs=(
            P(("rep", "ep"), None),
            P(("rep", "ep"), None),
            P(("rep", "ep"), None),
            P(("rep", "ep"), None),
            P(),
            P(),
            P("rep", "ep"),
            P("rep", "ep"),
            P("rep", "ep"),
        ),
        out_specs=(
            P(("rep", "ep"), None),
            P(("rep", "ep"), None),
            P("rep", "ep"),
            P("rep", "ep"),
            P("rep", "ep"),
        ),
        check_vma=False,
    )
```

time: 139 us -> 92.9 us (0.67)
  blocking collectives: 35.9 us -> 0 us
  starting transfers between devices: 15.2 us -> 37.4 us
  between operations: 15 us -> 0.84 us
  other arithmetic: 13.9 us -> 0.81 us
  matrix products: 9.75 us -> 0 us
  Pallas kernels: 0 us -> 9.13 us
  waiting for transfers between devices: 39.2 us -> 33.5 us
  local copies, waits for them, and re-layouts: 9.07 us -> 10.7 us
    ppermute x0 -> x38, starting transfers between devices: none -> 37.4 us  [send(): return lax.ppermute(array, ('rep', 'ep'), pairs)]
    ppermute x0 -> x38, waiting for transfers between devices: none -> 33.5 us  [send(): return lax.ppermute(array, ('rep', 'ep'), pairs)]
    all_to_all x4 -> x0, waiting for transfers between devices: 31.7 us -> none  [the longest x1 20.4 us: local(): lax.all_to_all(partial_x, 'ep', split_axis=2, concat_axis=2, tiled=True,...]
    unnamed x1 -> x0, blocking collectives: 15.7 us -> none
    all_to_all x4 -> x0, starting transfers between devices: 15.2 us -> none  [the longest x1 5.02 us: local(): lax.all_to_all(partial_x, 'ep', split_axis=2, concat_axis=2, tiled=True,...]
    all_to_all x1 -> x0, blocking collectives: 10.7 us -> none  [local(): got = lax.all_to_all(send, 'rep', split_axis=0, concat_axis=0, tiled=True)]
    dot_general x11 -> x0, matrix products: 9.75 us -> none  [the longest x3 3.41 us: weight_grad(): lax.dot_general(inputs, hidden_grad, contract_rows, preferred_element_typ...]
    all_gather x1 -> x0, blocking collectives: 9.47 us -> none  [local(): grads = lax.all_gather(grads, 'rep', axis=0, tiled=True)]
  transfers between devices with their start and end apart: 5 -> 38, of which waited for: 4 -> 15; matrix products, arithmetic and copies ran while one was open for 10% -> 1% of each run, Pallas kernels for 0% -> 7%
where the time goes in v2:
time: 92.9 us; the launch traced here: 92.4 us
  starting transfers between devices  37.4 us (40%)
  waiting for transfers between devices  33.5 us (36%)
  local copies, waits for them, and re-layouts  10.7 us (12%)
  Pallas kernels  9.13 us (10%)
    ppermute x38, starting transfers between devices, send(): return lax.ppermute(array, ('rep', 'ep'), pairs)  37.4 us
    ppermute x38, waiting for transfers between devices, send(): return lax.ppermute(array, ('rep', 'ep'), pairs)  33.5 us
    unnamed x51, local copies, waits for them, and re-layouts  10.6 us
    pallas_call x7, Pallas kernels, call(): pl.pallas_call(kernel, out_shape=tuple(outs), in_specs=[SMEM] * scalars +...  9.13 us
  transfers between devices with their start and end apart: 38, of which 15 were waited for; matrix products, arithmetic and copies ran while one was open for 1% of the time, Pallas kernels for 7%

profile of v2, /device:TPU:0, one launch (start us, length us, event | category | flops | bytes accessed | tf_op | source)
XLA Modules:
  0.0 92.4 jit_solution(2600293050024831640)
XLA Ops:
  2.1 1.2 %copy-done = bf16[128,3584]{1,0:T(8,128)(2,1)S(1)} copy-done((bf16[128,3584]{1,0:T(8,128)(2,1)S(1)}, bf16[128,3584]{1,0:T(8,128)(2,1)}, u32[]{:S(2)}) %copy-start) | copy-done | bytes 917528
  3.3 1.2 %copy-done.1 = bf16[128,3584]{1,0:T(8,128)(2,1)S(1)} copy-done((bf16[128,3584]{1,0:T(8,128)(2,1)S(1)}, bf16[128,3584]{1,0:T(8,128)(2,1)}, u32[]{:S(2)}) %copy-start.1) | copy-done | bytes 917528
  4.5 1.2 %shard_map.128 = (bf16[1,2,16,896]{3,2,1,0:T(8,128)(2,1)S(1)}, bf16[1,2,16,896]{3,2,1,0:T(8,128)(2,1)S(1)}, bf16[1,2,16,896]{3,2,1,0:T(8,128)(2,1)S(1)}, bf16[1,...) custom-call(s32[4]{0:T(128)S(1)} %copy-done.15, ...), custom_call_target="tpu_custom_call" | custom-call | bytes 2111504 | tf_op jit(solution)/shard_map/pallas_call | solution.py:31
  6.2 2.6 %collective-permute-start.3 = (bf16[1,2,16,896]{3,2,1,0:T(8,128)(2,1)S(1)}, bf16[1,2,16,896]{3,2,1,0:T(8,128)(2,1)S(1)}, u32[]{:S(2)}, u32[]{:S(2)}) collective-permute-start(bf16[1,2,16,896]{3,2,1,0:T(8,128)(2,1)S(1)} %get-tuple-element.40), channel_id=1, source_target_pairs={{0,8},{1,9},{2,10},{3,11},{4,12},{5,13},{6,14},{7,15},{8,0},{9,1},... | collective-permute-start | bytes 172040 | tf_op jit(solution)/shard_map/ppermute | solution.py:221
  8.8 1.5 %collective-permute-start.4 = (bf16[1,2,16,896]{3,2,1,0:T(8,128)(2,1)S(1)}, bf16[1,2,16,896]{3,2,1,0:T(8,128)(2,1)S(1)}, u32[]{:S(2)}, u32[]{:S(2)}) collective-permute-start(bf16[1,2,16,896]{3,2,1,0:T(8,128)(2,1)S(1)} %get-tuple-element.41), channel_id=1, source_target_pairs={{0,16},{1,17},{2,18},{3,19},{4,20},{5,21},{6,22},{7,23},{8,24},{9,... | collective-permute-start | bytes 172040 | tf_op jit(solution)/shard_map/ppermute | solution.py:221
  10.4 2.1 %collective-permute-start.1 = (f32[2,16,128]{2,1,0:T(8,128)S(1)}, f32[2,16,128]{2,1,0:T(8,128)S(1)}, u32[]{:S(2)}, u32[]{:S(2)}) collective-permute-start(f32[2,16,128]{2,1,0:T(8,128)S(1)} %pad_maximum_fusion.2), channel_id=1, source_target_pairs={{0,2},{1,3},{2,0},{3,1},{4,6},{5,7},{6,4},{7,5},{8,10},{9,11},{10,... | collective-permute-start | bytes 49160 | tf_op jit(solution)/shard_map/ppermute | solution.py:221
  12.9 2.4 %collective-permute-done.5.refs_3_ = bf16[1,2,16,896]{3,2,1,0:T(8,128)(2,1)S(1)} collective-permute-done((bf16[1,2,16,896]{3,2,1,0:T(8,128)(2,1)S(1)}, bf16[1,2,16,896]{3,2,1,0:T(8,128)(2,1)S(1)}, u32[]{:S(2)}, u32[]{:S(2)}) %collective-permute-start.5) | collective-permute-done | bytes 57376 | tf_op jit(solution)/shard_map/ppermute | solution.py:221
  15.4 1.6 %collective-permute-start.6 = (bf16[4,16,896]{2,1,0:T(8,128)(2,1)S(1)}, bf16[4,16,896]{2,1,0:T(8,128)(2,1)S(1)}, u32[]{:S(2)}, u32[]{:S(2)}) collective-permute-start(bf16[4,16,896]{2,1,0:T(8,128)(2,1)S(1)} %get-tuple-element.45.refs_0_), channel_id=1, source_target_pairs={{0,2},{1,3},{2,0},{3,1},{4,6},{5,7},{6,4},{7,5},{8,10},{9,11},{10,... | collective-permute-start | bytes 344072 | tf_op jit(solution)/shard_map/ppermute | solution.py:221
  17.6 2.6 %collective-permute-start.2 = (f32[4,16,128]{2,1,0:T(8,128)S(1)}, f32[4,16,128]{2,1,0:T(8,128)S(1)}, u32[]{:S(2)}, u32[]{:S(2)}) collective-permute-start(f32[4,16,128]{2,1,0:T(8,128)S(1)} %pad_maximum_fusion.1), channel_id=1, source_target_pairs={{0,4},{1,5},{2,6},{3,7},{4,0},{5,1},{6,2},{7,3},{8,12},{9,13},{10,... | collective-permute-start | bytes 98312 | tf_op jit(solution)/shard_map/ppermute | solution.py:221
  21.0 2.6 %collective-permute-start.14 = (bf16[4,16,896]{2,1,0:T(8,128)(2,1)S(1)}, bf16[4,16,896]{2,1,0:T(8,128)(2,1)S(1)}, u32[]{:S(2)}, u32[]{:S(2)}) collective-permute-start(bf16[4,16,896]{2,1,0:T(8,128)(2,1)S(1)} %get-tuple-element.50.refs_0_), channel_id=1, source_target_pairs={{0,4},{1,5},{2,6},{3,7},{4,0},{5,1},{6,2},{7,3},{8,12},{9,13},{10,... | collective-permute-start | bytes 344072 | tf_op jit(solution)/shard_map/ppermute | solution.py:221
  24.2 1.5 %collective-permute-start.15 = (bf16[4,16,896]{2,1,0:T(8,128)(2,1)S(1)}, bf16[4,16,896]{2,1,0:T(8,128)(2,1)S(1)}, u32[]{:S(2)}, u32[]{:S(2)}) collective-permute-start(bf16[4,16,896]{2,1,0:T(8,128)(2,1)S(1)} %get-tuple-element.50.refs_0_), channel_id=1, source_target_pairs={{0,6},{1,7},{2,4},{3,5},{4,2},{5,3},{6,0},{7,1},{8,14},{9,15},{10,... | collective-permute-start | bytes 344072 | tf_op jit(solution)/shard_map/ppermute | solution.py:221
  25.7 7.6 %collective-permute-done.7.refs_2_ = bf16[4,16,896]{2,1,0:T(8,128)(2,1)S(1)} collective-permute-done((bf16[4,16,896]{2,1,0:T(8,128)(2,1)S(1)}, bf16[4,16,896]{2,1,0:T(8,128)(2,1)S(1)}, u32[]{:S(2)}, u32[]{:S(2)}) %collective-permute-start.7) | collective-permute-done | bytes 114720 | tf_op jit(solution)/shard_map/ppermute | solution.py:221
  34.4 1.4 %collective-permute-done.14.refs_2_ = bf16[4,16,896]{2,1,0:T(8,128)(2,1)S(1)} collective-permute-done((bf16[4,16,896]{2,1,0:T(8,128)(2,1)S(1)}, bf16[4,16,896]{2,1,0:T(8,128)(2,1)S(1)}, u32[]{:S(2)}, u32[]{:S(2)}) %collective-permute-start.14) | collective-permute-done | bytes 114720 | tf_op jit(solution)/shard_map/ppermute | solution.py:221
  35.8 1.0 %collective-permute-start.24 = (bf16[896,256]{1,0:T(8,128)(2,1)S(1)}, bf16[896,256]{1,0:T(8,128)(2,1)S(1)}, u32[]{:S(2)}, u32[]{:S(2)}) collective-permute-start(bf16[896,256]{1,0:T(8,128)(2,1)S(1)} %constant_dynamic-update-slice_fusion.refs_4_.refs_8_), channel_id=1, source_target_pairs={{0,24},{1,25},{2,26},{3,27},{4,28},{5,29},{6,30},{7,31},{8,16},{9,... | collective-permute-start | bytes 1376264 | tf_op jit(solution)/shard_map/ppermute | solution.py:221
  36.8 1.5 %collective-permute-done.16.refs_5_ = bf16[896,128]{1,0:T(8,128)(2,1)S(1)} collective-permute-done((bf16[896,128]{1,0:T(8,128)(2,1)S(1)}, bf16[896,128]{1,0:T(8,128)(2,1)S(1)}, u32[]{:S(2)}, u32[]{:S(2)}) %collective-permute-start.16) | collective-permute-done | bytes 229408 | tf_op jit(solution)/shard_map/ppermute | solution.py:221
  38.3 1.1 %collective-permute-start.8 = (bf16[4,16,896]{2,1,0:T(8,128)(2,1)S(1)}, bf16[4,16,896]{2,1,0:T(8,128)(2,1)S(1)}, u32[]{:S(2)}, u32[]{:S(2)}) collective-permute-start(bf16[4,16,896]{2,1,0:T(8,128)(2,1)S(1)} %get-tuple-element.45.refs_0_), channel_id=1, source_target_pairs={{0,6},{1,7},{2,4},{3,5},{4,2},{5,3},{6,0},{7,1},{8,14},{9,15},{10,... | collective-permute-start | bytes 344072 | tf_op jit(solution)/shard_map/ppermute | solution.py:221
  39.9 5.5 %collective-permute-done.8.refs_3_ = bf16[4,16,896]{2,1,0:T(8,128)(2,1)S(1)} collective-permute-done((bf16[4,16,896]{2,1,0:T(8,128)(2,1)S(1)}, bf16[4,16,896]{2,1,0:T(8,128)(2,1)S(1)}, u32[]{:S(2)}, u32[]{:S(2)}) %collective-permute-start.8) | collective-permute-done | bytes 114720 | tf_op jit(solution)/shard_map/ppermute | solution.py:221
  46.3 1.4 %collective-permute-start.18 = (bf16[64,256]{1,0:T(8,128)(2,1)S(1)}, bf16[64,256]{1,0:T(8,128)(2,1)S(1)}, u32[]{:S(2)}, u32[]{:S(2)}) collective-permute-start(bf16[64,256]{1,0:T(8,128)(2,1)S(1)} %get-tuple-element.53), channel_id=1, source_target_pairs={{0,16},{1,17},{2,18},{3,19},{4,20},{5,21},{6,22},{7,23},{8,24},{9,... | collective-permute-start | bytes 98312 | tf_op jit(solution)/shard_map/ppermute | solution.py:221
  48.5 4.3 %collective-permute-done.17.refs_5_ = bf16[64,256]{1,0:T(8,128)(2,1)S(1)} collective-permute-done((bf16[64,256]{1,0:T(8,128)(2,1)S(1)}, bf16[64,256]{1,0:T(8,128)(2,1)S(1)}, u32[]{:S(2)}, u32[]{:S(2)}) %collective-permute-start.17) | collective-permute-done | bytes 32800 | tf_op jit(solution)/shard_map/ppermute | solution.py:221
  54.6 1.4 %collective-permute-start.19 = (bf16[64,256]{1,0:T(8,128)(2,1)S(1)}, bf16[64,256]{1,0:T(8,128)(2,1)S(1)}, u32[]{:S(2)}, u32[]{:S(2)}) collective-permute-start(bf16[64,256]{1,0:T(8,128)(2,1)S(1)} %get-tuple-element.54), channel_id=1, source_target_pairs={{0,24},{1,25},{2,26},{3,27},{4,28},{5,29},{6,30},{7,31},{8,16},{9,... | collective-permute-start | bytes 98312 | tf_op jit(solution)/shard_map/ppermute | solution.py:221
  56.0 3.4 %collective-permute-done.19.refs_7_ = bf16[64,256]{1,0:T(8,128)(2,1)S(1)} collective-permute-done((bf16[64,256]{1,0:T(8,128)(2,1)S(1)}, bf16[64,256]{1,0:T(8,128)(2,1)S(1)}, u32[]{:S(2)}, u32[]{:S(2)}) %collective-permute-start.19) | collective-permute-done | bytes 32800 | tf_op jit(solution)/shard_map/ppermute | solution.py:221
  60.1 2.8 %collective-permute-start.12 = (bf16[64,512]{1,0:T(8,128)(2,1)S(1)}, bf16[64,512]{1,0:T(8,128)(2,1)S(1)}, u32[]{:S(2)}, u32[]{:S(2)}) collective-permute-start(bf16[64,512]{1,0:T(8,128)(2,1)S(1)} %get-tuple-element.49), channel_id=1, source_target_pairs={{0,24},{1,25},{2,26},{3,27},{4,28},{5,29},{6,30},{7,31},{8,16},{9,... | collective-permute-start | bytes 196616 | tf_op jit(solution)/shard_map/ppermute | solution.py:221
  69.3 2.6 %shard_map.132 = (bf16[16,3712]{1,0:T(8,128)(2,1)S(1)}, bf16[16,3712]{1,0:T(8,128)(2,1)S(1)}, bf16[16,3712]{1,0:T(8,128)(2,1)S(1)}, bf16[16,3712]{1,0:T(8,128)(2...) custom-call(s32[4,1]{1,0:T(4,128)S(1)} %copy.16.cap_ref, f32[8,16,128]{2,1,0:T(8,128)S(1)} %pad_maximum_fusion.hdr_ref, ...), custom_call_target="tpu_custom_call" | custom-call | flops 234881024 | bytes 4800528 | tf_op jit(solution)/shard_map/pallas_call | solution.py:31
  72.4 1.8 %collective-permute-start.32 = (bf16[64,384]{1,0:T(8,128)(2,1)S(1)}, bf16[64,384]{1,0:T(8,128)(2,1)S(1)}, u32[]{:S(2)}, u32[]{:S(2)}) collective-permute-start(bf16[64,384]{1,0:T(8,128)(2,1)S(1)} %get-tuple-element.64.refs_0_), channel_id=1, source_target_pairs={{0,8},{1,9},{2,10},{3,11},{4,12},{5,13},{6,14},{7,15},{8,0},{9,1},... | collective-permute-start | bytes 147464 | tf_op jit(solution)/shard_map/ppermute | solution.py:221
  74.3 1.6 %collective-permute-start.34 = (bf16[64,384]{1,0:T(8,128)(2,1)S(1)}, bf16[64,384]{1,0:T(8,128)(2,1)S(1)}, u32[]{:S(2)}, u32[]{:S(2)}) collective-permute-start(bf16[64,384]{1,0:T(8,128)(2,1)S(1)} %get-tuple-element.64.refs_0_), channel_id=1, source_target_pairs={{0,16},{1,17},{2,18},{3,19},{4,20},{5,21},{6,22},{7,23},{8,24},{9,... | collective-permute-start | bytes 147464 | tf_op jit(solution)/shard_map/ppermute | solution.py:221
  76.5 1.3 %collective-permute-start.27 = (bf16[16,3712]{1,0:T(8,128)(2,1)S(1)}, bf16[16,3712]{1,0:T(8,128)(2,1)S(1)}, u32[]{:S(2)}, u32[]{:S(2)}) collective-permute-start(bf16[16,3712]{1,0:T(8,128)(2,1)S(1)} %get-tuple-element.58), channel_id=1, source_target_pairs={{0,4},{1,5},{2,6},{3,7},{4,0},{5,1},{6,2},{7,3},{8,12},{9,13},{10,... | collective-permute-start | bytes 356360 | tf_op jit(solution)/shard_map/ppermute | solution.py:221
  78.3 2.3 %collective-permute-start.28 = (bf16[16,3712]{1,0:T(8,128)(2,1)S(1)}, bf16[16,3712]{1,0:T(8,128)(2,1)S(1)}, u32[]{:S(2)}, u32[]{:S(2)}) collective-permute-start(bf16[16,3712]{1,0:T(8,128)(2,1)S(1)} %get-tuple-element.59), channel_id=1, source_target_pairs={{0,6},{1,7},{2,4},{3,5},{4,2},{5,3},{6,0},{7,1},{8,14},{9,15},{10,... | collective-permute-start | bytes 356360 | tf_op jit(solution)/shard_map/ppermute | solution.py:221
  80.6 2.6 %collective-permute-start.36 = (bf16[64,384]{1,0:T(8,128)(2,1)S(1)}, bf16[64,384]{1,0:T(8,128)(2,1)S(1)}, u32[]{:S(2)}, u32[]{:S(2)}) collective-permute-start(bf16[64,384]{1,0:T(8,128)(2,1)S(1)} %get-tuple-element.64.refs_0_), channel_id=1, source_target_pairs={{0,24},{1,25},{2,26},{3,27},{4,28},{5,29},{6,30},{7,31},{8,16},{9,... | collective-permute-start | bytes 147464 | tf_op jit(solution)/shard_map/ppermute | solution.py:221
  83.2 2.3 %collective-permute-done.36.refs_6_ = bf16[64,384]{1,0:T(8,128)(2,1)S(1)} collective-permute-done((bf16[64,384]{1,0:T(8,128)(2,1)S(1)}, bf16[64,384]{1,0:T(8,128)(2,1)S(1)}, u32[]{:S(2)}, u32[]{:S(2)}) %collective-permute-start.36) | collective-permute-done | bytes 49184 | tf_op jit(solution)/shard_map/ppermute | solution.py:221
  85.6 2.1 %collective-permute-done.37.refs_7_ = bf16[64,384]{1,0:T(8,128)(2,1)S(1)} collective-permute-done((bf16[64,384]{1,0:T(8,128)(2,1)S(1)}, bf16[64,384]{1,0:T(8,128)(2,1)S(1)}, u32[]{:S(2)}, u32[]{:S(2)}) %collective-permute-start.37) | collective-permute-done | bytes 49184 | tf_op jit(solution)/shard_map/ppermute | solution.py:221
  87.6 2.7 %shard_map.134 = (bf16[896,128]{1,0:T(8,128)(2,1)}, bf16[896,128]{1,0:T(8,128)(2,1)}, bf16[896,128]{1,0:T(8,128)(2,1)}) custom-call(bf16[4,64,896]{2,1,0:T(8,128)(2,1)S(1)} %get-tuple-element.62.x_own, bf16[4,64,896]{2,1,0:T(8,128)(2,1)} %collective-permute-done.29.x_other, bf16[4,64,896]{2,1,0:T(8,128)(2,1)S(1)} %get-tuple-element.63.d_own, ...), custom_call_target="tpu_custom_call" | custom-call | flops 352321536 | bytes 2916352 | tf_op jit(solution)/shard_map/pallas_call | solution.py:31
  90.3 1.4 %shard_map.133 = (bf16[128,3584]{1,0:T(8,128)(2,1)}, f32[128,8]{1,0:T(8,128)S(1)}) custom-call(bf16[1,128,128]{2,1,0:T(8,128)(2,1)S(1)} %copy-done.14, s32[128,8]{1,0:T(8,128)S(1)} %copy.14.ids_ref, bf16[16,3712]{1,0:T(8,128)(2,1)S(1)} %get-tuple-element.56.refs_0_, bf16[16,3712]{1,0:T(8,128)(2,1)S(1)} %collective-permute-done.26.refs_1_, ...), custom_call_target="tpu_custom_call" | custom-call | flops 58720256 | bytes 1433600 | tf_op jit(solution)/shard_map/pallas_call | solution.py:31
  (106 shorter events, 18.8 us)
Async XLA Ops:
  5.7 4.7 %collective-permute-start = (f32[1,16,128]{2,1,0:T(8,128)S(1)}, f32[1,16,128]{2,1,0:T(8,128)S(1)}, u32[]{:S(2)}, u32[]{:S(2)}) collective-permute-start(f32[1,16,128]{2,1,0:T(8,128)S(1)} %get-tuple-element.38), channel_id=1, source_target_pairs={{0,1},{1,0},{2,3},{3,2},{4,5},{5,4},{6,7},{7,6},{8,9},{9,8},{10,11... | collective-permute-start | bytes 24584 | tf_op jit(solution)/shard_map/ppermute | solution.py:221
  6.2 6.4 %collective-permute-start.3 = (bf16[1,2,16,896]{3,2,1,0:T(8,128)(2,1)S(1)}, bf16[1,2,16,896]{3,2,1,0:T(8,128)(2,1)S(1)}, u32[]{:S(2)}, u32[]{:S(2)}) collective-permute-start(bf16[1,2,16,896]{3,2,1,0:T(8,128)(2,1)S(1)} %get-tuple-element.40), channel_id=1, source_target_pairs={{0,8},{1,9},{2,10},{3,11},{4,12},{5,13},{6,14},{7,15},{8,0},{9,1},... | collective-permute-start | bytes 172040 | tf_op jit(solution)/shard_map/ppermute | solution.py:221
  8.8 4.2 %collective-permute-start.4 = (bf16[1,2,16,896]{3,2,1,0:T(8,128)(2,1)S(1)}, bf16[1,2,16,896]{3,2,1,0:T(8,128)(2,1)S(1)}, u32[]{:S(2)}, u32[]{:S(2)}) collective-permute-start(bf16[1,2,16,896]{3,2,1,0:T(8,128)(2,1)S(1)} %get-tuple-element.41), channel_id=1, source_target_pairs={{0,16},{1,17},{2,18},{3,19},{4,20},{5,21},{6,22},{7,23},{8,24},{9,... | collective-permute-start | bytes 172040 | tf_op jit(solution)/shard_map/ppermute | solution.py:221
  10.3 5.1 %collective-permute-start.5 = (bf16[1,2,16,896]{3,2,1,0:T(8,128)(2,1)S(1)}, bf16[1,2,16,896]{3,2,1,0:T(8,128)(2,1)S(1)}, u32[]{:S(2)}, u32[]{:S(2)}) collective-permute-start(bf16[1,2,16,896]{3,2,1,0:T(8,128)(2,1)S(1)} %get-tuple-element.42), channel_id=1, source_target_pairs={{0,24},{1,25},{2,26},{3,27},{4,28},{5,29},{6,30},{7,31},{8,16},{9,... | collective-permute-start | bytes 172040 | tf_op jit(solution)/shard_map/ppermute | solution.py:221
  10.4 6.6 %collective-permute-start.1 = (f32[2,16,128]{2,1,0:T(8,128)S(1)}, f32[2,16,128]{2,1,0:T(8,128)S(1)}, u32[]{:S(2)}, u32[]{:S(2)}) collective-permute-start(f32[2,16,128]{2,1,0:T(8,128)S(1)} %pad_maximum_fusion.2), channel_id=1, source_target_pairs={{0,2},{1,3},{2,0},{3,1},{4,6},{5,7},{6,4},{7,5},{8,10},{9,11},{10,... | collective-permute-start | bytes 49160 | tf_op jit(solution)/shard_map/ppermute | solution.py:221
  15.4 10.3 %collective-permute-start.6 = (bf16[4,16,896]{2,1,0:T(8,128)(2,1)S(1)}, bf16[4,16,896]{2,1,0:T(8,128)(2,1)S(1)}, u32[]{:S(2)}, u32[]{:S(2)}) collective-permute-start(bf16[4,16,896]{2,1,0:T(8,128)(2,1)S(1)} %get-tuple-element.45.refs_0_), channel_id=1, source_target_pairs={{0,2},{1,3},{2,0},{3,1},{4,6},{5,7},{6,4},{7,5},{8,10},{9,11},{10,... | collective-permute-start | bytes 344072 | tf_op jit(solution)/shard_map/ppermute | solution.py:221
  17.6 6.6 %collective-permute-start.2 = (f32[4,16,128]{2,1,0:T(8,128)S(1)}, f32[4,16,128]{2,1,0:T(8,128)S(1)}, u32[]{:S(2)}, u32[]{:S(2)}) collective-permute-start(f32[4,16,128]{2,1,0:T(8,128)S(1)} %pad_maximum_fusion.1), channel_id=1, source_target_pairs={{0,4},{1,5},{2,6},{3,7},{4,0},{5,1},{6,2},{7,3},{8,12},{9,13},{10,... | collective-permute-start | bytes 98312 | tf_op jit(solution)/shard_map/ppermute | solution.py:221
  20.2 13.1 %collective-permute-start.7 = (bf16[4,16,896]{2,1,0:T(8,128)(2,1)S(1)}, bf16[4,16,896]{2,1,0:T(8,128)(2,1)S(1)}, u32[]{:S(2)}, u32[]{:S(2)}) collective-permute-start(bf16[4,16,896]{2,1,0:T(8,128)(2,1)S(1)} %get-tuple-element.45.refs_0_), channel_id=1, source_target_pairs={{0,4},{1,5},{2,6},{3,7},{4,0},{5,1},{6,2},{7,3},{8,12},{9,13},{10,... | collective-permute-start | bytes 344072 | tf_op jit(solution)/shard_map/ppermute | solution.py:221
  20.5 13.3 %collective-permute-start.13 = (bf16[4,16,896]{2,1,0:T(8,128)(2,1)S(1)}, bf16[4,16,896]{2,1,0:T(8,128)(2,1)S(1)}, u32[]{:S(2)}, u32[]{:S(2)}) collective-permute-start(bf16[4,16,896]{2,1,0:T(8,128)(2,1)S(1)} %get-tuple-element.50.refs_0_), channel_id=1, source_target_pairs={{0,2},{1,3},{2,0},{3,1},{4,6},{5,7},{6,4},{7,5},{8,10},{9,11},{10,... | collective-permute-start | bytes 344072 | tf_op jit(solution)/shard_map/ppermute | solution.py:221
  21.0 14.8 %collective-permute-start.14 = (bf16[4,16,896]{2,1,0:T(8,128)(2,1)S(1)}, bf16[4,16,896]{2,1,0:T(8,128)(2,1)S(1)}, u32[]{:S(2)}, u32[]{:S(2)}) collective-permute-start(bf16[4,16,896]{2,1,0:T(8,128)(2,1)S(1)} %get-tuple-element.50.refs_0_), channel_id=1, source_target_pairs={{0,4},{1,5},{2,6},{3,7},{4,0},{5,1},{6,2},{7,3},{8,12},{9,13},{10,... | collective-permute-start | bytes 344072 | tf_op jit(solution)/shard_map/ppermute | solution.py:221
  24.2 12.6 %collective-permute-start.15 = (bf16[4,16,896]{2,1,0:T(8,128)(2,1)S(1)}, bf16[4,16,896]{2,1,0:T(8,128)(2,1)S(1)}, u32[]{:S(2)}, u32[]{:S(2)}) collective-permute-start(bf16[4,16,896]{2,1,0:T(8,128)(2,1)S(1)} %get-tuple-element.50.refs_0_), channel_id=1, source_target_pairs={{0,6},{1,7},{2,4},{3,5},{4,2},{5,3},{6,0},{7,1},{8,14},{9,15},{10,... | collective-permute-start | bytes 344072 | tf_op jit(solution)/shard_map/ppermute | solution.py:221
  25.7 20.7 %collective-permute-start.9 = (bf16[896,256]{1,0:T(8,128)(2,1)S(1)}, bf16[896,256]{1,0:T(8,128)(2,1)S(1)}, u32[]{:S(2)}, u32[]{:S(2)}) collective-permute-start(bf16[896,256]{1,0:T(8,128)(2,1)S(1)} %constant_dynamic-update-slice_fusion.refs_4_.refs_8_), channel_id=1, source_target_pairs={{0,1},{1,0},{2,3},{3,2},{4,5},{5,4},{6,7},{7,6},{8,9},{9,8},{10,11... | collective-permute-start | bytes 1376264 | tf_op jit(solution)/shard_map/ppermute | solution.py:221
  33.3 26.8 %collective-permute-start.20 = (bf16[896,256]{1,0:T(8,128)(2,1)S(1)}, bf16[896,256]{1,0:T(8,128)(2,1)S(1)}, u32[]{:S(2)}, u32[]{:S(2)}) collective-permute-start(bf16[896,256]{1,0:T(8,128)(2,1)S(1)} %constant_dynamic-update-slice_fusion.refs_4_.refs_8_), channel_id=1, source_target_pairs={{0,8},{1,9},{2,10},{3,11},{4,12},{5,13},{6,14},{7,15},{8,0},{9,1},... | collective-permute-start | bytes 1376264 | tf_op jit(solution)/shard_map/ppermute | solution.py:221
  33.8 29.1 %collective-permute-start.22 = (bf16[896,256]{1,0:T(8,128)(2,1)S(1)}, bf16[896,256]{1,0:T(8,128)(2,1)S(1)}, u32[]{:S(2)}, u32[]{:S(2)}) collective-permute-start(bf16[896,256]{1,0:T(8,128)(2,1)S(1)} %constant_dynamic-update-slice_fusion.refs_4_.refs_8_), channel_id=1, source_target_pairs={{0,16},{1,17},{2,18},{3,19},{4,20},{5,21},{6,22},{7,23},{8,24},{9,... | collective-permute-start | bytes 1376264 | tf_op jit(solution)/shard_map/ppermute | solution.py:221
  35.8 27.2 %collective-permute-start.24 = (bf16[896,256]{1,0:T(8,128)(2,1)S(1)}, bf16[896,256]{1,0:T(8,128)(2,1)S(1)}, u32[]{:S(2)}, u32[]{:S(2)}) collective-permute-start(bf16[896,256]{1,0:T(8,128)(2,1)S(1)} %constant_dynamic-update-slice_fusion.refs_4_.refs_8_), channel_id=1, source_target_pairs={{0,24},{1,25},{2,26},{3,27},{4,28},{5,29},{6,30},{7,31},{8,16},{9,... | collective-permute-start | bytes 1376264 | tf_op jit(solution)/shard_map/ppermute | solution.py:221
  38.3 7.1 %collective-permute-start.8 = (bf16[4,16,896]{2,1,0:T(8,128)(2,1)S(1)}, bf16[4,16,896]{2,1,0:T(8,128)(2,1)S(1)}, u32[]{:S(2)}, u32[]{:S(2)}) collective-permute-start(bf16[4,16,896]{2,1,0:T(8,128)(2,1)S(1)} %get-tuple-element.45.refs_0_), channel_id=1, source_target_pairs={{0,6},{1,7},{2,4},{3,5},{4,2},{5,3},{6,0},{7,1},{8,14},{9,15},{10,... | collective-permute-start | bytes 344072 | tf_op jit(solution)/shard_map/ppermute | solution.py:221
  45.4 7.5 %collective-permute-start.17 = (bf16[64,256]{1,0:T(8,128)(2,1)S(1)}, bf16[64,256]{1,0:T(8,128)(2,1)S(1)}, u32[]{:S(2)}, u32[]{:S(2)}) collective-permute-start(bf16[64,256]{1,0:T(8,128)(2,1)S(1)} %get-tuple-element.52), channel_id=1, source_target_pairs={{0,8},{1,9},{2,10},{3,11},{4,12},{5,13},{6,14},{7,15},{8,0},{9,1},... | collective-permute-start | bytes 98312 | tf_op jit(solution)/shard_map/ppermute | solution.py:221
  46.3 7.6 %collective-permute-start.18 = (bf16[64,256]{1,0:T(8,128)(2,1)S(1)}, bf16[64,256]{1,0:T(8,128)(2,1)S(1)}, u32[]{:S(2)}, u32[]{:S(2)}) collective-permute-start(bf16[64,256]{1,0:T(8,128)(2,1)S(1)} %get-tuple-element.53), channel_id=1, source_target_pairs={{0,16},{1,17},{2,18},{3,19},{4,20},{5,21},{6,22},{7,23},{8,24},{9,... | collective-permute-start | bytes 98312 | tf_op jit(solution)/shard_map/ppermute | solution.py:221
  53.5 10.0 %collective-permute-start.10 = (bf16[64,512]{1,0:T(8,128)(2,1)S(1)}, bf16[64,512]{1,0:T(8,128)(2,1)S(1)}, u32[]{:S(2)}, u32[]{:S(2)}) collective-permute-start(bf16[64,512]{1,0:T(8,128)(2,1)S(1)} %get-tuple-element.47), channel_id=1, source_target_pairs={{0,8},{1,9},{2,10},{3,11},{4,12},{5,13},{6,14},{7,15},{8,0},{9,1},... | collective-permute-start | bytes 196616 | tf_op jit(solution)/shard_map/ppermute | solution.py:221
  54.6 4.8 %collective-permute-start.19 = (bf16[64,256]{1,0:T(8,128)(2,1)S(1)}, bf16[64,256]{1,0:T(8,128)(2,1)S(1)}, u32[]{:S(2)}, u32[]{:S(2)}) collective-permute-start(bf16[64,256]{1,0:T(8,128)(2,1)S(1)} %get-tuple-element.54), channel_id=1, source_target_pairs={{0,24},{1,25},{2,26},{3,27},{4,28},{5,29},{6,30},{7,31},{8,16},{9,... | collective-permute-start | bytes 98312 | tf_op jit(solution)/shard_map/ppermute | solution.py:221
  60.0 4.3 %collective-permute-start.11 = (bf16[64,512]{1,0:T(8,128)(2,1)S(1)}, bf16[64,512]{1,0:T(8,128)(2,1)S(1)}, u32[]{:S(2)}, u32[]{:S(2)}) collective-permute-start(bf16[64,512]{1,0:T(8,128)(2,1)S(1)} %get-tuple-element.48), channel_id=1, source_target_pairs={{0,16},{1,17},{2,18},{3,19},{4,20},{5,21},{6,22},{7,23},{8,24},{9,... | collective-permute-start | bytes 196616 | tf_op jit(solution)/shard_map/ppermute | solution.py:221
  60.1 5.2 %collective-permute-start.12 = (bf16[64,512]{1,0:T(8,128)(2,1)S(1)}, bf16[64,512]{1,0:T(8,128)(2,1)S(1)}, u32[]{:S(2)}, u32[]{:S(2)}) collective-permute-start(bf16[64,512]{1,0:T(8,128)(2,1)S(1)} %get-tuple-element.49), channel_id=1, source_target_pairs={{0,24},{1,25},{2,26},{3,27},{4,28},{5,29},{6,30},{7,31},{8,16},{9,... | collective-permute-start | bytes 196616 | tf_op jit(solution)/shard_map/ppermute | solution.py:221
  64.9 9.4 %collective-permute-start.30 = (bf16[4,64,896]{2,1,0:T(8,128)(2,1)S(1)}, bf16[4,64,896]{2,1,0:T(8,128)(2,1)}, u32[]{:S(2)}, u32[]{:S(2)}) collective-permute-start(bf16[4,64,896]{2,1,0:T(8,128)(2,1)S(1)} %get-tuple-element.63.d_own), channel_id=1, source_target_pairs={{0,1},{1,0},{2,3},{3,2},{4,5},{5,4},{6,7},{7,6},{8,9},{9,8},{10,11... | collective-permute-start | bytes 1376264 | tf_op jit(solution)/shard_map/ppermute | solution.py:221
  65.9 9.9 %collective-permute-start.29 = (bf16[4,64,896]{2,1,0:T(8,128)(2,1)S(1)}, bf16[4,64,896]{2,1,0:T(8,128)(2,1)}, u32[]{:S(2)}, u32[]{:S(2)}) collective-permute-start(bf16[4,64,896]{2,1,0:T(8,128)(2,1)S(1)} %get-tuple-element.62.x_own), channel_id=1, source_target_pairs={{0,1},{1,0},{2,3},{3,2},{4,5},{5,4},{6,7},{7,6},{8,9},{9,8},{10,11... | collective-permute-start | bytes 1376264 | tf_op jit(solution)/shard_map/ppermute | solution.py:221
  72.0 4.2 %collective-permute-start.31 = (bf16[64,384]{1,0:T(8,128)(2,1)S(1)}, bf16[64,384]{1,0:T(8,128)(2,1)S(1)}, u32[]{:S(2)}, u32[]{:S(2)}) collective-permute-start(bf16[64,384]{1,0:T(8,128)(2,1)S(1)} %get-tuple-element.65), channel_id=1, source_target_pairs={{0,1},{1,0},{2,3},{3,2},{4,5},{5,4},{6,7},{7,6},{8,9},{9,8},{10,11... | collective-permute-start | bytes 147464 | tf_op jit(solution)/shard_map/ppermute | solution.py:221
  74.3 6.3 %collective-permute-start.34 = (bf16[64,384]{1,0:T(8,128)(2,1)S(1)}, bf16[64,384]{1,0:T(8,128)(2,1)S(1)}, u32[]{:S(2)}, u32[]{:S(2)}) collective-permute-start(bf16[64,384]{1,0:T(8,128)(2,1)S(1)} %get-tuple-element.64.refs_0_), channel_id=1, source_target_pairs={{0,16},{1,17},{2,18},{3,19},{4,20},{5,21},{6,22},{7,23},{8,24},{9,... | collective-permute-start | bytes 147464 | tf_op jit(solution)/shard_map/ppermute | solution.py:221
  75.9 7.3 %collective-permute-start.35 = (bf16[64,384]{1,0:T(8,128)(2,1)S(1)}, bf16[64,384]{1,0:T(8,128)(2,1)S(1)}, u32[]{:S(2)}, u32[]{:S(2)}) collective-permute-start(bf16[64,384]{1,0:T(8,128)(2,1)S(1)} %get-tuple-element.65), channel_id=1, source_target_pairs={{0,17},{1,16},{2,19},{3,18},{4,21},{5,20},{6,23},{7,22},{8,25},{9,... | collective-permute-start | bytes 147464 | tf_op jit(solution)/shard_map/ppermute | solution.py:221
  76.2 14.1 %collective-permute-start.26 = (bf16[16,3712]{1,0:T(8,128)(2,1)S(1)}, bf16[16,3712]{1,0:T(8,128)(2,1)S(1)}, u32[]{:S(2)}, u32[]{:S(2)}) collective-permute-start(bf16[16,3712]{1,0:T(8,128)(2,1)S(1)} %get-tuple-element.57), channel_id=1, source_target_pairs={{0,2},{1,3},{2,0},{3,1},{4,6},{5,7},{6,4},{7,5},{8,10},{9,11},{10,... | collective-permute-start | bytes 356360 | tf_op jit(solution)/shard_map/ppermute | solution.py:221
  76.5 13.8 %collective-permute-start.27 = (bf16[16,3712]{1,0:T(8,128)(2,1)S(1)}, bf16[16,3712]{1,0:T(8,128)(2,1)S(1)}, u32[]{:S(2)}, u32[]{:S(2)}) collective-permute-start(bf16[16,3712]{1,0:T(8,128)(2,1)S(1)} %get-tuple-element.58), channel_id=1, source_target_pairs={{0,4},{1,5},{2,6},{3,7},{4,0},{5,1},{6,2},{7,3},{8,12},{9,13},{10,... | collective-permute-start | bytes 356360 | tf_op jit(solution)/shard_map/ppermute | solution.py:221
  78.3 12.0 %collective-permute-start.28 = (bf16[16,3712]{1,0:T(8,128)(2,1)S(1)}, bf16[16,3712]{1,0:T(8,128)(2,1)S(1)}, u32[]{:S(2)}, u32[]{:S(2)}) collective-permute-start(bf16[16,3712]{1,0:T(8,128)(2,1)S(1)} %get-tuple-element.59), channel_id=1, source_target_pairs={{0,6},{1,7},{2,4},{3,5},{4,2},{5,3},{6,0},{7,1},{8,14},{9,15},{10,... | collective-permute-start | bytes 356360 | tf_op jit(solution)/shard_map/ppermute | solution.py:221
  80.6 5.0 %collective-permute-start.36 = (bf16[64,384]{1,0:T(8,128)(2,1)S(1)}, bf16[64,384]{1,0:T(8,128)(2,1)S(1)}, u32[]{:S(2)}, u32[]{:S(2)}) collective-permute-start(bf16[64,384]{1,0:T(8,128)(2,1)S(1)} %get-tuple-element.64.refs_0_), channel_id=1, source_target_pairs={{0,24},{1,25},{2,26},{3,27},{4,28},{5,29},{6,30},{7,31},{8,16},{9,... | collective-permute-start | bytes 147464 | tf_op jit(solution)/shard_map/ppermute | solution.py:221
  83.2 4.4 %collective-permute-start.37 = (bf16[64,384]{1,0:T(8,128)(2,1)S(1)}, bf16[64,384]{1,0:T(8,128)(2,1)S(1)}, u32[]{:S(2)}, u32[]{:S(2)}) collective-permute-start(bf16[64,384]{1,0:T(8,128)(2,1)S(1)} %get-tuple-element.65), channel_id=1, source_target_pairs={{0,25},{1,24},{2,27},{3,26},{4,29},{5,28},{6,31},{7,30},{8,17},{9,... | collective-permute-start | bytes 147464 | tf_op jit(solution)/shard_map/ppermute | solution.py:221
  (29 other events, 103.5 us)

commit v3 on v2

v3 whole, which is shorter than its diff:
```python
import functools

import jax
import jax.numpy as jnp
from jax import lax
from jax.experimental import pallas as pl
from jax.experimental.pallas import tpu as pltpu
from jax.sharding import PartitionSpec as P

EXPERTS = 128
SLOT = 16
BLOCK = 128
SPLIT = 8
CORES = 2
CHIPS = SPLIT // CORES
LANES = 128
F32 = jnp.float32
BF16 = jnp.bfloat16
PARTS = 4
ANY = pl.BlockSpec(memory_space=pl.ANY)
VMEM = pl.BlockSpec(memory_space=pltpu.VMEM)


def shape(dims, kind=BF16):
    return jax.ShapeDtypeStruct(dims, kind)


def call(kernel, outs, args, outside=0, scratch=(), flops=0):
    size = sum(a.size * a.dtype.itemsize for a in args) + sum(
        o.size * o.dtype.itemsize for o in outs
    )
    return pl.pallas_call(
        kernel,
        out_shape=tuple(outs),
        in_specs=[ANY] * outside + [VMEM] * (len(args) - outside),
        out_specs=tuple([VMEM] * len(outs)),
        scratch_shapes=scratch,
        compiler_params=pltpu.CompilerParams(vmem_limit_bytes=24 * 1024 * 1024),
        cost_estimate=pl.CostEstimate(flops=flops, bytes_accessed=size, transcendentals=0),
    )(*args)


def dot(a, b, dims=((1,), (0,))):
    return lax.dot_general(a, b, (dims, ((), ())), preferred_element_type=F32)


def iota(dims, axis):
    return lax.broadcasted_iota(jnp.int32, dims, axis)


def ring_chip(place):
    return jnp.bitwise_xor(place, place // 2)


def pack_kernel(rep, flight, live_ref, tok_ref, grad_ref, ids_ref, rw_ref, *refs):
    pays, placed_ref = refs[:flight], refs[flight]
    live, data, rows, sems = refs[flight + 1 :]
    r = lax.axis_index("rep")
    mine = lax.axis_index("ep") // SPLIT
    count, model = tok_ref.shape
    width = model // rep
    spacing = EXPERTS // flight
    live_copy = pltpu.make_async_copy(live_ref, live, sems.at[2 * PARTS])
    live_copy.start()
    copies = []
    for part, ref in enumerate((tok_ref, grad_ref)):
        for p in range(PARTS):
            some = pl.ds(p * (count // PARTS), count // PARTS)
            copy = pltpu.make_async_copy(
                ref.at[some], data.at[part, some], sems.at[part * PARTS + p]
            )
            copy.start()
            copies.append(copy)
    live_copy.wait()
    token = iota((1, count), 1)
    upper = (iota((count, count), 0) <= iota((count, count), 1)).astype(BF16)
    slot = iota((SLOT, count), 0).astype(F32)
    lane = iota((SLOT, LANES), 1)
    ids = ids_ref[...]
    weights = rw_ref[...].astype(F32)
    firsts, headers = [], []
    for w in range(flight):
        expert = jnp.bitwise_xor(mine, w)
        match = ids == expert * spacing
        routed = jnp.any(match, axis=0, keepdims=True) & (token < live[r])
        weight = jnp.sum(jnp.where(match, weights, 0.0), axis=0, keepdims=True)
        routed = jnp.broadcast_to(jnp.where(routed, 1.0, 0.0), (SLOT, count))
        rank = dot(routed.astype(BF16), upper) - 1.0
        placed = jnp.where(rank == slot, routed, 0.0)
        column = jnp.sum(placed * weight, axis=1, keepdims=True)
        headers.append(jnp.where(lane == 0, column, 0.0).astype(BF16))
        placed = placed.astype(BF16)
        firsts.append(placed)
        placed_ref[w] = jnp.concatenate([placed] * CHIPS, axis=0)
    for part in range(2):
        for p in range(PARTS):
            copies[part * PARTS + p].wait()
        for w in range(flight):
            chosen = dot(firsts[w], data[part]).astype(BF16)
            for b in range(rep):
                rows[b] = chosen[:, b * width : (b + 1) * width]
            for k in range(rep):
                pays[w][part, :, k * width : (k + 1) * width] = rows[jnp.bitwise_xor(r, k)]
            pays[w][part, :, model:] = headers[w]


def forward_kernel(rep, count, *refs):
    blocks, pieces, outs = refs[:count], refs[count : -(rep + 3)], refs[-(rep + 3) :]
    pre_x, pre_d, header_ref, parts = outs[0], outs[1], outs[2], outs[3:]
    half, columns = pieces[0].shape
    width = 2 * half
    units = columns // 3
    rows = [jnp.concatenate([b[part] for b in blocks], axis=0) for part in range(2)]
    for j in range(count):
        header_ref[j] = blocks[j][0, :, rep * width :]
    for k in range(rep):
        for part in range(2):
            parts[k][part] = rows[part][:, k * width : (k + 1) * width]
    for i in range(CORES):
        sum_x, sum_d = 0.0, 0.0
        for p in range(len(pieces) // CORES):
            piece = pieces[CORES * p + i]
            some = slice(p * half, (p + 1) * half)
            sum_x = sum_x + dot(rows[0][:, some], piece[:, : 2 * units])
            sum_d = sum_d + dot(rows[1][:, some], piece[:, 2 * units :])
        pre_x[:, 2 * i * units : 2 * (i + 1) * units] = sum_x
        pre_d[:, i * units : (i + 1) * units] = sum_d


def hidden_kernel(rep, count, cap_ref, own_ref, other_ref, pre_x, pre_d, *refs):
    parts, pieces = refs[0], refs[1 : 1 + 4 * rep]
    back_refs, grad_refs = refs[1 + 4 * rep : 1 + 4 * rep + count], refs[1 + 4 * rep + count : -2]
    cap, sem = refs[-2:]
    cap_copy = pltpu.make_async_copy(cap_ref, cap, sem)
    cap_copy.start()
    half, columns = pieces[0].shape
    width = 2 * half
    units = columns // 3
    r = lax.axis_index("rep")
    e = lax.axis_index("ep")
    mine = e // SPLIT
    place = ring_chip((e % SPLIT) // CORES)
    cap_copy.wait()
    capacity = (BLOCK * cap[r, mine]).astype(F32)
    lane = iota((SLOT, LANES), 1)
    sources, rates, counts = [], [], []
    for core, ref in enumerate((own_ref, other_ref)):
        for j in range(count):
            chip = ring_chip((place + CHIPS - j % CHIPS) % CHIPS)
            expert = jnp.bitwise_xor(mine, j // CHIPS)
            source = expert * SPLIT + chip * CORES + jnp.bitwise_xor(e % CORES, core)
            rate = jnp.where(lane == 0, ref[j].astype(F32), 0.0)
            rate = jnp.sum(rate, axis=1, keepdims=True)
            sources.append(source)
            rates.append(rate)
            counts.append(jnp.sum(jnp.where(rate > 0.0, 1.0, 0.0), axis=0, keepdims=True))
    slot = iota((SLOT, 1), 0).astype(F32)
    rate_rows, kept_rows = [], []
    for j in range(count):
        start = jnp.zeros((1, 1), F32)
        for other in range(len(sources)):
            start = start + jnp.where(sources[other] < sources[j], counts[other], 0.0)
        kept = jnp.where((rates[j] > 0.0) & (start + slot < capacity), 1.0, 0.0)
        kept_rows.append(kept)
        rate_rows.append(rates[j] * kept)
    rate = jnp.concatenate(rate_rows, axis=0)
    kept = jnp.concatenate(kept_rows, axis=0)

    lane = iota((count * SLOT, LANES), 1)
    scores = jnp.zeros((count * SLOT, LANES), F32)
    pairs = []
    for i in range(CORES):
        sum_x = pre_x[:, 2 * i * units : 2 * (i + 1) * units]
        sum_d = pre_d[:, i * units : (i + 1) * units]
        for h in range(2):
            piece = pieces[CORES * (2 * rep - 2 + h) + i]
            some = slice(h * half, (h + 1) * half)
            sum_x = sum_x + dot(parts[0, :, some], piece[:, : 2 * units])
            sum_d = sum_d + dot(parts[1, :, some], piece[:, 2 * units :])
        pre_gate, pre_up, back_hidden = sum_x[:, :units], sum_x[:, units:], sum_d
        sig = 1.0 / (1.0 + jnp.exp(-pre_gate))
        activated = pre_gate * sig
        hidden = activated * pre_up
        score = jnp.sum(hidden * back_hidden, axis=1, keepdims=True) * kept
        scores = jnp.where(lane == i, score, scores)
        scaled = back_hidden * rate
        gate_grad = (scaled * pre_up * sig * (1.0 + pre_gate * (1.0 - sig))).astype(BF16)
        up_grad = (scaled * activated).astype(BF16)
        grad_refs[i][:, :units] = gate_grad
        grad_refs[i][:, units : 2 * units] = up_grad
        grad_refs[i][:, 2 * units :] = (hidden * rate).astype(BF16)
        pairs.append(jnp.concatenate([gate_grad, up_grad], axis=1))
    for p in range(2 * rep):
        back = dot(pairs[0], pieces[CORES * p][:, : 2 * units], ((1,), (1,)))
        back = back + dot(pairs[1], pieces[CORES * p + 1][:, : 2 * units], ((1,), (1,)))
        back = back.astype(BF16)
        for j in range(count):
            back_refs[j][:, p * half : (p + 1) * half] = back[j * SLOT : (j + 1) * SLOT]
    scores = scores.astype(BF16)
    for j in range(count):
        back_refs[j][:, rep * width :] = scores[j * SLOT : (j + 1) * SLOT]


def weight_kernel(rep, units, *refs):
    own, other, grads, outs = refs[:rep], refs[rep : 2 * rep], refs[2 * rep : 3 * rep], refs[-3:]
    width = own[0].shape[2]
    got = jnp.concatenate([g[...] for g in grads], axis=0)
    rows = [
        jnp.concatenate([ref[part] for k in range(rep) for ref in (own[k], other[k])], axis=0)
        for part in range(2)
    ]
    gate_up = dot(rows[0], got[:, : 2 * units], ((0,), (0,)))
    outs[0][...] = gate_up[:, :units].astype(BF16)
    outs[1][...] = gate_up[:, units:].astype(BF16)
    outs[2][...] = dot(rows[1], got[:, 2 * units :], ((0,), (0,))).astype(BF16)


def token_kernel(rep, flight, placed_ref, ids_ref, *refs):
    backs, out_ref, weight_ref, blocks = refs[:-3], refs[-3], refs[-2], refs[-1]
    r = lax.axis_index("rep")
    mine = lax.axis_index("ep") // SPLIT
    spacing = EXPERTS // flight
    width = out_ref.shape[1] // rep
    joined = [
        jnp.concatenate([b[...] for b in backs[w * CHIPS : (w + 1) * CHIPS]], axis=0)
        for w in range(flight)
    ]
    for k in range(rep):
        total = 0.0
        for w in range(flight):
            some = joined[w][:, k * width : (k + 1) * width]
            total = total + dot(placed_ref[w], some, ((0,), (0,)))
        blocks[jnp.bitwise_xor(r, k)] = total.astype(BF16)
    for b in range(rep):
        out_ref[:, b * width : (b + 1) * width] = blocks[b]
    result = jnp.zeros(weight_ref.shape, F32)
    for w in range(flight):
        score = dot(joined[w][:, rep * width :], placed_ref[w], ((0,), (0,)))
        score = jnp.sum(score, axis=0, keepdims=True)
        match = ids_ref[...] == jnp.bitwise_xor(mine, w) * spacing
        result = result + jnp.where(match, score, 0.0)
    weight_ref[...] = result


def local(
    tokens, out_grad, expert_ids, route_weight, live_count, cap_blocks, w_gate, w_up, w_down_t
):
    rep = lax.axis_size("rep")
    ep = lax.axis_size("ep")
    flight = ep // SPLIT
    count = ep // CORES
    tok_count, model_dim = tokens.shape
    width, units = w_gate.shape
    half = width // 2
    rows = count * SLOT
    payload = model_dim + LANES

    def send(array, rep_bits, ep_bits):
        mask = rep_bits * ep + ep_bits
        pairs = [(a, a ^ mask) for a in range(rep * ep)]
        return lax.ppermute(array, ("rep", "ep"), pairs)

    def send_ring(array, step):
        pairs = []
        for expert in range(flight):
            for p in range(CHIPS):
                q = (p + step) % CHIPS
                for core in range(CORES):
                    first = expert * SPLIT + core
                    pairs.append((first + CORES * (p ^ p // 2), first + CORES * (q ^ q // 2)))
        return lax.ppermute(array, "ep", pairs)

    first, second = (
        jnp.concatenate([w[h * half : (h + 1) * half] for w in (w_gate, w_up, w_down_t)], axis=1)
        for h in range(2)
    )
    halves = {(0, 0): first, (0, 1): second}
    for k in range(1, rep):
        low, high = k & -k, 1 << (k.bit_length() - 1)
        halves[k, 0] = send(halves[k ^ low, 0], low, 0)
        halves[k, 1] = send(halves[k ^ high, 1], high, 0)
    pieces = []
    for k in range(rep):
        for h in range(2):
            pieces += [halves[k, h], send(halves[k, h], 0, 1)]

    packed = call(
        functools.partial(pack_kernel, rep, flight),
        [shape((2, SLOT, payload))] * flight + [shape((flight, CHIPS * SLOT, tok_count))],
        [live_count, tokens, out_grad, expert_ids.T, route_weight.T],
        outside=3,
        scratch=[
            pltpu.SMEM(live_count.shape, jnp.int32),
            pltpu.VMEM((2, tok_count, model_dim), BF16),
            pltpu.VMEM((rep, SLOT, width), BF16),
            pltpu.SemaphoreType.DMA((2 * PARTS + 1,)),
        ],
    )
    pays, placed = packed[:flight], packed[flight]
    blocks = []
    for w in range(flight):
        block = pays[w] if w == 0 else send(pays[w], 0, w * SPLIT)
        blocks.append(block)
        for _ in range(1, CHIPS):
            block = send_ring(block, 1)
            blocks.append(block)

    results = call(
        functools.partial(forward_kernel, rep, count),
        [
            shape((rows, 2 * CORES * units), F32),
            shape((rows, CORES * units), F32),
            shape((count, SLOT, LANES)),
        ]
        + [shape((2, rows, width))] * rep,
        blocks + pieces[: -2 * CORES],
        flops=2 * rows * model_dim * 3 * CORES * units,
    )
    pre_x, pre_d, header, parts = results[0], results[1], results[2], list(results[3:])
    header_other = send(header, 0, 1)
    results = call(
        functools.partial(hidden_kernel, rep, count),
        [shape((SLOT, payload))] * count + [shape((rows, 3 * units))] * CORES,
        [cap_blocks, header, header_other, pre_x, pre_d, parts[-1]] + pieces,
        outside=1,
        scratch=[pltpu.SMEM(cap_blocks.shape, jnp.int32), pltpu.SemaphoreType.DMA(())],
        flops=2 * rows * model_dim * 4 * units,
    )
    backs, grads = results[:count], results[count:]
    grads = jnp.concatenate([grads[0], send(grads[1], 0, 1)], axis=0)
    returned = [backs[0]]
    for j in range(1, count):
        back = send_ring(backs[j], CHIPS - j % CHIPS) if j % CHIPS else backs[j]
        returned.append(send(back, 0, j // CHIPS * SPLIT) if j >= CHIPS else back)

    own_rows = [parts[0]] + [send(parts[k], k, 0) for k in range(1, rep)]
    other_rows = [send(own_rows[k], 0, 1) for k in range(rep)]
    group_grads = [grads] + [send(grads, k, 0) for k in range(1, rep)]
    grad_gate, grad_up, grad_down = call(
        functools.partial(weight_kernel, rep, units),
        [shape((width, units))] * 3,
        own_rows + other_rows + group_grads,
        flops=2 * 2 * rep * rows * width * 3 * units,
    )
    grad_tokens, grad_weight = call(
        functools.partial(token_kernel, rep, flight),
        [shape((tok_count, model_dim)), shape(expert_ids.shape[::-1], F32)],
        [placed, expert_ids.T] + returned,
        scratch=[pltpu.VMEM((rep, tok_count, width), BF16)],
        flops=2 * tok_count * CHIPS * SLOT * model_dim,
    )
    return grad_tokens, grad_weight.T, grad_gate, grad_up, grad_down


def solution(mesh):
    return jax.shard_map(
        local,
        mesh=mesh,
        in_specs=(
            P(("rep", "ep"), None),
            P(("rep", "ep"), None),
            P(("rep", "ep"), None),
            P(("rep", "ep"), None),
            P(),
            P(),
            P("rep", "ep"),
            P("rep", "ep"),
            P("rep", "ep"),
        ),
        out_specs=(
            P(("rep", "ep"), None),
            P(("rep", "ep"), None),
            P("rep", "ep"),
            P("rep", "ep"),
            P("rep", "ep"),
        ),
        check_vma=False,
    )
```

time: 92.9 us -> 85.4 us (0.919)
  waiting for transfers between devices: 33.5 us -> 27.5 us
  Pallas kernels: 9.13 us -> 12.4 us
  starting transfers between devices: 37.4 us -> 34.5 us
  local copies, waits for them, and re-layouts: 10.7 us -> 9.71 us
    ppermute x38 -> x26, waiting for transfers between devices: 33.5 us -> 12.2 us  [send(): return lax.ppermute(array, ('rep', 'ep'), pairs)]
    ppermute x38 -> x26, starting transfers between devices: 37.4 us -> 18.6 us  [send(): return lax.ppermute(array, ('rep', 'ep'), pairs)]
    ppermute x0 -> x6, starting transfers between devices: none -> 15.9 us  [send_ring(): return lax.ppermute(array, 'ep', pairs)]
    ppermute x0 -> x6, waiting for transfers between devices: none -> 15.2 us  [send_ring(): return lax.ppermute(array, 'ep', pairs)]
    pallas_call x7 -> x5, Pallas kernels: 9.13 us -> 12.4 us  [call(): pl.pallas_call(kernel, out_shape=tuple(outs), in_specs=[ANY] * outside +...]
    unnamed x51 -> x40, local copies, waits for them, and re-layouts: 10.6 us -> 7.56 us
    slice x0 -> x2, local copies, waits for them, and re-layouts: none -> 2.13 us  [local(): w[h * half:(h + 1) * half]]
  transfers between devices with their start and end apart: 38 -> 32, of which waited for: 15 -> 14; matrix products, arithmetic and copies ran while one was open for 1% -> 0% of each run, Pallas kernels for 7% -> 11%
where the time goes in v3:
time: 85.4 us; the launch traced here: 85 us
  starting transfers between devices  34.5 us (40%)
  waiting for transfers between devices  27.5 us (32%)
  Pallas kernels  12.4 us (15%)
  local copies, waits for them, and re-layouts  9.71 us (11%)
    ppermute x26, starting transfers between devices, send(): return lax.ppermute(array, ('rep', 'ep'), pairs)  18.6 us
    ppermute x6, starting transfers between devices, send_ring(): return lax.ppermute(array, 'ep', pairs)  15.9 us
    ppermute x6, waiting for transfers between devices, send_ring(): return lax.ppermute(array, 'ep', pairs)  15.2 us
    pallas_call x5, Pallas kernels, call(): pl.pallas_call(kernel, out_shape=tuple(outs), in_specs=[ANY] * outside +...  12.4 us
    ppermute x26, waiting for transfers between devices, send(): return lax.ppermute(array, ('rep', 'ep'), pairs)  12.2 us
    unnamed x40, local copies, waits for them, and re-layouts  7.56 us
    slice x2, local copies, waits for them, and re-layouts, local(): w[h * half:(h + 1) * half]  2.13 us
  transfers between devices with their start and end apart: 32, of which 14 were waited for; matrix products, arithmetic and copies ran while one was open for 0% of the time, Pallas kernels for 11%

profile of v3, /device:TPU:0, one launch (start us, length us, event | category | flops | bytes accessed | tf_op | source)
XLA Modules:
  0.0 85.0 jit_solution(4278874198374592456)
XLA Ops:
  0.7 1.1 %fusion.2 = (bf16[448,128]{1,0:T(8,128)(2,1)S(1)}, bf16[448,128]{1,0:T(8,128)(2,1)S(1)}) fusion(bf16[896,128]{1,0:T(8,128)(2,1)} %param.17), kind=kLoop, calls=%fused_computation.6 | loop fusion | bytes 458752 | tf_op jit(solution)/shard_map/slice | solution.py:274
  1.7 1.1 %fusion = (bf16[448,128]{1,0:T(8,128)(2,1)S(1)}, bf16[448,128]{1,0:T(8,128)(2,1)S(1)}, bf16[448,128]{1,0:T(8,128)(2,1)S(1)}, bf16[448,128]{1,0:T(8,128)(2,1)S(1)}) fusion(bf16[896,128]{1,0:T(8,128)(2,1)S(1)} %copy-done.17, bf16[896,128]{1,0:T(8,128)(2,1)} %param.16), kind=kLoop, calls=%fused_computation.4 | loop fusion | bytes 917504 | tf_op jit(solution)/shard_map/slice | solution.py:274
  4.1 3.1 %shard_map.128 = (bf16[2,16,3712]{2,1,0:T(8,128)(2,1)S(1)}, bf16[1,64,128]{2,1,0:T(8,128)(2,1)S(1)}) custom-call(s32[4]{0:T(128)S(1)} %copy-done.16, bf16[128,3584]{1,0:T(8,128)(2,1)S(1)} %copy-done.4, bf16[128,3584]{1,0:T(8,128)(2,1)S(1)} %copy-done.5, s32[8,128]{1,0:T(8,128)S(1)} %bitcast.3, bf16[8,128]{1,0:T(8,128)(2,1)S(1)} %bitcast.5), custom_call_target="tpu_custom_call" | custom-call | bytes 2095120 | tf_op jit(solution)/shard_map/pallas_call | solution.py:32
  7.8 2.6 %collective-permute-start = (bf16[2,16,3712]{2,1,0:T(8,128)(2,1)S(1)}, bf16[2,16,3712]{2,1,0:T(8,128)(2,1)S(1)}, u32[]{:S(2)}, u32[]{:S(2)}) collective-permute-start(bf16[2,16,3712]{2,1,0:T(8,128)(2,1)S(1)} %get-tuple-element.26.refs_0_), channel_id=1, source_target_pairs={{0,2},{1,3},{2,6},{3,7},{6,4},{7,5},{4,0},{5,1},{8,10},{9,11},{10,... | collective-permute-start | bytes 712712 | tf_op jit(solution)/shard_map/ppermute | solution.py:271
  10.4 1.5 %collective-permute-start.5 = (bf16[448,384]{1,0:T(8,128)(2,1)S(1)}, bf16[448,384]{1,0:T(8,128)(2,1)S(1)}, u32[]{:S(2)}, u32[]{:S(2)}) collective-permute-start(bf16[448,384]{1,0:T(8,128)(2,1)S(1)} %pad_maximum_fusion.refs_4_.refs_1_), channel_id=1, source_target_pairs={{0,8},{1,9},{2,10},{3,11},{4,12},{5,13},{6,14},{7,15},{8,0},{9,1},... | collective-permute-start | bytes 1032200 | tf_op jit(solution)/shard_map/ppermute | solution.py:261
  11.9 1.5 %collective-permute-start.9 = (bf16[448,384]{1,0:T(8,128)(2,1)S(1)}, bf16[448,384]{1,0:T(8,128)(2,1)S(1)}, u32[]{:S(2)}, u32[]{:S(2)}) collective-permute-start(bf16[448,384]{1,0:T(8,128)(2,1)S(1)} %pad_maximum_fusion.refs_4_.refs_1_), channel_id=1, source_target_pairs={{0,16},{1,17},{2,18},{3,19},{4,20},{5,21},{6,22},{7,23},{8,24},{9,... | collective-permute-start | bytes 1032200 | tf_op jit(solution)/shard_map/ppermute | solution.py:261
  13.6 4.3 %collective-permute-done.refs_1_ = bf16[2,16,3712]{2,1,0:T(8,128)(2,1)S(1)} collective-permute-done((bf16[2,16,3712]{2,1,0:T(8,128)(2,1)S(1)}, bf16[2,16,3712]{2,1,0:T(8,128)(2,1)S(1)}, u32[]{:S(2)}, u32[]{:S(2)}) %collective-permute-start) | collective-permute-done | bytes 237600 | tf_op jit(solution)/shard_map/ppermute | solution.py:271
  17.8 1.5 %collective-permute-start.7 = (bf16[448,384]{1,0:T(8,128)(2,1)S(1)}, bf16[448,384]{1,0:T(8,128)(2,1)S(1)}, u32[]{:S(2)}, u32[]{:S(2)}) collective-permute-start(bf16[448,384]{1,0:T(8,128)(2,1)S(1)} %pad_maximum_fusion.1.refs_6_.refs_3_), channel_id=1, source_target_pairs={{0,8},{1,9},{2,10},{3,11},{4,12},{5,13},{6,14},{7,15},{8,0},{9,1},... | collective-permute-start | bytes 1032200 | tf_op jit(solution)/shard_map/ppermute | solution.py:261
  19.4 1.5 %collective-permute-start.11 = (bf16[448,384]{1,0:T(8,128)(2,1)S(1)}, bf16[448,384]{1,0:T(8,128)(2,1)S(1)}, u32[]{:S(2)}, u32[]{:S(2)}) collective-permute-start(bf16[448,384]{1,0:T(8,128)(2,1)S(1)} %pad_maximum_fusion.1.refs_6_.refs_3_), channel_id=1, source_target_pairs={{0,16},{1,17},{2,18},{3,19},{4,20},{5,21},{6,22},{7,23},{8,24},{9,... | collective-permute-start | bytes 1032200 | tf_op jit(solution)/shard_map/ppermute | solution.py:261
  20.9 1.2 %collective-permute-done.9.refs_12_.refs_9_ = bf16[448,384]{1,0:T(8,128)(2,1)S(1)} collective-permute-done((bf16[448,384]{1,0:T(8,128)(2,1)S(1)}, bf16[448,384]{1,0:T(8,128)(2,1)S(1)}, u32[]{:S(2)}, u32[]{:S(2)}) %collective-permute-start.9) | collective-permute-done | bytes 344096 | tf_op jit(solution)/shard_map/ppermute | solution.py:261
  22.5 3.5 %collective-permute-start.1 = (bf16[2,16,3712]{2,1,0:T(8,128)(2,1)S(1)}, bf16[2,16,3712]{2,1,0:T(8,128)(2,1)S(1)}, u32[]{:S(2)}, u32[]{:S(2)}) collective-permute-start(bf16[2,16,3712]{2,1,0:T(8,128)(2,1)S(1)} %collective-permute-done.refs_1_), channel_id=1, source_target_pairs={{0,2},{1,3},{2,6},{3,7},{6,4},{7,5},{4,0},{5,1},{8,10},{9,11},{10,... | collective-permute-start | bytes 712712 | tf_op jit(solution)/shard_map/ppermute | solution.py:271
  26.0 2.8 %collective-permute-done.7.refs_10_.refs_7_ = bf16[448,384]{1,0:T(8,128)(2,1)S(1)} collective-permute-done((bf16[448,384]{1,0:T(8,128)(2,1)S(1)}, bf16[448,384]{1,0:T(8,128)(2,1)S(1)}, u32[]{:S(2)}, u32[]{:S(2)}) %collective-permute-start.7) | collective-permute-done | bytes 344096 | tf_op jit(solution)/shard_map/ppermute | solution.py:261
  29.2 1.5 %collective-permute-start.16 = (bf16[448,384]{1,0:T(8,128)(2,1)S(1)}, bf16[448,384]{1,0:T(8,128)(2,1)}, u32[]{:S(2)}, u32[]{:S(2)}) collective-permute-start(bf16[448,384]{1,0:T(8,128)(2,1)S(1)} %collective-permute-done.7.refs_10_.refs_7_), channel_id=1, source_target_pairs={{0,16},{1,17},{2,18},{3,19},{4,20},{5,21},{6,22},{7,23},{8,24},{9,... | collective-permute-start | bytes 1032200 | tf_op jit(solution)/shard_map/ppermute | solution.py:261
  31.8 3.6 %collective-permute-done.14.refs_13_ = bf16[448,384]{1,0:T(8,128)(2,1)S(1)} collective-permute-done((bf16[448,384]{1,0:T(8,128)(2,1)S(1)}, bf16[448,384]{1,0:T(8,128)(2,1)S(1)}, u32[]{:S(2)}, u32[]{:S(2)}) %collective-permute-start.14) | collective-permute-done | bytes 344096 | tf_op jit(solution)/shard_map/ppermute | solution.py:261
  35.3 2.6 %collective-permute-start.2 = (bf16[2,16,3712]{2,1,0:T(8,128)(2,1)S(1)}, bf16[2,16,3712]{2,1,0:T(8,128)(2,1)S(1)}, u32[]{:S(2)}, u32[]{:S(2)}) collective-permute-start(bf16[2,16,3712]{2,1,0:T(8,128)(2,1)S(1)} %collective-permute-done.1.refs_2_), channel_id=1, source_target_pairs={{0,2},{1,3},{2,6},{3,7},{6,4},{7,5},{4,0},{5,1},{8,10},{9,11},{10,... | collective-permute-start | bytes 712712 | tf_op jit(solution)/shard_map/ppermute | solution.py:271
  38.0 1.4 %collective-permute-done.16.refs_15_ = bf16[448,384]{1,0:T(8,128)(2,1)} collective-permute-done((bf16[448,384]{1,0:T(8,128)(2,1)S(1)}, bf16[448,384]{1,0:T(8,128)(2,1)}, u32[]{:S(2)}, u32[]{:S(2)}) %collective-permute-start.16) | collective-permute-done | bytes 344096 | tf_op jit(solution)/shard_map/ppermute | solution.py:261
  39.4 5.0 %collective-permute-done.2.refs_3_ = bf16[2,16,3712]{2,1,0:T(8,128)(2,1)S(1)} collective-permute-done((bf16[2,16,3712]{2,1,0:T(8,128)(2,1)S(1)}, bf16[2,16,3712]{2,1,0:T(8,128)(2,1)S(1)}, u32[]{:S(2)}, u32[]{:S(2)}) %collective-permute-start.2) | collective-permute-done | bytes 237600 | tf_op jit(solution)/shard_map/ppermute | solution.py:271
  44.4 1.6 %shard_map.129 = (f32[64,512]{1,0:T(8,128)S(1)}, f32[64,256]{1,0:T(8,128)S(1)}, bf16[4,16,128]{2,1,0:T(8,128)(2,1)S(1)}, bf16[2,64,896]{2,1,0:T(8,128)(2,1)}, bf...) custom-call(bf16[2,16,3712]{2,1,0:T(8,128)(2,1)S(1)} %get-tuple-element.26.refs_0_, ...), custom_call_target="tpu_custom_call" | custom-call | flops 352321536 | bytes 6209536 | tf_op jit(solution)/shard_map/pallas_call | solution.py:32
  46.7 1.5 %collective-permute-start.21 = (bf16[2,64,896]{2,1,0:T(8,128)(2,1)}, bf16[2,64,896]{2,1,0:T(8,128)(2,1)}, u32[]{:S(2)}, u32[]{:S(2)}) collective-permute-start(bf16[2,64,896]{2,1,0:T(8,128)(2,1)} %get-tuple-element.38), channel_id=1, source_target_pairs={{0,8},{1,9},{2,10},{3,11},{4,12},{5,13},{6,14},{7,15},{8,0},{9,1},... | collective-permute-start | bytes 688136 | tf_op jit(solution)/shard_map/ppermute | solution.py:261
  48.2 1.5 %collective-permute-start.22 = (bf16[2,64,896]{2,1,0:T(8,128)(2,1)}, bf16[2,64,896]{2,1,0:T(8,128)(2,1)}, u32[]{:S(2)}, u32[]{:S(2)}) collective-permute-start(bf16[2,64,896]{2,1,0:T(8,128)(2,1)} %get-tuple-element.39), channel_id=1, source_target_pairs={{0,16},{1,17},{2,18},{3,19},{4,20},{5,21},{6,22},{7,23},{8,24},{9,... | collective-permute-start | bytes 688136 | tf_op jit(solution)/shard_map/ppermute | solution.py:261
  49.7 1.1 %collective-permute-start.23 = (bf16[2,64,896]{2,1,0:T(8,128)(2,1)}, bf16[2,64,896]{2,1,0:T(8,128)(2,1)}, u32[]{:S(2)}, u32[]{:S(2)}) collective-permute-start(bf16[2,64,896]{2,1,0:T(8,128)(2,1)} %get-tuple-element.30.refs_0_), channel_id=1, source_target_pairs={{0,24},{1,25},{2,26},{3,27},{4,28},{5,29},{6,30},{7,31},{8,16},{9,... | collective-permute-start | bytes 688136 | tf_op jit(solution)/shard_map/ppermute | solution.py:261
  56.5 3.3 %shard_map.130 = (bf16[16,3712]{1,0:T(8,128)(2,1)S(1)}, bf16[16,3712]{1,0:T(8,128)(2,1)S(1)}, bf16[16,3712]{1,0:T(8,128)(2,1)S(1)}, bf16[16,3712]{1,0:T(8,128)(2...) custom-call(s32[4,1]{1,0:T(4,128)S(1)} %copy.14.cap_ref, ...), custom_call_target="tpu_custom_call" | custom-call | flops 234881024 | bytes 6537232 | tf_op jit(solution)/shard_map/pallas_call | solution.py:32
  59.9 1.2 %collective-permute-start.18 = (bf16[16,3712]{1,0:T(8,128)(2,1)S(1)}, bf16[16,3712]{1,0:T(8,128)(2,1)S(1)}, u32[]{:S(2)}, u32[]{:S(2)}) collective-permute-start(bf16[16,3712]{1,0:T(8,128)(2,1)S(1)} %get-tuple-element.32), channel_id=1, source_target_pairs={{0,4},{1,5},{2,0},{3,1},{6,2},{7,3},{4,6},{5,7},{8,12},{9,13},{10,... | collective-permute-start | bytes 356360 | tf_op jit(solution)/shard_map/ppermute | solution.py:271
  62.3 3.0 %collective-permute-start.19 = (bf16[16,3712]{1,0:T(8,128)(2,1)S(1)}, bf16[16,3712]{1,0:T(8,128)(2,1)S(1)}, u32[]{:S(2)}, u32[]{:S(2)}) collective-permute-start(bf16[16,3712]{1,0:T(8,128)(2,1)S(1)} %get-tuple-element.33), channel_id=1, source_target_pairs={{0,6},{1,7},{2,4},{3,5},{6,0},{7,1},{4,2},{5,3},{8,14},{9,15},{10,... | collective-permute-start | bytes 356360 | tf_op jit(solution)/shard_map/ppermute | solution.py:271
  65.6 3.1 %collective-permute-start.20 = (bf16[16,3712]{1,0:T(8,128)(2,1)S(1)}, bf16[16,3712]{1,0:T(8,128)(2,1)S(1)}, u32[]{:S(2)}, u32[]{:S(2)}) collective-permute-start(bf16[16,3712]{1,0:T(8,128)(2,1)S(1)} %get-tuple-element.34), channel_id=1, source_target_pairs={{0,2},{1,3},{2,6},{3,7},{6,4},{7,5},{4,0},{5,1},{8,10},{9,11},{10,... | collective-permute-start | bytes 356360 | tf_op jit(solution)/shard_map/ppermute | solution.py:271
  68.7 1.9 %collective-permute-done.19.refs_2_ = bf16[16,3712]{1,0:T(8,128)(2,1)S(1)} collective-permute-done((bf16[16,3712]{1,0:T(8,128)(2,1)S(1)}, bf16[16,3712]{1,0:T(8,128)(2,1)S(1)}, u32[]{:S(2)}, u32[]{:S(2)}) %collective-permute-start.19) | collective-permute-done | bytes 118816 | tf_op jit(solution)/shard_map/ppermute | solution.py:271
  70.6 1.5 %collective-permute-start.29 = (bf16[128,384]{1,0:T(8,128)(2,1)S(1)}, bf16[128,384]{1,0:T(8,128)(2,1)S(1)}, u32[]{:S(2)}, u32[]{:S(2)}) collective-permute-start(bf16[128,384]{1,0:T(8,128)(2,1)S(1)} %constant_dynamic-update-slice_fusion.refs_8_), channel_id=1, source_target_pairs={{0,8},{1,9},{2,10},{3,11},{4,12},{5,13},{6,14},{7,15},{8,0},{9,1},... | collective-permute-start | bytes 294920 | tf_op jit(solution)/shard_map/ppermute | solution.py:261
  72.1 3.2 %collective-permute-done.20.refs_3_ = bf16[16,3712]{1,0:T(8,128)(2,1)S(1)} collective-permute-done((bf16[16,3712]{1,0:T(8,128)(2,1)S(1)}, bf16[16,3712]{1,0:T(8,128)(2,1)S(1)}, u32[]{:S(2)}, u32[]{:S(2)}) %collective-permute-start.20) | collective-permute-done | bytes 118816 | tf_op jit(solution)/shard_map/ppermute | solution.py:271
  76.1 2.1 %collective-permute-start.31 = (bf16[128,384]{1,0:T(8,128)(2,1)S(1)}, bf16[128,384]{1,0:T(8,128)(2,1)S(1)}, u32[]{:S(2)}, u32[]{:S(2)}) collective-permute-start(bf16[128,384]{1,0:T(8,128)(2,1)S(1)} %constant_dynamic-update-slice_fusion.refs_8_), channel_id=1, source_target_pairs={{0,24},{1,25},{2,26},{3,27},{4,28},{5,29},{6,30},{7,31},{8,16},{9,... | collective-permute-start | bytes 294920 | tf_op jit(solution)/shard_map/ppermute | solution.py:261
  78.2 1.4 %shard_map.131 = (bf16[128,3584]{1,0:T(8,128)(2,1)}, f32[8,128]{1,0:T(8,128)}) custom-call(bf16[1,64,128]{2,1,0:T(8,128)(2,1)S(1)} %copy-done.14, s32[8,128]{1,0:T(8,128)S(1)} %bitcast.4, bf16[16,3712]{1,0:T(8,128)(2,1)S(1)} %get-tuple-element.31.refs_0_, bf16[16,3712]{1,0:T(8,128)(2,1)S(1)} %collective-permute-done.18.refs_1_, ...), custom_call_target="tpu_custom_call" | custom-call | flops 58720256 | bytes 1417216 | tf_op jit(solution)/shard_map/pallas_call | solution.py:32
  79.7 2.5 %collective-permute-done.30.refs_10_ = bf16[128,384]{1,0:T(8,128)(2,1)S(1)} collective-permute-done((bf16[128,384]{1,0:T(8,128)(2,1)S(1)}, bf16[128,384]{1,0:T(8,128)(2,1)S(1)}, u32[]{:S(2)}, u32[]{:S(2)}) %collective-permute-start.30) | collective-permute-done | bytes 98336 | tf_op jit(solution)/shard_map/ppermute | solution.py:261
  82.1 2.9 %shard_map.132 = (bf16[896,128]{1,0:T(8,128)(2,1)}, bf16[896,128]{1,0:T(8,128)(2,1)}, bf16[896,128]{1,0:T(8,128)(2,1)}) custom-call(bf16[2,64,896]{2,1,0:T(8,128)(2,1)} %get-tuple-element.37.refs_0_, bf16[2,64,896]{2,1,0:T(8,128)(2,1)} %collective-permute-done.21.refs_1_, bf16[2,64,896]{2,1,0:T(8,128)(2,1)} %collective-permute-done.22.refs_2_, ...), custom_call_target="tpu_custom_call" | custom-call | flops 352321536 | bytes 2916352 | tf_op jit(solution)/shard_map/pallas_call | solution.py:32
  (82 shorter events, 12.5 us)
Async XLA Ops:
  2.9 16.5 %collective-permute-start.3 = (bf16[448,384]{1,0:T(8,128)(2,1)S(1)}, bf16[448,384]{1,0:T(8,128)(2,1)S(1)}, u32[]{:S(2)}, u32[]{:S(2)}) collective-permute-start(bf16[448,384]{1,0:T(8,128)(2,1)S(1)} %pad_maximum_fusion.refs_4_.refs_1_), channel_id=1, source_target_pairs={{0,1},{1,0},{2,3},{3,2},{4,5},{5,4},{6,7},{7,6},{8,9},{9,8},{10,11... | collective-permute-start | bytes 1032200 | tf_op jit(solution)/shard_map/ppermute | solution.py:261
  7.8 10.0 %collective-permute-start = (bf16[2,16,3712]{2,1,0:T(8,128)(2,1)S(1)}, bf16[2,16,3712]{2,1,0:T(8,128)(2,1)S(1)}, u32[]{:S(2)}, u32[]{:S(2)}) collective-permute-start(bf16[2,16,3712]{2,1,0:T(8,128)(2,1)S(1)} %get-tuple-element.26.refs_0_), channel_id=1, source_target_pairs={{0,2},{1,3},{2,6},{3,7},{6,4},{7,5},{4,0},{5,1},{8,10},{9,11},{10,... | collective-permute-start | bytes 712712 | tf_op jit(solution)/shard_map/ppermute | solution.py:271
  10.4 10.5 %collective-permute-start.5 = (bf16[448,384]{1,0:T(8,128)(2,1)S(1)}, bf16[448,384]{1,0:T(8,128)(2,1)S(1)}, u32[]{:S(2)}, u32[]{:S(2)}) collective-permute-start(bf16[448,384]{1,0:T(8,128)(2,1)S(1)} %pad_maximum_fusion.refs_4_.refs_1_), channel_id=1, source_target_pairs={{0,8},{1,9},{2,10},{3,11},{4,12},{5,13},{6,14},{7,15},{8,0},{9,1},... | collective-permute-start | bytes 1032200 | tf_op jit(solution)/shard_map/ppermute | solution.py:261
  11.9 10.2 %collective-permute-start.9 = (bf16[448,384]{1,0:T(8,128)(2,1)S(1)}, bf16[448,384]{1,0:T(8,128)(2,1)S(1)}, u32[]{:S(2)}, u32[]{:S(2)}) collective-permute-start(bf16[448,384]{1,0:T(8,128)(2,1)S(1)} %pad_maximum_fusion.refs_4_.refs_1_), channel_id=1, source_target_pairs={{0,16},{1,17},{2,18},{3,19},{4,20},{5,21},{6,22},{7,23},{8,24},{9,... | collective-permute-start | bytes 1032200 | tf_op jit(solution)/shard_map/ppermute | solution.py:261
  13.5 9.0 %collective-permute-start.4 = (bf16[448,384]{1,0:T(8,128)(2,1)S(1)}, bf16[448,384]{1,0:T(8,128)(2,1)S(1)}, u32[]{:S(2)}, u32[]{:S(2)}) collective-permute-start(bf16[448,384]{1,0:T(8,128)(2,1)S(1)} %pad_maximum_fusion.1.refs_6_.refs_3_), channel_id=1, source_target_pairs={{0,1},{1,0},{2,3},{3,2},{4,5},{5,4},{6,7},{7,6},{8,9},{9,8},{10,11... | collective-permute-start | bytes 1032200 | tf_op jit(solution)/shard_map/ppermute | solution.py:261
  17.8 10.9 %collective-permute-start.7 = (bf16[448,384]{1,0:T(8,128)(2,1)S(1)}, bf16[448,384]{1,0:T(8,128)(2,1)S(1)}, u32[]{:S(2)}, u32[]{:S(2)}) collective-permute-start(bf16[448,384]{1,0:T(8,128)(2,1)S(1)} %pad_maximum_fusion.1.refs_6_.refs_3_), channel_id=1, source_target_pairs={{0,8},{1,9},{2,10},{3,11},{4,12},{5,13},{6,14},{7,15},{8,0},{9,1},... | collective-permute-start | bytes 1032200 | tf_op jit(solution)/shard_map/ppermute | solution.py:261
  19.4 9.8 %collective-permute-start.11 = (bf16[448,384]{1,0:T(8,128)(2,1)S(1)}, bf16[448,384]{1,0:T(8,128)(2,1)S(1)}, u32[]{:S(2)}, u32[]{:S(2)}) collective-permute-start(bf16[448,384]{1,0:T(8,128)(2,1)S(1)} %pad_maximum_fusion.1.refs_6_.refs_3_), channel_id=1, source_target_pairs={{0,16},{1,17},{2,18},{3,19},{4,20},{5,21},{6,22},{7,23},{8,24},{9,... | collective-permute-start | bytes 1032200 | tf_op jit(solution)/shard_map/ppermute | solution.py:261
  20.9 10.3 %collective-permute-start.6 = (bf16[448,384]{1,0:T(8,128)(2,1)S(1)}, bf16[448,384]{1,0:T(8,128)(2,1)S(1)}, u32[]{:S(2)}, u32[]{:S(2)}) collective-permute-start(bf16[448,384]{1,0:T(8,128)(2,1)S(1)} %collective-permute-done.5.refs_8_.refs_5_), channel_id=1, source_target_pairs={{0,1},{1,0},{2,3},{3,2},{4,5},{5,4},{6,7},{7,6},{8,9},{9,8},{10,11... | collective-permute-start | bytes 1032200 | tf_op jit(solution)/shard_map/ppermute | solution.py:261
  22.1 13.2 %collective-permute-start.14 = (bf16[448,384]{1,0:T(8,128)(2,1)S(1)}, bf16[448,384]{1,0:T(8,128)(2,1)S(1)}, u32[]{:S(2)}, u32[]{:S(2)}) collective-permute-start(bf16[448,384]{1,0:T(8,128)(2,1)S(1)} %collective-permute-done.9.refs_12_.refs_9_), channel_id=1, source_target_pairs={{0,8},{1,9},{2,10},{3,11},{4,12},{5,13},{6,14},{7,15},{8,0},{9,1},... | collective-permute-start | bytes 1032200 | tf_op jit(solution)/shard_map/ppermute | solution.py:261
  22.5 8.7 %collective-permute-start.1 = (bf16[2,16,3712]{2,1,0:T(8,128)(2,1)S(1)}, bf16[2,16,3712]{2,1,0:T(8,128)(2,1)S(1)}, u32[]{:S(2)}, u32[]{:S(2)}) collective-permute-start(bf16[2,16,3712]{2,1,0:T(8,128)(2,1)S(1)} %collective-permute-done.refs_1_), channel_id=1, source_target_pairs={{0,2},{1,3},{2,6},{3,7},{6,4},{7,5},{4,0},{5,1},{8,10},{9,11},{10,... | collective-permute-start | bytes 712712 | tf_op jit(solution)/shard_map/ppermute | solution.py:271
  28.8 6.5 %collective-permute-start.8 = (bf16[448,384]{1,0:T(8,128)(2,1)S(1)}, bf16[448,384]{1,0:T(8,128)(2,1)S(1)}, u32[]{:S(2)}, u32[]{:S(2)}) collective-permute-start(bf16[448,384]{1,0:T(8,128)(2,1)S(1)} %collective-permute-done.7.refs_10_.refs_7_), channel_id=1, source_target_pairs={{0,1},{1,0},{2,3},{3,2},{4,5},{5,4},{6,7},{7,6},{8,9},{9,8},{10,11... | collective-permute-start | bytes 1032200 | tf_op jit(solution)/shard_map/ppermute | solution.py:261
  29.2 10.2 %collective-permute-start.16 = (bf16[448,384]{1,0:T(8,128)(2,1)S(1)}, bf16[448,384]{1,0:T(8,128)(2,1)}, u32[]{:S(2)}, u32[]{:S(2)}) collective-permute-start(bf16[448,384]{1,0:T(8,128)(2,1)S(1)} %collective-permute-done.7.refs_10_.refs_7_), channel_id=1, source_target_pairs={{0,16},{1,17},{2,18},{3,19},{4,20},{5,21},{6,22},{7,23},{8,24},{9,... | collective-permute-start | bytes 1032200 | tf_op jit(solution)/shard_map/ppermute | solution.py:261
  31.2 8.1 %collective-permute-start.10 = (bf16[448,384]{1,0:T(8,128)(2,1)S(1)}, bf16[448,384]{1,0:T(8,128)(2,1)S(1)}, u32[]{:S(2)}, u32[]{:S(2)}) collective-permute-start(bf16[448,384]{1,0:T(8,128)(2,1)S(1)} %collective-permute-done.9.refs_12_.refs_9_), channel_id=1, source_target_pairs={{0,1},{1,0},{2,3},{3,2},{4,5},{5,4},{6,7},{7,6},{8,9},{9,8},{10,11... | collective-permute-start | bytes 1032200 | tf_op jit(solution)/shard_map/ppermute | solution.py:261
  31.2 8.1 %collective-permute-start.12 = (bf16[448,384]{1,0:T(8,128)(2,1)S(1)}, bf16[448,384]{1,0:T(8,128)(2,1)S(1)}, u32[]{:S(2)}, u32[]{:S(2)}) collective-permute-start(bf16[448,384]{1,0:T(8,128)(2,1)S(1)} %collective-permute-done.11.refs_14_.refs_11_), channel_id=1, source_target_pairs={{0,1},{1,0},{2,3},{3,2},{4,5},{5,4},{6,7},{7,6},{8,9},{9,8},{10,11... | collective-permute-start | bytes 1032200 | tf_op jit(solution)/shard_map/ppermute | solution.py:261
  35.3 15.6 %collective-permute-start.15 = (bf16[448,384]{1,0:T(8,128)(2,1)S(1)}, bf16[448,384]{1,0:T(8,128)(2,1)S(1)}, u32[]{:S(2)}, u32[]{:S(2)}) collective-permute-start(bf16[448,384]{1,0:T(8,128)(2,1)S(1)} %collective-permute-done.14.refs_13_), channel_id=1, source_target_pairs={{0,1},{1,0},{2,3},{3,2},{4,5},{5,4},{6,7},{7,6},{8,9},{9,8},{10,11... | collective-permute-start | bytes 1032200 | tf_op jit(solution)/shard_map/ppermute | solution.py:261
  35.3 9.1 %collective-permute-start.2 = (bf16[2,16,3712]{2,1,0:T(8,128)(2,1)S(1)}, bf16[2,16,3712]{2,1,0:T(8,128)(2,1)S(1)}, u32[]{:S(2)}, u32[]{:S(2)}) collective-permute-start(bf16[2,16,3712]{2,1,0:T(8,128)(2,1)S(1)} %collective-permute-done.1.refs_2_), channel_id=1, source_target_pairs={{0,2},{1,3},{2,6},{3,7},{6,4},{7,5},{4,0},{5,1},{8,10},{9,11},{10,... | collective-permute-start | bytes 712712 | tf_op jit(solution)/shard_map/ppermute | solution.py:271
  39.4 12.3 %collective-permute-start.17 = (bf16[448,384]{1,0:T(8,128)(2,1)}, bf16[448,384]{1,0:T(8,128)(2,1)}, u32[]{:S(2)}, u32[]{:S(2)}) collective-permute-start(bf16[448,384]{1,0:T(8,128)(2,1)} %collective-permute-done.16.refs_15_), channel_id=1, source_target_pairs={{0,1},{1,0},{2,3},{3,2},{4,5},{5,4},{6,7},{7,6},{8,9},{9,8},{10,11... | collective-permute-start | bytes 1032200 | tf_op jit(solution)/shard_map/ppermute | solution.py:261
  46.7 14.3 %collective-permute-start.21 = (bf16[2,64,896]{2,1,0:T(8,128)(2,1)}, bf16[2,64,896]{2,1,0:T(8,128)(2,1)}, u32[]{:S(2)}, u32[]{:S(2)}) collective-permute-start(bf16[2,64,896]{2,1,0:T(8,128)(2,1)} %get-tuple-element.38), channel_id=1, source_target_pairs={{0,8},{1,9},{2,10},{3,11},{4,12},{5,13},{6,14},{7,15},{8,0},{9,1},... | collective-permute-start | bytes 688136 | tf_op jit(solution)/shard_map/ppermute | solution.py:261
  48.2 1.5 %collective-permute-start.13 = (bf16[4,16,128]{2,1,0:T(8,128)(2,1)S(1)}, bf16[4,16,128]{2,1,0:T(8,128)(2,1)S(1)}, u32[]{:S(2)}, u32[]{:S(2)}) collective-permute-start(bf16[4,16,128]{2,1,0:T(8,128)(2,1)S(1)} %get-tuple-element.27.own_ref), channel_id=1, source_target_pairs={{0,1},{1,0},{2,3},{3,2},{4,5},{5,4},{6,7},{7,6},{8,9},{9,8},{10,11... | collective-permute-start | bytes 49160 | tf_op jit(solution)/shard_map/ppermute | solution.py:261
  48.2 13.2 %collective-permute-start.22 = (bf16[2,64,896]{2,1,0:T(8,128)(2,1)}, bf16[2,64,896]{2,1,0:T(8,128)(2,1)}, u32[]{:S(2)}, u32[]{:S(2)}) collective-permute-start(bf16[2,64,896]{2,1,0:T(8,128)(2,1)} %get-tuple-element.39), channel_id=1, source_target_pairs={{0,16},{1,17},{2,18},{3,19},{4,20},{5,21},{6,22},{7,23},{8,24},{9,... | collective-permute-start | bytes 688136 | tf_op jit(solution)/shard_map/ppermute | solution.py:261
  49.7 11.8 %collective-permute-start.23 = (bf16[2,64,896]{2,1,0:T(8,128)(2,1)}, bf16[2,64,896]{2,1,0:T(8,128)(2,1)}, u32[]{:S(2)}, u32[]{:S(2)}) collective-permute-start(bf16[2,64,896]{2,1,0:T(8,128)(2,1)} %get-tuple-element.30.refs_0_), channel_id=1, source_target_pairs={{0,24},{1,25},{2,26},{3,27},{4,28},{5,29},{6,30},{7,31},{8,16},{9,... | collective-permute-start | bytes 688136 | tf_op jit(solution)/shard_map/ppermute | solution.py:261
  51.6 10.4 %collective-permute-start.24 = (bf16[2,64,896]{2,1,0:T(8,128)(2,1)}, bf16[2,64,896]{2,1,0:T(8,128)(2,1)}, u32[]{:S(2)}, u32[]{:S(2)}) collective-permute-start(bf16[2,64,896]{2,1,0:T(8,128)(2,1)} %get-tuple-element.37.refs_0_), channel_id=1, source_target_pairs={{0,1},{1,0},{2,3},{3,2},{4,5},{5,4},{6,7},{7,6},{8,9},{9,8},{10,11... | collective-permute-start | bytes 688136 | tf_op jit(solution)/shard_map/ppermute | solution.py:261
  59.9 5.7 %collective-permute-start.18 = (bf16[16,3712]{1,0:T(8,128)(2,1)S(1)}, bf16[16,3712]{1,0:T(8,128)(2,1)S(1)}, u32[]{:S(2)}, u32[]{:S(2)}) collective-permute-start(bf16[16,3712]{1,0:T(8,128)(2,1)S(1)} %get-tuple-element.32), channel_id=1, source_target_pairs={{0,4},{1,5},{2,0},{3,1},{6,2},{7,3},{4,6},{5,7},{8,12},{9,13},{10,... | collective-permute-start | bytes 356360 | tf_op jit(solution)/shard_map/ppermute | solution.py:271
  61.1 1.2 %collective-permute-start.28 = (bf16[64,384]{1,0:T(8,128)(2,1)S(1)}, bf16[64,384]{1,0:T(8,128)(2,1)S(1)}, u32[]{:S(2)}, u32[]{:S(2)}) collective-permute-start(bf16[64,384]{1,0:T(8,128)(2,1)S(1)} %get-tuple-element.41), channel_id=1, source_target_pairs={{0,1},{1,0},{2,3},{3,2},{4,5},{5,4},{6,7},{7,6},{8,9},{9,8},{10,11... | collective-permute-start | bytes 147464 | tf_op jit(solution)/shard_map/ppermute | solution.py:261
  61.5 14.6 %collective-permute-start.25 = (bf16[2,64,896]{2,1,0:T(8,128)(2,1)}, bf16[2,64,896]{2,1,0:T(8,128)(2,1)S(1)}, u32[]{:S(2)}, u32[]{:S(2)}) collective-permute-start(bf16[2,64,896]{2,1,0:T(8,128)(2,1)} %collective-permute-done.21.refs_1_), channel_id=1, source_target_pairs={{0,1},{1,0},{2,3},{3,2},{4,5},{5,4},{6,7},{7,6},{8,9},{9,8},{10,11... | collective-permute-start | bytes 688136 | tf_op jit(solution)/shard_map/ppermute | solution.py:261
  61.6 18.1 %collective-permute-start.26 = (bf16[2,64,896]{2,1,0:T(8,128)(2,1)}, bf16[2,64,896]{2,1,0:T(8,128)(2,1)S(1)}, u32[]{:S(2)}, u32[]{:S(2)}) collective-permute-start(bf16[2,64,896]{2,1,0:T(8,128)(2,1)} %collective-permute-done.22.refs_2_), channel_id=1, source_target_pairs={{0,1},{1,0},{2,3},{3,2},{4,5},{5,4},{6,7},{7,6},{8,9},{9,8},{10,11... | collective-permute-start | bytes 688136 | tf_op jit(solution)/shard_map/ppermute | solution.py:261
  62.0 17.7 %collective-permute-start.27 = (bf16[2,64,896]{2,1,0:T(8,128)(2,1)}, bf16[2,64,896]{2,1,0:T(8,128)(2,1)S(1)}, u32[]{:S(2)}, u32[]{:S(2)}) collective-permute-start(bf16[2,64,896]{2,1,0:T(8,128)(2,1)} %collective-permute-done.23.refs_3_), channel_id=1, source_target_pairs={{0,1},{1,0},{2,3},{3,2},{4,5},{5,4},{6,7},{7,6},{8,9},{9,8},{10,11... | collective-permute-start | bytes 688136 | tf_op jit(solution)/shard_map/ppermute | solution.py:261
  62.3 8.3 %collective-permute-start.19 = (bf16[16,3712]{1,0:T(8,128)(2,1)S(1)}, bf16[16,3712]{1,0:T(8,128)(2,1)S(1)}, u32[]{:S(2)}, u32[]{:S(2)}) collective-permute-start(bf16[16,3712]{1,0:T(8,128)(2,1)S(1)} %get-tuple-element.33), channel_id=1, source_target_pairs={{0,6},{1,7},{2,4},{3,5},{6,0},{7,1},{4,2},{5,3},{8,14},{9,15},{10,... | collective-permute-start | bytes 356360 | tf_op jit(solution)/shard_map/ppermute | solution.py:271
  65.6 9.7 %collective-permute-start.20 = (bf16[16,3712]{1,0:T(8,128)(2,1)S(1)}, bf16[16,3712]{1,0:T(8,128)(2,1)S(1)}, u32[]{:S(2)}, u32[]{:S(2)}) collective-permute-start(bf16[16,3712]{1,0:T(8,128)(2,1)S(1)} %get-tuple-element.34), channel_id=1, source_target_pairs={{0,2},{1,3},{2,6},{3,7},{6,4},{7,5},{4,0},{5,1},{8,10},{9,11},{10,... | collective-permute-start | bytes 356360 | tf_op jit(solution)/shard_map/ppermute | solution.py:271
  70.6 9.1 %collective-permute-start.29 = (bf16[128,384]{1,0:T(8,128)(2,1)S(1)}, bf16[128,384]{1,0:T(8,128)(2,1)S(1)}, u32[]{:S(2)}, u32[]{:S(2)}) collective-permute-start(bf16[128,384]{1,0:T(8,128)(2,1)S(1)} %constant_dynamic-update-slice_fusion.refs_8_), channel_id=1, source_target_pairs={{0,8},{1,9},{2,10},{3,11},{4,12},{5,13},{6,14},{7,15},{8,0},{9,1},... | collective-permute-start | bytes 294920 | tf_op jit(solution)/shard_map/ppermute | solution.py:261
  75.2 6.9 %collective-permute-start.30 = (bf16[128,384]{1,0:T(8,128)(2,1)S(1)}, bf16[128,384]{1,0:T(8,128)(2,1)S(1)}, u32[]{:S(2)}, u32[]{:S(2)}) collective-permute-start(bf16[128,384]{1,0:T(8,128)(2,1)S(1)} %constant_dynamic-update-slice_fusion.refs_8_), channel_id=1, source_target_pairs={{0,16},{1,17},{2,18},{3,19},{4,20},{5,21},{6,22},{7,23},{8,24},{9,... | collective-permute-start | bytes 294920 | tf_op jit(solution)/shard_map/ppermute | solution.py:261
  76.1 6.0 %collective-permute-start.31 = (bf16[128,384]{1,0:T(8,128)(2,1)S(1)}, bf16[128,384]{1,0:T(8,128)(2,1)S(1)}, u32[]{:S(2)}, u32[]{:S(2)}) collective-permute-start(bf16[128,384]{1,0:T(8,128)(2,1)S(1)} %constant_dynamic-update-slice_fusion.refs_8_), channel_id=1, source_target_pairs={{0,24},{1,25},{2,26},{3,27},{4,28},{5,29},{6,30},{7,31},{8,16},{9,... | collective-permute-start | bytes 294920 | tf_op jit(solution)/shard_map/ppermute | solution.py:261
  (19 other events, 50.0 us)

commit v4 on v3

v4 whole, which is shorter than its diff:
```python
import functools

import jax
import jax.numpy as jnp
from jax import lax
from jax.experimental import pallas as pl
from jax.experimental.pallas import tpu as pltpu
from jax.sharding import PartitionSpec as P

EXPERTS = 128
SLOT = 16
BLOCK = 128
SPLIT = 8
CORES = 2
CHIPS = SPLIT // CORES
LANES = 128
F32 = jnp.float32
BF16 = jnp.bfloat16
PARTS = 4
ANY = pl.BlockSpec(memory_space=pl.ANY)
VMEM = pl.BlockSpec(memory_space=pltpu.VMEM)


def shape(dims, kind=BF16):
    return jax.ShapeDtypeStruct(dims, kind)


def call(kernel, outs, args, inside=(), scratch=(), flops=0):
    size = sum(a.size * a.dtype.itemsize for a in args) + sum(
        o.size * o.dtype.itemsize for o in outs
    )
    return pl.pallas_call(
        kernel,
        out_shape=tuple(outs),
        in_specs=[VMEM if n in inside else ANY for n in range(len(args))],
        out_specs=tuple([VMEM] * len(outs)),
        scratch_shapes=scratch,
        compiler_params=pltpu.CompilerParams(vmem_limit_bytes=24 * 1024 * 1024),
        cost_estimate=pl.CostEstimate(flops=flops, bytes_accessed=size, transcendentals=0),
    )(*args)


def buffers(arrays):
    held = [pltpu.VMEM(a.shape, a.dtype) for a in arrays]
    return held + [pltpu.SemaphoreType.DMA((len(arrays),))]


def fetch(refs, held, sems):
    copies = [
        pltpu.make_async_copy(ref, buffer, sems.at[n])
        for n, (ref, buffer) in enumerate(zip(refs, held))
    ]
    for copy in copies:
        copy.start()
    return copies


def dot(a, b, dims=((1,), (0,))):
    return lax.dot_general(a, b, (dims, ((), ())), preferred_element_type=F32)


def iota(dims, axis):
    return lax.broadcasted_iota(jnp.int32, dims, axis)


def pack_kernel(rep, flight, live_ref, tok_ref, grad_ref, ids_ref, rw_ref, *refs):
    pays, placed_ref = refs[:flight], refs[flight]
    live, data, rows, sems = refs[flight + 1 :]
    r = lax.axis_index("rep")
    mine = lax.axis_index("ep") // SPLIT
    count, model = tok_ref.shape
    width = model // rep
    spacing = EXPERTS // flight
    live_copy = pltpu.make_async_copy(live_ref, live, sems.at[2 * PARTS])
    live_copy.start()
    copies = []
    for part, ref in enumerate((tok_ref, grad_ref)):
        for p in range(PARTS):
            some = pl.ds(p * (count // PARTS), count // PARTS)
            copy = pltpu.make_async_copy(
                ref.at[some], data.at[part, some], sems.at[part * PARTS + p]
            )
            copy.start()
            copies.append(copy)
    live_copy.wait()
    token = iota((1, count), 1)
    upper = (iota((count, count), 0) <= iota((count, count), 1)).astype(BF16)
    slot = iota((SLOT, count), 0).astype(F32)
    lane = iota((SLOT, LANES), 1)
    ids = ids_ref[...]
    weights = rw_ref[...].astype(F32)
    firsts, headers = [], []
    for w in range(flight):
        expert = jnp.bitwise_xor(mine, w)
        match = ids == expert * spacing
        routed = jnp.any(match, axis=0, keepdims=True) & (token < live[r])
        weight = jnp.sum(jnp.where(match, weights, 0.0), axis=0, keepdims=True)
        routed = jnp.broadcast_to(jnp.where(routed, 1.0, 0.0), (SLOT, count))
        rank = dot(routed.astype(BF16), upper) - 1.0
        placed = jnp.where(rank == slot, routed, 0.0)
        column = jnp.sum(placed * weight, axis=1, keepdims=True)
        headers.append(jnp.where(lane == 0, column, 0.0).astype(BF16))
        placed = placed.astype(BF16)
        firsts.append(placed)
        placed_ref[w] = jnp.concatenate([placed] * CHIPS, axis=0)
    for part in range(2):
        for p in range(PARTS):
            copies[part * PARTS + p].wait()
        for w in range(flight):
            chosen = dot(firsts[w], data[part]).astype(BF16)
            for b in range(rep):
                rows[b] = chosen[:, b * width : (b + 1) * width]
            for k in range(rep):
                pays[w][part, :, k * width : (k + 1) * width] = rows[jnp.bitwise_xor(r, k)]
            pays[w][part, :, model:] = headers[w]


def halves_kernel(gate_ref, up_ref, down_ref, first_ref, second_ref, sems):
    half = first_ref.shape[0]
    copies = []
    for h, out in enumerate((first_ref, second_ref)):
        for n, ref in enumerate((gate_ref, up_ref, down_ref)):
            units = ref.shape[1]
            copy = pltpu.make_async_copy(
                ref.at[pl.ds(h * half, half)],
                out.at[:, pl.ds(n * units, units)],
                sems.at[3 * h + n],
            )
            copy.start()
            copies.append(copy)
    for copy in copies:
        copy.wait()


def forward_kernel(rep, count, *refs):
    blocks, pieces = refs[: 2 * count], refs[2 * count : 2 * count + 2 * rep - 2]
    many = len(blocks) + len(pieces)
    outs, held, sems = refs[many : many + rep + 3], refs[many + rep + 3 : -1], refs[-1]
    pre_ref, rates_ref, last_ref, parts = outs[0], outs[1], outs[2], outs[3:]
    copies = fetch(blocks + pieces, held, sems)
    blocks, pieces = held[: 2 * count], held[2 * count :]
    half, columns = pieces[0].shape
    width = 2 * half
    units = columns // 3
    for n in range(2 * count):
        copies[n].wait()
    rows = [jnp.concatenate([b[part] for b in blocks], axis=0) for part in range(2)]
    for j in range(2 * count):
        rates_ref[j] = blocks[j][0, :, rep * width :]
    for k in range(rep):
        for part in range(2):
            own = rows[part][: parts[k].shape[1], k * width : (k + 1) * width]
            parts[k][part] = own
    for part in range(2):
        last_ref[part] = rows[part][:, (rep - 1) * width : rep * width]
    sum_x, sum_d = 0.0, 0.0
    for p in range(len(pieces)):
        copies[2 * count + p].wait()
        some = slice(p * half, (p + 1) * half)
        sum_x = sum_x + dot(rows[0][:, some], pieces[p][:, : 2 * units])
        sum_d = sum_d + dot(rows[1][:, some], pieces[p][:, 2 * units :])
    pre_ref[:, : 2 * units] = sum_x
    pre_ref[:, 2 * units :] = sum_d


def hidden_kernel(rep, count, cap_ref, rates_ref, pre_ref, last_ref, *refs):
    pieces, outs, rest = refs[: 2 * rep], refs[2 * rep : 2 * rep + 3], refs[2 * rep + 3 :]
    own_ref, other_ref, grads_ref = outs
    held, sems, cap, sem = rest[: 2 * rep], rest[-3], rest[-2], rest[-1]
    cap_copy = pltpu.make_async_copy(cap_ref, cap, sem)
    cap_copy.start()
    order = list(range(2 * rep - 2, 2 * rep)) + list(range(2 * rep - 2))
    copies = fetch([pieces[p] for p in order], [held[p] for p in order], sems)
    copies = {p: copy for p, copy in zip(order, copies)}
    half, columns = pieces[0].shape
    width = 2 * half
    units = columns // 3
    own_rows = count * SLOT
    r = lax.axis_index("rep")
    e = lax.axis_index("ep")
    mine = e // SPLIT
    cap_copy.wait()
    capacity = (BLOCK * cap[r, mine]).astype(F32)
    lane = iota((SLOT, LANES), 1)
    sources, rates, counts = [], [], []
    for n in range(2 * count):
        core, j = n // count, n % count
        sources.append(jnp.bitwise_xor(e, CORES * j + core))
        rate = jnp.where(lane == 0, rates_ref[n].astype(F32), 0.0)
        rate = jnp.sum(rate, axis=1, keepdims=True)
        rates.append(rate)
        counts.append(jnp.sum(jnp.where(rate > 0.0, 1.0, 0.0), axis=0, keepdims=True))
    slot = iota((SLOT, 1), 0).astype(F32)
    rate_rows, kept_rows = [], []
    for n in range(2 * count):
        start = jnp.zeros((1, 1), F32)
        for other in range(2 * count):
            start = start + jnp.where(sources[other] < sources[n], counts[other], 0.0)
        kept = jnp.where((rates[n] > 0.0) & (start + slot < capacity), 1.0, 0.0)
        kept_rows.append(kept)
        rate_rows.append(rates[n] * kept)
    rate = jnp.concatenate(rate_rows, axis=0)
    kept = jnp.concatenate(kept_rows, axis=0)

    sum_x = pre_ref[:, : 2 * units]
    sum_d = pre_ref[:, 2 * units :]
    for h in range(2):
        p = 2 * rep - 2 + h
        copies[p].wait()
        some = slice(h * half, (h + 1) * half)
        sum_x = sum_x + dot(last_ref[0, :, some], held[p][:, : 2 * units])
        sum_d = sum_d + dot(last_ref[1, :, some], held[p][:, 2 * units :])
    pre_gate, pre_up, back_hidden = sum_x[:, :units], sum_x[:, units:], sum_d
    sig = 1.0 / (1.0 + jnp.exp(-pre_gate))
    activated = pre_gate * sig
    hidden = activated * pre_up
    score = jnp.sum(hidden * back_hidden, axis=1, keepdims=True) * kept
    lane = iota((2 * own_rows, LANES), 1)
    scores = jnp.where(lane == e % CORES, score, 0.0).astype(BF16)
    scaled = back_hidden * rate
    gate_grad = (scaled * pre_up * sig * (1.0 + pre_gate * (1.0 - sig))).astype(BF16)
    up_grad = (scaled * activated).astype(BF16)
    grads_ref[:, :units] = gate_grad
    grads_ref[:, units : 2 * units] = up_grad
    grads_ref[:, 2 * units :] = (hidden * rate).astype(BF16)
    pair = jnp.concatenate([gate_grad, up_grad], axis=1)
    for p in range(2 * rep):
        if p < 2 * rep - 2:
            copies[p].wait()
        back = dot(pair, held[p][:, : 2 * units], ((1,), (1,))).astype(BF16)
        own_ref[:, p * half : (p + 1) * half] = back[:own_rows]
        other_ref[:, p * half : (p + 1) * half] = back[own_rows:]
    own_ref[:, rep * width :] = scores[:own_rows]
    other_ref[:, rep * width :] = scores[own_rows:]


def sum_kernel(own_ref, got_ref, *outs):
    for j, out in enumerate(outs):
        some = slice(j * SLOT, (j + 1) * SLOT)
        out[...] = (own_ref[some].astype(F32) + got_ref[some].astype(F32)).astype(BF16)


def weight_kernel(rep, units, *refs):
    many = 3 * rep - 1
    outs, held, sems = refs[many : many + 3], refs[many + 3 : -1], refs[-1]
    for copy in fetch(refs[:many], held, sems):
        copy.wait()
    own, other, grads = held[:rep], held[rep : 2 * rep - 1], held[2 * rep - 1 :]
    got = jnp.concatenate([g[...] for g in grads], axis=0)
    rows = [
        jnp.concatenate(
            [own[0][part]]
            + [ref[part] for k in range(1, rep) for ref in (own[k], other[k - 1])],
            axis=0,
        )
        for part in range(2)
    ]
    gate_up = dot(rows[0], got[:, : 2 * units], ((0,), (0,)))
    outs[0][...] = gate_up[:, :units].astype(BF16)
    outs[1][...] = gate_up[:, units:].astype(BF16)
    outs[2][...] = dot(rows[1], got[:, 2 * units :], ((0,), (0,))).astype(BF16)


def token_kernel(rep, flight, placed_ref, ids_ref, *refs):
    many = flight * CHIPS
    out_ref, weight_ref, blocks = refs[many : many + 3]
    held, sems = refs[many + 3 : -1], refs[-1]
    for copy in fetch(refs[:many], held, sems):
        copy.wait()
    r = lax.axis_index("rep")
    mine = lax.axis_index("ep") // SPLIT
    spacing = EXPERTS // flight
    width = out_ref.shape[1] // rep
    joined = [
        jnp.concatenate([b[...] for b in held[w * CHIPS : (w + 1) * CHIPS]], axis=0)
        for w in range(flight)
    ]
    for k in range(rep):
        total = 0.0
        for w in range(flight):
            some = joined[w][:, k * width : (k + 1) * width]
            total = total + dot(placed_ref[w], some, ((0,), (0,)))
        blocks[jnp.bitwise_xor(r, k)] = total.astype(BF16)
    for b in range(rep):
        out_ref[:, b * width : (b + 1) * width] = blocks[b]
    result = jnp.zeros(weight_ref.shape, F32)
    for w in range(flight):
        score = dot(joined[w][:, rep * width :], placed_ref[w], ((0,), (0,)))
        score = jnp.sum(score, axis=0, keepdims=True)
        match = ids_ref[...] == jnp.bitwise_xor(mine, w) * spacing
        result = result + jnp.where(match, score, 0.0)
    weight_ref[...] = result


def local(
    tokens, out_grad, expert_ids, route_weight, live_count, cap_blocks, w_gate, w_up, w_down_t
):
    rep = lax.axis_size("rep")
    ep = lax.axis_size("ep")
    flight = ep // SPLIT
    count = ep // CORES
    tok_count, model_dim = tokens.shape
    width, units = w_gate.shape
    half = width // 2
    rows = count * SLOT
    payload = model_dim + LANES

    def send(array, rep_bits, ep_bits):
        mask = rep_bits * ep + ep_bits
        pairs = [(a, a ^ mask) for a in range(rep * ep)]
        return lax.ppermute(array, ("rep", "ep"), pairs)

    first, second = call(
        halves_kernel,
        [shape((half, 3 * units))] * 2,
        [w_gate, w_up, w_down_t],
        scratch=[pltpu.SemaphoreType.DMA((6,))],
    )
    halves = {(0, 0): first, (0, 1): second}
    for k in range(1, rep):
        low, high = k & -k, 1 << (k.bit_length() - 1)
        halves[k, 0] = send(halves[k ^ low, 0], low, 0)
        halves[k, 1] = send(halves[k ^ high, 1], high, 0)
    pieces = [halves[k, h] for k in range(rep) for h in range(2)]

    packed = call(
        functools.partial(pack_kernel, rep, flight),
        [shape((2, SLOT, payload))] * flight + [shape((flight, CHIPS * SLOT, tok_count))],
        [live_count, tokens, out_grad, expert_ids.T, route_weight.T],
        inside=(3, 4),
        scratch=[
            pltpu.SMEM(live_count.shape, jnp.int32),
            pltpu.VMEM((2, tok_count, model_dim), BF16),
            pltpu.VMEM((rep, SLOT, width), BF16),
            pltpu.SemaphoreType.DMA((2 * PARTS + 1,)),
        ],
    )
    pays, placed = packed[:flight], packed[flight]
    blocks = [pays[0]] + [send(pays[j // CHIPS], 0, CORES * j) for j in range(1, count)]
    blocks = blocks + [send(block, 0, 1) for block in blocks]

    operands = blocks + pieces[:-2]
    results = call(
        functools.partial(forward_kernel, rep, count),
        [shape((2 * rows, 3 * units), F32), shape((2 * count, SLOT, LANES))]
        + [shape((2, 2 * rows, width))] * 2
        + [shape((2, rows, width))] * (rep - 1),
        operands,
        scratch=buffers(operands),
        flops=2 * 2 * rows * model_dim * 3 * units,
    )
    pre, rates, last, parts = results[0], results[1], results[2], list(results[3:])
    own, other, grads = call(
        functools.partial(hidden_kernel, rep, count),
        [shape((rows, payload))] * 2 + [shape((2 * rows, 3 * units))],
        [cap_blocks, rates, pre, last] + pieces,
        inside=(1, 2, 3),
        scratch=buffers(pieces)
        + [pltpu.SMEM(cap_blocks.shape, jnp.int32), pltpu.SemaphoreType.DMA(())],
        flops=2 * 2 * rows * model_dim * 2 * units,
    )
    backs = call(
        sum_kernel, [shape((SLOT, payload))] * count, [own, send(other, 0, 1)], inside=(0, 1)
    )
    backs = [backs[0]] + [send(backs[j], 0, CORES * j) for j in range(1, count)]

    parts, grads = lax.optimization_barrier((parts, grads))
    moved = [send(parts[k], k, 0) for k in range(1, rep)]
    own_rows = [parts[0]] + moved
    other_rows = [send(block, 0, 1) for block in moved]
    group_grads = [grads] + [send(grads, k, 0) for k in range(1, rep)]
    operands = own_rows + other_rows + group_grads
    grad_gate, grad_up, grad_down = call(
        functools.partial(weight_kernel, rep, units),
        [shape((width, units))] * 3,
        operands,
        scratch=buffers(operands),
        flops=2 * 2 * rep * rows * width * 3 * units,
    )
    grad_tokens, grad_weight = call(
        functools.partial(token_kernel, rep, flight),
        [shape((tok_count, model_dim)), shape(expert_ids.shape[::-1], F32)],
        [placed, expert_ids.T] + backs,
        inside=(0, 1),
        scratch=[pltpu.VMEM((rep, tok_count, width), BF16)] + buffers(backs),
        flops=2 * tok_count * CHIPS * SLOT * model_dim,
    )
    return grad_tokens, grad_weight.T, grad_gate, grad_up, grad_down


def solution(mesh):
    return jax.shard_map(
        local,
        mesh=mesh,
        in_specs=(
            P(("rep", "ep"), None),
            P(("rep", "ep"), None),
            P(("rep", "ep"), None),
            P(("rep", "ep"), None),
            P(),
            P(),
            P("rep", "ep"),
            P("rep", "ep"),
            P("rep", "ep"),
        ),
        out_specs=(
            P(("rep", "ep"), None),
            P(("rep", "ep"), None),
            P("rep", "ep"),
            P("rep", "ep"),
            P("rep", "ep"),
        ),
        check_vma=False,
    )
```

time: 85.4 us -> 86.5 us (1.013)
  waiting for transfers between devices: 27.5 us -> 34.8 us
  starting transfers between devices: 34.5 us -> 27.8 us
  Pallas kernels: 12.4 us -> 17.4 us
  local copies, waits for them, and re-layouts: 9.71 us -> 5.46 us
    ppermute x26, waiting for transfers between devices: 12.2 us -> 34.8 us  [send(): return lax.ppermute(array, ('rep', 'ep'), pairs)]
    ppermute x6 -> x0, starting transfers between devices: 15.9 us -> none  [send_ring(): return lax.ppermute(array, 'ep', pairs)]
    ppermute x6 -> x0, waiting for transfers between devices: 15.2 us -> none  [send_ring(): return lax.ppermute(array, 'ep', pairs)]
    ppermute x26, starting transfers between devices: 18.6 us -> 27.8 us  [send(): return lax.ppermute(array, ('rep', 'ep'), pairs)]
    pallas_call x5 -> x7, Pallas kernels: 12.4 us -> 17.4 us  [call(): pl.pallas_call(kernel, out_shape=tuple(outs), in_specs=[VMEM if n in insi...]
    slice x2 -> x0, local copies, waits for them, and re-layouts: 2.13 us -> none  [local(): w[h * half:(h + 1) * half]]
    unnamed x40 -> x25, local copies, waits for them, and re-layouts: 7.56 us -> 5.46 us
  transfers between devices with their start and end apart: 32 -> 26, of which waited for: 14 -> 10; matrix products, arithmetic and copies ran while one was open for 0% -> 0% of each run, Pallas kernels for 11% -> 10%
where the time goes in v4:
time: 86.5 us; the launch traced here: 86.2 us
  waiting for transfers between devices  34.8 us (40%)
  starting transfers between devices  27.8 us (32%)
  Pallas kernels  17.4 us (20%)
  local copies, waits for them, and re-layouts  5.46 us (6%)
    ppermute x26, waiting for transfers between devices, send(): return lax.ppermute(array, ('rep', 'ep'), pairs)  34.8 us
    ppermute x26, starting transfers between devices, send(): return lax.ppermute(array, ('rep', 'ep'), pairs)  27.8 us
    pallas_call x7, Pallas kernels, call(): pl.pallas_call(kernel, out_shape=tuple(outs), in_specs=[VMEM if n in insi...  17.4 us
    unnamed x25, local copies, waits for them, and re-layouts  5.46 us
  transfers between devices with their start and end apart: 26, of which 10 were waited for; matrix products, arithmetic and copies ran while one was open for 0% of the time, Pallas kernels for 10%

profile of v4, /device:TPU:0, one launch (start us, length us, event | category | flops | bytes accessed | tf_op | source)
XLA Modules:
  0.0 86.2 jit_solution(15233510444460865716)
XLA Ops:
  1.3 1.2 %copy-done = bf16[128,3584]{1,0:T(8,128)(2,1)S(1)} copy-done((bf16[128,3584]{1,0:T(8,128)(2,1)S(1)}, bf16[128,3584]{1,0:T(8,128)(2,1)}, u32[]{:S(2)}) %copy-start) | copy-done | bytes 917528
  2.5 1.2 %copy-done.1 = bf16[128,3584]{1,0:T(8,128)(2,1)S(1)} copy-done((bf16[128,3584]{1,0:T(8,128)(2,1)S(1)}, bf16[128,3584]{1,0:T(8,128)(2,1)}, u32[]{:S(2)}) %copy-start.1) | copy-done | bytes 917528
  4.4 3.2 %shard_map.128 = (bf16[2,16,3712]{2,1,0:T(8,128)(2,1)S(1)}, bf16[1,64,128]{2,1,0:T(8,128)(2,1)S(1)}) custom-call(s32[4]{0:T(128)S(1)} %copy-done.10, bf16[128,3584]{1,0:T(8,128)(2,1)S(1)} %copy-done, bf16[128,3584]{1,0:T(8,128)(2,1)S(1)} %copy-done.1, s32[8,128]{1,0:T(8,128)S(1)} %bitcast.3, bf16[8,128]{1,0:T(8,128)(2,1)S(1)} %bitcast.5), custom_call_target="tpu_custom_call" | custom-call | bytes 2095120 | tf_op jit(solution)/shard_map/pallas_call | solution.py:32
  7.5 3.1 %collective-permute-start = (bf16[2,16,3712]{2,1,0:T(8,128)(2,1)S(1)}, bf16[2,16,3712]{2,1,0:T(8,128)(2,1)S(1)}, u32[]{:S(2)}, u32[]{:S(2)}) collective-permute-start(bf16[2,16,3712]{2,1,0:T(8,128)(2,1)S(1)} %get-tuple-element.34.refs_0_), channel_id=1, source_target_pairs={{0,2},{1,3},{2,0},{3,1},{4,6},{5,7},{6,4},{7,5},{8,10},{9,11},{10,... | collective-permute-start | bytes 712712 | tf_op jit(solution)/shard_map/ppermute | solution.py:311
  10.6 2.6 %collective-permute-start.1 = (bf16[2,16,3712]{2,1,0:T(8,128)(2,1)S(1)}, bf16[2,16,3712]{2,1,0:T(8,128)(2,1)S(1)}, u32[]{:S(2)}, u32[]{:S(2)}) collective-permute-start(bf16[2,16,3712]{2,1,0:T(8,128)(2,1)S(1)} %get-tuple-element.34.refs_0_), channel_id=1, source_target_pairs={{0,4},{1,5},{2,6},{3,7},{4,0},{5,1},{6,2},{7,3},{8,12},{9,13},{10,... | collective-permute-start | bytes 712712 | tf_op jit(solution)/shard_map/ppermute | solution.py:311
  13.4 1.8 %collective-permute-start.9 = (bf16[448,384]{1,0:T(8,128)(2,1)S(1)}, bf16[448,384]{1,0:T(8,128)(2,1)S(1)}, u32[]{:S(2)}, u32[]{:S(2)}) collective-permute-start(bf16[448,384]{1,0:T(8,128)(2,1)S(1)} %get-tuple-element.35.refs_8_.refs_0_), channel_id=1, source_target_pairs={{0,16},{1,17},{2,18},{3,19},{4,20},{5,21},{6,22},{7,23},{8,24},{9,... | collective-permute-start | bytes 1032200 | tf_op jit(solution)/shard_map/ppermute | solution.py:311
  15.2 1.5 %collective-permute-start.8 = (bf16[448,384]{1,0:T(8,128)(2,1)S(1)}, bf16[448,384]{1,0:T(8,128)(2,1)S(1)}, u32[]{:S(2)}, u32[]{:S(2)}) collective-permute-start(bf16[448,384]{1,0:T(8,128)(2,1)S(1)} %get-tuple-element.36.refs_9_.refs_1_), channel_id=1, source_target_pairs={{0,8},{1,9},{2,10},{3,11},{4,12},{5,13},{6,14},{7,15},{8,0},{9,1},... | collective-permute-start | bytes 1032200 | tf_op jit(solution)/shard_map/ppermute | solution.py:311
  16.7 4.0 %collective-permute-done.refs_1_ = bf16[2,16,3712]{2,1,0:T(8,128)(2,1)S(1)} collective-permute-done((bf16[2,16,3712]{2,1,0:T(8,128)(2,1)S(1)}, bf16[2,16,3712]{2,1,0:T(8,128)(2,1)S(1)}, u32[]{:S(2)}, u32[]{:S(2)}) %collective-permute-start) | collective-permute-done | bytes 237600 | tf_op jit(solution)/shard_map/ppermute | solution.py:311
  20.7 1.7 %collective-permute-start.10 = (bf16[448,384]{1,0:T(8,128)(2,1)S(1)}, bf16[448,384]{1,0:T(8,128)(2,1)S(1)}, u32[]{:S(2)}, u32[]{:S(2)}) collective-permute-start(bf16[448,384]{1,0:T(8,128)(2,1)S(1)} %get-tuple-element.36.refs_9_.refs_1_), channel_id=1, source_target_pairs={{0,16},{1,17},{2,18},{3,19},{4,20},{5,21},{6,22},{7,23},{8,24},{9,... | collective-permute-start | bytes 1032200 | tf_op jit(solution)/shard_map/ppermute | solution.py:311
  22.4 8.0 %collective-permute-done.1.refs_2_ = bf16[2,16,3712]{2,1,0:T(8,128)(2,1)S(1)} collective-permute-done((bf16[2,16,3712]{2,1,0:T(8,128)(2,1)S(1)}, bf16[2,16,3712]{2,1,0:T(8,128)(2,1)S(1)}, u32[]{:S(2)}, u32[]{:S(2)}) %collective-permute-start.1) | collective-permute-done | bytes 237600 | tf_op jit(solution)/shard_map/ppermute | solution.py:311
  30.4 1.5 %collective-permute-start.7 = (bf16[448,384]{1,0:T(8,128)(2,1)S(1)}, bf16[448,384]{1,0:T(8,128)(2,1)S(1)}, u32[]{:S(2)}, u32[]{:S(2)}) collective-permute-start(bf16[448,384]{1,0:T(8,128)(2,1)S(1)} %get-tuple-element.35.refs_8_.refs_0_), channel_id=1, source_target_pairs={{0,8},{1,9},{2,10},{3,11},{4,12},{5,13},{6,14},{7,15},{8,0},{9,1},... | collective-permute-start | bytes 1032200 | tf_op jit(solution)/shard_map/ppermute | solution.py:311
  32.5 1.5 %collective-permute-start.12 = (bf16[448,384]{1,0:T(8,128)(2,1)S(1)}, bf16[448,384]{1,0:T(8,128)(2,1)S(1)}, u32[]{:S(2)}, u32[]{:S(2)}) collective-permute-start(bf16[448,384]{1,0:T(8,128)(2,1)S(1)} %collective-permute-done.8.refs_11_.refs_3_), channel_id=1, source_target_pairs={{0,16},{1,17},{2,18},{3,19},{4,20},{5,21},{6,22},{7,23},{8,24},{9,... | collective-permute-start | bytes 1032200 | tf_op jit(solution)/shard_map/ppermute | solution.py:311
  34.1 0.7 copy-done.2
  35.3 5.0 %collective-permute-done.7.refs_10_.refs_2_ = bf16[448,384]{1,0:T(8,128)(2,1)S(1)} collective-permute-done((bf16[448,384]{1,0:T(8,128)(2,1)S(1)}, bf16[448,384]{1,0:T(8,128)(2,1)S(1)}, u32[]{:S(2)}, u32[]{:S(2)}) %collective-permute-start.7) | collective-permute-done | bytes 344096 | tf_op jit(solution)/shard_map/ppermute | solution.py:311
  40.4 1.7 %collective-permute-done.6.refs_7_ = bf16[2,16,3712]{2,1,0:T(8,128)(2,1)} collective-permute-done((bf16[2,16,3712]{2,1,0:T(8,128)(2,1)}, bf16[2,16,3712]{2,1,0:T(8,128)(2,1)}, u32[]{:S(2)}, u32[]{:S(2)}) %collective-permute-start.6) | collective-permute-done | bytes 237600 | tf_op jit(solution)/shard_map/ppermute | solution.py:311
  42.2 0.9 %copy-done.3 = bf16[2,16,3712]{2,1,0:T(8,128)(2,1)S(1)} copy-done((bf16[2,16,3712]{2,1,0:T(8,128)(2,1)S(1)}, bf16[2,16,3712]{2,1,0:T(8,128)(2,1)}, u32[]{:S(2)}) %copy-start.3) | copy-done | bytes 237592
  43.1 4.1 %shard_map.130 = (f32[128,384]{1,0:T(8,128)S(1)}, bf16[8,16,128]{2,1,0:T(8,128)(2,1)S(1)}, bf16[2,128,896]{2,1,0:T(8,128)(2,1)S(1)}, bf16[2,128,896]{2,1,0:T(8,1...) custom-call(bf16[2,16,3712]{2,1,0:T(8,128)(2,1)S(1)} %get-tuple-elem, ...), custom_call_target="tpu_custom_call" | custom-call | flops 352321536 | bytes 5799936 | tf_op jit(solution)/shard_map/pallas_call | solution.py:32
  47.3 3.5 %shard_map.131 = (bf16[64,3712]{1,0:T(8,128)(2,1)S(1)}, bf16[64,3712]{1,0:T(8,128)(2,1)S(1)}, bf16[128,384]{1,0:T(8,128)(2,1)S(1)}) custom-call(s32[4,1]{1,0:T(4,128)S(1)} %copy.14.cap_ref, bf16[8,16,128]{2,1,0:T(8,128)(2,1)S(1)} %get-tuple-element.37.rates_ref, f32[128,384]{1,0:T(8,128)S(1)} %get-tuple-element.38.pre_ref, ...), custom_call_target="tpu_custom_call" | custom-call | flops 234881024 | bytes 4489232 | tf_op jit(solution)/shard_map/pallas_call | solution.py:32
  51.0 2.5 %collective-permute-start.17 = (bf16[2,64,896]{2,1,0:T(8,128)(2,1)S(1)}, bf16[2,64,896]{2,1,0:T(8,128)(2,1)S(1)}, u32[]{:S(2)}, u32[]{:S(2)}) collective-permute-start(bf16[2,64,896]{2,1,0:T(8,128)(2,1)S(1)} %get-tuple-element.54), channel_id=1, source_target_pairs={{0,8},{1,9},{2,10},{3,11},{4,12},{5,13},{6,14},{7,15},{8,0},{9,1},... | collective-permute-start | bytes 688136 | tf_op jit(solution)/shard_map/ppermute | solution.py:311
  53.5 1.5 %collective-permute-start.18 = (bf16[2,64,896]{2,1,0:T(8,128)(2,1)S(1)}, bf16[2,64,896]{2,1,0:T(8,128)(2,1)S(1)}, u32[]{:S(2)}, u32[]{:S(2)}) collective-permute-start(bf16[2,64,896]{2,1,0:T(8,128)(2,1)S(1)} %get-tuple-element.55), channel_id=1, source_target_pairs={{0,16},{1,17},{2,18},{3,19},{4,20},{5,21},{6,22},{7,23},{8,24},{9,... | collective-permute-start | bytes 688136 | tf_op jit(solution)/shard_map/ppermute | solution.py:311
  55.0 4.9 %collective-permute-done.17.refs_1_ = bf16[2,64,896]{2,1,0:T(8,128)(2,1)S(1)} collective-permute-done((bf16[2,64,896]{2,1,0:T(8,128)(2,1)S(1)}, bf16[2,64,896]{2,1,0:T(8,128)(2,1)S(1)}, u32[]{:S(2)}, u32[]{:S(2)}) %collective-permute-start.17) | collective-permute-done | bytes 229408 | tf_op jit(solution)/shard_map/ppermute | solution.py:311
  59.9 2.0 %collective-permute-start.23 = (bf16[128,384]{1,0:T(8,128)(2,1)S(1)}, bf16[128,384]{1,0:T(8,128)(2,1)S(1)}, u32[]{:S(2)}, u32[]{:S(2)}) collective-permute-start(bf16[128,384]{1,0:T(8,128)(2,1)S(1)} %get-tuple-element.57.refs_7_), channel_id=1, source_target_pairs={{0,8},{1,9},{2,10},{3,11},{4,12},{5,13},{6,14},{7,15},{8,0},{9,1},... | collective-permute-start | bytes 294920 | tf_op jit(solution)/shard_map/ppermute | solution.py:311
  61.9 4.1 %collective-permute-done.18.refs_2_ = bf16[2,64,896]{2,1,0:T(8,128)(2,1)S(1)} collective-permute-done((bf16[2,64,896]{2,1,0:T(8,128)(2,1)S(1)}, bf16[2,64,896]{2,1,0:T(8,128)(2,1)S(1)}, u32[]{:S(2)}, u32[]{:S(2)}) %collective-permute-start.18) | collective-permute-done | bytes 229408 | tf_op jit(solution)/shard_map/ppermute | solution.py:311
  66.7 1.5 %collective-permute-start.24 = (bf16[128,384]{1,0:T(8,128)(2,1)S(1)}, bf16[128,384]{1,0:T(8,128)(2,1)S(1)}, u32[]{:S(2)}, u32[]{:S(2)}) collective-permute-start(bf16[128,384]{1,0:T(8,128)(2,1)S(1)} %get-tuple-element.57.refs_7_), channel_id=1, source_target_pairs={{0,16},{1,17},{2,18},{3,19},{4,20},{5,21},{6,22},{7,23},{8,24},{9,... | collective-permute-start | bytes 294920 | tf_op jit(solution)/shard_map/ppermute | solution.py:311
  68.2 1.6 %collective-permute-start.25 = (bf16[128,384]{1,0:T(8,128)(2,1)S(1)}, bf16[128,384]{1,0:T(8,128)(2,1)S(1)}, u32[]{:S(2)}, u32[]{:S(2)}) collective-permute-start(bf16[128,384]{1,0:T(8,128)(2,1)S(1)} %get-tuple-element.57.refs_7_), channel_id=1, source_target_pairs={{0,24},{1,25},{2,26},{3,27},{4,28},{5,29},{6,30},{7,31},{8,16},{9,... | collective-permute-start | bytes 294920 | tf_op jit(solution)/shard_map/ppermute | solution.py:311
  70.0 2.5 %collective-permute-done.24.refs_9_ = bf16[128,384]{1,0:T(8,128)(2,1)S(1)} collective-permute-done((bf16[128,384]{1,0:T(8,128)(2,1)S(1)}, bf16[128,384]{1,0:T(8,128)(2,1)S(1)}, u32[]{:S(2)}, u32[]{:S(2)}) %collective-permute-start.24) | collective-permute-done | bytes 98336 | tf_op jit(solution)/shard_map/ppermute | solution.py:311
  72.4 1.3 %collective-permute-done.25.refs_10_ = bf16[128,384]{1,0:T(8,128)(2,1)S(1)} collective-permute-done((bf16[128,384]{1,0:T(8,128)(2,1)S(1)}, bf16[128,384]{1,0:T(8,128)(2,1)S(1)}, u32[]{:S(2)}, u32[]{:S(2)}) %collective-permute-start.25) | collective-permute-done | bytes 98336 | tf_op jit(solution)/shard_map/ppermute | solution.py:311
  73.7 1.8 %collective-permute-start.15 = (bf16[16,3712]{1,0:T(8,128)(2,1)S(1)}, bf16[16,3712]{1,0:T(8,128)(2,1)S(1)}, u32[]{:S(2)}, u32[]{:S(2)}) collective-permute-start(bf16[16,3712]{1,0:T(8,128)(2,1)S(1)} %get-tuple-element.44), channel_id=1, source_target_pairs={{0,4},{1,5},{2,6},{3,7},{4,0},{5,1},{6,2},{7,3},{8,12},{9,13},{10,... | collective-permute-start | bytes 356360 | tf_op jit(solution)/shard_map/ppermute | solution.py:311
  75.5 1.4 %collective-permute-start.16 = (bf16[16,3712]{1,0:T(8,128)(2,1)S(1)}, bf16[16,3712]{1,0:T(8,128)(2,1)S(1)}, u32[]{:S(2)}, u32[]{:S(2)}) collective-permute-start(bf16[16,3712]{1,0:T(8,128)(2,1)S(1)} %get-tuple-element.45), channel_id=1, source_target_pairs={{0,6},{1,7},{2,4},{3,5},{4,2},{5,3},{6,0},{7,1},{8,14},{9,15},{10,... | collective-permute-start | bytes 356360 | tf_op jit(solution)/shard_map/ppermute | solution.py:311
  76.8 4.2 %shard_map.134 = (bf16[896,128]{1,0:T(8,128)(2,1)}, bf16[896,128]{1,0:T(8,128)(2,1)}, bf16[896,128]{1,0:T(8,128)(2,1)}) custom-call(bf16[2,128,896]{2,1,0:T(8,128)(2,1)S(1)} %get-tuple-element.53.refs_0_, bf16[2,64,896]{2,1,0:T(8,128)(2,1)S(1)} %collective-permute-done.17.refs_1_, bf16[2,64,896]{2,1,0:T(8,128)(2,1)S(1)} %collective-permute-done.18.refs_2_, ...), custom_call_target="tpu_custom_call" | custom-call | flops 352321536 | bytes 2916352 | tf_op jit(solution)/shard_map/pallas_call | solution.py:32
  81.0 3.1 %collective-permute-done.15.refs_2_ = bf16[16,3712]{1,0:T(8,128)(2,1)S(1)} collective-permute-done((bf16[16,3712]{1,0:T(8,128)(2,1)S(1)}, bf16[16,3712]{1,0:T(8,128)(2,1)S(1)}, u32[]{:S(2)}, u32[]{:S(2)}) %collective-permute-start.15) | collective-permute-done | bytes 118816 | tf_op jit(solution)/shard_map/ppermute | solution.py:311
  84.1 2.1 %shard_map.133 = (bf16[128,3584]{1,0:T(8,128)(2,1)}, f32[8,128]{1,0:T(8,128)}) custom-call(bf16[1,64,128]{2,1,0:T(8,128)(2,1)S(1)} %get-tuple-element.33.placed_ref, s32[8,128]{1,0:T(8,128)S(1)} %bitcast.4, bf16[16,3712]{1,0:T(8,128)(2,1)S(1)} %get-tuple-element.42.refs_0_, bf16[16,3712]{1,0:T(8,128)(2,1)S(1)} %collective-permute-done.14.refs_1_, ...), custom_call_target="tpu_custom_call" | custom-call | flops 58720256 | bytes 1417216 | tf_op jit(solution)/shard_map/pallas_call | solution.py:32
  (52 shorter events, 3.8 us)
Async XLA Ops:
  1.3 1.2 %copy-start = (bf16[128,3584]{1,0:T(8,128)(2,1)S(1)}, bf16[128,3584]{1,0:T(8,128)(2,1)}, u32[]{:S(2)}) copy-start(bf16[128,3584]{1,0:T(8,128)(2,1)} %tok_ref.1) | copy-start | bytes 2752516
  4.4 8.9 %copy-start.4 = (bf16[896,128]{1,0:T(8,128)(2,1)S(1)}, bf16[896,128]{1,0:T(8,128)(2,1)}, u32[]{:S(2)}) copy-start(bf16[896,128]{1,0:T(8,128)(2,1)} %gate_ref.1) | copy-start | bytes 688132
  4.4 8.9 %copy-start.5 = (bf16[896,128]{1,0:T(8,128)(2,1)S(1)}, bf16[896,128]{1,0:T(8,128)(2,1)}, u32[]{:S(2)}) copy-start(bf16[896,128]{1,0:T(8,128)(2,1)} %up_ref.1) | copy-start | bytes 688132
  4.4 8.9 %copy-start.6 = (bf16[896,128]{1,0:T(8,128)(2,1)S(1)}, bf16[896,128]{1,0:T(8,128)(2,1)}, u32[]{:S(2)}) copy-start(bf16[896,128]{1,0:T(8,128)(2,1)} %down_ref.1) | copy-start | bytes 688132
  7.5 13.2 %collective-permute-start = (bf16[2,16,3712]{2,1,0:T(8,128)(2,1)S(1)}, bf16[2,16,3712]{2,1,0:T(8,128)(2,1)S(1)}, u32[]{:S(2)}, u32[]{:S(2)}) collective-permute-start(bf16[2,16,3712]{2,1,0:T(8,128)(2,1)S(1)} %get-tuple-element.34.refs_0_), channel_id=1, source_target_pairs={{0,2},{1,3},{2,0},{3,1},{4,6},{5,7},{6,4},{7,5},{8,10},{9,11},{10,... | collective-permute-start | bytes 712712 | tf_op jit(solution)/shard_map/ppermute | solution.py:311
  10.6 19.8 %collective-permute-start.1 = (bf16[2,16,3712]{2,1,0:T(8,128)(2,1)S(1)}, bf16[2,16,3712]{2,1,0:T(8,128)(2,1)S(1)}, u32[]{:S(2)}, u32[]{:S(2)}) collective-permute-start(bf16[2,16,3712]{2,1,0:T(8,128)(2,1)S(1)} %get-tuple-element.34.refs_0_), channel_id=1, source_target_pairs={{0,4},{1,5},{2,6},{3,7},{4,0},{5,1},{6,2},{7,3},{8,12},{9,13},{10,... | collective-permute-start | bytes 712712 | tf_op jit(solution)/shard_map/ppermute | solution.py:311
  13.2 18.7 %collective-permute-start.2 = (bf16[2,16,3712]{2,1,0:T(8,128)(2,1)S(1)}, bf16[2,16,3712]{2,1,0:T(8,128)(2,1)}, u32[]{:S(2)}, u32[]{:S(2)}) collective-permute-start(bf16[2,16,3712]{2,1,0:T(8,128)(2,1)S(1)} %get-tuple-element.34.refs_0_), channel_id=1, source_target_pairs={{0,6},{1,7},{2,4},{3,5},{4,2},{5,3},{6,0},{7,1},{8,14},{9,15},{10,... | collective-permute-start | bytes 712712 | tf_op jit(solution)/shard_map/ppermute | solution.py:311
  13.4 26.9 %copy-start.11 = (s32[4,1]{0,1:T(1,128)S(1)}, s32[4,1]{0,1:T(1,128)}, u32[]{:S(2)}) copy-start(s32[4,1]{0,1:T(1,128)} %param.14) | copy-start | bytes 52
  13.4 18.5 %collective-permute-start.9 = (bf16[448,384]{1,0:T(8,128)(2,1)S(1)}, bf16[448,384]{1,0:T(8,128)(2,1)S(1)}, u32[]{:S(2)}, u32[]{:S(2)}) collective-permute-start(bf16[448,384]{1,0:T(8,128)(2,1)S(1)} %get-tuple-element.35.refs_8_.refs_0_), channel_id=1, source_target_pairs={{0,16},{1,17},{2,18},{3,19},{4,20},{5,21},{6,22},{7,23},{8,24},{9,... | collective-permute-start | bytes 1032200 | tf_op jit(solution)/shard_map/ppermute | solution.py:311
  15.2 17.3 %collective-permute-start.8 = (bf16[448,384]{1,0:T(8,128)(2,1)S(1)}, bf16[448,384]{1,0:T(8,128)(2,1)S(1)}, u32[]{:S(2)}, u32[]{:S(2)}) collective-permute-start(bf16[448,384]{1,0:T(8,128)(2,1)S(1)} %get-tuple-element.36.refs_9_.refs_1_), channel_id=1, source_target_pairs={{0,8},{1,9},{2,10},{3,11},{4,12},{5,13},{6,14},{7,15},{8,0},{9,1},... | collective-permute-start | bytes 1032200 | tf_op jit(solution)/shard_map/ppermute | solution.py:311
  20.7 14.0 %collective-permute-start.10 = (bf16[448,384]{1,0:T(8,128)(2,1)S(1)}, bf16[448,384]{1,0:T(8,128)(2,1)S(1)}, u32[]{:S(2)}, u32[]{:S(2)}) collective-permute-start(bf16[448,384]{1,0:T(8,128)(2,1)S(1)} %get-tuple-element.36.refs_9_.refs_1_), channel_id=1, source_target_pairs={{0,16},{1,17},{2,18},{3,19},{4,20},{5,21},{6,22},{7,23},{8,24},{9,... | collective-permute-start | bytes 1032200 | tf_op jit(solution)/shard_map/ppermute | solution.py:311
  30.4 9.9 %collective-permute-start.7 = (bf16[448,384]{1,0:T(8,128)(2,1)S(1)}, bf16[448,384]{1,0:T(8,128)(2,1)S(1)}, u32[]{:S(2)}, u32[]{:S(2)}) collective-permute-start(bf16[448,384]{1,0:T(8,128)(2,1)S(1)} %get-tuple-element.35.refs_8_.refs_0_), channel_id=1, source_target_pairs={{0,8},{1,9},{2,10},{3,11},{4,12},{5,13},{6,14},{7,15},{8,0},{9,1},... | collective-permute-start | bytes 1032200 | tf_op jit(solution)/shard_map/ppermute | solution.py:311
  31.9 2.1 %collective-permute-start.3 = (bf16[2,16,3712]{2,1,0:T(8,128)(2,1)S(1)}, bf16[2,16,3712]{2,1,0:T(8,128)(2,1)S(1)}, u32[]{:S(2)}, u32[]{:S(2)}) collective-permute-start(bf16[2,16,3712]{2,1,0:T(8,128)(2,1)S(1)} %get-tuple-element.34.refs_0_), channel_id=1, source_target_pairs={{0,1},{1,0},{2,3},{3,2},{4,5},{5,4},{6,7},{7,6},{8,9},{9,8},{10,11... | collective-permute-start | bytes 712712 | tf_op jit(solution)/shard_map/ppermute | solution.py:311
  31.9 15.3 %collective-permute-start.11 = (bf16[448,384]{1,0:T(8,128)(2,1)S(1)}, bf16[448,384]{1,0:T(8,128)(2,1)S(1)}, u32[]{:S(2)}, u32[]{:S(2)}) collective-permute-start(bf16[448,384]{1,0:T(8,128)(2,1)S(1)} %collective-permute-done.9.refs_12_.refs_4_), channel_id=1, source_target_pairs={{0,8},{1,9},{2,10},{3,11},{4,12},{5,13},{6,14},{7,15},{8,0},{9,1},... | collective-permute-start | bytes 1032200 | tf_op jit(solution)/shard_map/ppermute | solution.py:311
  32.5 14.7 %collective-permute-start.12 = (bf16[448,384]{1,0:T(8,128)(2,1)S(1)}, bf16[448,384]{1,0:T(8,128)(2,1)S(1)}, u32[]{:S(2)}, u32[]{:S(2)}) collective-permute-start(bf16[448,384]{1,0:T(8,128)(2,1)S(1)} %collective-permute-done.8.refs_11_.refs_3_), channel_id=1, source_target_pairs={{0,16},{1,17},{2,18},{3,19},{4,20},{5,21},{6,22},{7,23},{8,24},{9,... | collective-permute-start | bytes 1032200 | tf_op jit(solution)/shard_map/ppermute | solution.py:311
  34.7 5.7 %collective-permute-start.4 = (bf16[2,16,3712]{2,1,0:T(8,128)(2,1)S(1)}, bf16[2,16,3712]{2,1,0:T(8,128)(2,1)}, u32[]{:S(2)}, u32[]{:S(2)}) collective-permute-start(bf16[2,16,3712]{2,1,0:T(8,128)(2,1)S(1)} %collective-permute-done.refs_1_), channel_id=1, source_target_pairs={{0,1},{1,0},{2,3},{3,2},{4,5},{5,4},{6,7},{7,6},{8,9},{9,8},{10,11... | collective-permute-start | bytes 712712 | tf_op jit(solution)/shard_map/ppermute | solution.py:311
  34.8 5.7 %collective-permute-start.5 = (bf16[2,16,3712]{2,1,0:T(8,128)(2,1)S(1)}, bf16[2,16,3712]{2,1,0:T(8,128)(2,1)}, u32[]{:S(2)}, u32[]{:S(2)}) collective-permute-start(bf16[2,16,3712]{2,1,0:T(8,128)(2,1)S(1)} %collective-permute-done.1.refs_2_), channel_id=1, source_target_pairs={{0,1},{1,0},{2,3},{3,2},{4,5},{5,4},{6,7},{7,6},{8,9},{9,8},{10,11... | collective-permute-start | bytes 712712 | tf_op jit(solution)/shard_map/ppermute | solution.py:311
  40.3 1.8 %collective-permute-start.6 = (bf16[2,16,3712]{2,1,0:T(8,128)(2,1)}, bf16[2,16,3712]{2,1,0:T(8,128)(2,1)}, u32[]{:S(2)}, u32[]{:S(2)}) collective-permute-start(bf16[2,16,3712]{2,1,0:T(8,128)(2,1)} %collective-permute-done.2.refs_3_), channel_id=1, source_target_pairs={{0,1},{1,0},{2,3},{3,2},{4,5},{5,4},{6,7},{7,6},{8,9},{9,8},{10,11... | collective-permute-start | bytes 712712 | tf_op jit(solution)/shard_map/ppermute | solution.py:311
  50.8 17.4 %collective-permute-start.13 = (bf16[64,3712]{1,0:T(8,128)(2,1)S(1)}, bf16[64,3712]{1,0:T(8,128)(2,1)S(1)}, u32[]{:S(2)}, u32[]{:S(2)}) collective-permute-start(bf16[64,3712]{1,0:T(8,128)(2,1)S(1)} %get-tuple-element.41), channel_id=1, source_target_pairs={{0,1},{1,0},{2,3},{3,2},{4,5},{5,4},{6,7},{7,6},{8,9},{9,8},{10,11... | collective-permute-start | bytes 1425416 | tf_op jit(solution)/shard_map/ppermute | solution.py:311
  51.0 8.9 %collective-permute-start.17 = (bf16[2,64,896]{2,1,0:T(8,128)(2,1)S(1)}, bf16[2,64,896]{2,1,0:T(8,128)(2,1)S(1)}, u32[]{:S(2)}, u32[]{:S(2)}) collective-permute-start(bf16[2,64,896]{2,1,0:T(8,128)(2,1)S(1)} %get-tuple-element.54), channel_id=1, source_target_pairs={{0,8},{1,9},{2,10},{3,11},{4,12},{5,13},{6,14},{7,15},{8,0},{9,1},... | collective-permute-start | bytes 688136 | tf_op jit(solution)/shard_map/ppermute | solution.py:311
  53.5 12.5 %collective-permute-start.18 = (bf16[2,64,896]{2,1,0:T(8,128)(2,1)S(1)}, bf16[2,64,896]{2,1,0:T(8,128)(2,1)S(1)}, u32[]{:S(2)}, u32[]{:S(2)}) collective-permute-start(bf16[2,64,896]{2,1,0:T(8,128)(2,1)S(1)} %get-tuple-element.55), channel_id=1, source_target_pairs={{0,16},{1,17},{2,18},{3,19},{4,20},{5,21},{6,22},{7,23},{8,24},{9,... | collective-permute-start | bytes 688136 | tf_op jit(solution)/shard_map/ppermute | solution.py:311
  55.0 11.0 %collective-permute-start.19 = (bf16[2,64,896]{2,1,0:T(8,128)(2,1)S(1)}, bf16[2,64,896]{2,1,0:T(8,128)(2,1)S(1)}, u32[]{:S(2)}, u32[]{:S(2)}) collective-permute-start(bf16[2,64,896]{2,1,0:T(8,128)(2,1)S(1)} %get-tuple-element.56), channel_id=1, source_target_pairs={{0,24},{1,25},{2,26},{3,27},{4,28},{5,29},{6,30},{7,31},{8,16},{9,... | collective-permute-start | bytes 688136 | tf_op jit(solution)/shard_map/ppermute | solution.py:311
  59.9 15.6 %collective-permute-start.20 = (bf16[2,64,896]{2,1,0:T(8,128)(2,1)S(1)}, bf16[2,64,896]{2,1,0:T(8,128)(2,1)S(1)}, u32[]{:S(2)}, u32[]{:S(2)}) collective-permute-start(bf16[2,64,896]{2,1,0:T(8,128)(2,1)S(1)} %collective-permute-done.17.refs_1_), channel_id=1, source_target_pairs={{0,1},{1,0},{2,3},{3,2},{4,5},{5,4},{6,7},{7,6},{8,9},{9,8},{10,11... | collective-permute-start | bytes 688136 | tf_op jit(solution)/shard_map/ppermute | solution.py:311
  59.9 6.7 %collective-permute-start.23 = (bf16[128,384]{1,0:T(8,128)(2,1)S(1)}, bf16[128,384]{1,0:T(8,128)(2,1)S(1)}, u32[]{:S(2)}, u32[]{:S(2)}) collective-permute-start(bf16[128,384]{1,0:T(8,128)(2,1)S(1)} %get-tuple-element.57.refs_7_), channel_id=1, source_target_pairs={{0,8},{1,9},{2,10},{3,11},{4,12},{5,13},{6,14},{7,15},{8,0},{9,1},... | collective-permute-start | bytes 294920 | tf_op jit(solution)/shard_map/ppermute | solution.py:311
  66.0 10.9 %collective-permute-start.21 = (bf16[2,64,896]{2,1,0:T(8,128)(2,1)S(1)}, bf16[2,64,896]{2,1,0:T(8,128)(2,1)S(1)}, u32[]{:S(2)}, u32[]{:S(2)}) collective-permute-start(bf16[2,64,896]{2,1,0:T(8,128)(2,1)S(1)} %collective-permute-done.18.refs_2_), channel_id=1, source_target_pairs={{0,1},{1,0},{2,3},{3,2},{4,5},{5,4},{6,7},{7,6},{8,9},{9,8},{10,11... | collective-permute-start | bytes 688136 | tf_op jit(solution)/shard_map/ppermute | solution.py:311
  66.0 10.9 %collective-permute-start.22 = (bf16[2,64,896]{2,1,0:T(8,128)(2,1)S(1)}, bf16[2,64,896]{2,1,0:T(8,128)(2,1)S(1)}, u32[]{:S(2)}, u32[]{:S(2)}) collective-permute-start(bf16[2,64,896]{2,1,0:T(8,128)(2,1)S(1)} %collective-permute-done.19.refs_3_), channel_id=1, source_target_pairs={{0,1},{1,0},{2,3},{3,2},{4,5},{5,4},{6,7},{7,6},{8,9},{9,8},{10,11... | collective-permute-start | bytes 688136 | tf_op jit(solution)/shard_map/ppermute | solution.py:311
  66.7 5.8 %collective-permute-start.24 = (bf16[128,384]{1,0:T(8,128)(2,1)S(1)}, bf16[128,384]{1,0:T(8,128)(2,1)S(1)}, u32[]{:S(2)}, u32[]{:S(2)}) collective-permute-start(bf16[128,384]{1,0:T(8,128)(2,1)S(1)} %get-tuple-element.57.refs_7_), channel_id=1, source_target_pairs={{0,16},{1,17},{2,18},{3,19},{4,20},{5,21},{6,22},{7,23},{8,24},{9,... | collective-permute-start | bytes 294920 | tf_op jit(solution)/shard_map/ppermute | solution.py:311
  68.2 5.5 %collective-permute-start.25 = (bf16[128,384]{1,0:T(8,128)(2,1)S(1)}, bf16[128,384]{1,0:T(8,128)(2,1)S(1)}, u32[]{:S(2)}, u32[]{:S(2)}) collective-permute-start(bf16[128,384]{1,0:T(8,128)(2,1)S(1)} %get-tuple-element.57.refs_7_), channel_id=1, source_target_pairs={{0,24},{1,25},{2,26},{3,27},{4,28},{5,29},{6,30},{7,31},{8,16},{9,... | collective-permute-start | bytes 294920 | tf_op jit(solution)/shard_map/ppermute | solution.py:311
  72.4 8.6 %collective-permute-start.14 = (bf16[16,3712]{1,0:T(8,128)(2,1)S(1)}, bf16[16,3712]{1,0:T(8,128)(2,1)S(1)}, u32[]{:S(2)}, u32[]{:S(2)}) collective-permute-start(bf16[16,3712]{1,0:T(8,128)(2,1)S(1)} %get-tuple-element.43), channel_id=1, source_target_pairs={{0,2},{1,3},{2,0},{3,1},{4,6},{5,7},{6,4},{7,5},{8,10},{9,11},{10,... | collective-permute-start | bytes 356360 | tf_op jit(solution)/shard_map/ppermute | solution.py:311
  73.7 10.4 %collective-permute-start.15 = (bf16[16,3712]{1,0:T(8,128)(2,1)S(1)}, bf16[16,3712]{1,0:T(8,128)(2,1)S(1)}, u32[]{:S(2)}, u32[]{:S(2)}) collective-permute-start(bf16[16,3712]{1,0:T(8,128)(2,1)S(1)} %get-tuple-element.44), channel_id=1, source_target_pairs={{0,4},{1,5},{2,6},{3,7},{4,0},{5,1},{6,2},{7,3},{8,12},{9,13},{10,... | collective-permute-start | bytes 356360 | tf_op jit(solution)/shard_map/ppermute | solution.py:311
  75.5 8.6 %collective-permute-start.16 = (bf16[16,3712]{1,0:T(8,128)(2,1)S(1)}, bf16[16,3712]{1,0:T(8,128)(2,1)S(1)}, u32[]{:S(2)}, u32[]{:S(2)}) collective-permute-start(bf16[16,3712]{1,0:T(8,128)(2,1)S(1)} %get-tuple-element.45), channel_id=1, source_target_pairs={{0,6},{1,7},{2,4},{3,5},{4,2},{5,3},{6,0},{7,1},{8,14},{9,15},{10,... | collective-permute-start | bytes 356360 | tf_op jit(solution)/shard_map/ppermute | solution.py:311
  76.8 7.2 %copy-start.8 = (s32[128,8]{0,1:T(8,128)S(1)}, s32[128,8]{0,1:T(8,128)}, u32[]{:S(2)}) copy-start(s32[128,8]{0,1:T(8,128)} %param.11) | copy-start | bytes 12292
  (6 other events, 4.9 us)

commit v5 on v3

v5 whole, which is shorter than its diff:
```python
import functools

import jax
import jax.numpy as jnp
from jax import lax
from jax.experimental import pallas as pl
from jax.experimental.pallas import tpu as pltpu
from jax.sharding import PartitionSpec as P

EXPERTS = 128
SLOT = 16
BLOCK = 128
SPLIT = 8
CORES = 2
CHIPS = SPLIT // CORES
LANES = 128
F32 = jnp.float32
BF16 = jnp.bfloat16
PARTS = 4
HBM = pl.BlockSpec(memory_space=pltpu.HBM)
VMEM = pl.BlockSpec(memory_space=pltpu.VMEM)


def shape(dims, kind=BF16):
    return jax.ShapeDtypeStruct(dims, kind)


def call(kernel, outs, args, stored=(), scratch=(), flops=0, grant=16):
    size = sum(a.size * a.dtype.itemsize for a in args) + sum(
        o.size * o.dtype.itemsize for o in outs
    )
    return pl.pallas_call(
        kernel,
        out_shape=tuple(outs),
        in_specs=[HBM if n in stored else VMEM for n in range(len(args))],
        out_specs=tuple([VMEM] * len(outs)),
        scratch_shapes=scratch,
        compiler_params=pltpu.CompilerParams(vmem_limit_bytes=grant * 1024 * 1024),
        cost_estimate=pl.CostEstimate(flops=flops, bytes_accessed=size, transcendentals=0),
    )(*args)


def fetch(pairs, sems, first=0):
    copies = [
        pltpu.make_async_copy(source, target, sems.at[first + n])
        for n, (source, target) in enumerate(pairs)
    ]
    for copy in copies:
        copy.start()
    return copies


def dot(a, b, dims=((1,), (0,))):
    return lax.dot_general(a, b, (dims, ((), ())), preferred_element_type=F32)


def iota(dims, axis):
    return lax.broadcasted_iota(jnp.int32, dims, axis)


def join_weights_kernel(gate_ref, up_ref, down_ref, all_ref, pair_ref, sems):
    units = gate_ref.shape[1]
    pairs = []
    for n, ref in enumerate((gate_ref, up_ref, down_ref)):
        pairs.append((ref, all_ref.at[:, pl.ds(n * units, units)]))
        if n < 2:
            pairs.append((ref, pair_ref.at[:, pl.ds(n * units, units)]))
    for copy in fetch(pairs, sems):
        copy.wait()


def pair_kernel(all_ref, pair_ref):
    pair_ref[...] = all_ref[:, : pair_ref.shape[1]]


def pack_kernel(rep, flight, live_ref, tok_ref, grad_ref, ids_ref, rw_ref, *refs):
    far = rep // 2
    pays, header_ref, placed_ref = refs[:far], refs[far], refs[far + 1]
    live, ids_held, rw_held, data, rows, sems = refs[far + 2 :]
    r = lax.axis_index("rep")
    mine = lax.axis_index("ep") // SPLIT
    count, model = tok_ref.shape
    width = model // rep
    spacing = EXPERTS // flight
    small = fetch([(live_ref, live), (ids_ref, ids_held), (rw_ref, rw_held)], sems)
    pairs = []
    for part, ref in enumerate((tok_ref, grad_ref)):
        for p in range(PARTS):
            some = pl.ds(p * (count // PARTS), count // PARTS)
            pairs.append((ref.at[some], data.at[part, some]))
    large = fetch(pairs, sems, len(small))
    for copy in small:
        copy.wait()
    token = iota((1, count), 1)
    upper = (iota((count, count), 0) <= iota((count, count), 1)).astype(BF16)
    slot = iota((SLOT, count), 0).astype(F32)
    lane = iota((SLOT, LANES), 1)
    ids = ids_held[...]
    weights = rw_held[...].astype(F32)
    firsts = []
    for w in range(flight):
        expert = jnp.bitwise_xor(mine, w)
        match = ids == expert * spacing
        routed = jnp.any(match, axis=0, keepdims=True) & (token < live[r])
        weight = jnp.sum(jnp.where(match, weights, 0.0), axis=0, keepdims=True)
        routed = jnp.broadcast_to(jnp.where(routed, 1.0, 0.0), (SLOT, count))
        rank = dot(routed.astype(BF16), upper) - 1.0
        placed = jnp.where(rank == slot, routed, 0.0)
        column = jnp.sum(placed * weight, axis=1, keepdims=True)
        header_ref[w] = jnp.where(lane == 0, column, 0.0).astype(BF16)
        placed = placed.astype(BF16)
        firsts.append(placed)
        placed_ref[w] = jnp.concatenate([placed] * CHIPS, axis=0)
    for part in range(2):
        for p in range(PARTS):
            large[part * PARTS + p].wait()
        for w in range(flight):
            chosen = dot(firsts[w], data[part]).astype(BF16)
            for b in range(rep):
                rows[b] = chosen[:, b * width : (b + 1) * width]
            for k in range(rep):
                some = slice(k % 2 * width, (k % 2 + 1) * width)
                pays[k // 2][w, part, :, some] = rows[jnp.bitwise_xor(r, k)]


def join_kernel(far, flight, header_ref, *refs):
    pays, outs = refs[:far], refs[far:]
    size = pays[0].shape[3]
    for w in range(flight):
        for k in range(far):
            for part in range(2):
                n = 2 * k + part
                outs[w][:, n * size : (n + 1) * size] = pays[k][w, part]
        outs[w][:, 2 * far * size :] = header_ref[w]


def forward_kernel(far, count, *refs):
    blocks, weights, outs = refs[:count], refs[count : count + 4], refs[count + 4 :]
    sums, near_refs, header_ref = outs[:far], outs[far : far + 2], outs[far + 2]
    width, columns = weights[0].shape
    units = columns // 3
    rows = count * SLOT
    for j in range(count):
        header_ref[j] = blocks[j][:, 4 * far * width :]
    for k in range(far):
        parts = []
        for part in range(2):
            n = 2 * (2 * k + part)
            for near in range(2):
                some = slice((n + near) * width, (n + near + 1) * width)
                chosen = jnp.concatenate([b[:, some] for b in blocks], axis=0)
                near_refs[near][part, k * rows : (k + 1) * rows] = chosen
                parts.append(chosen)
        for i in range(CORES):
            first, second = weights[i], weights[CORES + i]
            total = dot(parts[0], first[:, : 2 * units]) + dot(parts[1], second[:, : 2 * units])
            start = i * columns
            sums[k][:, start : start + 2 * units] = total.astype(sums[k].dtype)
            total = dot(parts[2], first[:, 2 * units :]) + dot(parts[3], second[:, 2 * units :])
            sums[k][:, start + 2 * units : start + columns] = total.astype(sums[k].dtype)


def hidden_kernel(rep, count, cap_ref, own_ref, other_ref, *refs):
    far = rep // 2
    sums, pieces, rest = refs[:far], refs[far : far + 2 * rep], refs[far + 2 * rep :]
    back_refs, grad_refs, cap, sem = rest[:count], rest[count:-2], rest[-2], rest[-1]
    cap_copy = pltpu.make_async_copy(cap_ref, cap, sem)
    cap_copy.start()
    width = pieces[0].shape[0]
    columns = sums[0].shape[1] // CORES
    units = columns // 3
    r = lax.axis_index("rep")
    e = lax.axis_index("ep")
    mine = e // SPLIT
    total = sums[0][...]
    for k in range(1, far):
        total = total + sums[k][...].astype(F32)
    cap_copy.wait()
    capacity = (BLOCK * cap[mine, r]).astype(F32)
    lane = iota((SLOT, LANES), 1)
    sources, rates, counts = [], [], []
    for core, ref in enumerate((own_ref, other_ref)):
        for j in range(count):
            sources.append(jnp.bitwise_xor(e, CORES * j + core))
            rate = jnp.where(lane == 0, ref[j].astype(F32), 0.0)
            rate = jnp.sum(rate, axis=1, keepdims=True)
            rates.append(rate)
            counts.append(jnp.sum(jnp.where(rate > 0.0, 1.0, 0.0), axis=0, keepdims=True))
    slot = iota((SLOT, 1), 0).astype(F32)
    rate_rows, kept_rows = [], []
    for j in range(count):
        start = jnp.zeros((1, 1), F32)
        for other in range(len(sources)):
            start = start + jnp.where(sources[other] < sources[j], counts[other], 0.0)
        kept = jnp.where((rates[j] > 0.0) & (start + slot < capacity), 1.0, 0.0)
        kept_rows.append(kept)
        rate_rows.append(rates[j] * kept)
    rate = jnp.concatenate(rate_rows, axis=0)
    kept = jnp.concatenate(kept_rows, axis=0)

    lane = iota((count * SLOT, LANES), 1)
    scores = jnp.zeros((count * SLOT, LANES), F32)
    pairs = []
    for i in range(CORES):
        pre_gate = total[:, i * columns : i * columns + units]
        pre_up = total[:, i * columns + units : i * columns + 2 * units]
        back_hidden = total[:, i * columns + 2 * units : (i + 1) * columns]
        sig = 1.0 / (1.0 + jnp.exp(-pre_gate))
        activated = pre_gate * sig
        hidden = activated * pre_up
        score = jnp.sum(hidden * back_hidden, axis=1, keepdims=True) * kept
        scores = jnp.where(lane == i, score, scores)
        scaled = back_hidden * rate
        gate_grad = (scaled * pre_up * sig * (1.0 + pre_gate * (1.0 - sig))).astype(BF16)
        up_grad = (scaled * activated).astype(BF16)
        grad_refs[i][:, :units] = gate_grad
        grad_refs[i][:, units : 2 * units] = up_grad
        grad_refs[i][:, 2 * units :] = (hidden * rate).astype(BF16)
        pairs.append(jnp.concatenate([gate_grad, up_grad], axis=1))
    for k in range(rep):
        back = dot(pairs[0], pieces[CORES * k][:, : 2 * units], ((1,), (1,)))
        back = back + dot(pairs[1], pieces[CORES * k + 1][:, : 2 * units], ((1,), (1,)))
        back = back.astype(BF16)
        for j in range(count):
            back_refs[j][:, k * width : (k + 1) * width] = back[j * SLOT : (j + 1) * SLOT]
    scores = scores.astype(BF16)
    for j in range(count):
        back_refs[j][:, rep * width :] = scores[j * SLOT : (j + 1) * SLOT]


def weight_kernel(rep, *refs):
    inputs, grads, outs = refs[:4], refs[4 : 4 + rep], refs[4 + rep :]
    units = outs[0].shape[1]
    rows = grads[0].shape[0] // CORES
    pair, down = 0.0, 0.0
    for near in range(2):
        for core in range(CORES):
            ref = inputs[CORES * near + core]
            some = slice(core * rows, (core + 1) * rows)
            got = jnp.concatenate([grads[k][some] for k in range(near, rep, 2)], axis=0)
            pair = pair + dot(got[:, : 2 * units], ref[0], ((0,), (0,)))
            down = down + dot(got[:, 2 * units :], ref[1], ((0,), (0,)))
    outs[0][...] = pair[:units].T.astype(BF16)
    outs[1][...] = pair[units:].T.astype(BF16)
    outs[2][...] = down.T.astype(BF16)


def token_kernel(rep, flight, ids_ref, placed_ref, *refs):
    backs, rest = refs[: flight * CHIPS], refs[flight * CHIPS :]
    out_ref, weight_ref, blocks, ids, sem = rest
    ids_copy = pltpu.make_async_copy(ids_ref, ids, sem)
    ids_copy.start()
    r = lax.axis_index("rep")
    mine = lax.axis_index("ep") // SPLIT
    spacing = EXPERTS // flight
    width = out_ref.shape[1] // rep
    joined = [
        jnp.concatenate([b[...] for b in backs[w * CHIPS : (w + 1) * CHIPS]], axis=0)
        for w in range(flight)
    ]
    for k in range(rep):
        total = 0.0
        for w in range(flight):
            some = joined[w][:, k * width : (k + 1) * width]
            total = total + dot(placed_ref[w], some, ((0,), (0,)))
        blocks[jnp.bitwise_xor(r, k)] = total.astype(BF16)
    for b in range(rep):
        out_ref[:, b * width : (b + 1) * width] = blocks[b]
    result = jnp.zeros(weight_ref.shape, F32)
    ids_copy.wait()
    for w in range(flight):
        score = dot(joined[w][:, rep * width :], placed_ref[w], ((0,), (0,)))
        score = jnp.sum(score, axis=0, keepdims=True)
        match = ids[...] == jnp.bitwise_xor(mine, w) * spacing
        result = result + jnp.where(match, score, 0.0)
    weight_ref[...] = result


def local(
    tokens, out_grad, expert_ids, route_weight, live_count, cap_blocks, w_gate, w_up, w_down_t
):
    rep = lax.axis_size("rep")
    ep = lax.axis_size("ep")
    far = rep // 2
    flight = ep // SPLIT
    count = ep // CORES
    tok_count, model_dim = tokens.shape
    width, units = w_gate.shape
    rows = count * SLOT
    ids_rows, rw_rows, caps = expert_ids.T, route_weight.T, cap_blocks.T

    def send(array, rep_bits, ep_bits):
        mask = rep_bits * ep + ep_bits
        pairs = [(a, a ^ mask) for a in range(rep * ep)]
        return lax.ppermute(array, ("rep", "ep"), pairs)

    weights, pair = call(
        join_weights_kernel,
        [shape((width, 3 * units)), shape((width, 2 * units))],
        [w_gate, w_up, w_down_t],
        stored=(0, 1, 2),
        scratch=[pltpu.SemaphoreType.DMA((5,))],
        grant=54,
    )
    near = send(weights, 1, 0)
    packed = call(
        functools.partial(pack_kernel, rep, flight),
        [shape((flight, 2, SLOT, 2 * width))] * far
        + [shape((flight, SLOT, LANES)), shape((flight, CHIPS * SLOT, tok_count))],
        [live_count, tokens, out_grad, ids_rows, rw_rows],
        stored=range(5),
        scratch=[
            pltpu.SMEM(live_count.shape, jnp.int32),
            pltpu.VMEM(ids_rows.shape, jnp.int32),
            pltpu.VMEM(rw_rows.shape, BF16),
            pltpu.VMEM((2, tok_count, model_dim), BF16),
            pltpu.VMEM((rep, SLOT, width), BF16),
            pltpu.SemaphoreType.DMA((2 * PARTS + 3,)),
        ],
        grant=53,
    )
    pays, header, placed = list(packed[:far]), packed[far], packed[far + 1]
    pays = [pays[0]] + [send(pays[k], 2 * k, 0) for k in range(1, far)]
    joined = call(
        functools.partial(join_kernel, far, flight),
        [shape((SLOT, 4 * far * width + LANES))] * flight,
        [header] + pays,
    )
    blocks = [joined[0]] + [send(joined[j // CHIPS], 0, CORES * j) for j in range(1, count)]
    weights_other = send(weights, 0, 1)
    near_other = send(near, 0, 1)
    (near_pair,) = call(pair_kernel, [shape((width, 2 * units))], [near])
    pieces = [weights, weights_other, near, near_other]
    for k in range(1, far):
        for array in (pair, near_pair):
            moved = send(array, 2 * k, 0)
            pieces += [moved, send(moved, 0, 1)]

    results = call(
        functools.partial(forward_kernel, far, count),
        [shape((rows, 3 * CORES * units), F32)]
        + [shape((rows, 3 * CORES * units))] * (far - 1)
        + [shape((2, far * rows, width))] * 2
        + [shape((count, SLOT, LANES))],
        blocks + pieces[:4],
        flops=2 * far * rows * 2 * width * 3 * CORES * units,
    )
    sums, rows_here, rows_near, header = results[:far], results[far], results[far + 1], results[-1]
    sums = [sums[0]] + [send(sums[k], 2 * k, 0) for k in range(1, far)]
    results = call(
        functools.partial(hidden_kernel, rep, count),
        [shape((SLOT, model_dim + LANES))] * count + [shape((rows, 3 * units))] * CORES,
        [caps, header, send(header, 0, 1)] + sums + pieces,
        stored=(0,),
        scratch=[pltpu.SMEM(caps.shape, jnp.int32), pltpu.SemaphoreType.DMA(())],
        flops=2 * rows * model_dim * 4 * units,
    )
    backs, grads = results[:count], results[count:]
    backs = [backs[0]] + [send(backs[j], 0, CORES * j) for j in range(1, count)]
    grads = jnp.concatenate([grads[0], send(grads[1], 0, 1)], axis=0)
    group_grads = [grads] + [send(grads, k, 0) for k in range(1, rep)]
    rows_near = send(rows_near, 1, 0)
    inputs = [rows_here, send(rows_here, 0, 1), rows_near, send(rows_near, 0, 1)]
    grad_gate, grad_up, grad_down = call(
        functools.partial(weight_kernel, rep),
        [shape((width, units))] * 3,
        inputs + group_grads,
        flops=2 * 2 * rep * rows * width * 3 * units,
    )
    grad_tokens, grad_weight = call(
        functools.partial(token_kernel, rep, flight),
        [shape((tok_count, model_dim)), shape(ids_rows.shape, F32)],
        [ids_rows, placed] + backs,
        stored=(0,),
        scratch=[
            pltpu.VMEM((rep, tok_count, width), BF16),
            pltpu.VMEM(ids_rows.shape, jnp.int32),
            pltpu.SemaphoreType.DMA(()),
        ],
        flops=2 * tok_count * CHIPS * SLOT * model_dim,
    )
    return grad_tokens, grad_weight.T, grad_gate, grad_up, grad_down


def solution(mesh):
    return jax.shard_map(
        local,
        mesh=mesh,
        in_specs=(
            P(("rep", "ep"), None),
            P(("rep", "ep"), None),
            P(("rep", "ep"), None),
            P(("rep", "ep"), None),
            P(),
            P(),
            P("rep", "ep"),
            P("rep", "ep"),
            P("rep", "ep"),
        ),
        out_specs=(
            P(("rep", "ep"), None),
            P(("rep", "ep"), None),
            P("rep", "ep"),
            P("rep", "ep"),
            P("rep", "ep"),
        ),
        check_vma=False,
    )
```

time: 85.4 us -> 88.3 us (1.034)
  waiting for transfers between devices: 27.5 us -> 43.9 us
  local copies, waits for them, and re-layouts: 9.71 us -> 1.34 us
  starting transfers between devices: 34.5 us -> 31.6 us
  Pallas kernels: 12.4 us -> 10.5 us
    ppermute x26 -> x23, waiting for transfers between devices: 12.2 us -> 43.9 us  [send(): return lax.ppermute(array, ('rep', 'ep'), pairs)]
    ppermute x6 -> x0, starting transfers between devices: 15.9 us -> none  [send_ring(): return lax.ppermute(array, 'ep', pairs)]
    ppermute x6 -> x0, waiting for transfers between devices: 15.2 us -> none  [send_ring(): return lax.ppermute(array, 'ep', pairs)]
    ppermute x26 -> x23, starting transfers between devices: 18.6 us -> 31.6 us  [send(): return lax.ppermute(array, ('rep', 'ep'), pairs)]
    unnamed x40 -> x13, local copies, waits for them, and re-layouts: 7.56 us -> 1.33 us
    slice x2 -> x0, local copies, waits for them, and re-layouts: 2.13 us -> none  [local(): w[h * half:(h + 1) * half]]
    pallas_call x5 -> x8, Pallas kernels: 12.4 us -> 10.5 us  [call(): pl.pallas_call(kernel, out_shape=tuple(outs), in_specs=[HBM if n in store...]
  transfers between devices with their start and end apart: 32 -> 23, of which waited for: 14 -> 11; matrix products, arithmetic and copies ran while one was open for 0% -> 0% of each run, Pallas kernels for 11% -> 7%
where the time goes in v5:
time: 88.3 us; the launch traced here: 88.1 us
  waiting for transfers between devices  43.9 us (50%)
  starting transfers between devices  31.6 us (36%)
  Pallas kernels  10.5 us (12%)
  local copies, waits for them, and re-layouts  1.34 us (2%)
    ppermute x23, waiting for transfers between devices, send(): return lax.ppermute(array, ('rep', 'ep'), pairs)  43.9 us
    ppermute x23, starting transfers between devices, send(): return lax.ppermute(array, ('rep', 'ep'), pairs)  31.6 us
    pallas_call x8, Pallas kernels, call(): pl.pallas_call(kernel, out_shape=tuple(outs), in_specs=[HBM if n in store...  10.5 us
  transfers between devices with their start and end apart: 23, of which 11 were waited for; matrix products, arithmetic and copies ran while one was open for 0% of the time, Pallas kernels for 7%

profile of v5, /device:TPU:0, one launch (start us, length us, event | category | flops | bytes accessed | tf_op | source)
XLA Modules:
  0.0 88.1 jit_solution(10614950176263632560)
XLA Ops:
  0.6 2.4 %shard_map.130 = (bf16[896,384]{1,0:T(8,128)(2,1)}, bf16[896,256]{1,0:T(8,128)(2,1)}) custom-call(bf16[896,128]{1,0:T(8,128)(2,1)} %gate_ref.1, bf16[896,128]{1,0:T(8,128)(2,1)} %up_ref.1, bf16[896,128]{1,0:T(8,128)(2,1)} %down_ref.1), custom_call_target="tpu_custom_call" | custom-call | bytes 1835008 | tf_op jit(solution)/shard_map/pallas_call | solution.py:32
  3.1 3.0 %collective-permute-start.5 = (bf16[896,384]{1,0:T(8,128)(2,1)}, bf16[896,384]{1,0:T(8,128)(2,1)S(1)}, u32[]{:S(2)}, u32[]{:S(2)}) collective-permute-start(bf16[896,384]{1,0:T(8,128)(2,1)} %get-tuple-element.31.refs_4_.refs_2_), channel_id=1, source_target_pairs={{0,8},{1,9},{2,10},{3,11},{4,12},{5,13},{6,14},{7,15},{8,0},{9,1},... | collective-permute-start | bytes 2064392 | tf_op jit(solution)/shard_map/ppermute | solution.py:295
  6.1 0.6 copy-done.3
  6.7 2.0 %shard_map.128 = (bf16[1,2,16,1792]{3,2,1,0:T(8,128)(2,1)S(1)}, bf16[1,2,16,1792]{3,2,1,0:T(8,128)(2,1)S(1)}, bf16[1,16,128]{2,1,0:T(8,128)(2,1)S(1)}, bf16[1,64,128]{2,1,0:T(8,128)(2,1)S(1)}) custom-call(s32[4]{0:T(128)S(1)} %copy-done.3, bf16[128,3584]{1,0:T(8,128)(2,1)} %tok_ref.1, bf16[128,3584]{1,0:T(8,128)(2,1)} %grad_ref.1, s32[8,128]{1,0:T(8,128)S(1)} %bitcast.4, ...), custom_call_target="tpu_custom_call" | custom-call | bytes 2091024 | tf_op jit(solution)/shard_map/pallas_call | solution.py:32
  8.7 1.6 %collective-permute-start = (bf16[1,2,16,1792]{3,2,1,0:T(8,128)(2,1)S(1)}, bf16[1,2,16,1792]{3,2,1,0:T(8,128)(2,1)S(1)}, u32[]{:S(2)}, u32[]{:S(2)}) collective-permute-start(bf16[1,2,16,1792]{3,2,1,0:T(8,128)(2,1)S(1)} %get-tuple-element.30), channel_id=1, source_target_pairs={{0,16},{1,17},{2,18},{3,19},{4,20},{5,21},{6,22},{7,23},{8,24},{9,... | collective-permute-start | bytes 344072 | tf_op jit(solution)/shard_map/ppermute | solution.py:295
  10.3 11.4 %collective-permute-done.5.refs_6_.all_ref.refs_4_ = bf16[896,384]{1,0:T(8,128)(2,1)S(1)} collective-permute-done((bf16[896,384]{1,0:T(8,128)(2,1)}, bf16[896,384]{1,0:T(8,128)(2,1)S(1)}, u32[]{:S(2)}, u32[]{:S(2)}) %collective-permute-start.5) | collective-permute-done | bytes 688160 | tf_op jit(solution)/shard_map/ppermute | solution.py:295
  21.7 1.9 %collective-permute-start.1 = (bf16[16,7296]{1,0:T(8,128)(2,1)S(1)}, bf16[16,7296]{1,0:T(8,128)(2,1)S(1)}, u32[]{:S(2)}, u32[]{:S(2)}) collective-permute-start(bf16[16,7296]{1,0:T(8,128)(2,1)S(1)} %shard_map.129.refs_0_), channel_id=1, source_target_pairs={{0,2},{1,3},{2,0},{3,1},{4,6},{5,7},{6,4},{7,5},{8,10},{9,11},{10,... | collective-permute-start | bytes 700424 | tf_op jit(solution)/shard_map/ppermute | solution.py:295
  23.6 2.6 %collective-permute-start.2 = (bf16[16,7296]{1,0:T(8,128)(2,1)S(1)}, bf16[16,7296]{1,0:T(8,128)(2,1)S(1)}, u32[]{:S(2)}, u32[]{:S(2)}) collective-permute-start(bf16[16,7296]{1,0:T(8,128)(2,1)S(1)} %shard_map.129.refs_0_), channel_id=1, source_target_pairs={{0,4},{1,5},{2,6},{3,7},{4,0},{5,1},{6,2},{7,3},{8,12},{9,13},{10,... | collective-permute-start | bytes 700424 | tf_op jit(solution)/shard_map/ppermute | solution.py:295
  26.2 1.5 %collective-permute-start.9 = (bf16[896,256]{1,0:T(8,128)(2,1)S(1)}, bf16[896,256]{1,0:T(8,128)(2,1)S(1)}, u32[]{:S(2)}, u32[]{:S(2)}) collective-permute-start(bf16[896,256]{1,0:T(8,128)(2,1)S(1)} %copy-done.5), channel_id=1, source_target_pairs={{0,16},{1,17},{2,18},{3,19},{4,20},{5,21},{6,22},{7,23},{8,24},{9,... | collective-permute-start | bytes 1376264 | tf_op jit(solution)/shard_map/ppermute | solution.py:295
  27.8 7.1 %collective-permute-done.1.refs_1_ = bf16[16,7296]{1,0:T(8,128)(2,1)S(1)} collective-permute-done((bf16[16,7296]{1,0:T(8,128)(2,1)S(1)}, bf16[16,7296]{1,0:T(8,128)(2,1)S(1)}, u32[]{:S(2)}, u32[]{:S(2)}) %collective-permute-start.1) | collective-permute-done | bytes 233504 | tf_op jit(solution)/shard_map/ppermute | solution.py:295
  34.9 1.7 %collective-permute-start.11 = (bf16[896,256]{1,0:T(8,128)(2,1)S(1)}, bf16[896,256]{1,0:T(8,128)(2,1)S(1)}, u32[]{:S(2)}, u32[]{:S(2)}) collective-permute-start(bf16[896,256]{1,0:T(8,128)(2,1)S(1)} %shard_map.132), channel_id=1, source_target_pairs={{0,16},{1,17},{2,18},{3,19},{4,20},{5,21},{6,22},{7,23},{8,24},{9,... | collective-permute-start | bytes 1376264 | tf_op jit(solution)/shard_map/ppermute | solution.py:295
  36.6 0.8 collective-permute-done.2.refs_2_
  37.4 2.5 %collective-permute-start.3 = (bf16[16,7296]{1,0:T(8,128)(2,1)S(1)}, bf16[16,7296]{1,0:T(8,128)(2,1)S(1)}, u32[]{:S(2)}, u32[]{:S(2)}) collective-permute-start(bf16[16,7296]{1,0:T(8,128)(2,1)S(1)} %shard_map.129.refs_0_), channel_id=1, source_target_pairs={{0,6},{1,7},{2,4},{3,5},{4,2},{5,3},{6,0},{7,1},{8,14},{9,15},{10,... | collective-permute-start | bytes 700424 | tf_op jit(solution)/shard_map/ppermute | solution.py:295
  39.9 5.6 %collective-permute-done.3.refs_3_ = bf16[16,7296]{1,0:T(8,128)(2,1)S(1)} collective-permute-done((bf16[16,7296]{1,0:T(8,128)(2,1)S(1)}, bf16[16,7296]{1,0:T(8,128)(2,1)S(1)}, u32[]{:S(2)}, u32[]{:S(2)}) %collective-permute-start.3) | collective-permute-done | bytes 233504 | tf_op jit(solution)/shard_map/ppermute | solution.py:295
  45.5 1.0 %shard_map.131 = (f32[64,768]{1,0:T(8,128)S(1)}, bf16[64,768]{1,0:T(8,128)(2,1)S(1)}, bf16[2,128,896]{2,1,0:T(8,128)(2,1)S(1)}, bf16[2,128,896]{2,1,0:T(8,128)(2,1)S(1)}, bf16[4,16,128]{2,1,0:T(8,128)(2,1)S(1)}) custom-call(bf16[16,7296]{1,0:T(8,128)(2,1)S(1)} %shard_map.129.refs_0_, bf16[16,7296]{1,0:T(8,128)(2,1)S(1)} %collective-permute-done.1.refs_1_, ...), custom_call_target="tpu_custom_call" | custom-call | flops 352321536 | bytes 4915200 | tf_op jit(solution)/shard_map/pallas_call | solution.py:32
  46.5 1.6 %collective-permute-start.17 = (bf16[2,128,896]{2,1,0:T(8,128)(2,1)S(1)}, bf16[2,128,896]{2,1,0:T(8,128)(2,1)S(1)}, u32[]{:S(2)}, u32[]{:S(2)}) collective-permute-start(bf16[2,128,896]{2,1,0:T(8,128)(2,1)S(1)} %get-tuple-element.43), channel_id=1, source_target_pairs={{0,8},{1,9},{2,10},{3,11},{4,12},{5,13},{6,14},{7,15},{8,0},{9,1},... | collective-permute-start | bytes 1376264 | tf_op jit(solution)/shard_map/ppermute | solution.py:295
  48.6 1.4 %collective-permute-start.8 = (bf16[64,768]{1,0:T(8,128)(2,1)S(1)}, bf16[64,768]{1,0:T(8,128)(2,1)S(1)}, u32[]{:S(2)}, u32[]{:S(2)}) collective-permute-start(bf16[64,768]{1,0:T(8,128)(2,1)S(1)} %get-tuple-element.34), channel_id=1, source_target_pairs={{0,16},{1,17},{2,18},{3,19},{4,20},{5,21},{6,22},{7,23},{8,24},{9,... | collective-permute-start | bytes 294920 | tf_op jit(solution)/shard_map/ppermute | solution.py:295
  50.2 6.5 %collective-permute-done.17.refs_2_ = bf16[2,128,896]{2,1,0:T(8,128)(2,1)S(1)} collective-permute-done((bf16[2,128,896]{2,1,0:T(8,128)(2,1)S(1)}, bf16[2,128,896]{2,1,0:T(8,128)(2,1)S(1)}, u32[]{:S(2)}, u32[]{:S(2)}) %collective-permute-start.17) | collective-permute-done | bytes 458784 | tf_op jit(solution)/shard_map/ppermute | solution.py:295
  57.2 1.3 %collective-permute-done.7.other_ref = bf16[4,16,128]{2,1,0:T(8,128)(2,1)S(1)} collective-permute-done((bf16[4,16,128]{2,1,0:T(8,128)(2,1)S(1)}, bf16[4,16,128]{2,1,0:T(8,128)(2,1)S(1)}, u32[]{:S(2)}, u32[]{:S(2)}) %collective-permute-start.7) | collective-permute-done | bytes 16416 | tf_op jit(solution)/shard_map/ppermute | solution.py:295
  58.5 0.7 copy-done.4
  59.2 1.9 %shard_map.133 = (bf16[16,3712]{1,0:T(8,128)(2,1)S(1)}, bf16[16,3712]{1,0:T(8,128)(2,1)S(1)}, bf16[16,3712]{1,0:T(8,128)(2,1)S(1)}, bf16[16,3712]{1,0:T(8,128)(2...) custom-call(s32[1,4]{1,0:T(1,128)S(1)} %bitcast.7, bf16[4,16,128]{2,1,0:T(8,128)(2,1)S(1)} %get-tuple-element.32.own_ref, ...), custom_call_target="tpu_custom_call" | custom-call | flops 234881024 | bytes 5488656 | tf_op jit(solution)/shard_map/pallas_call | solution.py:32
  61.3 6.1 %collective-permute-start.13 = (bf16[16,3712]{1,0:T(8,128)(2,1)S(1)}, bf16[16,3712]{1,0:T(8,128)(2,1)S(1)}, u32[]{:S(2)}, u32[]{:S(2)}) collective-permute-start(bf16[16,3712]{1,0:T(8,128)(2,1)S(1)} %get-tuple-element.37), channel_id=1, source_target_pairs={{0,2},{1,3},{2,0},{3,1},{4,6},{5,7},{6,4},{7,5},{8,10},{9,11},{10,... | collective-permute-start | bytes 356360 | tf_op jit(solution)/shard_map/ppermute | solution.py:295
  67.4 2.4 %collective-permute-start.15 = (bf16[16,3712]{1,0:T(8,128)(2,1)S(1)}, bf16[16,3712]{1,0:T(8,128)(2,1)S(1)}, u32[]{:S(2)}, u32[]{:S(2)}) collective-permute-start(bf16[16,3712]{1,0:T(8,128)(2,1)S(1)} %get-tuple-element.39), channel_id=1, source_target_pairs={{0,6},{1,7},{2,4},{3,5},{4,2},{5,3},{6,0},{7,1},{8,14},{9,15},{10,... | collective-permute-start | bytes 356360 | tf_op jit(solution)/shard_map/ppermute | solution.py:295
  69.8 1.9 %collective-permute-done.13.refs_1_ = bf16[16,3712]{1,0:T(8,128)(2,1)S(1)} collective-permute-done((bf16[16,3712]{1,0:T(8,128)(2,1)S(1)}, bf16[16,3712]{1,0:T(8,128)(2,1)S(1)}, u32[]{:S(2)}, u32[]{:S(2)}) %collective-permute-start.13) | collective-permute-done | bytes 118816 | tf_op jit(solution)/shard_map/ppermute | solution.py:295
  71.7 1.5 %collective-permute-start.20 = (bf16[128,384]{1,0:T(8,128)(2,1)S(1)}, bf16[128,384]{1,0:T(8,128)(2,1)S(1)}, u32[]{:S(2)}, u32[]{:S(2)}) collective-permute-start(bf16[128,384]{1,0:T(8,128)(2,1)S(1)} %constant_dynamic-update-slice_fusion.refs_4_), channel_id=1, source_target_pairs={{0,8},{1,9},{2,10},{3,11},{4,12},{5,13},{6,14},{7,15},{8,0},{9,1},... | collective-permute-start | bytes 294920 | tf_op jit(solution)/shard_map/ppermute | solution.py:295
  73.1 6.0 %collective-permute-done.14.refs_2_ = bf16[16,3712]{1,0:T(8,128)(2,1)S(1)} collective-permute-done((bf16[16,3712]{1,0:T(8,128)(2,1)S(1)}, bf16[16,3712]{1,0:T(8,128)(2,1)S(1)}, u32[]{:S(2)}, u32[]{:S(2)}) %collective-permute-start.14) | collective-permute-done | bytes 118816 | tf_op jit(solution)/shard_map/ppermute | solution.py:295
  79.2 1.7 %collective-permute-start.21 = (bf16[128,384]{1,0:T(8,128)(2,1)S(1)}, bf16[128,384]{1,0:T(8,128)(2,1)S(1)}, u32[]{:S(2)}, u32[]{:S(2)}) collective-permute-start(bf16[128,384]{1,0:T(8,128)(2,1)S(1)} %constant_dynamic-update-slice_fusion.refs_4_), channel_id=1, source_target_pairs={{0,16},{1,17},{2,18},{3,19},{4,20},{5,21},{6,22},{7,23},{8,24},{9,... | collective-permute-start | bytes 294920 | tf_op jit(solution)/shard_map/ppermute | solution.py:295
  80.8 1.3 %collective-permute-start.22 = (bf16[128,384]{1,0:T(8,128)(2,1)S(1)}, bf16[128,384]{1,0:T(8,128)(2,1)S(1)}, u32[]{:S(2)}, u32[]{:S(2)}) collective-permute-start(bf16[128,384]{1,0:T(8,128)(2,1)S(1)} %constant_dynamic-update-slice_fusion.refs_4_), channel_id=1, source_target_pairs={{0,24},{1,25},{2,26},{3,27},{4,28},{5,29},{6,30},{7,31},{8,16},{9,... | collective-permute-start | bytes 294920 | tf_op jit(solution)/shard_map/ppermute | solution.py:295
  82.1 1.4 %shard_map.134 = (bf16[128,3584]{1,0:T(8,128)(2,1)}, f32[8,128]{1,0:T(8,128)}) custom-call(s32[8,128]{1,0:T(8,128)S(1)} %bitcast.5, bf16[1,64,128]{2,1,0:T(8,128)(2,1)S(1)} %get-tuple-element.27.placed_ref, bf16[16,3712]{1,0:T(8,128)(2,1)S(1)} %get-tuple-element.36.refs_0_, bf16[16,3712]{1,0:T(8,128)(2,1)S(1)} %collective-permute-done.13.refs_1_, ...), custom_call_target="tpu_custom_call" | custom-call | flops 58720256 | bytes 1417216 | tf_op jit(solution)/shard_map/pallas_call | solution.py:32
  83.6 1.2 %collective-permute-done.21.refs_6_ = bf16[128,384]{1,0:T(8,128)(2,1)S(1)} collective-permute-done((bf16[128,384]{1,0:T(8,128)(2,1)S(1)}, bf16[128,384]{1,0:T(8,128)(2,1)S(1)}, u32[]{:S(2)}, u32[]{:S(2)}) %collective-permute-start.21) | collective-permute-done | bytes 98336 | tf_op jit(solution)/shard_map/ppermute | solution.py:295
  84.8 1.5 %collective-permute-done.22.refs_7_ = bf16[128,384]{1,0:T(8,128)(2,1)S(1)} collective-permute-done((bf16[128,384]{1,0:T(8,128)(2,1)S(1)}, bf16[128,384]{1,0:T(8,128)(2,1)S(1)}, u32[]{:S(2)}, u32[]{:S(2)}) %collective-permute-start.22) | collective-permute-done | bytes 98336 | tf_op jit(solution)/shard_map/ppermute | solution.py:295
  86.4 1.8 %shard_map.135 = (bf16[896,128]{1,0:T(8,128)(2,1)}, bf16[896,128]{1,0:T(8,128)(2,1)}, bf16[896,128]{1,0:T(8,128)(2,1)}) custom-call(bf16[2,128,896]{2,1,0:T(8,128)(2,1)S(1)} %get-tuple-element.42.refs_0_, bf16[2,128,896]{2,1,0:T(8,128)(2,1)S(1)} %collective-permute-done.16.refs_1_, bf16[2,128,896]{2,1,0:T(8,128)(2,1)S(1)} %collective-permute-done.17.refs_2_, ...), custom_call_target="tpu_custom_call" | custom-call | flops 352321536 | bytes 2916352 | tf_op jit(solution)/shard_map/pallas_call | solution.py:32
  (36 shorter events, 1.6 us)
Async XLA Ops:
  0.6 5.4 %copy-start.2 = (bf16[128,8]{0,1:T(8,128)(2,1)S(1)}, bf16[128,8]{0,1:T(8,128)(2,1)}, u32[]{:S(2)}) copy-start(bf16[128,8]{0,1:T(8,128)(2,1)} %param.12) | copy-start | bytes 6148
  3.1 3.0 %copy-start.1 = (s32[128,8]{0,1:T(8,128)S(1)}, s32[128,8]{0,1:T(8,128)}, u32[]{:S(2)}) copy-start(s32[128,8]{0,1:T(8,128)} %param.11) | copy-start | bytes 12292
  3.1 18.6 %collective-permute-start.5 = (bf16[896,384]{1,0:T(8,128)(2,1)}, bf16[896,384]{1,0:T(8,128)(2,1)S(1)}, u32[]{:S(2)}, u32[]{:S(2)}) collective-permute-start(bf16[896,384]{1,0:T(8,128)(2,1)} %get-tuple-element.31.refs_4_.refs_2_), channel_id=1, source_target_pairs={{0,8},{1,9},{2,10},{3,11},{4,12},{5,13},{6,14},{7,15},{8,0},{9,1},... | collective-permute-start | bytes 2064392 | tf_op jit(solution)/shard_map/ppermute | solution.py:295
  6.1 0.7 copy-start.3
  6.7 3.6 %copy-start = (bf16[896,384]{1,0:T(8,128)(2,1)S(1)}, bf16[896,384]{1,0:T(8,128)(2,1)}, u32[]{:S(2)}) copy-start(bf16[896,384]{1,0:T(8,128)(2,1)} %get-tuple-element.31.refs_4_.refs_2_) | copy-start | bytes 2064388
  8.7 17.5 %copy-start.5 = (bf16[896,256]{1,0:T(8,128)(2,1)S(1)}, bf16[896,256]{1,0:T(8,128)(2,1)}, u32[]{:S(2)}) copy-start(bf16[896,256]{1,0:T(8,128)(2,1)} %get-tuple-element.35) | copy-start | bytes 1376260
  8.7 13.0 %collective-permute-start = (bf16[1,2,16,1792]{3,2,1,0:T(8,128)(2,1)S(1)}, bf16[1,2,16,1792]{3,2,1,0:T(8,128)(2,1)S(1)}, u32[]{:S(2)}, u32[]{:S(2)}) collective-permute-start(bf16[1,2,16,1792]{3,2,1,0:T(8,128)(2,1)S(1)} %get-tuple-element.30), channel_id=1, source_target_pairs={{0,16},{1,17},{2,18},{3,19},{4,20},{5,21},{6,22},{7,23},{8,24},{9,... | collective-permute-start | bytes 344072 | tf_op jit(solution)/shard_map/ppermute | solution.py:295
  10.3 35.2 %collective-permute-start.4 = (bf16[896,384]{1,0:T(8,128)(2,1)S(1)}, bf16[896,384]{1,0:T(8,128)(2,1)S(1)}, u32[]{:S(2)}, u32[]{:S(2)}) collective-permute-start(bf16[896,384]{1,0:T(8,128)(2,1)S(1)} %copy-done), channel_id=1, source_target_pairs={{0,1},{1,0},{2,3},{3,2},{4,5},{5,4},{6,7},{7,6},{8,9},{9,8},{10,11... | collective-permute-start | bytes 2064392 | tf_op jit(solution)/shard_map/ppermute | solution.py:295
  21.7 23.8 %collective-permute-start.6 = (bf16[896,384]{1,0:T(8,128)(2,1)S(1)}, bf16[896,384]{1,0:T(8,128)(2,1)S(1)}, u32[]{:S(2)}, u32[]{:S(2)}) collective-permute-start(bf16[896,384]{1,0:T(8,128)(2,1)S(1)} %collective-permute-done.5.refs_6_.all_ref.refs_4_), channel_id=1, source_target_pairs={{0,1},{1,0},{2,3},{3,2},{4,5},{5,4},{6,7},{7,6},{8,9},{9,8},{10,11... | collective-permute-start | bytes 2064392 | tf_op jit(solution)/shard_map/ppermute | solution.py:295
  21.7 13.1 %collective-permute-start.1 = (bf16[16,7296]{1,0:T(8,128)(2,1)S(1)}, bf16[16,7296]{1,0:T(8,128)(2,1)S(1)}, u32[]{:S(2)}, u32[]{:S(2)}) collective-permute-start(bf16[16,7296]{1,0:T(8,128)(2,1)S(1)} %shard_map.129.refs_0_), channel_id=1, source_target_pairs={{0,2},{1,3},{2,0},{3,1},{4,6},{5,7},{6,4},{7,5},{8,10},{9,11},{10,... | collective-permute-start | bytes 700424 | tf_op jit(solution)/shard_map/ppermute | solution.py:295
  23.6 13.8 %collective-permute-start.2 = (bf16[16,7296]{1,0:T(8,128)(2,1)S(1)}, bf16[16,7296]{1,0:T(8,128)(2,1)S(1)}, u32[]{:S(2)}, u32[]{:S(2)}) collective-permute-start(bf16[16,7296]{1,0:T(8,128)(2,1)S(1)} %shard_map.129.refs_0_), channel_id=1, source_target_pairs={{0,4},{1,5},{2,6},{3,7},{4,0},{5,1},{6,2},{7,3},{8,12},{9,13},{10,... | collective-permute-start | bytes 700424 | tf_op jit(solution)/shard_map/ppermute | solution.py:295
  26.2 21.9 %collective-permute-start.9 = (bf16[896,256]{1,0:T(8,128)(2,1)S(1)}, bf16[896,256]{1,0:T(8,128)(2,1)S(1)}, u32[]{:S(2)}, u32[]{:S(2)}) collective-permute-start(bf16[896,256]{1,0:T(8,128)(2,1)S(1)} %copy-done.5), channel_id=1, source_target_pairs={{0,16},{1,17},{2,18},{3,19},{4,20},{5,21},{6,22},{7,23},{8,24},{9,... | collective-permute-start | bytes 1376264 | tf_op jit(solution)/shard_map/ppermute | solution.py:295
  34.9 13.5 %collective-permute-start.11 = (bf16[896,256]{1,0:T(8,128)(2,1)S(1)}, bf16[896,256]{1,0:T(8,128)(2,1)S(1)}, u32[]{:S(2)}, u32[]{:S(2)}) collective-permute-start(bf16[896,256]{1,0:T(8,128)(2,1)S(1)} %shard_map.132), channel_id=1, source_target_pairs={{0,16},{1,17},{2,18},{3,19},{4,20},{5,21},{6,22},{7,23},{8,24},{9,... | collective-permute-start | bytes 1376264 | tf_op jit(solution)/shard_map/ppermute | solution.py:295
  37.4 8.1 %collective-permute-start.3 = (bf16[16,7296]{1,0:T(8,128)(2,1)S(1)}, bf16[16,7296]{1,0:T(8,128)(2,1)S(1)}, u32[]{:S(2)}, u32[]{:S(2)}) collective-permute-start(bf16[16,7296]{1,0:T(8,128)(2,1)S(1)} %shard_map.129.refs_0_), channel_id=1, source_target_pairs={{0,6},{1,7},{2,4},{3,5},{4,2},{5,3},{6,0},{7,1},{8,14},{9,15},{10,... | collective-permute-start | bytes 700424 | tf_op jit(solution)/shard_map/ppermute | solution.py:295
  46.5 10.2 %collective-permute-start.17 = (bf16[2,128,896]{2,1,0:T(8,128)(2,1)S(1)}, bf16[2,128,896]{2,1,0:T(8,128)(2,1)S(1)}, u32[]{:S(2)}, u32[]{:S(2)}) collective-permute-start(bf16[2,128,896]{2,1,0:T(8,128)(2,1)S(1)} %get-tuple-element.43), channel_id=1, source_target_pairs={{0,8},{1,9},{2,10},{3,11},{4,12},{5,13},{6,14},{7,15},{8,0},{9,1},... | collective-permute-start | bytes 1376264 | tf_op jit(solution)/shard_map/ppermute | solution.py:295
  48.1 8.6 %collective-permute-start.10 = (bf16[896,256]{1,0:T(8,128)(2,1)S(1)}, bf16[896,256]{1,0:T(8,128)(2,1)S(1)}, u32[]{:S(2)}, u32[]{:S(2)}) collective-permute-start(bf16[896,256]{1,0:T(8,128)(2,1)S(1)} %collective-permute-done.9.refs_6_), channel_id=1, source_target_pairs={{0,1},{1,0},{2,3},{3,2},{4,5},{5,4},{6,7},{7,6},{8,9},{9,8},{10,11... | collective-permute-start | bytes 1376264 | tf_op jit(solution)/shard_map/ppermute | solution.py:295
  48.4 10.1 %collective-permute-start.12 = (bf16[896,256]{1,0:T(8,128)(2,1)S(1)}, bf16[896,256]{1,0:T(8,128)(2,1)S(1)}, u32[]{:S(2)}, u32[]{:S(2)}) collective-permute-start(bf16[896,256]{1,0:T(8,128)(2,1)S(1)} %collective-permute-done.11.refs_8_), channel_id=1, source_target_pairs={{0,1},{1,0},{2,3},{3,2},{4,5},{5,4},{6,7},{7,6},{8,9},{9,8},{10,11... | collective-permute-start | bytes 1376264 | tf_op jit(solution)/shard_map/ppermute | solution.py:295
  48.6 9.9 %collective-permute-start.8 = (bf16[64,768]{1,0:T(8,128)(2,1)S(1)}, bf16[64,768]{1,0:T(8,128)(2,1)S(1)}, u32[]{:S(2)}, u32[]{:S(2)}) collective-permute-start(bf16[64,768]{1,0:T(8,128)(2,1)S(1)} %get-tuple-element.34), channel_id=1, source_target_pairs={{0,16},{1,17},{2,18},{3,19},{4,20},{5,21},{6,22},{7,23},{8,24},{9,... | collective-permute-start | bytes 294920 | tf_op jit(solution)/shard_map/ppermute | solution.py:295
  50.0 36.4 %collective-permute-start.16 = (bf16[2,128,896]{2,1,0:T(8,128)(2,1)S(1)}, bf16[2,128,896]{2,1,0:T(8,128)(2,1)S(1)}, u32[]{:S(2)}, u32[]{:S(2)}) collective-permute-start(bf16[2,128,896]{2,1,0:T(8,128)(2,1)S(1)} %get-tuple-element.42.refs_0_), channel_id=1, source_target_pairs={{0,1},{1,0},{2,3},{3,2},{4,5},{5,4},{6,7},{7,6},{8,9},{9,8},{10,11... | collective-permute-start | bytes 1376264 | tf_op jit(solution)/shard_map/ppermute | solution.py:295
  56.7 29.7 %collective-permute-start.18 = (bf16[2,128,896]{2,1,0:T(8,128)(2,1)S(1)}, bf16[2,128,896]{2,1,0:T(8,128)(2,1)S(1)}, u32[]{:S(2)}, u32[]{:S(2)}) collective-permute-start(bf16[2,128,896]{2,1,0:T(8,128)(2,1)S(1)} %collective-permute-done.17.refs_2_), channel_id=1, source_target_pairs={{0,1},{1,0},{2,3},{3,2},{4,5},{5,4},{6,7},{7,6},{8,9},{9,8},{10,11... | collective-permute-start | bytes 1376264 | tf_op jit(solution)/shard_map/ppermute | solution.py:295
  56.7 1.8 %collective-permute-start.7 = (bf16[4,16,128]{2,1,0:T(8,128)(2,1)S(1)}, bf16[4,16,128]{2,1,0:T(8,128)(2,1)S(1)}, u32[]{:S(2)}, u32[]{:S(2)}) collective-permute-start(bf16[4,16,128]{2,1,0:T(8,128)(2,1)S(1)} %get-tuple-element.32.own_ref), channel_id=1, source_target_pairs={{0,1},{1,0},{2,3},{3,2},{4,5},{5,4},{6,7},{7,6},{8,9},{9,8},{10,11... | collective-permute-start | bytes 49160 | tf_op jit(solution)/shard_map/ppermute | solution.py:295
  58.5 0.7 copy-start.4
  61.1 6.3 %collective-permute-start.19 = (bf16[64,384]{1,0:T(8,128)(2,1)S(1)}, bf16[64,384]{1,0:T(8,128)(2,1)S(1)}, u32[]{:S(2)}, u32[]{:S(2)}) collective-permute-start(bf16[64,384]{1,0:T(8,128)(2,1)S(1)} %get-tuple-element.45), channel_id=1, source_target_pairs={{0,1},{1,0},{2,3},{3,2},{4,5},{5,4},{6,7},{7,6},{8,9},{9,8},{10,11... | collective-permute-start | bytes 147464 | tf_op jit(solution)/shard_map/ppermute | solution.py:295
  61.3 10.3 %collective-permute-start.13 = (bf16[16,3712]{1,0:T(8,128)(2,1)S(1)}, bf16[16,3712]{1,0:T(8,128)(2,1)S(1)}, u32[]{:S(2)}, u32[]{:S(2)}) collective-permute-start(bf16[16,3712]{1,0:T(8,128)(2,1)S(1)} %get-tuple-element.37), channel_id=1, source_target_pairs={{0,2},{1,3},{2,0},{3,1},{4,6},{5,7},{6,4},{7,5},{8,10},{9,11},{10,... | collective-permute-start | bytes 356360 | tf_op jit(solution)/shard_map/ppermute | solution.py:295
  67.4 11.8 %collective-permute-start.14 = (bf16[16,3712]{1,0:T(8,128)(2,1)S(1)}, bf16[16,3712]{1,0:T(8,128)(2,1)S(1)}, u32[]{:S(2)}, u32[]{:S(2)}) collective-permute-start(bf16[16,3712]{1,0:T(8,128)(2,1)S(1)} %get-tuple-element.38), channel_id=1, source_target_pairs={{0,4},{1,5},{2,6},{3,7},{4,0},{5,1},{6,2},{7,3},{8,12},{9,13},{10,... | collective-permute-start | bytes 356360 | tf_op jit(solution)/shard_map/ppermute | solution.py:295
  67.4 13.5 %collective-permute-start.15 = (bf16[16,3712]{1,0:T(8,128)(2,1)S(1)}, bf16[16,3712]{1,0:T(8,128)(2,1)S(1)}, u32[]{:S(2)}, u32[]{:S(2)}) collective-permute-start(bf16[16,3712]{1,0:T(8,128)(2,1)S(1)} %get-tuple-element.39), channel_id=1, source_target_pairs={{0,6},{1,7},{2,4},{3,5},{4,2},{5,3},{6,0},{7,1},{8,14},{9,15},{10,... | collective-permute-start | bytes 356360 | tf_op jit(solution)/shard_map/ppermute | solution.py:295
  71.7 11.9 %collective-permute-start.20 = (bf16[128,384]{1,0:T(8,128)(2,1)S(1)}, bf16[128,384]{1,0:T(8,128)(2,1)S(1)}, u32[]{:S(2)}, u32[]{:S(2)}) collective-permute-start(bf16[128,384]{1,0:T(8,128)(2,1)S(1)} %constant_dynamic-update-slice_fusion.refs_4_), channel_id=1, source_target_pairs={{0,8},{1,9},{2,10},{3,11},{4,12},{5,13},{6,14},{7,15},{8,0},{9,1},... | collective-permute-start | bytes 294920 | tf_op jit(solution)/shard_map/ppermute | solution.py:295
  79.2 5.7 %collective-permute-start.21 = (bf16[128,384]{1,0:T(8,128)(2,1)S(1)}, bf16[128,384]{1,0:T(8,128)(2,1)S(1)}, u32[]{:S(2)}, u32[]{:S(2)}) collective-permute-start(bf16[128,384]{1,0:T(8,128)(2,1)S(1)} %constant_dynamic-update-slice_fusion.refs_4_), channel_id=1, source_target_pairs={{0,16},{1,17},{2,18},{3,19},{4,20},{5,21},{6,22},{7,23},{8,24},{9,... | collective-permute-start | bytes 294920 | tf_op jit(solution)/shard_map/ppermute | solution.py:295
  80.8 5.5 %collective-permute-start.22 = (bf16[128,384]{1,0:T(8,128)(2,1)S(1)}, bf16[128,384]{1,0:T(8,128)(2,1)S(1)}, u32[]{:S(2)}, u32[]{:S(2)}) collective-permute-start(bf16[128,384]{1,0:T(8,128)(2,1)S(1)} %constant_dynamic-update-slice_fusion.refs_4_), channel_id=1, source_target_pairs={{0,24},{1,25},{2,26},{3,27},{4,28},{5,29},{6,30},{7,31},{8,16},{9,... | collective-permute-start | bytes 294920 | tf_op jit(solution)/shard_map/ppermute | solution.py:295

commit v6 on v5

v6 whole, which is shorter than its diff:
```python
import functools

import jax
import jax.numpy as jnp
from jax import lax
from jax.experimental import pallas as pl
from jax.experimental.pallas import tpu as pltpu
from jax.sharding import PartitionSpec as P

EXPERTS = 128
SLOT = 16
BLOCK = 128
SPLIT = 8
CORES = 2
CHIPS = SPLIT // CORES
LANES = 128
F32 = jnp.float32
BF16 = jnp.bfloat16
PARTS = 4
HBM = pl.BlockSpec(memory_space=pltpu.HBM)
VMEM = pl.BlockSpec(memory_space=pltpu.VMEM)


def shape(dims, kind=BF16):
    return jax.ShapeDtypeStruct(dims, kind)


def call(kernel, outs, args, stored=(), kept=(), scratch=(), flops=0, grant=16):
    size = sum(a.size * a.dtype.itemsize for a in args) + sum(
        o.size * o.dtype.itemsize for o in outs
    )
    return pl.pallas_call(
        kernel,
        out_shape=tuple(outs),
        in_specs=[HBM if n in stored else VMEM for n in range(len(args))],
        out_specs=tuple([HBM if n in kept else VMEM for n in range(len(outs))]),
        scratch_shapes=scratch,
        compiler_params=pltpu.CompilerParams(vmem_limit_bytes=grant * 1024 * 1024),
        cost_estimate=pl.CostEstimate(flops=flops, bytes_accessed=size, transcendentals=0),
    )(*args)


def fetch(pairs, sems, first=0):
    copies = [
        pltpu.make_async_copy(source, target, sems.at[first + n])
        for n, (source, target) in enumerate(pairs)
    ]
    for copy in copies:
        copy.start()
    return copies


def dot(a, b, dims=((1,), (0,))):
    return lax.dot_general(a, b, (dims, ((), ())), preferred_element_type=F32)


def iota(dims, axis):
    return lax.broadcasted_iota(jnp.int32, dims, axis)


def pack_kernel(rep, flight, live_ref, tok_ref, grad_ref, ids_ref, rw_ref, *refs):
    stored, pays, placed_ref, all_ref = refs[:3], refs[3 : 3 + flight], refs[-8], refs[-7]
    live, ids_held, rw_held, data, rows, sems = refs[-6:]
    r = lax.axis_index("rep")
    mine = lax.axis_index("ep") // SPLIT
    count, model = tok_ref.shape
    width = model // rep
    spacing = EXPERTS // flight
    small = fetch([(live_ref, live), (ids_ref, ids_held), (rw_ref, rw_held)], sems)
    pairs = []
    for part, ref in enumerate((tok_ref, grad_ref)):
        for p in range(PARTS):
            some = pl.ds(p * (count // PARTS), count // PARTS)
            pairs.append((ref.at[some], data.at[part, some]))
    large = fetch(pairs, sems, len(small))
    units = stored[0].shape[1]
    pairs = [(ref, all_ref.at[:, pl.ds(n * units, units)]) for n, ref in enumerate(stored)]
    weights_copies = fetch(pairs, sems, len(small) + len(large))
    for copy in small:
        copy.wait()
    token = iota((1, count), 1)
    upper = (iota((count, count), 0) <= iota((count, count), 1)).astype(BF16)
    slot = iota((SLOT, count), 0).astype(F32)
    lane = iota((SLOT, LANES), 1)
    ids = ids_held[...]
    weights = rw_held[...].astype(F32)
    firsts = []
    for w in range(flight):
        expert = jnp.bitwise_xor(mine, w)
        match = ids == expert * spacing
        routed = jnp.any(match, axis=0, keepdims=True) & (token < live[r])
        weight = jnp.sum(jnp.where(match, weights, 0.0), axis=0, keepdims=True)
        routed = jnp.broadcast_to(jnp.where(routed, 1.0, 0.0), (SLOT, count))
        rank = dot(routed.astype(BF16), upper) - 1.0
        placed = jnp.where(rank == slot, routed, 0.0)
        column = jnp.sum(placed * weight, axis=1, keepdims=True)
        pays[w][:, 2 * model :] = jnp.where(lane == 0, column, 0.0).astype(BF16)
        placed = placed.astype(BF16)
        firsts.append(placed)
        placed_ref[w] = jnp.concatenate([placed] * CHIPS, axis=0)
    for part in range(2):
        for p in range(PARTS):
            large[part * PARTS + p].wait()
        for w in range(flight):
            chosen = dot(firsts[w], data[part]).astype(BF16)
            for b in range(rep):
                rows[b] = chosen[:, b * width : (b + 1) * width]
            for k in range(rep):
                n = 2 * k + part
                pays[w][:, n * width : (n + 1) * width] = rows[jnp.bitwise_xor(r, k)]
    for copy in weights_copies:
        copy.wait()


def half_kernel(start, all_ref, half_ref):
    half_ref[...] = all_ref[start : start + half_ref.shape[0]]


def hidden_kernel(rep, count, spans, cap_ref, *refs):
    blocks, pieces = refs[: 2 * count], refs[2 * count : 2 * count + len(spans)]
    outs, cap, sem = refs[2 * count + len(spans) : -2], refs[-2], refs[-1]
    own_ref, other_ref, grads_ref, here_ref, away_refs = *outs[:4], outs[4:]
    cap_copy = pltpu.make_async_copy(cap_ref, cap, sem)
    cap_copy.start()
    width = here_ref.shape[2]
    units = pieces[0].shape[1] // 3
    own_rows = count * SLOT
    r = lax.axis_index("rep")
    e = lax.axis_index("ep")
    mine = e // SPLIT
    inputs = [[], []]
    for k in range(rep):
        for part in range(2):
            n = 2 * k + part
            chosen = [b[:, n * width : (n + 1) * width] for b in blocks]
            chosen = jnp.concatenate(chosen, axis=0)
            inputs[part].append(chosen)
            if k == 0:
                here_ref[part] = chosen
            else:
                some = slice(part * own_rows, (part + 1) * own_rows)
                away_refs[k - 1][some, :width] = chosen[:own_rows]
    sum_x, sum_d = 0.0, 0.0
    for (k, start, stop), piece in zip(spans, pieces):
        sum_x = sum_x + dot(inputs[0][k][:, start:stop], piece[:, : 2 * units])
        sum_d = sum_d + dot(inputs[1][k][:, start:stop], piece[:, 2 * units :])

    cap_copy.wait()
    capacity = (BLOCK * cap[mine, r]).astype(F32)
    lane = iota((SLOT, LANES), 1)
    sources, rates, counts = [], [], []
    for n in range(2 * count):
        sources.append(jnp.bitwise_xor(e, CORES * (n % count) + n // count))
        rate = jnp.where(lane == 0, blocks[n][:, 2 * rep * width :].astype(F32), 0.0)
        rate = jnp.sum(rate, axis=1, keepdims=True)
        rates.append(rate)
        counts.append(jnp.sum(jnp.where(rate > 0.0, 1.0, 0.0), axis=0, keepdims=True))
    slot = iota((SLOT, 1), 0).astype(F32)
    rate_rows, kept_rows = [], []
    for n in range(2 * count):
        start = jnp.zeros((1, 1), F32)
        for other in range(2 * count):
            start = start + jnp.where(sources[other] < sources[n], counts[other], 0.0)
        kept = jnp.where((rates[n] > 0.0) & (start + slot < capacity), 1.0, 0.0)
        kept_rows.append(kept)
        rate_rows.append(rates[n] * kept)
    rate = jnp.concatenate(rate_rows, axis=0)
    kept = jnp.concatenate(kept_rows, axis=0)

    pre_gate, pre_up, back_hidden = sum_x[:, :units], sum_x[:, units:], sum_d
    sig = 1.0 / (1.0 + jnp.exp(-pre_gate))
    activated = pre_gate * sig
    hidden = activated * pre_up
    score = jnp.sum(hidden * back_hidden, axis=1, keepdims=True) * kept
    lane = iota((2 * own_rows, LANES), 1)
    scores = jnp.where(lane == e % CORES, score, 0.0).astype(BF16)
    scaled = back_hidden * rate
    gate_grad = (scaled * pre_up * sig * (1.0 + pre_gate * (1.0 - sig))).astype(BF16)
    up_grad = (scaled * activated).astype(BF16)
    weighted = (hidden * rate).astype(BF16)
    grads_ref[...] = jnp.concatenate([gate_grad, up_grad, weighted], axis=1)
    for ref in away_refs:
        ref[:, width:] = grads_ref[...]
    pair = jnp.concatenate([gate_grad, up_grad], axis=1)
    for (k, start, stop), piece in zip(spans, pieces):
        back = dot(pair, piece[:, : 2 * units], ((1,), (1,))).astype(BF16)
        some = slice(k * width + start, k * width + stop)
        own_ref[:, some] = back[:own_rows]
        other_ref[:, some] = back[own_rows:]
    own_ref[:, rep * width :] = scores[:own_rows]
    other_ref[:, rep * width :] = scores[own_rows:]


def sum_kernel(own_ref, got_ref, *outs):
    for j, out in enumerate(outs):
        some = slice(j * SLOT, (j + 1) * SLOT)
        out[...] = (own_ref[some].astype(F32) + got_ref[some].astype(F32)).astype(BF16)


def stack_kernel(*refs):
    for k, ref in enumerate(refs[:-1]):
        refs[-1][k] = ref[:, : refs[-1].shape[2]]


def weight_kernel(rep, here_ref, grads_ref, other_ref, *refs):
    away, outs = refs[: rep - 1], refs[rep - 1 :]
    units = outs[0].shape[1]
    width = here_ref.shape[2]
    half = grads_ref.shape[0] // 2
    sums = []
    for part, columns in enumerate((slice(0, 2 * units), slice(2 * units, 3 * units))):
        some = slice(part * half, (part + 1) * half)
        rows = [here_ref[part]]
        got = [grads_ref[:, columns]]
        for k, ref in enumerate(away):
            rows += [ref[some, :width], other_ref[k, some]]
            got.append(ref[:, width + columns.start : width + columns.stop])
        rows = jnp.concatenate(rows, axis=0)
        got = jnp.concatenate(got, axis=0)
        sums.append(dot(got, rows, ((0,), (0,))))
    outs[0][...] = sums[0][:units].T.astype(BF16)
    outs[1][...] = sums[0][units:].T.astype(BF16)
    outs[2][...] = sums[1].T.astype(BF16)


def token_kernel(rep, flight, ids_ref, placed_ref, *refs):
    backs, rest = refs[: flight * CHIPS], refs[flight * CHIPS :]
    out_ref, weight_ref, blocks, ids, sem = rest
    ids_copy = pltpu.make_async_copy(ids_ref, ids, sem)
    ids_copy.start()
    r = lax.axis_index("rep")
    mine = lax.axis_index("ep") // SPLIT
    spacing = EXPERTS // flight
    width = out_ref.shape[1] // rep
    joined = [
        jnp.concatenate([b[...] for b in backs[w * CHIPS : (w + 1) * CHIPS]], axis=0)
        for w in range(flight)
    ]
    for k in range(rep):
        total = 0.0
        for w in range(flight):
            some = joined[w][:, k * width : (k + 1) * width]
            total = total + dot(placed_ref[w], some, ((0,), (0,)))
        blocks[jnp.bitwise_xor(r, k)] = total.astype(BF16)
    for b in range(rep):
        out_ref[:, b * width : (b + 1) * width] = blocks[b]
    result = jnp.zeros(weight_ref.shape, F32)
    ids_copy.wait()
    for w in range(flight):
        score = dot(joined[w][:, rep * width :], placed_ref[w], ((0,), (0,)))
        score = jnp.sum(score, axis=0, keepdims=True)
        match = ids[...] == jnp.bitwise_xor(mine, w) * spacing
        result = result + jnp.where(match, score, 0.0)
    weight_ref[...] = result


def local(
    tokens, out_grad, expert_ids, route_weight, live_count, cap_blocks, w_gate, w_up, w_down_t
):
    rep = lax.axis_size("rep")
    ep = lax.axis_size("ep")
    far = rep // 2
    flight = ep // SPLIT
    count = ep // CORES
    tok_count, model_dim = tokens.shape
    width, units = w_gate.shape
    rows = count * SLOT
    ids_rows, rw_rows, caps = expert_ids.T, route_weight.T, cap_blocks.T

    def send(array, rep_bits, ep_bits):
        mask = rep_bits * ep + ep_bits
        pairs = [(a, a ^ mask) for a in range(rep * ep)]
        return lax.ppermute(array, ("rep", "ep"), pairs)

    def after(array, *others):
        return lax.optimization_barrier((array,) + others)[0]

    packed = call(
        functools.partial(pack_kernel, rep, flight),
        [shape((SLOT, 2 * model_dim + LANES))] * flight
        + [shape((flight, CHIPS * SLOT, tok_count)), shape((width, 3 * units))],
        [live_count, tokens, out_grad, ids_rows, rw_rows, w_gate, w_up, w_down_t],
        stored=range(8),
        kept=(flight + 1,),
        scratch=[
            pltpu.SMEM(live_count.shape, jnp.int32),
            pltpu.VMEM(ids_rows.shape, jnp.int32),
            pltpu.VMEM(rw_rows.shape, BF16),
            pltpu.VMEM((2, tok_count, model_dim), BF16),
            pltpu.VMEM((rep, SLOT, width), BF16),
            pltpu.SemaphoreType.DMA((2 * PARTS + 6,)),
        ],
        grant=54,
    )
    pays, placed, weights = packed[:flight], packed[flight], packed[flight + 1]

    half = width // 2
    whole = {0: weights}
    halves = {}
    for k in range(1, rep):
        low, high = k & -k, 1 << (k.bit_length() - 1)
        if low == high:
            whole[k] = send(weights, k, 0)
            for h in range(2):
                kernel = functools.partial(half_kernel, h * half)
                (halves[k, h],) = call(kernel, [shape((half, 3 * units))], [whole[k]])
        else:
            halves[k, 0] = send(halves[k ^ low, 0], low, 0)
            halves[k, 1] = send(halves[k ^ high, 1], high, 0)
    spans, pieces = [], []
    for k in range(rep):
        if k in whole:
            spans.append((k, 0, width))
            pieces.append(whole[k])
        else:
            spans += [(k, 0, half), (k, half, width)]
            pieces += [halves[k, 0], halves[k, 1]]

    blocks = [pays[0]] + [send(pays[j // CHIPS], 0, CORES * j) for j in range(1, count)]
    blocks = blocks + [send(block, 0, 1) for block in blocks]
    results = call(
        functools.partial(hidden_kernel, rep, count, tuple(spans)),
        [shape((rows, model_dim + LANES))] * 2
        + [shape((2 * rows, 3 * units)), shape((2, 2 * rows, width))]
        + [shape((2 * rows, width + 3 * units))] * (rep - 1),
        [caps] + blocks + pieces,
        stored=(0,),
        scratch=[pltpu.SMEM(caps.shape, jnp.int32), pltpu.SemaphoreType.DMA(())],
        flops=2 * 2 * rows * model_dim * 5 * units,
    )
    own, other, grads, here, away = *results[:4], results[4:]
    summed = call(sum_kernel, [shape((SLOT, model_dim + LANES))] * count, [own, send(other, 0, 1)])
    backs = [send(summed[j], 0, CORES * j) if j else summed[0] for j in range(count)]
    backs = [backs[j ^ (CHIPS - 1)] for j in range(count)]

    moved = [send(away[k - 1], k, 0) for k in range(1, rep)]
    (own_rows,) = call(stack_kernel, [shape((rep - 1, 2 * rows, width))], moved)
    other_rows = send(own_rows, 0, 1)
    grad_gate, grad_up, grad_down = call(
        functools.partial(weight_kernel, rep),
        [shape((width, units))] * 3,
        [here, grads, other_rows] + moved,
        flops=2 * 2 * rep * rows * width * 3 * units,
    )
    grad_tokens, grad_weight = call(
        functools.partial(token_kernel, rep, flight),
        [shape((tok_count, model_dim)), shape(ids_rows.shape, F32)],
        [ids_rows, placed] + backs,
        stored=(0,),
        scratch=[
            pltpu.VMEM((rep, tok_count, width), BF16),
            pltpu.VMEM(ids_rows.shape, jnp.int32),
            pltpu.SemaphoreType.DMA(()),
        ],
        flops=1000 * 2 * tok_count * CHIPS * SLOT * model_dim,
    )
    return grad_tokens, grad_weight.T, grad_gate, grad_up, grad_down


def solution(mesh):
    return jax.shard_map(
        local,
        mesh=mesh,
        in_specs=(
            P(("rep", "ep"), None),
            P(("rep", "ep"), None),
            P(("rep", "ep"), None),
            P(("rep", "ep"), None),
            P(),
            P(),
            P("rep", "ep"),
            P("rep", "ep"),
            P("rep", "ep"),
        ),
        out_specs=(
            P(("rep", "ep"), None),
            P(("rep", "ep"), None),
            P("rep", "ep"),
            P("rep", "ep"),
            P("rep", "ep"),
        ),
        check_vma=False,
    )
```

time: 88.3 us -> 79.6 us (0.901)
  Pallas kernels: 10.5 us -> 27.6 us
  waiting for transfers between devices: 43.9 us -> 30.6 us
  starting transfers between devices: 31.6 us -> 20.4 us
  local copies, waits for them, and re-layouts: 1.34 us -> 0.02 us
    pallas_call x8, Pallas kernels: 10.5 us -> 27.6 us  [call(): pl.pallas_call(kernel, out_shape=tuple(outs), in_specs=[HBM if n in store...]
    ppermute x23 -> x19, waiting for transfers between devices: 43.9 us -> 30.6 us  [send(): return lax.ppermute(array, ('rep', 'ep'), pairs)]
    ppermute x23 -> x19, starting transfers between devices: 31.6 us -> 20.4 us  [send(): return lax.ppermute(array, ('rep', 'ep'), pairs)]
    unnamed x13 -> x10, local copies, waits for them, and re-layouts: 1.33 us -> 0.02 us
  transfers between devices with their start and end apart: 23 -> 19, of which waited for: 11 -> 7; matrix products, arithmetic and copies ran while one was open for 0% -> 0% of each run, Pallas kernels for 7% -> 2%
where the time goes in v6:
time: 79.6 us; the launch traced here: 79.4 us
  waiting for transfers between devices  30.6 us (38%)
  Pallas kernels  27.6 us (35%)
  starting transfers between devices  20.4 us (26%)
  between operations  0.8 us (1%)
    ppermute x19, waiting for transfers between devices, send(): return lax.ppermute(array, ('rep', 'ep'), pairs)  30.6 us
    pallas_call x8, Pallas kernels, call(): pl.pallas_call(kernel, out_shape=tuple(outs), in_specs=[HBM if n in store...  27.6 us
    ppermute x19, starting transfers between devices, send(): return lax.ppermute(array, ('rep', 'ep'), pairs)  20.4 us
  transfers between devices with their start and end apart: 19, of which 7 were waited for; matrix products, arithmetic and copies ran while one was open for 0% of the time, Pallas kernels for 2%

profile of v6, /device:TPU:0, one launch (start us, length us, event | category | flops | bytes accessed | tf_op | source)
XLA Modules:
  0.0 79.4 jit_solution(17062948795599354192)
XLA Ops:
  0.6 22.8 %shard_map.128 = (bf16[16,7296]{1,0:T(8,128)(2,1)}, bf16[1,64,128]{2,1,0:T(8,128)(2,1)}, bf16[896,384]{1,0:T(8,128)(2,1)}) custom-call(s32[4]{0:T(128)} %live_ref.1, bf16[128,3584]{1,0:T(8,128)(2,1)} %tok_ref.1, bf16[128,3584]{1,0:T(8,128)(2,1)} %grad_ref.1, s32[8,128]{1,0:T(8,128)} %bitcast.4, bf16[8,128]{1,0:T(8,128)(2,1)} %bitcast.7, ...), custom_call_target="tpu_custom_call" | custom-call | bytes 3467280 | tf_op jit(solution)/shard_map/pallas_call | solution.py:32
  23.4 3.0 %collective-permute-start.8 = (bf16[896,384]{1,0:T(8,128)(2,1)}, bf16[896,384]{1,0:T(8,128)(2,1)S(1)}, u32[]{:S(2)}, u32[]{:S(2)}) collective-permute-start(bf16[896,384]{1,0:T(8,128)(2,1)} %get-tuple-element.26.refs_8_), channel_id=1, source_target_pairs={{0,16},{1,17},{2,18},{3,19},{4,20},{5,21},{6,22},{7,23},{8,24},{9,... | collective-permute-start | bytes 2064392 | tf_op jit(solution)/shard_map/ppermute | solution.py:273
  26.5 1.5 %collective-permute-start.7 = (bf16[896,384]{1,0:T(8,128)(2,1)}, bf16[896,384]{1,0:T(8,128)(2,1)S(1)}, u32[]{:S(2)}, u32[]{:S(2)}) collective-permute-start(bf16[896,384]{1,0:T(8,128)(2,1)} %get-tuple-element.26.refs_8_), channel_id=1, source_target_pairs={{0,8},{1,9},{2,10},{3,11},{4,12},{5,13},{6,14},{7,15},{8,0},{9,1},... | collective-permute-start | bytes 2064392 | tf_op jit(solution)/shard_map/ppermute | solution.py:273
  28.0 3.6 %collective-permute-start.2 = (bf16[16,7296]{1,0:T(8,128)(2,1)}, bf16[16,7296]{1,0:T(8,128)(2,1)S(1)}, u32[]{:S(2)}, u32[]{:S(2)}) collective-permute-start(bf16[16,7296]{1,0:T(8,128)(2,1)} %get-tuple-element.25.refs_0_), channel_id=1, source_target_pairs={{0,6},{1,7},{2,4},{3,5},{4,2},{5,3},{6,0},{7,1},{8,14},{9,15},{10,... | collective-permute-start | bytes 700424 | tf_op jit(solution)/shard_map/ppermute | solution.py:273
  31.6 10.5 %collective-permute-done.8.all_ref.refs_10_ = bf16[896,384]{1,0:T(8,128)(2,1)S(1)} collective-permute-done((bf16[896,384]{1,0:T(8,128)(2,1)}, bf16[896,384]{1,0:T(8,128)(2,1)S(1)}, u32[]{:S(2)}, u32[]{:S(2)}) %collective-permute-start.8) | collective-permute-done | bytes 688160 | tf_op jit(solution)/shard_map/ppermute | solution.py:273
  42.1 1.8 %collective-permute-start = (bf16[16,7296]{1,0:T(8,128)(2,1)}, bf16[16,7296]{1,0:T(8,128)(2,1)S(1)}, u32[]{:S(2)}, u32[]{:S(2)}) collective-permute-start(bf16[16,7296]{1,0:T(8,128)(2,1)} %get-tuple-element.25.refs_0_), channel_id=1, source_target_pairs={{0,2},{1,3},{2,0},{3,1},{4,6},{5,7},{6,4},{7,5},{8,10},{9,11},{10,... | collective-permute-start | bytes 700424 | tf_op jit(solution)/shard_map/ppermute | solution.py:273
  43.9 0.0 copy-start
  44.0 1.6 %collective-permute-start.9 = (bf16[448,384]{1,0:T(8,128)(2,1)S(1)}, bf16[448,384]{1,0:T(8,128)(2,1)S(1)}, u32[]{:S(2)}, u32[]{:S(2)}) collective-permute-start(bf16[448,384]{1,0:T(8,128)(2,1)S(1)} %shard_map.129), channel_id=1, source_target_pairs={{0,8},{1,9},{2,10},{3,11},{4,12},{5,13},{6,14},{7,15},{8,0},{9,1},... | collective-permute-start | bytes 1032200 | tf_op jit(solution)/shard_map/ppermute | solution.py:273
  45.6 0.0 copy-start.3
  45.6 1.6 %collective-permute-start.10 = (bf16[448,384]{1,0:T(8,128)(2,1)S(1)}, bf16[448,384]{1,0:T(8,128)(2,1)S(1)}, u32[]{:S(2)}, u32[]{:S(2)}) collective-permute-start(bf16[448,384]{1,0:T(8,128)(2,1)S(1)} %shard_map.130), channel_id=1, source_target_pairs={{0,16},{1,17},{2,18},{3,19},{4,20},{5,21},{6,22},{7,23},{8,24},{9,... | collective-permute-start | bytes 1032200 | tf_op jit(solution)/shard_map/ppermute | solution.py:273
  47.2 0.0 collective-permute-done.2.refs_3_
  47.2 0.0 collective-permute-start.6
  47.2 5.2 %collective-permute-done.1.refs_2_ = bf16[16,7296]{1,0:T(8,128)(2,1)S(1)} collective-permute-done((bf16[16,7296]{1,0:T(8,128)(2,1)}, bf16[16,7296]{1,0:T(8,128)(2,1)S(1)}, u32[]{:S(2)}, u32[]{:S(2)}) %collective-permute-start.1) | collective-permute-done | bytes 233504 | tf_op jit(solution)/shard_map/ppermute | solution.py:273
  52.4 0.0 collective-permute-start.5
  52.4 1.8 %collective-permute-done.refs_1_ = bf16[16,7296]{1,0:T(8,128)(2,1)S(1)} collective-permute-done((bf16[16,7296]{1,0:T(8,128)(2,1)}, bf16[16,7296]{1,0:T(8,128)(2,1)S(1)}, u32[]{:S(2)}, u32[]{:S(2)}) %collective-permute-start) | collective-permute-done | bytes 233504 | tf_op jit(solution)/shard_map/ppermute | solution.py:273
  54.2 1.5 %collective-permute-done.4.refs_5_ = bf16[16,7296]{1,0:T(8,128)(2,1)S(1)} collective-permute-done((bf16[16,7296]{1,0:T(8,128)(2,1)S(1)}, bf16[16,7296]{1,0:T(8,128)(2,1)S(1)}, u32[]{:S(2)}, u32[]{:S(2)}) %collective-permute-start.4) | collective-permute-done | bytes 233504 | tf_op jit(solution)/shard_map/ppermute | solution.py:273
  55.7 0.0 collective-permute-done.9.refs_11_
  55.7 1.7 %shard_map.131 = (bf16[64,3712]{1,0:T(8,128)(2,1)S(1)}, bf16[64,3712]{1,0:T(8,128)(2,1)S(1)}, bf16[128,384]{1,0:T(8,128)(2,1)S(1)}, bf16[2,128,896]{2,1,0:T(8,12...) custom-call(s32[1,4]{1,0:T(1,128)S(1)} %bitcast.6, ...), custom_call_target="tpu_custom_call" | custom-call | flops 587202560 | bytes 7110672 | tf_op jit(solution)/shard_map/pallas_call | solution.py:32
  57.5 0.2 collective-permute-start.11
  57.7 1.4 %collective-permute-start.15 = (bf16[128,1280]{1,0:T(8,128)(2,1)S(1)}, bf16[128,1280]{1,0:T(8,128)(2,1)S(1)}, u32[]{:S(2)}, u32[]{:S(2)}) collective-permute-start(bf16[128,1280]{1,0:T(8,128)(2,1)S(1)} %get-tuple-element.37), channel_id=1, source_target_pairs={{0,8},{1,9},{2,10},{3,11},{4,12},{5,13},{6,14},{7,15},{8,0},{9,1},... | collective-permute-start | bytes 983048 | tf_op jit(solution)/shard_map/ppermute | solution.py:273
  59.1 1.5 %collective-permute-start.16 = (bf16[128,1280]{1,0:T(8,128)(2,1)S(1)}, bf16[128,1280]{1,0:T(8,128)(2,1)S(1)}, u32[]{:S(2)}, u32[]{:S(2)}) collective-permute-start(bf16[128,1280]{1,0:T(8,128)(2,1)S(1)} %get-tuple-element.38), channel_id=1, source_target_pairs={{0,16},{1,17},{2,18},{3,19},{4,20},{5,21},{6,22},{7,23},{8,24},{9,... | collective-permute-start | bytes 983048 | tf_op jit(solution)/shard_map/ppermute | solution.py:273
  60.6 0.6 collective-permute-start.17
  61.2 0.1 shard_map.132
  61.3 3.6 %collective-permute-start.12 = (bf16[16,3712]{1,0:T(8,128)(2,1)S(1)}, bf16[16,3712]{1,0:T(8,128)(2,1)S(1)}, u32[]{:S(2)}, u32[]{:S(2)}) collective-permute-start(bf16[16,3712]{1,0:T(8,128)(2,1)S(1)} %get-tuple-element.29), channel_id=1, source_target_pairs={{0,6},{1,7},{2,4},{3,5},{4,2},{5,3},{6,0},{7,1},{8,14},{9,15},{10,... | collective-permute-start | bytes 356360 | tf_op jit(solution)/shard_map/ppermute | solution.py:273
  64.9 3.3 %collective-permute-done.15.refs_0_ = bf16[128,1280]{1,0:T(8,128)(2,1)S(1)} collective-permute-done((bf16[128,1280]{1,0:T(8,128)(2,1)S(1)}, bf16[128,1280]{1,0:T(8,128)(2,1)S(1)}, u32[]{:S(2)}, u32[]{:S(2)}) %collective-permute-start.15) | collective-permute-done | bytes 327712 | tf_op jit(solution)/shard_map/ppermute | solution.py:273
  68.2 7.6 %collective-permute-done.16.refs_1_ = bf16[128,1280]{1,0:T(8,128)(2,1)S(1)} collective-permute-done((bf16[128,1280]{1,0:T(8,128)(2,1)S(1)}, bf16[128,1280]{1,0:T(8,128)(2,1)S(1)}, u32[]{:S(2)}, u32[]{:S(2)}) %collective-permute-start.16) | collective-permute-done | bytes 327712 | tf_op jit(solution)/shard_map/ppermute | solution.py:273
  75.8 0.0 collective-permute-done.17.refs_2_
  75.8 0.1 shard_map.134
  75.9 0.1 collective-permute-start.18
  76.0 1.4 %shard_map.133 = (bf16[128,3584]{1,0:T(8,128)(2,1)}, f32[8,128]{1,0:T(8,128)}) custom-call(s32[8,128]{1,0:T(8,128)S(1)} %bitcast.5, bf16[1,64,128]{2,1,0:T(8,128)(2,1)S(1)} %copy-done.4, bf16[16,3712]{1,0:T(8,128)(2,1)S(1)} %collective-permute-done.12.refs_0_, bf16[16,3712]{1,0:T(8,128)(2,1)S(1)} %collective-permute-done.13.refs_1_, ...), custom_call_target="tpu_custom_call" | custom-call | flops 58720256000 | bytes 1417216 | tf_op jit(solution)/shard_map/pallas_call | solution.py:32
  77.5 0.6 collective-permute-done.18.other_ref
  78.1 1.4 %shard_map.135 = (bf16[896,128]{1,0:T(8,128)(2,1)}, bf16[896,128]{1,0:T(8,128)(2,1)}, bf16[896,128]{1,0:T(8,128)(2,1)}) custom-call(bf16[2,128,896]{2,1,0:T(8,128)(2,1)S(1)} %get-tuple-element.35.here_ref, bf16[128,384]{1,0:T(8,128)(2,1)S(1)} %get-tuple-element.36.grads_ref, bf16[3,128,896]{2,1,0:T(8,128)(2,1)S(1)} %collective-permute-done.18.other_ref, ...), custom_call_target="tpu_custom_call" | custom-call | flops 352321536 | bytes 2916352 | tf_op jit(solution)/shard_map/pallas_call | solution.py:32
  (24 shorter events, 0.1 us)
Async XLA Ops:
  23.4 18.7 %collective-permute-start.8 = (bf16[896,384]{1,0:T(8,128)(2,1)}, bf16[896,384]{1,0:T(8,128)(2,1)S(1)}, u32[]{:S(2)}, u32[]{:S(2)}) collective-permute-start(bf16[896,384]{1,0:T(8,128)(2,1)} %get-tuple-element.26.refs_8_), channel_id=1, source_target_pairs={{0,16},{1,17},{2,18},{3,19},{4,20},{5,21},{6,22},{7,23},{8,24},{9,... | collective-permute-start | bytes 2064392 | tf_op jit(solution)/shard_map/ppermute | solution.py:273
  26.5 17.5 %collective-permute-start.7 = (bf16[896,384]{1,0:T(8,128)(2,1)}, bf16[896,384]{1,0:T(8,128)(2,1)S(1)}, u32[]{:S(2)}, u32[]{:S(2)}) collective-permute-start(bf16[896,384]{1,0:T(8,128)(2,1)} %get-tuple-element.26.refs_8_), channel_id=1, source_target_pairs={{0,8},{1,9},{2,10},{3,11},{4,12},{5,13},{6,14},{7,15},{8,0},{9,1},... | collective-permute-start | bytes 2064392 | tf_op jit(solution)/shard_map/ppermute | solution.py:273
  28.0 17.6 %collective-permute-start.3 = (bf16[16,7296]{1,0:T(8,128)(2,1)}, bf16[16,7296]{1,0:T(8,128)(2,1)S(1)}, u32[]{:S(2)}, u32[]{:S(2)}) collective-permute-start(bf16[16,7296]{1,0:T(8,128)(2,1)} %get-tuple-element.25.refs_0_), channel_id=1, source_target_pairs={{0,1},{1,0},{2,3},{3,2},{4,5},{5,4},{6,7},{7,6},{8,9},{9,8},{10,11... | collective-permute-start | bytes 700424 | tf_op jit(solution)/shard_map/ppermute | solution.py:273
  28.0 19.2 %collective-permute-start.2 = (bf16[16,7296]{1,0:T(8,128)(2,1)}, bf16[16,7296]{1,0:T(8,128)(2,1)S(1)}, u32[]{:S(2)}, u32[]{:S(2)}) collective-permute-start(bf16[16,7296]{1,0:T(8,128)(2,1)} %get-tuple-element.25.refs_0_), channel_id=1, source_target_pairs={{0,6},{1,7},{2,4},{3,5},{4,2},{5,3},{6,0},{7,1},{8,14},{9,15},{10,... | collective-permute-start | bytes 700424 | tf_op jit(solution)/shard_map/ppermute | solution.py:273
  31.6 20.8 %collective-permute-start.1 = (bf16[16,7296]{1,0:T(8,128)(2,1)}, bf16[16,7296]{1,0:T(8,128)(2,1)S(1)}, u32[]{:S(2)}, u32[]{:S(2)}) collective-permute-start(bf16[16,7296]{1,0:T(8,128)(2,1)} %get-tuple-element.25.refs_0_), channel_id=1, source_target_pairs={{0,4},{1,5},{2,6},{3,7},{4,0},{5,1},{6,2},{7,3},{8,12},{9,13},{10,... | collective-permute-start | bytes 700424 | tf_op jit(solution)/shard_map/ppermute | solution.py:273
  42.1 12.1 %collective-permute-start = (bf16[16,7296]{1,0:T(8,128)(2,1)}, bf16[16,7296]{1,0:T(8,128)(2,1)S(1)}, u32[]{:S(2)}, u32[]{:S(2)}) collective-permute-start(bf16[16,7296]{1,0:T(8,128)(2,1)} %get-tuple-element.25.refs_0_), channel_id=1, source_target_pairs={{0,2},{1,3},{2,0},{3,1},{4,6},{5,7},{6,4},{7,5},{8,10},{9,11},{10,... | collective-permute-start | bytes 700424 | tf_op jit(solution)/shard_map/ppermute | solution.py:273
  43.9 11.8 %copy-start = (bf16[896,384]{1,0:T(8,128)(2,1)S(1)}, bf16[896,384]{1,0:T(8,128)(2,1)}, u32[]{:S(2)}) copy-start(bf16[896,384]{1,0:T(8,128)(2,1)} %get-tuple-element.26.refs_8_) | copy-start | bytes 2064388
  44.0 11.8 %copy-start.1 = (bf16[16,7296]{1,0:T(8,128)(2,1)S(1)}, bf16[16,7296]{1,0:T(8,128)(2,1)}, u32[]{:S(2)}) copy-start(bf16[16,7296]{1,0:T(8,128)(2,1)} %get-tuple-element.25.refs_0_) | copy-start | bytes 700420
  44.0 11.7 %collective-permute-start.9 = (bf16[448,384]{1,0:T(8,128)(2,1)S(1)}, bf16[448,384]{1,0:T(8,128)(2,1)S(1)}, u32[]{:S(2)}, u32[]{:S(2)}) collective-permute-start(bf16[448,384]{1,0:T(8,128)(2,1)S(1)} %shard_map.129), channel_id=1, source_target_pairs={{0,8},{1,9},{2,10},{3,11},{4,12},{5,13},{6,14},{7,15},{8,0},{9,1},... | collective-permute-start | bytes 1032200 | tf_op jit(solution)/shard_map/ppermute | solution.py:273
  45.6 10.2 %copy-start.3 = (s32[4,1]{0,1:T(1,128)S(1)}, s32[4,1]{0,1:T(1,128)}, u32[]{:S(2)}) copy-start(s32[4,1]{0,1:T(1,128)} %param.14) | copy-start | bytes 52
  45.6 10.1 %collective-permute-start.10 = (bf16[448,384]{1,0:T(8,128)(2,1)S(1)}, bf16[448,384]{1,0:T(8,128)(2,1)S(1)}, u32[]{:S(2)}, u32[]{:S(2)}) collective-permute-start(bf16[448,384]{1,0:T(8,128)(2,1)S(1)} %shard_map.130), channel_id=1, source_target_pairs={{0,16},{1,17},{2,18},{3,19},{4,20},{5,21},{6,22},{7,23},{8,24},{9,... | collective-permute-start | bytes 1032200 | tf_op jit(solution)/shard_map/ppermute | solution.py:273
  47.2 7.0 %collective-permute-start.6 = (bf16[16,7296]{1,0:T(8,128)(2,1)S(1)}, bf16[16,7296]{1,0:T(8,128)(2,1)S(1)}, u32[]{:S(2)}, u32[]{:S(2)}) collective-permute-start(bf16[16,7296]{1,0:T(8,128)(2,1)S(1)} %collective-permute-done.2.refs_3_), channel_id=1, source_target_pairs={{0,1},{1,0},{2,3},{3,2},{4,5},{5,4},{6,7},{7,6},{8,9},{9,8},{10,11... | collective-permute-start | bytes 700424 | tf_op jit(solution)/shard_map/ppermute | solution.py:273
  52.4 1.8 %collective-permute-start.5 = (bf16[16,7296]{1,0:T(8,128)(2,1)S(1)}, bf16[16,7296]{1,0:T(8,128)(2,1)S(1)}, u32[]{:S(2)}, u32[]{:S(2)}) collective-permute-start(bf16[16,7296]{1,0:T(8,128)(2,1)S(1)} %collective-permute-done.1.refs_2_), channel_id=1, source_target_pairs={{0,1},{1,0},{2,3},{3,2},{4,5},{5,4},{6,7},{7,6},{8,9},{9,8},{10,11... | collective-permute-start | bytes 700424 | tf_op jit(solution)/shard_map/ppermute | solution.py:273
  54.2 1.5 %collective-permute-start.4 = (bf16[16,7296]{1,0:T(8,128)(2,1)S(1)}, bf16[16,7296]{1,0:T(8,128)(2,1)S(1)}, u32[]{:S(2)}, u32[]{:S(2)}) collective-permute-start(bf16[16,7296]{1,0:T(8,128)(2,1)S(1)} %collective-permute-done.refs_1_), channel_id=1, source_target_pairs={{0,1},{1,0},{2,3},{3,2},{4,5},{5,4},{6,7},{7,6},{8,9},{9,8},{10,11... | collective-permute-start | bytes 700424 | tf_op jit(solution)/shard_map/ppermute | solution.py:273
  57.5 3.7 %collective-permute-start.11 = (bf16[64,3712]{1,0:T(8,128)(2,1)S(1)}, bf16[64,3712]{1,0:T(8,128)(2,1)S(1)}, u32[]{:S(2)}, u32[]{:S(2)}) collective-permute-start(bf16[64,3712]{1,0:T(8,128)(2,1)S(1)} %get-tuple-element.28), channel_id=1, source_target_pairs={{0,1},{1,0},{2,3},{3,2},{4,5},{5,4},{6,7},{7,6},{8,9},{9,8},{10,11... | collective-permute-start | bytes 1425416 | tf_op jit(solution)/shard_map/ppermute | solution.py:273
  57.7 10.5 %collective-permute-start.15 = (bf16[128,1280]{1,0:T(8,128)(2,1)S(1)}, bf16[128,1280]{1,0:T(8,128)(2,1)S(1)}, u32[]{:S(2)}, u32[]{:S(2)}) collective-permute-start(bf16[128,1280]{1,0:T(8,128)(2,1)S(1)} %get-tuple-element.37), channel_id=1, source_target_pairs={{0,8},{1,9},{2,10},{3,11},{4,12},{5,13},{6,14},{7,15},{8,0},{9,1},... | collective-permute-start | bytes 983048 | tf_op jit(solution)/shard_map/ppermute | solution.py:273
  59.1 16.7 %collective-permute-start.16 = (bf16[128,1280]{1,0:T(8,128)(2,1)S(1)}, bf16[128,1280]{1,0:T(8,128)(2,1)S(1)}, u32[]{:S(2)}, u32[]{:S(2)}) collective-permute-start(bf16[128,1280]{1,0:T(8,128)(2,1)S(1)} %get-tuple-element.38), channel_id=1, source_target_pairs={{0,16},{1,17},{2,18},{3,19},{4,20},{5,21},{6,22},{7,23},{8,24},{9,... | collective-permute-start | bytes 983048 | tf_op jit(solution)/shard_map/ppermute | solution.py:273
  60.6 15.2 %collective-permute-start.17 = (bf16[128,1280]{1,0:T(8,128)(2,1)S(1)}, bf16[128,1280]{1,0:T(8,128)(2,1)S(1)}, u32[]{:S(2)}, u32[]{:S(2)}) collective-permute-start(bf16[128,1280]{1,0:T(8,128)(2,1)S(1)} %get-tuple-element.39), channel_id=1, source_target_pairs={{0,24},{1,25},{2,26},{3,27},{4,28},{5,29},{6,30},{7,31},{8,16},{9,... | collective-permute-start | bytes 983048 | tf_op jit(solution)/shard_map/ppermute | solution.py:273
  61.3 14.6 %collective-permute-start.12 = (bf16[16,3712]{1,0:T(8,128)(2,1)S(1)}, bf16[16,3712]{1,0:T(8,128)(2,1)S(1)}, u32[]{:S(2)}, u32[]{:S(2)}) collective-permute-start(bf16[16,3712]{1,0:T(8,128)(2,1)S(1)} %get-tuple-element.29), channel_id=1, source_target_pairs={{0,6},{1,7},{2,4},{3,5},{4,2},{5,3},{6,0},{7,1},{8,14},{9,15},{10,... | collective-permute-start | bytes 356360 | tf_op jit(solution)/shard_map/ppermute | solution.py:273
  64.9 11.1 %collective-permute-start.13 = (bf16[16,3712]{1,0:T(8,128)(2,1)S(1)}, bf16[16,3712]{1,0:T(8,128)(2,1)S(1)}, u32[]{:S(2)}, u32[]{:S(2)}) collective-permute-start(bf16[16,3712]{1,0:T(8,128)(2,1)S(1)} %get-tuple-element.30), channel_id=1, source_target_pairs={{0,4},{1,5},{2,6},{3,7},{4,0},{5,1},{6,2},{7,3},{8,12},{9,13},{10,... | collective-permute-start | bytes 356360 | tf_op jit(solution)/shard_map/ppermute | solution.py:273
  68.2 7.8 %copy-start.2 = (s32[128,8]{0,1:T(8,128)S(1)}, s32[128,8]{0,1:T(8,128)}, u32[]{:S(2)}) copy-start(s32[128,8]{0,1:T(8,128)} %param.11) | copy-start | bytes 12292
  68.2 7.8 %copy-start.4 = (bf16[1,64,128]{2,1,0:T(8,128)(2,1)S(1)}, bf16[1,64,128]{2,1,0:T(8,128)(2,1)}, u32[]{:S(2)}) copy-start(bf16[1,64,128]{2,1,0:T(8,128)(2,1)} %get-tuple-element.24.placed_ref) | copy-start | bytes 49156
  68.2 7.7 %collective-permute-start.14 = (bf16[16,3712]{1,0:T(8,128)(2,1)S(1)}, bf16[16,3712]{1,0:T(8,128)(2,1)S(1)}, u32[]{:S(2)}, u32[]{:S(2)}) collective-permute-start(bf16[16,3712]{1,0:T(8,128)(2,1)S(1)} %get-tuple-element.31), channel_id=1, source_target_pairs={{0,2},{1,3},{2,0},{3,1},{4,6},{5,7},{6,4},{7,5},{8,10},{9,11},{10,... | collective-permute-start | bytes 356360 | tf_op jit(solution)/shard_map/ppermute | solution.py:273
  75.9 2.2 %collective-permute-start.18 = (bf16[3,128,896]{2,1,0:T(8,128)(2,1)S(1)}, bf16[3,128,896]{2,1,0:T(8,128)(2,1)S(1)}, u32[]{:S(2)}, u32[]{:S(2)}) collective-permute-start(bf16[3,128,896]{2,1,0:T(8,128)(2,1)S(1)} %shard_map.134), channel_id=1, source_target_pairs={{0,1},{1,0},{2,3},{3,2},{4,5},{5,4},{6,7},{7,6},{8,9},{9,8},{10,11... | collective-permute-start | bytes 2064392 | tf_op jit(solution)/shard_map/ppermute | solution.py:273

commit v7 on v6

--- a/solution.py
+++ b/solution.py
@@ -58,9 +58,13 @@
     return lax.broadcasted_iota(jnp.int32, dims, axis)
 
 
+def turned(n):
+    return n ^ (CHIPS - 1)
+
+
 def pack_kernel(rep, flight, live_ref, tok_ref, grad_ref, ids_ref, rw_ref, *refs):
-    stored, pays, placed_ref, all_ref = refs[:3], refs[3 : 3 + flight], refs[-8], refs[-7]
-    live, ids_held, rw_held, data, rows, sems = refs[-6:]
+    stored, pays, placed_ref, all_ref = refs[:3], refs[3 : 3 + flight], refs[-9], refs[-8]
+    live, ids_held, rw_held, data, rows, joined, sems = refs[-7:]
     r = lax.axis_index("rep")
     mine = lax.axis_index("ep") // SPLIT
     count, model = tok_ref.shape
@@ -74,8 +78,8 @@
             pairs.append((ref.at[some], data.at[part, some]))
     large = fetch(pairs, sems, len(small))
     units = stored[0].shape[1]
-    pairs = [(ref, all_ref.at[:, pl.ds(n * units, units)]) for n, ref in enumerate(stored)]
-    weights_copies = fetch(pairs, sems, len(small) + len(large))
+    pairs = [(ref, joined.at[:, pl.ds(n * units, units)]) for n, ref in enumerate(stored)]
+    weight_copies = fetch(pairs, sems, len(small) + len(large))
     for copy in small:
         copy.wait()
     token = iota((1, count), 1)
@@ -98,6 +102,9 @@
         placed = placed.astype(BF16)
         firsts.append(placed)
         placed_ref[w] = jnp.concatenate([placed] * CHIPS, axis=0)
+    for copy in weight_copies:
+        copy.wait()
+    (out_copy,) = fetch([(joined, all_ref)], sems, len(small) + len(large) + len(weight_copies))
     for part in range(2):
         for p in range(PARTS):
             large[part * PARTS + p].wait()
@@ -108,8 +115,7 @@
             for k in range(rep):
                 n = 2 * k + part
                 pays[w][:, n * width : (n + 1) * width] = rows[jnp.bitwise_xor(r, k)]
-    for copy in weights_copies:
-        copy.wait()
+    out_copy.wait()
 
 
 def half_kernel(start, all_ref, half_ref):
@@ -150,7 +156,7 @@
     lane = iota((SLOT, LANES), 1)
     sources, rates, counts = [], [], []
     for n in range(2 * count):
-        sources.append(jnp.bitwise_xor(e, CORES * (n % count) + n // count))
+        sources.append(jnp.bitwise_xor(e, CORES * turned(n % count) + n // count))
         rate = jnp.where(lane == 0, blocks[n][:, 2 * rep * width :].astype(F32), 0.0)
         rate = jnp.sum(rate, axis=1, keepdims=True)
         rates.append(rate)
@@ -288,7 +294,8 @@
             pltpu.VMEM(rw_rows.shape, BF16),
             pltpu.VMEM((2, tok_count, model_dim), BF16),
             pltpu.VMEM((rep, SLOT, width), BF16),
-            pltpu.SemaphoreType.DMA((2 * PARTS + 6,)),
+            pltpu.VMEM((width, 3 * units), BF16),
+            pltpu.SemaphoreType.DMA((2 * PARTS + 7,)),
         ],
         grant=54,
     )
@@ -316,8 +323,11 @@
             spans += [(k, 0, half), (k, half, width)]
             pieces += [halves[k, 0], halves[k, 1]]
 
-    blocks = [pays[0]] + [send(pays[j // CHIPS], 0, CORES * j) for j in range(1, count)]
-    blocks = blocks + [send(block, 0, 1) for block in blocks]
+    order = [turned(n) for n in range(count)]
+    blocks = [send(pays[j // CHIPS], 0, CORES * j) if j else pays[0] for j in order]
+    nearest = blocks[order.index(1)]
+    ready = [after(b, nearest) if j == 0 else b for j, b in zip(order, blocks)]
+    blocks = blocks + [send(block, 0, 1) for block in ready]
     results = call(
         functools.partial(hidden_kernel, rep, count, tuple(spans)),
         [shape((rows, model_dim + LANES))] * 2
@@ -330,8 +340,7 @@
     )
     own, other, grads, here, away = *results[:4], results[4:]
     summed = call(sum_kernel, [shape((SLOT, model_dim + LANES))] * count, [own, send(other, 0, 1)])
-    backs = [send(summed[j], 0, CORES * j) if j else summed[0] for j in range(count)]
-    backs = [backs[j ^ (CHIPS - 1)] for j in range(count)]
+    backs = [send(part, 0, CORES * j) if j else part for j, part in zip(order, summed)]
 
     moved = [send(away[k - 1], k, 0) for k in range(1, rep)]
     (own_rows,) = call(stack_kernel, [shape((rep - 1, 2 * rows, width))], moved)

time: 79.6 us -> 57.1 us (0.72)
  Pallas kernels: 27.6 us -> 8.27 us
  waiting for transfers between devices: 30.6 us -> 25.6 us
  starting transfers between devices: 20.4 us -> 22.3 us
    pallas_call x8, Pallas kernels: 27.6 us -> 8.27 us  [call(): pl.pallas_call(kernel, out_shape=tuple(outs), in_specs=[HBM if n in store...]
    ppermute x19, waiting for transfers between devices: 30.6 us -> 25.6 us  [send(): return lax.ppermute(array, ('rep', 'ep'), pairs)]
    ppermute x19, starting transfers between devices: 20.4 us -> 22.3 us  [send(): return lax.ppermute(array, ('rep', 'ep'), pairs)]
  transfers between devices with their start and end apart: 19 -> 19, of which waited for: 7 -> 11; matrix products, arithmetic and copies ran while one was open for 0% -> 0% of each run, Pallas kernels for 2% -> 3%
where the time goes in v7:
time: 57.1 us; the launch traced here: 57 us
  waiting for transfers between devices  25.6 us (45%)
  starting transfers between devices  22.3 us (39%)
  Pallas kernels  8.27 us (14%)
  between operations  0.77 us (1%)
    ppermute x19, waiting for transfers between devices, send(): return lax.ppermute(array, ('rep', 'ep'), pairs)  25.6 us
    ppermute x19, starting transfers between devices, send(): return lax.ppermute(array, ('rep', 'ep'), pairs)  22.3 us
    pallas_call x8, Pallas kernels, call(): pl.pallas_call(kernel, out_shape=tuple(outs), in_specs=[HBM if n in store...  8.27 us
  transfers between devices with their start and end apart: 19, of which 11 were waited for; matrix products, arithmetic and copies ran while one was open for 0% of the time, Pallas kernels for 3%

profile of v7, /device:TPU:0, one launch (start us, length us, event | category | flops | bytes accessed | tf_op | source)
XLA Modules:
  0.0 57.0 jit_solution(3622956644938896370)
XLA Ops:
  0.6 3.5 %shard_map.128 = (bf16[16,7296]{1,0:T(8,128)(2,1)}, bf16[1,64,128]{2,1,0:T(8,128)(2,1)}, bf16[896,384]{1,0:T(8,128)(2,1)}) custom-call(s32[4]{0:T(128)} %live_ref.1, bf16[128,3584]{1,0:T(8,128)(2,1)} %tok_ref.1, bf16[128,3584]{1,0:T(8,128)(2,1)} %grad_ref.1, s32[8,128]{1,0:T(8,128)} %bitcast.4, bf16[8,128]{1,0:T(8,128)(2,1)} %bitcast.7, ...), custom_call_target="tpu_custom_call" | custom-call | bytes 3467280 | tf_op jit(solution)/shard_map/pallas_call | solution.py:32
  4.1 3.0 %collective-permute-start.8 = (bf16[896,384]{1,0:T(8,128)(2,1)}, bf16[896,384]{1,0:T(8,128)(2,1)S(1)}, u32[]{:S(2)}, u32[]{:S(2)}) collective-permute-start(bf16[896,384]{1,0:T(8,128)(2,1)} %get-tuple-element.28.refs_8_), channel_id=1, source_target_pairs={{0,16},{1,17},{2,18},{3,19},{4,20},{5,21},{6,22},{7,23},{8,24},{9,... | collective-permute-start | bytes 2064392 | tf_op jit(solution)/shard_map/ppermute | solution.py:279
  7.1 1.5 %collective-permute-start.7 = (bf16[896,384]{1,0:T(8,128)(2,1)}, bf16[896,384]{1,0:T(8,128)(2,1)S(1)}, u32[]{:S(2)}, u32[]{:S(2)}) collective-permute-start(bf16[896,384]{1,0:T(8,128)(2,1)} %get-tuple-element.28.refs_8_), channel_id=1, source_target_pairs={{0,8},{1,9},{2,10},{3,11},{4,12},{5,13},{6,14},{7,15},{8,0},{9,1},... | collective-permute-start | bytes 2064392 | tf_op jit(solution)/shard_map/ppermute | solution.py:279
  8.6 1.6 %collective-permute-start.2 = (bf16[16,7296]{1,0:T(8,128)(2,1)}, bf16[16,7296]{1,0:T(8,128)(2,1)S(1)}, u32[]{:S(2)}, u32[]{:S(2)}) collective-permute-start(bf16[16,7296]{1,0:T(8,128)(2,1)} %get-tuple-element.27.refs_3_), channel_id=1, source_target_pairs={{0,2},{1,3},{2,0},{3,1},{4,6},{5,7},{6,4},{7,5},{8,10},{9,11},{10,... | collective-permute-start | bytes 700424 | tf_op jit(solution)/shard_map/ppermute | solution.py:279
  10.2 2.6 %collective-permute-start.1 = (bf16[16,7296]{1,0:T(8,128)(2,1)}, bf16[16,7296]{1,0:T(8,128)(2,1)S(1)}, u32[]{:S(2)}, u32[]{:S(2)}) collective-permute-start(bf16[16,7296]{1,0:T(8,128)(2,1)} %get-tuple-element.27.refs_3_), channel_id=1, source_target_pairs={{0,4},{1,5},{2,6},{3,7},{4,0},{5,1},{6,2},{7,3},{8,12},{9,13},{10,... | collective-permute-start | bytes 700424 | tf_op jit(solution)/shard_map/ppermute | solution.py:279
  12.8 0.2 collective-permute-start
  13.0 6.6 %collective-permute-done.2.refs_2_ = bf16[16,7296]{1,0:T(8,128)(2,1)S(1)} collective-permute-done((bf16[16,7296]{1,0:T(8,128)(2,1)}, bf16[16,7296]{1,0:T(8,128)(2,1)S(1)}, u32[]{:S(2)}, u32[]{:S(2)}) %collective-permute-start.2) | collective-permute-done | bytes 233504 | tf_op jit(solution)/shard_map/ppermute | solution.py:279
  19.7 3.1 %collective-permute-done.8.all_ref.refs_10_ = bf16[896,384]{1,0:T(8,128)(2,1)S(1)} collective-permute-done((bf16[896,384]{1,0:T(8,128)(2,1)}, bf16[896,384]{1,0:T(8,128)(2,1)S(1)}, u32[]{:S(2)}, u32[]{:S(2)}) %collective-permute-start.8) | collective-permute-done | bytes 688160 | tf_op jit(solution)/shard_map/ppermute | solution.py:279
  22.8 1.8 %collective-permute-start.9 = (bf16[448,384]{1,0:T(8,128)(2,1)S(1)}, bf16[448,384]{1,0:T(8,128)(2,1)S(1)}, u32[]{:S(2)}, u32[]{:S(2)}) collective-permute-start(bf16[448,384]{1,0:T(8,128)(2,1)S(1)} %shard_map.129), channel_id=1, source_target_pairs={{0,8},{1,9},{2,10},{3,11},{4,12},{5,13},{6,14},{7,15},{8,0},{9,1},... | collective-permute-start | bytes 1032200 | tf_op jit(solution)/shard_map/ppermute | solution.py:279
  24.7 1.6 %collective-permute-start.10 = (bf16[448,384]{1,0:T(8,128)(2,1)S(1)}, bf16[448,384]{1,0:T(8,128)(2,1)S(1)}, u32[]{:S(2)}, u32[]{:S(2)}) collective-permute-start(bf16[448,384]{1,0:T(8,128)(2,1)S(1)} %shard_map.130), channel_id=1, source_target_pairs={{0,16},{1,17},{2,18},{3,19},{4,20},{5,21},{6,22},{7,23},{8,24},{9,... | collective-permute-start | bytes 1032200 | tf_op jit(solution)/shard_map/ppermute | solution.py:279
  26.3 3.7 %collective-permute-done.1.refs_1_ = bf16[16,7296]{1,0:T(8,128)(2,1)S(1)} collective-permute-done((bf16[16,7296]{1,0:T(8,128)(2,1)}, bf16[16,7296]{1,0:T(8,128)(2,1)S(1)}, u32[]{:S(2)}, u32[]{:S(2)}) %collective-permute-start.1) | collective-permute-done | bytes 233504 | tf_op jit(solution)/shard_map/ppermute | solution.py:279
  30.0 0.5 collective-permute-start.4
  30.5 0.1 collective-permute-start.3
  30.5 0.9 %collective-permute-done.5.refs_6_ = bf16[16,7296]{1,0:T(8,128)(2,1)S(1)} collective-permute-done((bf16[16,7296]{1,0:T(8,128)(2,1)S(1)}, bf16[16,7296]{1,0:T(8,128)(2,1)S(1)}, u32[]{:S(2)}, u32[]{:S(2)}) %collective-permute-start.5) | collective-permute-done | bytes 233504 | tf_op jit(solution)/shard_map/ppermute | solution.py:279
  31.5 0.3 collective-permute-done.4.refs_5_
  31.8 0.3 collective-permute-done.3.refs_4_
  32.2 1.2 %collective-permute-done.10.refs_12_ = bf16[448,384]{1,0:T(8,128)(2,1)S(1)} collective-permute-done((bf16[448,384]{1,0:T(8,128)(2,1)S(1)}, bf16[448,384]{1,0:T(8,128)(2,1)S(1)}, u32[]{:S(2)}, u32[]{:S(2)}) %collective-permute-start.10) | collective-permute-done | bytes 344096 | tf_op jit(solution)/shard_map/ppermute | solution.py:279
  33.4 1.8 %shard_map.131 = (bf16[64,3712]{1,0:T(8,128)(2,1)S(1)}, bf16[64,3712]{1,0:T(8,128)(2,1)S(1)}, bf16[128,384]{1,0:T(8,128)(2,1)S(1)}, bf16[2,128,896]{2,1,0:T(8,12...) custom-call(s32[1,4]{1,0:T(1,128)S(1)} %bitcast.6, ...), custom_call_target="tpu_custom_call" | custom-call | flops 587202560 | bytes 7110672 | tf_op jit(solution)/shard_map/pallas_call | solution.py:32
  35.2 0.1 collective-permute-start.11
  35.2 1.1 %collective-permute-start.15 = (bf16[128,1280]{1,0:T(8,128)(2,1)S(1)}, bf16[128,1280]{1,0:T(8,128)(2,1)S(1)}, u32[]{:S(2)}, u32[]{:S(2)}) collective-permute-start(bf16[128,1280]{1,0:T(8,128)(2,1)S(1)} %get-tuple-element.39), channel_id=1, source_target_pairs={{0,8},{1,9},{2,10},{3,11},{4,12},{5,13},{6,14},{7,15},{8,0},{9,1},... | collective-permute-start | bytes 983048 | tf_op jit(solution)/shard_map/ppermute | solution.py:279
  36.4 1.0 %collective-permute-start.16 = (bf16[128,1280]{1,0:T(8,128)(2,1)S(1)}, bf16[128,1280]{1,0:T(8,128)(2,1)S(1)}, u32[]{:S(2)}, u32[]{:S(2)}) collective-permute-start(bf16[128,1280]{1,0:T(8,128)(2,1)S(1)} %get-tuple-element.40), channel_id=1, source_target_pairs={{0,16},{1,17},{2,18},{3,19},{4,20},{5,21},{6,22},{7,23},{8,24},{9,... | collective-permute-start | bytes 983048 | tf_op jit(solution)/shard_map/ppermute | solution.py:279
  37.4 1.4 %collective-permute-start.17 = (bf16[128,1280]{1,0:T(8,128)(2,1)S(1)}, bf16[128,1280]{1,0:T(8,128)(2,1)S(1)}, u32[]{:S(2)}, u32[]{:S(2)}) collective-permute-start(bf16[128,1280]{1,0:T(8,128)(2,1)S(1)} %get-tuple-element.41), channel_id=1, source_target_pairs={{0,24},{1,25},{2,26},{3,27},{4,28},{5,29},{6,30},{7,31},{8,16},{9,... | collective-permute-start | bytes 983048 | tf_op jit(solution)/shard_map/ppermute | solution.py:279
  38.8 0.1 shard_map.132
  38.9 3.7 %collective-permute-start.12 = (bf16[16,3712]{1,0:T(8,128)(2,1)S(1)}, bf16[16,3712]{1,0:T(8,128)(2,1)S(1)}, u32[]{:S(2)}, u32[]{:S(2)}) collective-permute-start(bf16[16,3712]{1,0:T(8,128)(2,1)S(1)} %get-tuple-element.31), channel_id=1, source_target_pairs={{0,6},{1,7},{2,4},{3,5},{4,2},{5,3},{6,0},{7,1},{8,14},{9,15},{10,... | collective-permute-start | bytes 356360 | tf_op jit(solution)/shard_map/ppermute | solution.py:279
  42.6 3.2 %collective-permute-done.15.refs_0_ = bf16[128,1280]{1,0:T(8,128)(2,1)S(1)} collective-permute-done((bf16[128,1280]{1,0:T(8,128)(2,1)S(1)}, bf16[128,1280]{1,0:T(8,128)(2,1)S(1)}, u32[]{:S(2)}, u32[]{:S(2)}) %collective-permute-start.15) | collective-permute-done | bytes 327712 | tf_op jit(solution)/shard_map/ppermute | solution.py:279
  45.8 2.1 %collective-permute-start.14 = (bf16[16,3712]{1,0:T(8,128)(2,1)S(1)}, bf16[16,3712]{1,0:T(8,128)(2,1)S(1)}, u32[]{:S(2)}, u32[]{:S(2)}) collective-permute-start(bf16[16,3712]{1,0:T(8,128)(2,1)S(1)} %get-tuple-element.33), channel_id=1, source_target_pairs={{0,2},{1,3},{2,0},{3,1},{4,6},{5,7},{6,4},{7,5},{8,10},{9,11},{10,... | collective-permute-start | bytes 356360 | tf_op jit(solution)/shard_map/ppermute | solution.py:279
  48.0 3.8 %collective-permute-done.16.refs_1_ = bf16[128,1280]{1,0:T(8,128)(2,1)S(1)} collective-permute-done((bf16[128,1280]{1,0:T(8,128)(2,1)S(1)}, bf16[128,1280]{1,0:T(8,128)(2,1)S(1)}, u32[]{:S(2)}, u32[]{:S(2)}) %collective-permute-start.16) | collective-permute-done | bytes 327712 | tf_op jit(solution)/shard_map/ppermute | solution.py:279
  51.7 1.6 %collective-permute-done.17.refs_2_ = bf16[128,1280]{1,0:T(8,128)(2,1)S(1)} collective-permute-done((bf16[128,1280]{1,0:T(8,128)(2,1)S(1)}, bf16[128,1280]{1,0:T(8,128)(2,1)S(1)}, u32[]{:S(2)}, u32[]{:S(2)}) %collective-permute-start.17) | collective-permute-done | bytes 327712 | tf_op jit(solution)/shard_map/ppermute | solution.py:279
  53.4 0.1 collective-permute-start.18
  53.5 1.4 %shard_map.133 = (bf16[128,3584]{1,0:T(8,128)(2,1)}, f32[8,128]{1,0:T(8,128)}) custom-call(s32[8,128]{1,0:T(8,128)S(1)} %bitcast.5, bf16[1,64,128]{2,1,0:T(8,128)(2,1)S(1)} %copy-done.4, bf16[16,3712]{1,0:T(8,128)(2,1)S(1)} %collective-permute-done.12.refs_0_, bf16[16,3712]{1,0:T(8,128)(2,1)S(1)} %collective-permute-done.13.refs_1_, ...), custom_call_target="tpu_custom_call" | custom-call | flops 58720256000 | bytes 1417216 | tf_op jit(solution)/shard_map/pallas_call | solution.py:32
  55.0 0.6 %collective-permute-done.18.other_ref = bf16[3,128,896]{2,1,0:T(8,128)(2,1)S(1)} collective-permute-done((bf16[3,128,896]{2,1,0:T(8,128)(2,1)S(1)}, bf16[3,128,896]{2,1,0:T(8,128)(2,1)S(1)}, u32[]{:S(2)}, u32[]{:S(2)}) %collective-permute-start.18) | collective-permute-done | bytes 688160 | tf_op jit(solution)/shard_map/ppermute | solution.py:279
  55.6 1.4 %shard_map.135 = (bf16[896,128]{1,0:T(8,128)(2,1)}, bf16[896,128]{1,0:T(8,128)(2,1)}, bf16[896,128]{1,0:T(8,128)(2,1)}) custom-call(bf16[2,128,896]{2,1,0:T(8,128)(2,1)S(1)} %get-tuple-element.37.here_ref, bf16[128,384]{1,0:T(8,128)(2,1)S(1)} %get-tuple-element.38.grads_ref, bf16[3,128,896]{2,1,0:T(8,128)(2,1)S(1)} %collective-permute-done.18.other_ref, ...), custom_call_target="tpu_custom_call" | custom-call | flops 352321536 | bytes 2916352 | tf_op jit(solution)/shard_map/pallas_call | solution.py:32
  (24 shorter events, 0.2 us)
Async XLA Ops:
  4.1 18.7 %collective-permute-start.8 = (bf16[896,384]{1,0:T(8,128)(2,1)}, bf16[896,384]{1,0:T(8,128)(2,1)S(1)}, u32[]{:S(2)}, u32[]{:S(2)}) collective-permute-start(bf16[896,384]{1,0:T(8,128)(2,1)} %get-tuple-element.28.refs_8_), channel_id=1, source_target_pairs={{0,16},{1,17},{2,18},{3,19},{4,20},{5,21},{6,22},{7,23},{8,24},{9,... | collective-permute-start | bytes 2064392 | tf_op jit(solution)/shard_map/ppermute | solution.py:279
  7.1 17.5 %collective-permute-start.7 = (bf16[896,384]{1,0:T(8,128)(2,1)}, bf16[896,384]{1,0:T(8,128)(2,1)S(1)}, u32[]{:S(2)}, u32[]{:S(2)}) collective-permute-start(bf16[896,384]{1,0:T(8,128)(2,1)} %get-tuple-element.28.refs_8_), channel_id=1, source_target_pairs={{0,8},{1,9},{2,10},{3,11},{4,12},{5,13},{6,14},{7,15},{8,0},{9,1},... | collective-permute-start | bytes 2064392 | tf_op jit(solution)/shard_map/ppermute | solution.py:279
  8.6 11.0 %collective-permute-start.2 = (bf16[16,7296]{1,0:T(8,128)(2,1)}, bf16[16,7296]{1,0:T(8,128)(2,1)S(1)}, u32[]{:S(2)}, u32[]{:S(2)}) collective-permute-start(bf16[16,7296]{1,0:T(8,128)(2,1)} %get-tuple-element.27.refs_3_), channel_id=1, source_target_pairs={{0,2},{1,3},{2,0},{3,1},{4,6},{5,7},{6,4},{7,5},{8,10},{9,11},{10,... | collective-permute-start | bytes 700424 | tf_op jit(solution)/shard_map/ppermute | solution.py:279
  10.2 19.7 %collective-permute-start.1 = (bf16[16,7296]{1,0:T(8,128)(2,1)}, bf16[16,7296]{1,0:T(8,128)(2,1)S(1)}, u32[]{:S(2)}, u32[]{:S(2)}) collective-permute-start(bf16[16,7296]{1,0:T(8,128)(2,1)} %get-tuple-element.27.refs_3_), channel_id=1, source_target_pairs={{0,4},{1,5},{2,6},{3,7},{4,0},{5,1},{6,2},{7,3},{8,12},{9,13},{10,... | collective-permute-start | bytes 700424 | tf_op jit(solution)/shard_map/ppermute | solution.py:279
  12.8 17.2 %collective-permute-start = (bf16[16,7296]{1,0:T(8,128)(2,1)}, bf16[16,7296]{1,0:T(8,128)(2,1)S(1)}, u32[]{:S(2)}, u32[]{:S(2)}) collective-permute-start(bf16[16,7296]{1,0:T(8,128)(2,1)} %get-tuple-element.27.refs_3_), channel_id=1, source_target_pairs={{0,6},{1,7},{2,4},{3,5},{4,2},{5,3},{6,0},{7,1},{8,14},{9,15},{10,... | collective-permute-start | bytes 700424 | tf_op jit(solution)/shard_map/ppermute | solution.py:279
  19.7 10.8 %collective-permute-start.6 = (bf16[16,7296]{1,0:T(8,128)(2,1)}, bf16[16,7296]{1,0:T(8,128)(2,1)S(1)}, u32[]{:S(2)}, u32[]{:S(2)}) collective-permute-start(bf16[16,7296]{1,0:T(8,128)(2,1)} %get-tuple-element.27.refs_3_), channel_id=1, source_target_pairs={{0,1},{1,0},{2,3},{3,2},{4,5},{5,4},{6,7},{7,6},{8,9},{9,8},{10,11... | collective-permute-start | bytes 700424 | tf_op jit(solution)/shard_map/ppermute | solution.py:279
  22.8 10.6 %copy-start = (bf16[896,384]{1,0:T(8,128)(2,1)S(1)}, bf16[896,384]{1,0:T(8,128)(2,1)}, u32[]{:S(2)}) copy-start(bf16[896,384]{1,0:T(8,128)(2,1)} %get-tuple-element.28.refs_8_) | copy-start | bytes 2064388
  22.8 10.6 %copy-start.1 = (bf16[16,7296]{1,0:T(8,128)(2,1)S(1)}, bf16[16,7296]{1,0:T(8,128)(2,1)}, u32[]{:S(2)}) copy-start(bf16[16,7296]{1,0:T(8,128)(2,1)} %get-tuple-element.27.refs_3_) | copy-start | bytes 700420
  22.8 9.3 %collective-permute-start.9 = (bf16[448,384]{1,0:T(8,128)(2,1)S(1)}, bf16[448,384]{1,0:T(8,128)(2,1)S(1)}, u32[]{:S(2)}, u32[]{:S(2)}) collective-permute-start(bf16[448,384]{1,0:T(8,128)(2,1)S(1)} %shard_map.129), channel_id=1, source_target_pairs={{0,8},{1,9},{2,10},{3,11},{4,12},{5,13},{6,14},{7,15},{8,0},{9,1},... | collective-permute-start | bytes 1032200 | tf_op jit(solution)/shard_map/ppermute | solution.py:279
  24.7 8.7 %copy-start.3 = (s32[4,1]{0,1:T(1,128)S(1)}, s32[4,1]{0,1:T(1,128)}, u32[]{:S(2)}) copy-start(s32[4,1]{0,1:T(1,128)} %param.14) | copy-start | bytes 52
  24.7 8.7 %collective-permute-start.10 = (bf16[448,384]{1,0:T(8,128)(2,1)S(1)}, bf16[448,384]{1,0:T(8,128)(2,1)S(1)}, u32[]{:S(2)}, u32[]{:S(2)}) collective-permute-start(bf16[448,384]{1,0:T(8,128)(2,1)S(1)} %shard_map.130), channel_id=1, source_target_pairs={{0,16},{1,17},{2,18},{3,19},{4,20},{5,21},{6,22},{7,23},{8,24},{9,... | collective-permute-start | bytes 1032200 | tf_op jit(solution)/shard_map/ppermute | solution.py:279
  30.0 1.5 %collective-permute-start.5 = (bf16[16,7296]{1,0:T(8,128)(2,1)S(1)}, bf16[16,7296]{1,0:T(8,128)(2,1)S(1)}, u32[]{:S(2)}, u32[]{:S(2)}) collective-permute-start(bf16[16,7296]{1,0:T(8,128)(2,1)S(1)} %collective-permute-done.2.refs_2_), channel_id=1, source_target_pairs={{0,1},{1,0},{2,3},{3,2},{4,5},{5,4},{6,7},{7,6},{8,9},{9,8},{10,11... | collective-permute-start | bytes 700424 | tf_op jit(solution)/shard_map/ppermute | solution.py:279
  30.0 1.8 %collective-permute-start.4 = (bf16[16,7296]{1,0:T(8,128)(2,1)S(1)}, bf16[16,7296]{1,0:T(8,128)(2,1)S(1)}, u32[]{:S(2)}, u32[]{:S(2)}) collective-permute-start(bf16[16,7296]{1,0:T(8,128)(2,1)S(1)} %collective-permute-done.1.refs_1_), channel_id=1, source_target_pairs={{0,1},{1,0},{2,3},{3,2},{4,5},{5,4},{6,7},{7,6},{8,9},{9,8},{10,11... | collective-permute-start | bytes 700424 | tf_op jit(solution)/shard_map/ppermute | solution.py:279
  30.5 1.6 %collective-permute-start.3 = (bf16[16,7296]{1,0:T(8,128)(2,1)S(1)}, bf16[16,7296]{1,0:T(8,128)(2,1)S(1)}, u32[]{:S(2)}, u32[]{:S(2)}) collective-permute-start(bf16[16,7296]{1,0:T(8,128)(2,1)S(1)} %collective-permute-done.refs_0_), channel_id=1, source_target_pairs={{0,1},{1,0},{2,3},{3,2},{4,5},{5,4},{6,7},{7,6},{8,9},{9,8},{10,11... | collective-permute-start | bytes 700424 | tf_op jit(solution)/shard_map/ppermute | solution.py:279
  35.2 3.6 %collective-permute-start.11 = (bf16[64,3712]{1,0:T(8,128)(2,1)S(1)}, bf16[64,3712]{1,0:T(8,128)(2,1)S(1)}, u32[]{:S(2)}, u32[]{:S(2)}) collective-permute-start(bf16[64,3712]{1,0:T(8,128)(2,1)S(1)} %get-tuple-element.30), channel_id=1, source_target_pairs={{0,1},{1,0},{2,3},{3,2},{4,5},{5,4},{6,7},{7,6},{8,9},{9,8},{10,11... | collective-permute-start | bytes 1425416 | tf_op jit(solution)/shard_map/ppermute | solution.py:279
  35.2 10.6 %collective-permute-start.15 = (bf16[128,1280]{1,0:T(8,128)(2,1)S(1)}, bf16[128,1280]{1,0:T(8,128)(2,1)S(1)}, u32[]{:S(2)}, u32[]{:S(2)}) collective-permute-start(bf16[128,1280]{1,0:T(8,128)(2,1)S(1)} %get-tuple-element.39), channel_id=1, source_target_pairs={{0,8},{1,9},{2,10},{3,11},{4,12},{5,13},{6,14},{7,15},{8,0},{9,1},... | collective-permute-start | bytes 983048 | tf_op jit(solution)/shard_map/ppermute | solution.py:279
  36.4 15.3 %collective-permute-start.16 = (bf16[128,1280]{1,0:T(8,128)(2,1)S(1)}, bf16[128,1280]{1,0:T(8,128)(2,1)S(1)}, u32[]{:S(2)}, u32[]{:S(2)}) collective-permute-start(bf16[128,1280]{1,0:T(8,128)(2,1)S(1)} %get-tuple-element.40), channel_id=1, source_target_pairs={{0,16},{1,17},{2,18},{3,19},{4,20},{5,21},{6,22},{7,23},{8,24},{9,... | collective-permute-start | bytes 983048 | tf_op jit(solution)/shard_map/ppermute | solution.py:279
  37.4 16.0 %collective-permute-start.17 = (bf16[128,1280]{1,0:T(8,128)(2,1)S(1)}, bf16[128,1280]{1,0:T(8,128)(2,1)S(1)}, u32[]{:S(2)}, u32[]{:S(2)}) collective-permute-start(bf16[128,1280]{1,0:T(8,128)(2,1)S(1)} %get-tuple-element.41), channel_id=1, source_target_pairs={{0,24},{1,25},{2,26},{3,27},{4,28},{5,29},{6,30},{7,31},{8,16},{9,... | collective-permute-start | bytes 983048 | tf_op jit(solution)/shard_map/ppermute | solution.py:279
  38.9 14.6 %collective-permute-start.12 = (bf16[16,3712]{1,0:T(8,128)(2,1)S(1)}, bf16[16,3712]{1,0:T(8,128)(2,1)S(1)}, u32[]{:S(2)}, u32[]{:S(2)}) collective-permute-start(bf16[16,3712]{1,0:T(8,128)(2,1)S(1)} %get-tuple-element.31), channel_id=1, source_target_pairs={{0,6},{1,7},{2,4},{3,5},{4,2},{5,3},{6,0},{7,1},{8,14},{9,15},{10,... | collective-permute-start | bytes 356360 | tf_op jit(solution)/shard_map/ppermute | solution.py:279
  42.6 10.9 %collective-permute-start.13 = (bf16[16,3712]{1,0:T(8,128)(2,1)S(1)}, bf16[16,3712]{1,0:T(8,128)(2,1)S(1)}, u32[]{:S(2)}, u32[]{:S(2)}) collective-permute-start(bf16[16,3712]{1,0:T(8,128)(2,1)S(1)} %get-tuple-element.32), channel_id=1, source_target_pairs={{0,4},{1,5},{2,6},{3,7},{4,0},{5,1},{6,2},{7,3},{8,12},{9,13},{10,... | collective-permute-start | bytes 356360 | tf_op jit(solution)/shard_map/ppermute | solution.py:279
  45.8 7.7 %copy-start.2 = (s32[128,8]{0,1:T(8,128)S(1)}, s32[128,8]{0,1:T(8,128)}, u32[]{:S(2)}) copy-start(s32[128,8]{0,1:T(8,128)} %param.11) | copy-start | bytes 12292
  45.8 7.7 %copy-start.4 = (bf16[1,64,128]{2,1,0:T(8,128)(2,1)S(1)}, bf16[1,64,128]{2,1,0:T(8,128)(2,1)}, u32[]{:S(2)}) copy-start(bf16[1,64,128]{2,1,0:T(8,128)(2,1)} %get-tuple-element.25.placed_ref) | copy-start | bytes 49156
  45.8 7.7 %collective-permute-start.14 = (bf16[16,3712]{1,0:T(8,128)(2,1)S(1)}, bf16[16,3712]{1,0:T(8,128)(2,1)S(1)}, u32[]{:S(2)}, u32[]{:S(2)}) collective-permute-start(bf16[16,3712]{1,0:T(8,128)(2,1)S(1)} %get-tuple-element.33), channel_id=1, source_target_pairs={{0,2},{1,3},{2,0},{3,1},{4,6},{5,7},{6,4},{7,5},{8,10},{9,11},{10,... | collective-permute-start | bytes 356360 | tf_op jit(solution)/shard_map/ppermute | solution.py:279
  53.4 2.2 %collective-permute-start.18 = (bf16[3,128,896]{2,1,0:T(8,128)(2,1)S(1)}, bf16[3,128,896]{2,1,0:T(8,128)(2,1)S(1)}, u32[]{:S(2)}, u32[]{:S(2)}) collective-permute-start(bf16[3,128,896]{2,1,0:T(8,128)(2,1)S(1)} %shard_map.134), channel_id=1, source_target_pairs={{0,1},{1,0},{2,3},{3,2},{4,5},{5,4},{6,7},{7,6},{8,9},{9,8},{10,11... | collective-permute-start | bytes 2064392 | tf_op jit(solution)/shard_map/ppermute | solution.py:279

commit v8 on v7

--- a/solution.py
+++ b/solution.py
@@ -58,13 +58,23 @@
     return lax.broadcasted_iota(jnp.int32, dims, axis)
 
 
+def join_kernel(gate_ref, up_ref, down_ref, all_ref, joined, sems):
+    units = gate_ref.shape[1]
+    refs = (gate_ref, up_ref, down_ref)
+    pairs = [(ref, joined.at[:, pl.ds(n * units, units)]) for n, ref in enumerate(refs)]
+    for copy in fetch(pairs, sems):
+        copy.wait()
+    (copy,) = fetch([(joined, all_ref)], sems, len(pairs))
+    copy.wait()
+
+
 def turned(n):
     return n ^ (CHIPS - 1)
 
 
 def pack_kernel(rep, flight, live_ref, tok_ref, grad_ref, ids_ref, rw_ref, *refs):
-    stored, pays, placed_ref, all_ref = refs[:3], refs[3 : 3 + flight], refs[-9], refs[-8]
-    live, ids_held, rw_held, data, rows, joined, sems = refs[-7:]
+    pays, placed_ref = refs[:flight], refs[flight]
+    live, ids_held, rw_held, data, rows, sems = refs[flight + 1 :]
     r = lax.axis_index("rep")
     mine = lax.axis_index("ep") // SPLIT
     count, model = tok_ref.shape
@@ -77,9 +87,6 @@
             some = pl.ds(p * (count // PARTS), count // PARTS)
             pairs.append((ref.at[some], data.at[part, some]))
     large = fetch(pairs, sems, len(small))
-    units = stored[0].shape[1]
-    pairs = [(ref, joined.at[:, pl.ds(n * units, units)]) for n, ref in enumerate(stored)]
-    weight_copies = fetch(pairs, sems, len(small) + len(large))
     for copy in small:
         copy.wait()
     token = iota((1, count), 1)
@@ -102,9 +109,6 @@
         placed = placed.astype(BF16)
         firsts.append(placed)
         placed_ref[w] = jnp.concatenate([placed] * CHIPS, axis=0)
-    for copy in weight_copies:
-        copy.wait()
-    (out_copy,) = fetch([(joined, all_ref)], sems, len(small) + len(large) + len(weight_copies))
     for part in range(2):
         for p in range(PARTS):
             large[part * PARTS + p].wait()
@@ -115,7 +119,17 @@
             for k in range(rep):
                 n = 2 * k + part
                 pays[w][:, n * width : (n + 1) * width] = rows[jnp.bitwise_xor(r, k)]
-    out_copy.wait()
+
+
+def parts_kernel(count, *refs):
+    blocks, outs = refs[:count], refs[count:]
+    rows, width = count * SLOT, outs[0].shape[1]
+    for k, out in enumerate(outs):
+        for part in range(2):
+            n = 2 * (k + 1) + part
+            for j in range(count):
+                start = part * rows + j * SLOT
+                out[start : start + SLOT] = blocks[j][:, n * width : (n + 1) * width]
 
 
 def half_kernel(start, all_ref, half_ref):
@@ -125,7 +139,7 @@
 def hidden_kernel(rep, count, spans, cap_ref, *refs):
     blocks, pieces = refs[: 2 * count], refs[2 * count : 2 * count + len(spans)]
     outs, cap, sem = refs[2 * count + len(spans) : -2], refs[-2], refs[-1]
-    own_ref, other_ref, grads_ref, here_ref, away_refs = *outs[:4], outs[4:]
+    own_ref, other_ref, grads_ref, here_ref = outs
     cap_copy = pltpu.make_async_copy(cap_ref, cap, sem)
     cap_copy.start()
     width = here_ref.shape[2]
@@ -143,9 +157,6 @@
             inputs[part].append(chosen)
             if k == 0:
                 here_ref[part] = chosen
-            else:
-                some = slice(part * own_rows, (part + 1) * own_rows)
-                away_refs[k - 1][some, :width] = chosen[:own_rows]
     sum_x, sum_d = 0.0, 0.0
     for (k, start, stop), piece in zip(spans, pieces):
         sum_x = sum_x + dot(inputs[0][k][:, start:stop], piece[:, : 2 * units])
@@ -185,8 +196,6 @@
     up_grad = (scaled * activated).astype(BF16)
     weighted = (hidden * rate).astype(BF16)
     grads_ref[...] = jnp.concatenate([gate_grad, up_grad, weighted], axis=1)
-    for ref in away_refs:
-        ref[:, width:] = grads_ref[...]
     pair = jnp.concatenate([gate_grad, up_grad], axis=1)
     for (k, start, stop), piece in zip(spans, pieces):
         back = dot(pair, piece[:, : 2 * units], ((1,), (1,))).astype(BF16)
@@ -205,24 +214,21 @@
 
 def stack_kernel(*refs):
     for k, ref in enumerate(refs[:-1]):
-        refs[-1][k] = ref[:, : refs[-1].shape[2]]
-
-
-def weight_kernel(rep, here_ref, grads_ref, other_ref, *refs):
-    away, outs = refs[: rep - 1], refs[rep - 1 :]
+        refs[-1][k] = ref[...]
+
+
+def weight_kernel(rep, here_ref, own_ref, other_ref, *refs):
+    grads, outs = refs[:rep], refs[rep:]
     units = outs[0].shape[1]
-    width = here_ref.shape[2]
-    half = grads_ref.shape[0] // 2
+    half = grads[0].shape[0] // 2
     sums = []
     for part, columns in enumerate((slice(0, 2 * units), slice(2 * units, 3 * units))):
         some = slice(part * half, (part + 1) * half)
         rows = [here_ref[part]]
-        got = [grads_ref[:, columns]]
-        for k, ref in enumerate(away):
-            rows += [ref[some, :width], other_ref[k, some]]
-            got.append(ref[:, width + columns.start : width + columns.stop])
+        for k in range(rep - 1):
+            rows += [own_ref[k, some], other_ref[k, some]]
         rows = jnp.concatenate(rows, axis=0)
-        got = jnp.concatenate(got, axis=0)
+        got = jnp.concatenate([ref[:, columns] for ref in grads], axis=0)
         sums.append(dot(got, rows, ((0,), (0,))))
     outs[0][...] = sums[0][:units].T.astype(BF16)
     outs[1][...] = sums[0][units:].T.astype(BF16)
@@ -281,29 +287,36 @@
     def after(array, *others):
         return lax.optimization_barrier((array,) + others)[0]
 
+    (weights,) = call(
+        join_kernel,
+        [shape((width, 3 * units))],
+        [w_gate, w_up, w_down_t],
+        stored=(0, 1, 2),
+        kept=(0,),
+        scratch=[pltpu.VMEM((width, 3 * units), BF16), pltpu.SemaphoreType.DMA((4,))],
+        grant=54,
+    )
     packed = call(
         functools.partial(pack_kernel, rep, flight),
         [shape((SLOT, 2 * model_dim + LANES))] * flight
-        + [shape((flight, CHIPS * SLOT, tok_count)), shape((width, 3 * units))],
-        [live_count, tokens, out_grad, ids_rows, rw_rows, w_gate, w_up, w_down_t],
-        stored=range(8),
-        kept=(flight + 1,),
+        + [shape((flight, CHIPS * SLOT, tok_count))],
+        [live_count, tokens, out_grad, ids_rows, rw_rows],
+        stored=range(5),
         scratch=[
             pltpu.SMEM(live_count.shape, jnp.int32),
             pltpu.VMEM(ids_rows.shape, jnp.int32),
             pltpu.VMEM(rw_rows.shape, BF16),
             pltpu.VMEM((2, tok_count, model_dim), BF16),
             pltpu.VMEM((rep, SLOT, width), BF16),
-            pltpu.VMEM((width, 3 * units), BF16),
-            pltpu.SemaphoreType.DMA((2 * PARTS + 7,)),
+            pltpu.SemaphoreType.DMA((2 * PARTS + 3,)),
         ],
-        grant=54,
-    )
-    pays, placed, weights = packed[:flight], packed[flight], packed[flight + 1]
+        grant=53,
+    )
+    pays, placed = packed[:flight], packed[flight]
 
     half = width // 2
     whole = {0: weights}
-    halves = {}
+    halves, sent = {}, []
     for k in range(1, rep):
         low, high = k & -k, 1 << (k.bit_length() - 1)
         if low == high:
@@ -311,6 +324,7 @@
             for h in range(2):
                 kernel = functools.partial(half_kernel, h * half)
                 (halves[k, h],) = call(kernel, [shape((half, 3 * units))], [whole[k]])
+                sent.append(halves[k, h])
         else:
             halves[k, 0] = send(halves[k ^ low, 0], low, 0)
             halves[k, 1] = send(halves[k ^ high, 1], high, 0)
@@ -325,30 +339,41 @@
 
     order = [turned(n) for n in range(count)]
     blocks = [send(pays[j // CHIPS], 0, CORES * j) if j else pays[0] for j in order]
-    nearest = blocks[order.index(1)]
-    ready = [after(b, nearest) if j == 0 else b for j, b in zip(order, blocks)]
+    parts = call(
+        functools.partial(parts_kernel, count),
+        [shape((2 * rows, width))] * (rep - 1),
+        [after(blocks[0], *sent)] + blocks[1:],
+    )
+    here, nearest = order.index(0), order.index(1)
+    ready = list(blocks)
+    ready[here] = after(blocks[here], blocks[nearest])
     blocks = blocks + [send(block, 0, 1) for block in ready]
     results = call(
         functools.partial(hidden_kernel, rep, count, tuple(spans)),
         [shape((rows, model_dim + LANES))] * 2
-        + [shape((2 * rows, 3 * units)), shape((2, 2 * rows, width))]
-        + [shape((2 * rows, width + 3 * units))] * (rep - 1),
+        + [shape((2 * rows, 3 * units)), shape((2, 2 * rows, width))],
         [caps] + blocks + pieces,
         stored=(0,),
         scratch=[pltpu.SMEM(caps.shape, jnp.int32), pltpu.SemaphoreType.DMA(())],
         flops=2 * 2 * rows * model_dim * 5 * units,
     )
-    own, other, grads, here, away = *results[:4], results[4:]
-    summed = call(sum_kernel, [shape((SLOT, model_dim + LANES))] * count, [own, send(other, 0, 1)])
+    own, other, grads, here = results
+    summed = call(
+        sum_kernel,
+        [shape((SLOT, model_dim + LANES))] * count,
+        [own, send(other, 0, 1)],
+        flops=2 * rows * model_dim,
+    )
     backs = [send(part, 0, CORES * j) if j else part for j, part in zip(order, summed)]
 
-    moved = [send(away[k - 1], k, 0) for k in range(1, rep)]
-    (own_rows,) = call(stack_kernel, [shape((rep - 1, 2 * rows, width))], moved)
+    moved = [send(part, k, 0) for k, part in enumerate(parts, 1)]
+    (own_rows,) = call(stack_kernel, [shape((rep - 1, 2 * rows, width))], [after(moved[0], grads)] + moved[1:])
     other_rows = send(own_rows, 0, 1)
+    group_grads = [grads] + [send(grads, k, 0) for k in range(1, rep)]
     grad_gate, grad_up, grad_down = call(
         functools.partial(weight_kernel, rep),
         [shape((width, units))] * 3,
-        [here, grads, other_rows] + moved,
+        [here, own_rows, other_rows] + group_grads,
         flops=2 * 2 * rep * rows * width * 3 * units,
     )
     grad_tokens, grad_weight = call(

time: 57.1 us -> 57.8 us (1.012)
  waiting for transfers between devices: 25.6 us -> 18.9 us
  starting transfers between devices: 22.3 us -> 28.3 us
  local copies, waits for them, and re-layouts: 0.02 us -> 0.67 us
    ppermute x19 -> x22, waiting for transfers between devices: 25.6 us -> 18.9 us  [send(): return lax.ppermute(array, ('rep', 'ep'), pairs)]
    ppermute x19 -> x22, starting transfers between devices: 22.3 us -> 28.3 us  [send(): return lax.ppermute(array, ('rep', 'ep'), pairs)]
    unnamed x10, local copies, waits for them, and re-layouts: 0.02 us -> 0.67 us
    pallas_call x8 -> x10, Pallas kernels: 8.27 us -> 8.75 us  [call(): pl.pallas_call(kernel, out_shape=tuple(outs), in_specs=[HBM if n in store...]
  transfers between devices with their start and end apart: 19 -> 22, of which waited for: 11 -> 10; matrix products, arithmetic and copies ran while one was open for 0% -> 0% of each run, Pallas kernels for 3% -> 6%
where the time goes in v8:
time: 57.8 us; the launch traced here: 57.3 us
  starting transfers between devices  28.3 us (49%)
  waiting for transfers between devices  18.9 us (33%)
  Pallas kernels  8.75 us (15%)
  between operations  0.77 us (1%)
  local copies, waits for them, and re-layouts  0.67 us (1%)
    ppermute x22, starting transfers between devices, send(): return lax.ppermute(array, ('rep', 'ep'), pairs)  28.3 us
    ppermute x22, waiting for transfers between devices, send(): return lax.ppermute(array, ('rep', 'ep'), pairs)  18.9 us
    pallas_call x10, Pallas kernels, call(): pl.pallas_call(kernel, out_shape=tuple(outs), in_specs=[HBM if n in store...  8.75 us
  transfers between devices with their start and end apart: 22, of which 10 were waited for; matrix products, arithmetic and copies ran while one was open for 0% of the time, Pallas kernels for 6%

profile of v8, /device:TPU:0, one launch (start us, length us, event | category | flops | bytes accessed | tf_op | source)
XLA Modules:
  0.0 57.3 jit_solution(8222142190157774721)
XLA Ops:
  0.6 2.0 %shard_map.129.refs_8_ = bf16[896,384]{1,0:T(8,128)(2,1)} custom-call(bf16[896,128]{1,0:T(8,128)(2,1)} %gate_ref.1, bf16[896,128]{1,0:T(8,128)(2,1)} %up_ref.1, bf16[896,128]{1,0:T(8,128)(2,1)} %down_ref.1), custom_call_target="tpu_custom_call" | custom-call | bytes 1376256 | tf_op jit(solution)/shard_map/pallas_call | solution.py:32
  2.7 3.0 %collective-permute-start.8 = (bf16[896,384]{1,0:T(8,128)(2,1)}, bf16[896,384]{1,0:T(8,128)(2,1)S(1)}, u32[]{:S(2)}, u32[]{:S(2)}) collective-permute-start(bf16[896,384]{1,0:T(8,128)(2,1)} %shard_map.129.refs_8_), channel_id=1, source_target_pairs={{0,16},{1,17},{2,18},{3,19},{4,20},{5,21},{6,22},{7,23},{8,24},{9,... | collective-permute-start | bytes 2064392 | tf_op jit(solution)/shard_map/ppermute | solution.py:285
  5.7 1.5 %collective-permute-start.7 = (bf16[896,384]{1,0:T(8,128)(2,1)}, bf16[896,384]{1,0:T(8,128)(2,1)S(1)}, u32[]{:S(2)}, u32[]{:S(2)}) collective-permute-start(bf16[896,384]{1,0:T(8,128)(2,1)} %shard_map.129.refs_8_), channel_id=1, source_target_pairs={{0,8},{1,9},{2,10},{3,11},{4,12},{5,13},{6,14},{7,15},{8,0},{9,1},... | collective-permute-start | bytes 2064392 | tf_op jit(solution)/shard_map/ppermute | solution.py:285
  7.2 0.6 %copy-done.3 = s32[4]{0:T(128)S(1)} copy-done((s32[4]{0:T(128)S(1)}, s32[4]{0:T(128)}, u32[]{:S(2)}) %copy-start.3) | copy-done | bytes 40
  7.9 1.9 %shard_map.128 = (bf16[16,7296]{1,0:T(8,128)(2,1)S(1)}, bf16[1,64,128]{2,1,0:T(8,128)(2,1)S(1)}) custom-call(s32[4]{0:T(128)S(1)} %copy-done.3, bf16[128,3584]{1,0:T(8,128)(2,1)} %tok_ref.1, bf16[128,3584]{1,0:T(8,128)(2,1)} %grad_ref.1, s32[8,128]{1,0:T(8,128)S(1)} %bitcast.4, bf16[8,128]{1,0:T(8,128)(2,1)S(1)} %bitcast.6), custom_call_target="tpu_custom_call" | custom-call | bytes 2091024 | tf_op jit(solution)/shard_map/pallas_call | solution.py:32
  9.8 1.6 %collective-permute-start.2 = (bf16[16,7296]{1,0:T(8,128)(2,1)S(1)}, bf16[16,7296]{1,0:T(8,128)(2,1)S(1)}, u32[]{:S(2)}, u32[]{:S(2)}) collective-permute-start(bf16[16,7296]{1,0:T(8,128)(2,1)S(1)} %get-tuple-element.28.refs_3_), channel_id=1, source_target_pairs={{0,2},{1,3},{2,0},{3,1},{4,6},{5,7},{6,4},{7,5},{8,10},{9,11},{10,... | collective-permute-start | bytes 700424 | tf_op jit(solution)/shard_map/ppermute | solution.py:285
  11.4 2.6 %collective-permute-start.1 = (bf16[16,7296]{1,0:T(8,128)(2,1)S(1)}, bf16[16,7296]{1,0:T(8,128)(2,1)S(1)}, u32[]{:S(2)}, u32[]{:S(2)}) collective-permute-start(bf16[16,7296]{1,0:T(8,128)(2,1)S(1)} %get-tuple-element.28.refs_3_), channel_id=1, source_target_pairs={{0,4},{1,5},{2,6},{3,7},{4,0},{5,1},{6,2},{7,3},{8,12},{9,13},{10,... | collective-permute-start | bytes 700424 | tf_op jit(solution)/shard_map/ppermute | solution.py:285
  14.2 6.4 %collective-permute-done.2.refs_2_ = bf16[16,7296]{1,0:T(8,128)(2,1)S(1)} collective-permute-done((bf16[16,7296]{1,0:T(8,128)(2,1)S(1)}, bf16[16,7296]{1,0:T(8,128)(2,1)S(1)}, u32[]{:S(2)}, u32[]{:S(2)}) %collective-permute-start.2) | collective-permute-done | bytes 233504 | tf_op jit(solution)/shard_map/ppermute | solution.py:285
  20.7 0.7 %collective-permute-done.8.all_ref.refs_10_ = bf16[896,384]{1,0:T(8,128)(2,1)S(1)} collective-permute-done((bf16[896,384]{1,0:T(8,128)(2,1)}, bf16[896,384]{1,0:T(8,128)(2,1)S(1)}, u32[]{:S(2)}, u32[]{:S(2)}) %collective-permute-start.8) | collective-permute-done | bytes 688160 | tf_op jit(solution)/shard_map/ppermute | solution.py:285
  21.4 1.8 %collective-permute-start.9 = (bf16[448,384]{1,0:T(8,128)(2,1)S(1)}, bf16[448,384]{1,0:T(8,128)(2,1)S(1)}, u32[]{:S(2)}, u32[]{:S(2)}) collective-permute-start(bf16[448,384]{1,0:T(8,128)(2,1)S(1)} %shard_map.130), channel_id=1, source_target_pairs={{0,8},{1,9},{2,10},{3,11},{4,12},{5,13},{6,14},{7,15},{8,0},{9,1},... | collective-permute-start | bytes 1032200 | tf_op jit(solution)/shard_map/ppermute | solution.py:285
  23.3 1.6 %collective-permute-start.10 = (bf16[448,384]{1,0:T(8,128)(2,1)S(1)}, bf16[448,384]{1,0:T(8,128)(2,1)S(1)}, u32[]{:S(2)}, u32[]{:S(2)}) collective-permute-start(bf16[448,384]{1,0:T(8,128)(2,1)S(1)} %shard_map.131), channel_id=1, source_target_pairs={{0,16},{1,17},{2,18},{3,19},{4,20},{5,21},{6,22},{7,23},{8,24},{9,... | collective-permute-start | bytes 1032200 | tf_op jit(solution)/shard_map/ppermute | solution.py:285
  24.8 6.1 %collective-permute-done.1.refs_1_ = bf16[16,7296]{1,0:T(8,128)(2,1)S(1)} collective-permute-done((bf16[16,7296]{1,0:T(8,128)(2,1)S(1)}, bf16[16,7296]{1,0:T(8,128)(2,1)S(1)}, u32[]{:S(2)}, u32[]{:S(2)}) %collective-permute-start.1) | collective-permute-done | bytes 233504 | tf_op jit(solution)/shard_map/ppermute | solution.py:285
  31.0 0.5 collective-permute-start.4
  31.6 0.9 %collective-permute-done.5.refs_6_ = bf16[16,7296]{1,0:T(8,128)(2,1)S(1)} collective-permute-done((bf16[16,7296]{1,0:T(8,128)(2,1)S(1)}, bf16[16,7296]{1,0:T(8,128)(2,1)S(1)}, u32[]{:S(2)}, u32[]{:S(2)}) %collective-permute-start.5) | collective-permute-done | bytes 233504 | tf_op jit(solution)/shard_map/ppermute | solution.py:285
  32.5 0.3 collective-permute-done.4.refs_5_
  32.8 0.3 collective-permute-done.3.refs_4_
  33.2 1.7 %shard_map.132 = (bf16[64,3712]{1,0:T(8,128)(2,1)S(1)}, bf16[64,3712]{1,0:T(8,128)(2,1)S(1)}, bf16[128,384]{1,0:T(8,128)(2,1)S(1)}, bf16[2,128,896]{2,1,0:T(8,128)(2,1)S(1)}) custom-call(s32[1,4]{1,0:T(1,128)S(1)} %bitcast.7, bf16[16,7296]{1,0:T(8,128)(2,1)S(1)} %collective-permute-done.refs_0_, bf16[16,7296]{1,0:T(8,128)(2,1)S(1)} %collective-permute-done.1.refs_1_, ...), custom_call_target="tpu_custom_call" | custom-call | flops 587202560 | bytes 6127632 | tf_op jit(solution)/shard_map/pallas_call | solution.py:32
  35.2 0.6 %collective-permute-start.15 = (bf16[128,896]{1,0:T(8,128)(2,1)S(1)}, bf16[128,896]{1,0:T(8,128)(2,1)S(1)}, u32[]{:S(2)}, u32[]{:S(2)}) collective-permute-start(bf16[128,896]{1,0:T(8,128)(2,1)S(1)} %get-tuple-element.39), channel_id=1, source_target_pairs={{0,8},{1,9},{2,10},{3,11},{4,12},{5,13},{6,14},{7,15},{8,0},{9,1},... | collective-permute-start | bytes 688136 | tf_op jit(solution)/shard_map/ppermute | solution.py:285
  35.8 0.5 collective-permute-start.16
  36.3 2.4 %collective-permute-start.17 = (bf16[128,896]{1,0:T(8,128)(2,1)S(1)}, bf16[128,896]{1,0:T(8,128)(2,1)S(1)}, u32[]{:S(2)}, u32[]{:S(2)}) collective-permute-start(bf16[128,896]{1,0:T(8,128)(2,1)S(1)} %get-tuple-element.43), channel_id=1, source_target_pairs={{0,24},{1,25},{2,26},{3,27},{4,28},{5,29},{6,30},{7,31},{8,16},{9,... | collective-permute-start | bytes 688136 | tf_op jit(solution)/shard_map/ppermute | solution.py:285
  38.9 2.5 %collective-permute-start.12 = (bf16[16,3712]{1,0:T(8,128)(2,1)S(1)}, bf16[16,3712]{1,0:T(8,128)(2,1)S(1)}, u32[]{:S(2)}, u32[]{:S(2)}) collective-permute-start(bf16[16,3712]{1,0:T(8,128)(2,1)S(1)} %get-tuple-element.31), channel_id=1, source_target_pairs={{0,6},{1,7},{2,4},{3,5},{4,2},{5,3},{6,0},{7,1},{8,14},{9,15},{10,... | collective-permute-start | bytes 356360 | tf_op jit(solution)/shard_map/ppermute | solution.py:285
  41.4 2.2 %collective-permute-start.13 = (bf16[16,3712]{1,0:T(8,128)(2,1)S(1)}, bf16[16,3712]{1,0:T(8,128)(2,1)S(1)}, u32[]{:S(2)}, u32[]{:S(2)}) collective-permute-start(bf16[16,3712]{1,0:T(8,128)(2,1)S(1)} %get-tuple-element.32), channel_id=1, source_target_pairs={{0,4},{1,5},{2,6},{3,7},{4,0},{5,1},{6,2},{7,3},{8,12},{9,13},{10,... | collective-permute-start | bytes 356360 | tf_op jit(solution)/shard_map/ppermute | solution.py:285
  43.7 3.2 %collective-permute-start.14 = (bf16[16,3712]{1,0:T(8,128)(2,1)S(1)}, bf16[16,3712]{1,0:T(8,128)(2,1)S(1)}, u32[]{:S(2)}, u32[]{:S(2)}) collective-permute-start(bf16[16,3712]{1,0:T(8,128)(2,1)S(1)} %get-tuple-element.33), channel_id=1, source_target_pairs={{0,2},{1,3},{2,0},{3,1},{4,6},{5,7},{6,4},{7,5},{8,10},{9,11},{10,... | collective-permute-start | bytes 356360 | tf_op jit(solution)/shard_map/ppermute | solution.py:285
  46.9 1.3 %collective-permute-done.16.refs_1_ = bf16[128,896]{1,0:T(8,128)(2,1)S(1)} collective-permute-done((bf16[128,896]{1,0:T(8,128)(2,1)S(1)}, bf16[128,896]{1,0:T(8,128)(2,1)S(1)}, u32[]{:S(2)}, u32[]{:S(2)}) %collective-permute-start.16) | collective-permute-done | bytes 229408 | tf_op jit(solution)/shard_map/ppermute | solution.py:285
  48.3 2.5 %collective-permute-start.21 = (bf16[128,384]{1,0:T(8,128)(2,1)S(1)}, bf16[128,384]{1,0:T(8,128)(2,1)S(1)}, u32[]{:S(2)}, u32[]{:S(2)}) collective-permute-start(bf16[128,384]{1,0:T(8,128)(2,1)S(1)} %get-tuple-element.40.refs_0_), channel_id=1, source_target_pairs={{0,24},{1,25},{2,26},{3,27},{4,28},{5,29},{6,30},{7,31},{8,16},{9,... | collective-permute-start | bytes 294920 | tf_op jit(solution)/shard_map/ppermute | solution.py:285
  50.8 0.5 collective-permute-start.20
  51.3 0.6 %collective-permute-start.19 = (bf16[128,384]{1,0:T(8,128)(2,1)S(1)}, bf16[128,384]{1,0:T(8,128)(2,1)S(1)}, u32[]{:S(2)}, u32[]{:S(2)}) collective-permute-start(bf16[128,384]{1,0:T(8,128)(2,1)S(1)} %get-tuple-element.40.refs_0_), channel_id=1, source_target_pairs={{0,8},{1,9},{2,10},{3,11},{4,12},{5,13},{6,14},{7,15},{8,0},{9,1},... | collective-permute-start | bytes 294920 | tf_op jit(solution)/shard_map/ppermute | solution.py:285
  51.9 1.1 %collective-permute-done.13.refs_1_ = bf16[16,3712]{1,0:T(8,128)(2,1)S(1)} collective-permute-done((bf16[16,3712]{1,0:T(8,128)(2,1)S(1)}, bf16[16,3712]{1,0:T(8,128)(2,1)S(1)}, u32[]{:S(2)}, u32[]{:S(2)}) %collective-permute-start.13) | collective-permute-done | bytes 118816 | tf_op jit(solution)/shard_map/ppermute | solution.py:285
  53.0 1.4 %shard_map.134 = (bf16[128,3584]{1,0:T(8,128)(2,1)}, f32[8,128]{1,0:T(8,128)}) custom-call(s32[8,128]{1,0:T(8,128)S(1)} %bitcast.5, bf16[1,64,128]{2,1,0:T(8,128)(2,1)S(1)} %get-tuple-element.26.placed_ref, bf16[16,3712]{1,0:T(8,128)(2,1)S(1)} %collective-permute-done.12.refs_0_, bf16[16,3712]{1,0:T(8,128)(2,1)S(1)} %collective-permute-done.13.refs_1_, ...), custom_call_target="tpu_custom_call" | custom-call | flops 58720256000 | bytes 1417216 | tf_op jit(solution)/shard_map/pallas_call | solution.py:32
  54.5 1.0 %collective-permute-done.20.refs_2_ = bf16[128,384]{1,0:T(8,128)(2,1)S(1)} collective-permute-done((bf16[128,384]{1,0:T(8,128)(2,1)S(1)}, bf16[128,384]{1,0:T(8,128)(2,1)S(1)}, u32[]{:S(2)}, u32[]{:S(2)}) %collective-permute-start.20) | collective-permute-done | bytes 98336 | tf_op jit(solution)/shard_map/ppermute | solution.py:285
  55.5 0.5 collective-permute-done.19.refs_1_
  56.0 1.4 %shard_map.137 = (bf16[896,128]{1,0:T(8,128)(2,1)}, bf16[896,128]{1,0:T(8,128)(2,1)}, bf16[896,128]{1,0:T(8,128)(2,1)}) custom-call(bf16[2,128,896]{2,1,0:T(8,128)(2,1)S(1)} %get-tuple-element.37.here_ref, bf16[3,128,896]{2,1,0:T(8,128)(2,1)S(1)} %shard_map.136.own_ref, bf16[3,128,896]{2,1,0:T(8,128)(2,1)S(1)} %collective-permute-done.18.other_ref, ...), custom_call_target="tpu_custom_call" | custom-call | flops 352321536 | bytes 2916352 | tf_op jit(solution)/shard_map/pallas_call | solution.py:32
  (32 shorter events, 0.9 us)
Async XLA Ops:
  0.6 6.6 %copy-start.1 = (s32[128,8]{0,1:T(8,128)S(1)}, s32[128,8]{0,1:T(8,128)}, u32[]{:S(2)}) copy-start(s32[128,8]{0,1:T(8,128)} %param.11) | copy-start | bytes 12292
  2.7 4.5 %copy-start.2 = (bf16[128,8]{0,1:T(8,128)(2,1)S(1)}, bf16[128,8]{0,1:T(8,128)(2,1)}, u32[]{:S(2)}) copy-start(bf16[128,8]{0,1:T(8,128)(2,1)} %param.12) | copy-start | bytes 6148
  2.7 18.7 %collective-permute-start.8 = (bf16[896,384]{1,0:T(8,128)(2,1)}, bf16[896,384]{1,0:T(8,128)(2,1)S(1)}, u32[]{:S(2)}, u32[]{:S(2)}) collective-permute-start(bf16[896,384]{1,0:T(8,128)(2,1)} %shard_map.129.refs_8_), channel_id=1, source_target_pairs={{0,16},{1,17},{2,18},{3,19},{4,20},{5,21},{6,22},{7,23},{8,24},{9,... | collective-permute-start | bytes 2064392 | tf_op jit(solution)/shard_map/ppermute | solution.py:285
  5.7 17.5 %collective-permute-start.7 = (bf16[896,384]{1,0:T(8,128)(2,1)}, bf16[896,384]{1,0:T(8,128)(2,1)S(1)}, u32[]{:S(2)}, u32[]{:S(2)}) collective-permute-start(bf16[896,384]{1,0:T(8,128)(2,1)} %shard_map.129.refs_8_), channel_id=1, source_target_pairs={{0,8},{1,9},{2,10},{3,11},{4,12},{5,13},{6,14},{7,15},{8,0},{9,1},... | collective-permute-start | bytes 2064392 | tf_op jit(solution)/shard_map/ppermute | solution.py:285
  7.2 0.7 %copy-start.3 = (s32[4]{0:T(128)S(1)}, s32[4]{0:T(128)}, u32[]{:S(2)}) copy-start(s32[4]{0:T(128)} %live_ref.1) | copy-start | bytes 52
  9.8 10.9 %collective-permute-start.2 = (bf16[16,7296]{1,0:T(8,128)(2,1)S(1)}, bf16[16,7296]{1,0:T(8,128)(2,1)S(1)}, u32[]{:S(2)}, u32[]{:S(2)}) collective-permute-start(bf16[16,7296]{1,0:T(8,128)(2,1)S(1)} %get-tuple-element.28.refs_3_), channel_id=1, source_target_pairs={{0,2},{1,3},{2,0},{3,1},{4,6},{5,7},{6,4},{7,5},{8,10},{9,11},{10,... | collective-permute-start | bytes 700424 | tf_op jit(solution)/shard_map/ppermute | solution.py:285
  11.4 19.5 %collective-permute-start.1 = (bf16[16,7296]{1,0:T(8,128)(2,1)S(1)}, bf16[16,7296]{1,0:T(8,128)(2,1)S(1)}, u32[]{:S(2)}, u32[]{:S(2)}) collective-permute-start(bf16[16,7296]{1,0:T(8,128)(2,1)S(1)} %get-tuple-element.28.refs_3_), channel_id=1, source_target_pairs={{0,4},{1,5},{2,6},{3,7},{4,0},{5,1},{6,2},{7,3},{8,12},{9,13},{10,... | collective-permute-start | bytes 700424 | tf_op jit(solution)/shard_map/ppermute | solution.py:285
  14.0 17.0 %collective-permute-start = (bf16[16,7296]{1,0:T(8,128)(2,1)S(1)}, bf16[16,7296]{1,0:T(8,128)(2,1)S(1)}, u32[]{:S(2)}, u32[]{:S(2)}) collective-permute-start(bf16[16,7296]{1,0:T(8,128)(2,1)S(1)} %get-tuple-element.28.refs_3_), channel_id=1, source_target_pairs={{0,6},{1,7},{2,4},{3,5},{4,2},{5,3},{6,0},{7,1},{8,14},{9,15},{10,... | collective-permute-start | bytes 700424 | tf_op jit(solution)/shard_map/ppermute | solution.py:285
  20.7 10.8 %collective-permute-start.6 = (bf16[16,7296]{1,0:T(8,128)(2,1)S(1)}, bf16[16,7296]{1,0:T(8,128)(2,1)S(1)}, u32[]{:S(2)}, u32[]{:S(2)}) collective-permute-start(bf16[16,7296]{1,0:T(8,128)(2,1)S(1)} %get-tuple-element.28.refs_3_), channel_id=1, source_target_pairs={{0,1},{1,0},{2,3},{3,2},{4,5},{5,4},{6,7},{7,6},{8,9},{9,8},{10,11... | collective-permute-start | bytes 700424 | tf_op jit(solution)/shard_map/ppermute | solution.py:285
  21.4 11.7 %copy-start = (bf16[896,384]{1,0:T(8,128)(2,1)S(1)}, bf16[896,384]{1,0:T(8,128)(2,1)}, u32[]{:S(2)}) copy-start(bf16[896,384]{1,0:T(8,128)(2,1)} %shard_map.129.refs_8_) | copy-start | bytes 2064388
  21.4 11.7 %collective-permute-start.9 = (bf16[448,384]{1,0:T(8,128)(2,1)S(1)}, bf16[448,384]{1,0:T(8,128)(2,1)S(1)}, u32[]{:S(2)}, u32[]{:S(2)}) collective-permute-start(bf16[448,384]{1,0:T(8,128)(2,1)S(1)} %shard_map.130), channel_id=1, source_target_pairs={{0,8},{1,9},{2,10},{3,11},{4,12},{5,13},{6,14},{7,15},{8,0},{9,1},... | collective-permute-start | bytes 1032200 | tf_op jit(solution)/shard_map/ppermute | solution.py:285
  23.2 9.9 %copy-start.4 = (s32[4,1]{0,1:T(1,128)S(1)}, s32[4,1]{0,1:T(1,128)}, u32[]{:S(2)}) copy-start(s32[4,1]{0,1:T(1,128)} %param.14) | copy-start | bytes 52
  23.3 9.9 %collective-permute-start.10 = (bf16[448,384]{1,0:T(8,128)(2,1)S(1)}, bf16[448,384]{1,0:T(8,128)(2,1)S(1)}, u32[]{:S(2)}, u32[]{:S(2)}) collective-permute-start(bf16[448,384]{1,0:T(8,128)(2,1)S(1)} %shard_map.131), channel_id=1, source_target_pairs={{0,16},{1,17},{2,18},{3,19},{4,20},{5,21},{6,22},{7,23},{8,24},{9,... | collective-permute-start | bytes 1032200 | tf_op jit(solution)/shard_map/ppermute | solution.py:285
  31.0 1.5 %collective-permute-start.5 = (bf16[16,7296]{1,0:T(8,128)(2,1)S(1)}, bf16[16,7296]{1,0:T(8,128)(2,1)S(1)}, u32[]{:S(2)}, u32[]{:S(2)}) collective-permute-start(bf16[16,7296]{1,0:T(8,128)(2,1)S(1)} %collective-permute-done.2.refs_2_), channel_id=1, source_target_pairs={{0,1},{1,0},{2,3},{3,2},{4,5},{5,4},{6,7},{7,6},{8,9},{9,8},{10,11... | collective-permute-start | bytes 700424 | tf_op jit(solution)/shard_map/ppermute | solution.py:285
  31.0 1.8 %collective-permute-start.4 = (bf16[16,7296]{1,0:T(8,128)(2,1)S(1)}, bf16[16,7296]{1,0:T(8,128)(2,1)S(1)}, u32[]{:S(2)}, u32[]{:S(2)}) collective-permute-start(bf16[16,7296]{1,0:T(8,128)(2,1)S(1)} %collective-permute-done.1.refs_1_), channel_id=1, source_target_pairs={{0,1},{1,0},{2,3},{3,2},{4,5},{5,4},{6,7},{7,6},{8,9},{9,8},{10,11... | collective-permute-start | bytes 700424 | tf_op jit(solution)/shard_map/ppermute | solution.py:285
  31.5 1.6 %collective-permute-start.3 = (bf16[16,7296]{1,0:T(8,128)(2,1)S(1)}, bf16[16,7296]{1,0:T(8,128)(2,1)S(1)}, u32[]{:S(2)}, u32[]{:S(2)}) collective-permute-start(bf16[16,7296]{1,0:T(8,128)(2,1)S(1)} %collective-permute-done.refs_0_), channel_id=1, source_target_pairs={{0,1},{1,0},{2,3},{3,2},{4,5},{5,4},{6,7},{7,6},{8,9},{9,8},{10,11... | collective-permute-start | bytes 700424 | tf_op jit(solution)/shard_map/ppermute | solution.py:285
  34.9 3.9 %collective-permute-start.11 = (bf16[64,3712]{1,0:T(8,128)(2,1)S(1)}, bf16[64,3712]{1,0:T(8,128)(2,1)S(1)}, u32[]{:S(2)}, u32[]{:S(2)}) collective-permute-start(bf16[64,3712]{1,0:T(8,128)(2,1)S(1)} %get-tuple-element.30), channel_id=1, source_target_pairs={{0,1},{1,0},{2,3},{3,2},{4,5},{5,4},{6,7},{7,6},{8,9},{9,8},{10,11... | collective-permute-start | bytes 1425416 | tf_op jit(solution)/shard_map/ppermute | solution.py:285
  35.2 8.5 %collective-permute-start.15 = (bf16[128,896]{1,0:T(8,128)(2,1)S(1)}, bf16[128,896]{1,0:T(8,128)(2,1)S(1)}, u32[]{:S(2)}, u32[]{:S(2)}) collective-permute-start(bf16[128,896]{1,0:T(8,128)(2,1)S(1)} %get-tuple-element.39), channel_id=1, source_target_pairs={{0,8},{1,9},{2,10},{3,11},{4,12},{5,13},{6,14},{7,15},{8,0},{9,1},... | collective-permute-start | bytes 688136 | tf_op jit(solution)/shard_map/ppermute | solution.py:285
  35.8 12.5 %collective-permute-start.16 = (bf16[128,896]{1,0:T(8,128)(2,1)S(1)}, bf16[128,896]{1,0:T(8,128)(2,1)S(1)}, u32[]{:S(2)}, u32[]{:S(2)}) collective-permute-start(bf16[128,896]{1,0:T(8,128)(2,1)S(1)} %get-tuple-element.42), channel_id=1, source_target_pairs={{0,16},{1,17},{2,18},{3,19},{4,20},{5,21},{6,22},{7,23},{8,24},{9,... | collective-permute-start | bytes 688136 | tf_op jit(solution)/shard_map/ppermute | solution.py:285
  36.3 14.5 %collective-permute-start.17 = (bf16[128,896]{1,0:T(8,128)(2,1)S(1)}, bf16[128,896]{1,0:T(8,128)(2,1)S(1)}, u32[]{:S(2)}, u32[]{:S(2)}) collective-permute-start(bf16[128,896]{1,0:T(8,128)(2,1)S(1)} %get-tuple-element.43), channel_id=1, source_target_pairs={{0,24},{1,25},{2,26},{3,27},{4,28},{5,29},{6,30},{7,31},{8,16},{9,... | collective-permute-start | bytes 688136 | tf_op jit(solution)/shard_map/ppermute | solution.py:285
  38.9 12.4 %collective-permute-start.12 = (bf16[16,3712]{1,0:T(8,128)(2,1)S(1)}, bf16[16,3712]{1,0:T(8,128)(2,1)S(1)}, u32[]{:S(2)}, u32[]{:S(2)}) collective-permute-start(bf16[16,3712]{1,0:T(8,128)(2,1)S(1)} %get-tuple-element.31), channel_id=1, source_target_pairs={{0,6},{1,7},{2,4},{3,5},{4,2},{5,3},{6,0},{7,1},{8,14},{9,15},{10,... | collective-permute-start | bytes 356360 | tf_op jit(solution)/shard_map/ppermute | solution.py:285
  41.4 11.6 %collective-permute-start.13 = (bf16[16,3712]{1,0:T(8,128)(2,1)S(1)}, bf16[16,3712]{1,0:T(8,128)(2,1)S(1)}, u32[]{:S(2)}, u32[]{:S(2)}) collective-permute-start(bf16[16,3712]{1,0:T(8,128)(2,1)S(1)} %get-tuple-element.32), channel_id=1, source_target_pairs={{0,4},{1,5},{2,6},{3,7},{4,0},{5,1},{6,2},{7,3},{8,12},{9,13},{10,... | collective-permute-start | bytes 356360 | tf_op jit(solution)/shard_map/ppermute | solution.py:285
  43.7 9.3 %collective-permute-start.14 = (bf16[16,3712]{1,0:T(8,128)(2,1)S(1)}, bf16[16,3712]{1,0:T(8,128)(2,1)S(1)}, u32[]{:S(2)}, u32[]{:S(2)}) collective-permute-start(bf16[16,3712]{1,0:T(8,128)(2,1)S(1)} %get-tuple-element.33), channel_id=1, source_target_pairs={{0,2},{1,3},{2,0},{3,1},{4,6},{5,7},{6,4},{7,5},{8,10},{9,11},{10,... | collective-permute-start | bytes 356360 | tf_op jit(solution)/shard_map/ppermute | solution.py:285
  48.3 6.2 %collective-permute-start.21 = (bf16[128,384]{1,0:T(8,128)(2,1)S(1)}, bf16[128,384]{1,0:T(8,128)(2,1)S(1)}, u32[]{:S(2)}, u32[]{:S(2)}) collective-permute-start(bf16[128,384]{1,0:T(8,128)(2,1)S(1)} %get-tuple-element.40.refs_0_), channel_id=1, source_target_pairs={{0,24},{1,25},{2,26},{3,27},{4,28},{5,29},{6,30},{7,31},{8,16},{9,... | collective-permute-start | bytes 294920 | tf_op jit(solution)/shard_map/ppermute | solution.py:285
  50.8 4.7 %collective-permute-start.20 = (bf16[128,384]{1,0:T(8,128)(2,1)S(1)}, bf16[128,384]{1,0:T(8,128)(2,1)S(1)}, u32[]{:S(2)}, u32[]{:S(2)}) collective-permute-start(bf16[128,384]{1,0:T(8,128)(2,1)S(1)} %get-tuple-element.40.refs_0_), channel_id=1, source_target_pairs={{0,16},{1,17},{2,18},{3,19},{4,20},{5,21},{6,22},{7,23},{8,24},{9,... | collective-permute-start | bytes 294920 | tf_op jit(solution)/shard_map/ppermute | solution.py:285
  51.3 4.7 %collective-permute-start.19 = (bf16[128,384]{1,0:T(8,128)(2,1)S(1)}, bf16[128,384]{1,0:T(8,128)(2,1)S(1)}, u32[]{:S(2)}, u32[]{:S(2)}) collective-permute-start(bf16[128,384]{1,0:T(8,128)(2,1)S(1)} %get-tuple-element.40.refs_0_), channel_id=1, source_target_pairs={{0,8},{1,9},{2,10},{3,11},{4,12},{5,13},{6,14},{7,15},{8,0},{9,1},... | collective-permute-start | bytes 294920 | tf_op jit(solution)/shard_map/ppermute | solution.py:285
  53.0 3.0 %collective-permute-start.18 = (bf16[3,128,896]{2,1,0:T(8,128)(2,1)S(1)}, bf16[3,128,896]{2,1,0:T(8,128)(2,1)S(1)}, u32[]{:S(2)}, u32[]{:S(2)}) collective-permute-start(bf16[3,128,896]{2,1,0:T(8,128)(2,1)S(1)} %shard_map.136.own_ref), channel_id=1, source_target_pairs={{0,1},{1,0},{2,3},{3,2},{4,5},{5,4},{6,7},{7,6},{8,9},{9,8},{10,11... | collective-permute-start | bytes 2064392 | tf_op jit(solution)/shard_map/ppermute | solution.py:285

commit v9 on v7

--- a/solution.py
+++ b/solution.py
@@ -71,15 +71,20 @@
     width = model // rep
     spacing = EXPERTS // flight
     small = fetch([(live_ref, live), (ids_ref, ids_held), (rw_ref, rw_held)], sems)
+    units = stored[0].shape[1]
+    piece = width // 2
+    pairs = []
+    for p in range(2):
+        some = pl.ds(p * piece, piece)
+        for n, ref in enumerate(stored):
+            pairs.append((ref.at[some], joined.at[some, pl.ds(n * units, units)]))
+    weight_copies = fetch(pairs, sems, 3)
     pairs = []
     for part, ref in enumerate((tok_ref, grad_ref)):
         for p in range(PARTS):
             some = pl.ds(p * (count // PARTS), count // PARTS)
             pairs.append((ref.at[some], data.at[part, some]))
-    large = fetch(pairs, sems, len(small))
-    units = stored[0].shape[1]
-    pairs = [(ref, joined.at[:, pl.ds(n * units, units)]) for n, ref in enumerate(stored)]
-    weight_copies = fetch(pairs, sems, len(small) + len(large))
+    large = fetch(pairs, sems, 9)
     for copy in small:
         copy.wait()
     token = iota((1, count), 1)
@@ -102,9 +107,12 @@
         placed = placed.astype(BF16)
         firsts.append(placed)
         placed_ref[w] = jnp.concatenate([placed] * CHIPS, axis=0)
-    for copy in weight_copies:
-        copy.wait()
-    (out_copy,) = fetch([(joined, all_ref)], sems, len(small) + len(large) + len(weight_copies))
+    out_copies = []
+    for p in range(2):
+        for n in range(len(stored)):
+            weight_copies[3 * p + n].wait()
+        some = pl.ds(p * piece, piece)
+        out_copies += fetch([(joined.at[some], all_ref.at[some])], sems, 9 + 2 * PARTS + p)
     for part in range(2):
         for p in range(PARTS):
             large[part * PARTS + p].wait()
@@ -115,7 +123,8 @@
             for k in range(rep):
                 n = 2 * k + part
                 pays[w][:, n * width : (n + 1) * width] = rows[jnp.bitwise_xor(r, k)]
-    out_copy.wait()
+    for copy in out_copies:
+        copy.wait()
 
 
 def half_kernel(start, all_ref, half_ref):
@@ -209,11 +218,11 @@
 
 
 def weight_kernel(rep, here_ref, grads_ref, other_ref, *refs):
-    away, outs = refs[: rep - 1], refs[rep - 1 :]
+    away, outs, held, sems = refs[: rep - 1], refs[rep - 1 : -4], refs[-4:-1], refs[-1]
     units = outs[0].shape[1]
     width = here_ref.shape[2]
     half = grads_ref.shape[0] // 2
-    sums = []
+    copies = []
     for part, columns in enumerate((slice(0, 2 * units), slice(2 * units, 3 * units))):
         some = slice(part * half, (part + 1) * half)
         rows = [here_ref[part]]
@@ -223,17 +232,18 @@
             got.append(ref[:, width + columns.start : width + columns.stop])
         rows = jnp.concatenate(rows, axis=0)
         got = jnp.concatenate(got, axis=0)
-        sums.append(dot(got, rows, ((0,), (0,))))
-    outs[0][...] = sums[0][:units].T.astype(BF16)
-    outs[1][...] = sums[0][units:].T.astype(BF16)
-    outs[2][...] = sums[1].T.astype(BF16)
+        total = dot(got, rows, ((0,), (0,)))
+        for n in range(total.shape[0] // units):
+            held[2 * part + n][...] = total[n * units : (n + 1) * units].T.astype(BF16)
+            copies += fetch([(held[2 * part + n], outs[2 * part + n])], sems, 2 * part + n)
+    for copy in copies:
+        copy.wait()
 
 
 def token_kernel(rep, flight, ids_ref, placed_ref, *refs):
     backs, rest = refs[: flight * CHIPS], refs[flight * CHIPS :]
-    out_ref, weight_ref, blocks, ids, sem = rest
-    ids_copy = pltpu.make_async_copy(ids_ref, ids, sem)
-    ids_copy.start()
+    out_ref, weight_ref, blocks, ids, sems = rest
+    (ids_copy,) = fetch([(ids_ref, ids)], sems)
     r = lax.axis_index("rep")
     mine = lax.axis_index("ep") // SPLIT
     spacing = EXPERTS // flight
@@ -295,7 +305,7 @@
             pltpu.VMEM((2, tok_count, model_dim), BF16),
             pltpu.VMEM((rep, SLOT, width), BF16),
             pltpu.VMEM((width, 3 * units), BF16),
-            pltpu.SemaphoreType.DMA((2 * PARTS + 7,)),
+            pltpu.SemaphoreType.DMA((2 * PARTS + 11,)),
         ],
         grant=54,
     )
@@ -349,6 +359,8 @@
         functools.partial(weight_kernel, rep),
         [shape((width, units))] * 3,
         [here, grads, other_rows] + moved,
+        kept=(0, 1, 2),
+        scratch=[pltpu.VMEM((width, units), BF16)] * 3 + [pltpu.SemaphoreType.DMA((3,))],
         flops=2 * 2 * rep * rows * width * 3 * units,
     )
     grad_tokens, grad_weight = call(
@@ -359,7 +371,7 @@
         scratch=[
             pltpu.VMEM((rep, tok_count, width), BF16),
             pltpu.VMEM(ids_rows.shape, jnp.int32),
-            pltpu.SemaphoreType.DMA(()),
+            pltpu.SemaphoreType.DMA((1,)),
         ],
         flops=1000 * 2 * tok_count * CHIPS * SLOT * model_dim,
     )

time: 57.1 us -> 56.6 us (level)
  no operation moved by 1% of the time
where the time goes in v9:
time: 56.6 us; the launch traced here: 56.4 us
  waiting for transfers between devices  25.6 us (45%)
  starting transfers between devices  22.4 us (40%)
  Pallas kernels  7.71 us (14%)
  between operations  0.77 us (1%)
    ppermute x19, waiting for transfers between devices, send(): return lax.ppermute(array, ('rep', 'ep'), pairs)  25.6 us
    ppermute x19, starting transfers between devices, send(): return lax.ppermute(array, ('rep', 'ep'), pairs)  22.4 us
    pallas_call x8, Pallas kernels, call(): pl.pallas_call(kernel, out_shape=tuple(outs), in_specs=[HBM if n in store...  7.71 us
  transfers between devices with their start and end apart: 19, of which 11 were waited for; matrix products, arithmetic and copies ran while one was open for 0% of the time, Pallas kernels for 3%

profile of v9, /device:TPU:0, one launch (start us, length us, event | category | flops | bytes accessed | tf_op | source)
XLA Modules:
  0.0 56.4 jit_solution(15245474805602064678)
XLA Ops:
  0.6 2.9 %shard_map.128 = (bf16[16,7296]{1,0:T(8,128)(2,1)}, bf16[1,64,128]{2,1,0:T(8,128)(2,1)}, bf16[896,384]{1,0:T(8,128)(2,1)}) custom-call(s32[4]{0:T(128)} %live_ref.1, bf16[128,3584]{1,0:T(8,128)(2,1)} %tok_ref.1, bf16[128,3584]{1,0:T(8,128)(2,1)} %grad_ref.1, s32[8,128]{1,0:T(8,128)} %bitcast.4, bf16[8,128]{1,0:T(8,128)(2,1)} %bitcast.7, ...), custom_call_target="tpu_custom_call" | custom-call | bytes 3467280 | tf_op jit(solution)/shard_map/pallas_call | solution.py:32
  3.5 3.0 %collective-permute-start.8 = (bf16[896,384]{1,0:T(8,128)(2,1)}, bf16[896,384]{1,0:T(8,128)(2,1)S(1)}, u32[]{:S(2)}, u32[]{:S(2)}) collective-permute-start(bf16[896,384]{1,0:T(8,128)(2,1)} %get-tuple-element.28.refs_8_), channel_id=1, source_target_pairs={{0,16},{1,17},{2,18},{3,19},{4,20},{5,21},{6,22},{7,23},{8,24},{9,... | collective-permute-start | bytes 2064392 | tf_op jit(solution)/shard_map/ppermute | solution.py:289
  6.6 1.5 %collective-permute-start.7 = (bf16[896,384]{1,0:T(8,128)(2,1)}, bf16[896,384]{1,0:T(8,128)(2,1)S(1)}, u32[]{:S(2)}, u32[]{:S(2)}) collective-permute-start(bf16[896,384]{1,0:T(8,128)(2,1)} %get-tuple-element.28.refs_8_), channel_id=1, source_target_pairs={{0,8},{1,9},{2,10},{3,11},{4,12},{5,13},{6,14},{7,15},{8,0},{9,1},... | collective-permute-start | bytes 2064392 | tf_op jit(solution)/shard_map/ppermute | solution.py:289
  8.1 1.6 %collective-permute-start.2 = (bf16[16,7296]{1,0:T(8,128)(2,1)}, bf16[16,7296]{1,0:T(8,128)(2,1)S(1)}, u32[]{:S(2)}, u32[]{:S(2)}) collective-permute-start(bf16[16,7296]{1,0:T(8,128)(2,1)} %get-tuple-element.27.refs_3_), channel_id=1, source_target_pairs={{0,2},{1,3},{2,0},{3,1},{4,6},{5,7},{6,4},{7,5},{8,10},{9,11},{10,... | collective-permute-start | bytes 700424 | tf_op jit(solution)/shard_map/ppermute | solution.py:289
  9.6 2.6 %collective-permute-start.1 = (bf16[16,7296]{1,0:T(8,128)(2,1)}, bf16[16,7296]{1,0:T(8,128)(2,1)S(1)}, u32[]{:S(2)}, u32[]{:S(2)}) collective-permute-start(bf16[16,7296]{1,0:T(8,128)(2,1)} %get-tuple-element.27.refs_3_), channel_id=1, source_target_pairs={{0,4},{1,5},{2,6},{3,7},{4,0},{5,1},{6,2},{7,3},{8,12},{9,13},{10,... | collective-permute-start | bytes 700424 | tf_op jit(solution)/shard_map/ppermute | solution.py:289
  12.2 0.2 collective-permute-start
  12.4 6.6 %collective-permute-done.2.refs_2_ = bf16[16,7296]{1,0:T(8,128)(2,1)S(1)} collective-permute-done((bf16[16,7296]{1,0:T(8,128)(2,1)}, bf16[16,7296]{1,0:T(8,128)(2,1)S(1)}, u32[]{:S(2)}, u32[]{:S(2)}) %collective-permute-start.2) | collective-permute-done | bytes 233504 | tf_op jit(solution)/shard_map/ppermute | solution.py:289
  19.1 3.1 %collective-permute-done.8.all_ref.refs_10_ = bf16[896,384]{1,0:T(8,128)(2,1)S(1)} collective-permute-done((bf16[896,384]{1,0:T(8,128)(2,1)}, bf16[896,384]{1,0:T(8,128)(2,1)S(1)}, u32[]{:S(2)}, u32[]{:S(2)}) %collective-permute-start.8) | collective-permute-done | bytes 688160 | tf_op jit(solution)/shard_map/ppermute | solution.py:289
  22.3 1.8 %collective-permute-start.9 = (bf16[448,384]{1,0:T(8,128)(2,1)S(1)}, bf16[448,384]{1,0:T(8,128)(2,1)S(1)}, u32[]{:S(2)}, u32[]{:S(2)}) collective-permute-start(bf16[448,384]{1,0:T(8,128)(2,1)S(1)} %shard_map.129), channel_id=1, source_target_pairs={{0,8},{1,9},{2,10},{3,11},{4,12},{5,13},{6,14},{7,15},{8,0},{9,1},... | collective-permute-start | bytes 1032200 | tf_op jit(solution)/shard_map/ppermute | solution.py:289
  24.1 1.6 %collective-permute-start.10 = (bf16[448,384]{1,0:T(8,128)(2,1)S(1)}, bf16[448,384]{1,0:T(8,128)(2,1)S(1)}, u32[]{:S(2)}, u32[]{:S(2)}) collective-permute-start(bf16[448,384]{1,0:T(8,128)(2,1)S(1)} %shard_map.130), channel_id=1, source_target_pairs={{0,16},{1,17},{2,18},{3,19},{4,20},{5,21},{6,22},{7,23},{8,24},{9,... | collective-permute-start | bytes 1032200 | tf_op jit(solution)/shard_map/ppermute | solution.py:289
  25.7 3.7 %collective-permute-done.1.refs_1_ = bf16[16,7296]{1,0:T(8,128)(2,1)S(1)} collective-permute-done((bf16[16,7296]{1,0:T(8,128)(2,1)}, bf16[16,7296]{1,0:T(8,128)(2,1)S(1)}, u32[]{:S(2)}, u32[]{:S(2)}) %collective-permute-start.1) | collective-permute-done | bytes 233504 | tf_op jit(solution)/shard_map/ppermute | solution.py:289
  29.4 0.5 collective-permute-start.4
  29.9 0.1 collective-permute-start.3
  30.0 0.9 %collective-permute-done.5.refs_6_ = bf16[16,7296]{1,0:T(8,128)(2,1)S(1)} collective-permute-done((bf16[16,7296]{1,0:T(8,128)(2,1)S(1)}, bf16[16,7296]{1,0:T(8,128)(2,1)S(1)}, u32[]{:S(2)}, u32[]{:S(2)}) %collective-permute-start.5) | collective-permute-done | bytes 233504 | tf_op jit(solution)/shard_map/ppermute | solution.py:289
  30.9 0.3 collective-permute-done.4.refs_5_
  31.2 0.3 collective-permute-done.3.refs_4_
  31.6 1.2 %collective-permute-done.10.refs_12_ = bf16[448,384]{1,0:T(8,128)(2,1)S(1)} collective-permute-done((bf16[448,384]{1,0:T(8,128)(2,1)S(1)}, bf16[448,384]{1,0:T(8,128)(2,1)S(1)}, u32[]{:S(2)}, u32[]{:S(2)}) %collective-permute-start.10) | collective-permute-done | bytes 344096 | tf_op jit(solution)/shard_map/ppermute | solution.py:289
  32.8 1.8 %shard_map.131 = (bf16[64,3712]{1,0:T(8,128)(2,1)S(1)}, bf16[64,3712]{1,0:T(8,128)(2,1)S(1)}, bf16[128,384]{1,0:T(8,128)(2,1)S(1)}, bf16[2,128,896]{2,1,0:T(8,12...) custom-call(s32[1,4]{1,0:T(1,128)S(1)} %bitcast.6, ...), custom_call_target="tpu_custom_call" | custom-call | flops 587202560 | bytes 7110672 | tf_op jit(solution)/shard_map/pallas_call | solution.py:32
  34.6 0.1 collective-permute-start.11
  34.7 1.1 %collective-permute-start.15 = (bf16[128,1280]{1,0:T(8,128)(2,1)S(1)}, bf16[128,1280]{1,0:T(8,128)(2,1)S(1)}, u32[]{:S(2)}, u32[]{:S(2)}) collective-permute-start(bf16[128,1280]{1,0:T(8,128)(2,1)S(1)} %get-tuple-element.39), channel_id=1, source_target_pairs={{0,8},{1,9},{2,10},{3,11},{4,12},{5,13},{6,14},{7,15},{8,0},{9,1},... | collective-permute-start | bytes 983048 | tf_op jit(solution)/shard_map/ppermute | solution.py:289
  35.8 1.0 %collective-permute-start.16 = (bf16[128,1280]{1,0:T(8,128)(2,1)S(1)}, bf16[128,1280]{1,0:T(8,128)(2,1)S(1)}, u32[]{:S(2)}, u32[]{:S(2)}) collective-permute-start(bf16[128,1280]{1,0:T(8,128)(2,1)S(1)} %get-tuple-element.40), channel_id=1, source_target_pairs={{0,16},{1,17},{2,18},{3,19},{4,20},{5,21},{6,22},{7,23},{8,24},{9,... | collective-permute-start | bytes 983048 | tf_op jit(solution)/shard_map/ppermute | solution.py:289
  36.8 1.4 %collective-permute-start.17 = (bf16[128,1280]{1,0:T(8,128)(2,1)S(1)}, bf16[128,1280]{1,0:T(8,128)(2,1)S(1)}, u32[]{:S(2)}, u32[]{:S(2)}) collective-permute-start(bf16[128,1280]{1,0:T(8,128)(2,1)S(1)} %get-tuple-element.41), channel_id=1, source_target_pairs={{0,24},{1,25},{2,26},{3,27},{4,28},{5,29},{6,30},{7,31},{8,16},{9,... | collective-permute-start | bytes 983048 | tf_op jit(solution)/shard_map/ppermute | solution.py:289
  38.2 0.1 shard_map.132
  38.3 3.7 %collective-permute-start.12 = (bf16[16,3712]{1,0:T(8,128)(2,1)S(1)}, bf16[16,3712]{1,0:T(8,128)(2,1)S(1)}, u32[]{:S(2)}, u32[]{:S(2)}) collective-permute-start(bf16[16,3712]{1,0:T(8,128)(2,1)S(1)} %get-tuple-element.31), channel_id=1, source_target_pairs={{0,6},{1,7},{2,4},{3,5},{4,2},{5,3},{6,0},{7,1},{8,14},{9,15},{10,... | collective-permute-start | bytes 356360 | tf_op jit(solution)/shard_map/ppermute | solution.py:289
  42.0 3.2 %collective-permute-done.15.refs_0_ = bf16[128,1280]{1,0:T(8,128)(2,1)S(1)} collective-permute-done((bf16[128,1280]{1,0:T(8,128)(2,1)S(1)}, bf16[128,1280]{1,0:T(8,128)(2,1)S(1)}, u32[]{:S(2)}, u32[]{:S(2)}) %collective-permute-start.15) | collective-permute-done | bytes 327712 | tf_op jit(solution)/shard_map/ppermute | solution.py:289
  45.2 2.1 %collective-permute-start.14 = (bf16[16,3712]{1,0:T(8,128)(2,1)S(1)}, bf16[16,3712]{1,0:T(8,128)(2,1)S(1)}, u32[]{:S(2)}, u32[]{:S(2)}) collective-permute-start(bf16[16,3712]{1,0:T(8,128)(2,1)S(1)} %get-tuple-element.33), channel_id=1, source_target_pairs={{0,2},{1,3},{2,0},{3,1},{4,6},{5,7},{6,4},{7,5},{8,10},{9,11},{10,... | collective-permute-start | bytes 356360 | tf_op jit(solution)/shard_map/ppermute | solution.py:289
  47.4 3.8 %collective-permute-done.16.refs_1_ = bf16[128,1280]{1,0:T(8,128)(2,1)S(1)} collective-permute-done((bf16[128,1280]{1,0:T(8,128)(2,1)S(1)}, bf16[128,1280]{1,0:T(8,128)(2,1)S(1)}, u32[]{:S(2)}, u32[]{:S(2)}) %collective-permute-start.16) | collective-permute-done | bytes 327712 | tf_op jit(solution)/shard_map/ppermute | solution.py:289
  51.1 1.6 %collective-permute-done.17.refs_2_ = bf16[128,1280]{1,0:T(8,128)(2,1)S(1)} collective-permute-done((bf16[128,1280]{1,0:T(8,128)(2,1)S(1)}, bf16[128,1280]{1,0:T(8,128)(2,1)S(1)}, u32[]{:S(2)}, u32[]{:S(2)}) %collective-permute-start.17) | collective-permute-done | bytes 327712 | tf_op jit(solution)/shard_map/ppermute | solution.py:289
  52.8 0.1 collective-permute-start.18
  53.0 1.4 %shard_map.133 = (bf16[128,3584]{1,0:T(8,128)(2,1)}, f32[8,128]{1,0:T(8,128)}) custom-call(s32[8,128]{1,0:T(8,128)S(1)} %bitcast.5, bf16[1,64,128]{2,1,0:T(8,128)(2,1)S(1)} %copy-done.4, bf16[16,3712]{1,0:T(8,128)(2,1)S(1)} %collective-permute-done.12.refs_0_, bf16[16,3712]{1,0:T(8,128)(2,1)S(1)} %collective-permute-done.13.refs_1_, ...), custom_call_target="tpu_custom_call" | custom-call | flops 58720256000 | bytes 1417216 | tf_op jit(solution)/shard_map/pallas_call | solution.py:32
  54.4 0.6 %collective-permute-done.18.other_ref = bf16[3,128,896]{2,1,0:T(8,128)(2,1)S(1)} collective-permute-done((bf16[3,128,896]{2,1,0:T(8,128)(2,1)S(1)}, bf16[3,128,896]{2,1,0:T(8,128)(2,1)S(1)}, u32[]{:S(2)}, u32[]{:S(2)}) %collective-permute-start.18) | collective-permute-done | bytes 688160 | tf_op jit(solution)/shard_map/ppermute | solution.py:289
  55.0 1.4 %shard_map.135 = (bf16[896,128]{1,0:T(8,128)(2,1)}, bf16[896,128]{1,0:T(8,128)(2,1)}, bf16[896,128]{1,0:T(8,128)(2,1)}) custom-call(bf16[2,128,896]{2,1,0:T(8,128)(2,1)S(1)} %get-tuple-element.37.here_ref, bf16[128,384]{1,0:T(8,128)(2,1)S(1)} %get-tuple-element.38.grads_ref, bf16[3,128,896]{2,1,0:T(8,128)(2,1)S(1)} %collective-permute-done.18.other_ref, ...), custom_call_target="tpu_custom_call" | custom-call | flops 352321536 | bytes 2916352 | tf_op jit(solution)/shard_map/pallas_call | solution.py:32
  (24 shorter events, 0.2 us)
Async XLA Ops:
  3.5 18.7 %collective-permute-start.8 = (bf16[896,384]{1,0:T(8,128)(2,1)}, bf16[896,384]{1,0:T(8,128)(2,1)S(1)}, u32[]{:S(2)}, u32[]{:S(2)}) collective-permute-start(bf16[896,384]{1,0:T(8,128)(2,1)} %get-tuple-element.28.refs_8_), channel_id=1, source_target_pairs={{0,16},{1,17},{2,18},{3,19},{4,20},{5,21},{6,22},{7,23},{8,24},{9,... | collective-permute-start | bytes 2064392 | tf_op jit(solution)/shard_map/ppermute | solution.py:289
  6.6 17.5 %collective-permute-start.7 = (bf16[896,384]{1,0:T(8,128)(2,1)}, bf16[896,384]{1,0:T(8,128)(2,1)S(1)}, u32[]{:S(2)}, u32[]{:S(2)}) collective-permute-start(bf16[896,384]{1,0:T(8,128)(2,1)} %get-tuple-element.28.refs_8_), channel_id=1, source_target_pairs={{0,8},{1,9},{2,10},{3,11},{4,12},{5,13},{6,14},{7,15},{8,0},{9,1},... | collective-permute-start | bytes 2064392 | tf_op jit(solution)/shard_map/ppermute | solution.py:289
  8.1 11.0 %collective-permute-start.2 = (bf16[16,7296]{1,0:T(8,128)(2,1)}, bf16[16,7296]{1,0:T(8,128)(2,1)S(1)}, u32[]{:S(2)}, u32[]{:S(2)}) collective-permute-start(bf16[16,7296]{1,0:T(8,128)(2,1)} %get-tuple-element.27.refs_3_), channel_id=1, source_target_pairs={{0,2},{1,3},{2,0},{3,1},{4,6},{5,7},{6,4},{7,5},{8,10},{9,11},{10,... | collective-permute-start | bytes 700424 | tf_op jit(solution)/shard_map/ppermute | solution.py:289
  9.6 19.7 %collective-permute-start.1 = (bf16[16,7296]{1,0:T(8,128)(2,1)}, bf16[16,7296]{1,0:T(8,128)(2,1)S(1)}, u32[]{:S(2)}, u32[]{:S(2)}) collective-permute-start(bf16[16,7296]{1,0:T(8,128)(2,1)} %get-tuple-element.27.refs_3_), channel_id=1, source_target_pairs={{0,4},{1,5},{2,6},{3,7},{4,0},{5,1},{6,2},{7,3},{8,12},{9,13},{10,... | collective-permute-start | bytes 700424 | tf_op jit(solution)/shard_map/ppermute | solution.py:289
  12.2 17.2 %collective-permute-start = (bf16[16,7296]{1,0:T(8,128)(2,1)}, bf16[16,7296]{1,0:T(8,128)(2,1)S(1)}, u32[]{:S(2)}, u32[]{:S(2)}) collective-permute-start(bf16[16,7296]{1,0:T(8,128)(2,1)} %get-tuple-element.27.refs_3_), channel_id=1, source_target_pairs={{0,6},{1,7},{2,4},{3,5},{4,2},{5,3},{6,0},{7,1},{8,14},{9,15},{10,... | collective-permute-start | bytes 700424 | tf_op jit(solution)/shard_map/ppermute | solution.py:289
  19.1 10.8 %collective-permute-start.6 = (bf16[16,7296]{1,0:T(8,128)(2,1)}, bf16[16,7296]{1,0:T(8,128)(2,1)S(1)}, u32[]{:S(2)}, u32[]{:S(2)}) collective-permute-start(bf16[16,7296]{1,0:T(8,128)(2,1)} %get-tuple-element.27.refs_3_), channel_id=1, source_target_pairs={{0,1},{1,0},{2,3},{3,2},{4,5},{5,4},{6,7},{7,6},{8,9},{9,8},{10,11... | collective-permute-start | bytes 700424 | tf_op jit(solution)/shard_map/ppermute | solution.py:289
  22.2 10.6 %copy-start = (bf16[896,384]{1,0:T(8,128)(2,1)S(1)}, bf16[896,384]{1,0:T(8,128)(2,1)}, u32[]{:S(2)}) copy-start(bf16[896,384]{1,0:T(8,128)(2,1)} %get-tuple-element.28.refs_8_) | copy-start | bytes 2064388
  22.2 10.6 %copy-start.1 = (bf16[16,7296]{1,0:T(8,128)(2,1)S(1)}, bf16[16,7296]{1,0:T(8,128)(2,1)}, u32[]{:S(2)}) copy-start(bf16[16,7296]{1,0:T(8,128)(2,1)} %get-tuple-element.27.refs_3_) | copy-start | bytes 700420
  22.3 9.3 %collective-permute-start.9 = (bf16[448,384]{1,0:T(8,128)(2,1)S(1)}, bf16[448,384]{1,0:T(8,128)(2,1)S(1)}, u32[]{:S(2)}, u32[]{:S(2)}) collective-permute-start(bf16[448,384]{1,0:T(8,128)(2,1)S(1)} %shard_map.129), channel_id=1, source_target_pairs={{0,8},{1,9},{2,10},{3,11},{4,12},{5,13},{6,14},{7,15},{8,0},{9,1},... | collective-permute-start | bytes 1032200 | tf_op jit(solution)/shard_map/ppermute | solution.py:289
  24.1 8.7 %copy-start.3 = (s32[4,1]{0,1:T(1,128)S(1)}, s32[4,1]{0,1:T(1,128)}, u32[]{:S(2)}) copy-start(s32[4,1]{0,1:T(1,128)} %param.14) | copy-start | bytes 52
  24.1 8.7 %collective-permute-start.10 = (bf16[448,384]{1,0:T(8,128)(2,1)S(1)}, bf16[448,384]{1,0:T(8,128)(2,1)S(1)}, u32[]{:S(2)}, u32[]{:S(2)}) collective-permute-start(bf16[448,384]{1,0:T(8,128)(2,1)S(1)} %shard_map.130), channel_id=1, source_target_pairs={{0,16},{1,17},{2,18},{3,19},{4,20},{5,21},{6,22},{7,23},{8,24},{9,... | collective-permute-start | bytes 1032200 | tf_op jit(solution)/shard_map/ppermute | solution.py:289
  29.4 1.5 %collective-permute-start.5 = (bf16[16,7296]{1,0:T(8,128)(2,1)S(1)}, bf16[16,7296]{1,0:T(8,128)(2,1)S(1)}, u32[]{:S(2)}, u32[]{:S(2)}) collective-permute-start(bf16[16,7296]{1,0:T(8,128)(2,1)S(1)} %collective-permute-done.2.refs_2_), channel_id=1, source_target_pairs={{0,1},{1,0},{2,3},{3,2},{4,5},{5,4},{6,7},{7,6},{8,9},{9,8},{10,11... | collective-permute-start | bytes 700424 | tf_op jit(solution)/shard_map/ppermute | solution.py:289
  29.4 1.8 %collective-permute-start.4 = (bf16[16,7296]{1,0:T(8,128)(2,1)S(1)}, bf16[16,7296]{1,0:T(8,128)(2,1)S(1)}, u32[]{:S(2)}, u32[]{:S(2)}) collective-permute-start(bf16[16,7296]{1,0:T(8,128)(2,1)S(1)} %collective-permute-done.1.refs_1_), channel_id=1, source_target_pairs={{0,1},{1,0},{2,3},{3,2},{4,5},{5,4},{6,7},{7,6},{8,9},{9,8},{10,11... | collective-permute-start | bytes 700424 | tf_op jit(solution)/shard_map/ppermute | solution.py:289
  29.9 1.6 %collective-permute-start.3 = (bf16[16,7296]{1,0:T(8,128)(2,1)S(1)}, bf16[16,7296]{1,0:T(8,128)(2,1)S(1)}, u32[]{:S(2)}, u32[]{:S(2)}) collective-permute-start(bf16[16,7296]{1,0:T(8,128)(2,1)S(1)} %collective-permute-done.refs_0_), channel_id=1, source_target_pairs={{0,1},{1,0},{2,3},{3,2},{4,5},{5,4},{6,7},{7,6},{8,9},{9,8},{10,11... | collective-permute-start | bytes 700424 | tf_op jit(solution)/shard_map/ppermute | solution.py:289
  34.6 3.6 %collective-permute-start.11 = (bf16[64,3712]{1,0:T(8,128)(2,1)S(1)}, bf16[64,3712]{1,0:T(8,128)(2,1)S(1)}, u32[]{:S(2)}, u32[]{:S(2)}) collective-permute-start(bf16[64,3712]{1,0:T(8,128)(2,1)S(1)} %get-tuple-element.30), channel_id=1, source_target_pairs={{0,1},{1,0},{2,3},{3,2},{4,5},{5,4},{6,7},{7,6},{8,9},{9,8},{10,11... | collective-permute-start | bytes 1425416 | tf_op jit(solution)/shard_map/ppermute | solution.py:289
  34.7 10.6 %collective-permute-start.15 = (bf16[128,1280]{1,0:T(8,128)(2,1)S(1)}, bf16[128,1280]{1,0:T(8,128)(2,1)S(1)}, u32[]{:S(2)}, u32[]{:S(2)}) collective-permute-start(bf16[128,1280]{1,0:T(8,128)(2,1)S(1)} %get-tuple-element.39), channel_id=1, source_target_pairs={{0,8},{1,9},{2,10},{3,11},{4,12},{5,13},{6,14},{7,15},{8,0},{9,1},... | collective-permute-start | bytes 983048 | tf_op jit(solution)/shard_map/ppermute | solution.py:289
  35.8 15.3 %collective-permute-start.16 = (bf16[128,1280]{1,0:T(8,128)(2,1)S(1)}, bf16[128,1280]{1,0:T(8,128)(2,1)S(1)}, u32[]{:S(2)}, u32[]{:S(2)}) collective-permute-start(bf16[128,1280]{1,0:T(8,128)(2,1)S(1)} %get-tuple-element.40), channel_id=1, source_target_pairs={{0,16},{1,17},{2,18},{3,19},{4,20},{5,21},{6,22},{7,23},{8,24},{9,... | collective-permute-start | bytes 983048 | tf_op jit(solution)/shard_map/ppermute | solution.py:289
  36.8 16.0 %collective-permute-start.17 = (bf16[128,1280]{1,0:T(8,128)(2,1)S(1)}, bf16[128,1280]{1,0:T(8,128)(2,1)S(1)}, u32[]{:S(2)}, u32[]{:S(2)}) collective-permute-start(bf16[128,1280]{1,0:T(8,128)(2,1)S(1)} %get-tuple-element.41), channel_id=1, source_target_pairs={{0,24},{1,25},{2,26},{3,27},{4,28},{5,29},{6,30},{7,31},{8,16},{9,... | collective-permute-start | bytes 983048 | tf_op jit(solution)/shard_map/ppermute | solution.py:289
  38.3 14.6 %collective-permute-start.12 = (bf16[16,3712]{1,0:T(8,128)(2,1)S(1)}, bf16[16,3712]{1,0:T(8,128)(2,1)S(1)}, u32[]{:S(2)}, u32[]{:S(2)}) collective-permute-start(bf16[16,3712]{1,0:T(8,128)(2,1)S(1)} %get-tuple-element.31), channel_id=1, source_target_pairs={{0,6},{1,7},{2,4},{3,5},{4,2},{5,3},{6,0},{7,1},{8,14},{9,15},{10,... | collective-permute-start | bytes 356360 | tf_op jit(solution)/shard_map/ppermute | solution.py:289
  42.0 10.9 %collective-permute-start.13 = (bf16[16,3712]{1,0:T(8,128)(2,1)S(1)}, bf16[16,3712]{1,0:T(8,128)(2,1)S(1)}, u32[]{:S(2)}, u32[]{:S(2)}) collective-permute-start(bf16[16,3712]{1,0:T(8,128)(2,1)S(1)} %get-tuple-element.32), channel_id=1, source_target_pairs={{0,4},{1,5},{2,6},{3,7},{4,0},{5,1},{6,2},{7,3},{8,12},{9,13},{10,... | collective-permute-start | bytes 356360 | tf_op jit(solution)/shard_map/ppermute | solution.py:289
  45.2 7.7 %copy-start.2 = (s32[128,8]{0,1:T(8,128)S(1)}, s32[128,8]{0,1:T(8,128)}, u32[]{:S(2)}) copy-start(s32[128,8]{0,1:T(8,128)} %param.11) | copy-start | bytes 12292
  45.2 7.7 %copy-start.4 = (bf16[1,64,128]{2,1,0:T(8,128)(2,1)S(1)}, bf16[1,64,128]{2,1,0:T(8,128)(2,1)}, u32[]{:S(2)}) copy-start(bf16[1,64,128]{2,1,0:T(8,128)(2,1)} %get-tuple-element.25.placed_ref) | copy-start | bytes 49156
  45.2 7.7 %collective-permute-start.14 = (bf16[16,3712]{1,0:T(8,128)(2,1)S(1)}, bf16[16,3712]{1,0:T(8,128)(2,1)S(1)}, u32[]{:S(2)}, u32[]{:S(2)}) collective-permute-start(bf16[16,3712]{1,0:T(8,128)(2,1)S(1)} %get-tuple-element.33), channel_id=1, source_target_pairs={{0,2},{1,3},{2,0},{3,1},{4,6},{5,7},{6,4},{7,5},{8,10},{9,11},{10,... | collective-permute-start | bytes 356360 | tf_op jit(solution)/shard_map/ppermute | solution.py:289
  52.8 2.2 %collective-permute-start.18 = (bf16[3,128,896]{2,1,0:T(8,128)(2,1)S(1)}, bf16[3,128,896]{2,1,0:T(8,128)(2,1)S(1)}, u32[]{:S(2)}, u32[]{:S(2)}) collective-permute-start(bf16[3,128,896]{2,1,0:T(8,128)(2,1)S(1)} %shard_map.134), channel_id=1, source_target_pairs={{0,1},{1,0},{2,3},{3,2},{4,5},{5,4},{6,7},{7,6},{8,9},{9,8},{10,11... | collective-permute-start | bytes 2064392 | tf_op jit(solution)/shard_map/ppermute | solution.py:289

commit v10 on v9

--- a/solution.py
+++ b/solution.py
@@ -127,6 +127,25 @@
         copy.wait()
 
 
+def near_groups(rep):
+    return [k for k in range(1, rep) if k & (k - 1) == 0]
+
+
+def far_groups(rep):
+    return [k for k in range(1, rep) if k & (k - 1)]
+
+
+def columns_kernel(groups, count, *refs):
+    blocks, outs = refs[:count], refs[count:]
+    rows, width = count * SLOT, outs[0].shape[1]
+    for k, out in zip(groups, outs):
+        for part in range(2):
+            n = 2 * k + part
+            for j in range(count):
+                start = part * rows + j * SLOT
+                out[start : start + SLOT] = blocks[j][:, n * width : (n + 1) * width]
+
+
 def half_kernel(start, all_ref, half_ref):
     half_ref[...] = all_ref[start : start + half_ref.shape[0]]
 
@@ -135,6 +154,7 @@
     blocks, pieces = refs[: 2 * count], refs[2 * count : 2 * count + len(spans)]
     outs, cap, sem = refs[2 * count + len(spans) : -2], refs[-2], refs[-1]
     own_ref, other_ref, grads_ref, here_ref, away_refs = *outs[:4], outs[4:]
+    far = far_groups(rep)
     cap_copy = pltpu.make_async_copy(cap_ref, cap, sem)
     cap_copy.start()
     width = here_ref.shape[2]
@@ -152,9 +172,9 @@
             inputs[part].append(chosen)
             if k == 0:
                 here_ref[part] = chosen
-            else:
+            elif k in far:
                 some = slice(part * own_rows, (part + 1) * own_rows)
-                away_refs[k - 1][some, :width] = chosen[:own_rows]
+                away_refs[far.index(k)][some, :width] = chosen[:own_rows]
     sum_x, sum_d = 0.0, 0.0
     for (k, start, stop), piece in zip(spans, pieces):
         sum_x = sum_x + dot(inputs[0][k][:, start:stop], piece[:, : 2 * units])
@@ -217,8 +237,10 @@
         refs[-1][k] = ref[:, : refs[-1].shape[2]]
 
 
-def weight_kernel(rep, here_ref, grads_ref, other_ref, *refs):
-    away, outs, held, sems = refs[: rep - 1], refs[rep - 1 : -4], refs[-4:-1], refs[-1]
+def weight_kernel(rep, here_ref, grads_ref, near_ref, near_other, far_other, *refs):
+    near, far = len(near_groups(rep)), len(far_groups(rep))
+    near_grads, away, outs = refs[:near], refs[near : near + far], refs[near + far : -4]
+    held, sems = refs[-4:-1], refs[-1]
     units = outs[0].shape[1]
     width = here_ref.shape[2]
     half = grads_ref.shape[0] // 2
@@ -227,8 +249,11 @@
         some = slice(part * half, (part + 1) * half)
         rows = [here_ref[part]]
         got = [grads_ref[:, columns]]
+        for k, ref in enumerate(near_grads):
+            rows += [near_ref[k, some], near_other[k, some]]
+            got.append(ref[:, columns])
         for k, ref in enumerate(away):
-            rows += [ref[some, :width], other_ref[k, some]]
+            rows += [ref[some, :width], far_other[k, some]]
             got.append(ref[:, width + columns.start : width + columns.stop])
         rows = jnp.concatenate(rows, axis=0)
         got = jnp.concatenate(got, axis=0)
@@ -313,7 +338,7 @@
 
     half = width // 2
     whole = {0: weights}
-    halves = {}
+    halves, sent = {}, []
     for k in range(1, rep):
         low, high = k & -k, 1 << (k.bit_length() - 1)
         if low == high:
@@ -321,6 +346,7 @@
             for h in range(2):
                 kernel = functools.partial(half_kernel, h * half)
                 (halves[k, h],) = call(kernel, [shape((half, 3 * units))], [whole[k]])
+                sent.append(halves[k, h])
         else:
             halves[k, 0] = send(halves[k ^ low, 0], low, 0)
             halves[k, 1] = send(halves[k ^ high, 1], high, 0)
@@ -335,6 +361,12 @@
 
     order = [turned(n) for n in range(count)]
     blocks = [send(pays[j // CHIPS], 0, CORES * j) if j else pays[0] for j in order]
+    near, far = near_groups(rep), far_groups(rep)
+    columns = call(
+        functools.partial(columns_kernel, near, count),
+        [shape((2 * rows, width))] * len(near),
+        [after(blocks[0], *sent)] + blocks[1:],
+    )
     nearest = blocks[order.index(1)]
     ready = [after(b, nearest) if j == 0 else b for j, b in zip(order, blocks)]
     blocks = blocks + [send(block, 0, 1) for block in ready]
@@ -342,23 +374,39 @@
         functools.partial(hidden_kernel, rep, count, tuple(spans)),
         [shape((rows, model_dim + LANES))] * 2
         + [shape((2 * rows, 3 * units)), shape((2, 2 * rows, width))]
-        + [shape((2 * rows, width + 3 * units))] * (rep - 1),
+        + [shape((2 * rows, width + 3 * units))] * len(far_groups(rep)),
         [caps] + blocks + pieces,
         stored=(0,),
         scratch=[pltpu.SMEM(caps.shape, jnp.int32), pltpu.SemaphoreType.DMA(())],
         flops=2 * 2 * rows * model_dim * 5 * units,
     )
     own, other, grads, here, away = *results[:4], results[4:]
-    summed = call(sum_kernel, [shape((SLOT, model_dim + LANES))] * count, [own, send(other, 0, 1)])
+    moved = [send(part, k, 0) for k, part in zip(near, columns)]
+    (near_rows,) = call(
+        stack_kernel,
+        [shape((len(near), 2 * rows, width))],
+        moved,
+        flops=64000 * rows * width,
+    )
+    near_other = send(near_rows, 0, 1)
+    summed = call(
+        sum_kernel,
+        [shape((SLOT, model_dim + LANES))] * count,
+        [after(own, near_rows), send(other, 0, 1)],
+        flops=2 * rows * model_dim,
+    )
     backs = [send(part, 0, CORES * j) if j else part for j, part in zip(order, summed)]
 
-    moved = [send(away[k - 1], k, 0) for k in range(1, rep)]
-    (own_rows,) = call(stack_kernel, [shape((rep - 1, 2 * rows, width))], moved)
-    other_rows = send(own_rows, 0, 1)
+    moved = [send(part, k, 0) for k, part in zip(far, away)]
+    ready = [after(moved[0], backs[0])] + moved[1:]
+    (far_rows,) = call(stack_kernel, [shape((len(far), 2 * rows, width))], ready)
+    far_other = send(far_rows, 0, 1)
+    late = after(grads, summed[0])
+    near_grads = [send(late, k, 0) for k in near]
     grad_gate, grad_up, grad_down = call(
         functools.partial(weight_kernel, rep),
         [shape((width, units))] * 3,
-        [here, grads, other_rows] + moved,
+        [here, grads, near_rows, near_other, far_other] + near_grads + moved,
         kept=(0, 1, 2),
         scratch=[pltpu.VMEM((width, units), BF16)] * 3 + [pltpu.SemaphoreType.DMA((3,))],
         flops=2 * 2 * rep * rows * width * 3 * units,

time: 56.6 us -> 62.7 us (1.11)
  waiting for transfers between devices: 25.6 us -> 32.1 us
    ppermute x19 -> x22, waiting for transfers between devices: 25.6 us -> 32.1 us  [send(): return lax.ppermute(array, ('rep', 'ep'), pairs)]
    ppermute x19 -> x22, starting transfers between devices: 22.4 us -> 21.9 us  [send(): return lax.ppermute(array, ('rep', 'ep'), pairs)]
    pallas_call x8 -> x10, Pallas kernels: 7.71 us -> 7.71 us  [call(): pl.pallas_call(kernel, out_shape=tuple(outs), in_specs=[HBM if n in store...]
  transfers between devices with their start and end apart: 19 -> 22, of which waited for: 11 -> 9; matrix products, arithmetic and copies ran while one was open for 0% -> 0% of each run, Pallas kernels for 3% -> 6%
where the time goes in v10:
time: 62.7 us; the launch traced here: 62.5 us
  waiting for transfers between devices  32.1 us (51%)
  starting transfers between devices  21.9 us (35%)
  Pallas kernels  7.71 us (12%)
  between operations  0.8 us (1%)
    ppermute x22, waiting for transfers between devices, send(): return lax.ppermute(array, ('rep', 'ep'), pairs)  32.1 us
    ppermute x22, starting transfers between devices, send(): return lax.ppermute(array, ('rep', 'ep'), pairs)  21.9 us
    pallas_call x10, Pallas kernels, call(): pl.pallas_call(kernel, out_shape=tuple(outs), in_specs=[HBM if n in store...  7.71 us
  transfers between devices with their start and end apart: 22, of which 9 were waited for; matrix products, arithmetic and copies ran while one was open for 0% of the time, Pallas kernels for 6%

profile of v10, /device:TPU:0, one launch (start us, length us, event | category | flops | bytes accessed | tf_op | source)
XLA Modules:
  0.0 62.5 jit_solution(1116145246114112825)
XLA Ops:
  0.6 2.9 %shard_map.128 = (bf16[16,7296]{1,0:T(8,128)(2,1)}, bf16[1,64,128]{2,1,0:T(8,128)(2,1)}, bf16[896,384]{1,0:T(8,128)(2,1)}) custom-call(s32[4]{0:T(128)} %live_ref.1, bf16[128,3584]{1,0:T(8,128)(2,1)} %tok_ref.1, bf16[128,3584]{1,0:T(8,128)(2,1)} %grad_ref.1, s32[8,128]{1,0:T(8,128)} %bitcast.4, bf16[8,128]{1,0:T(8,128)(2,1)} %bitcast.7, ...), custom_call_target="tpu_custom_call" | custom-call | bytes 3467280 | tf_op jit(solution)/shard_map/pallas_call | solution.py:32
  3.5 3.0 %collective-permute-start.8 = (bf16[896,384]{1,0:T(8,128)(2,1)}, bf16[896,384]{1,0:T(8,128)(2,1)S(1)}, u32[]{:S(2)}, u32[]{:S(2)}) collective-permute-start(bf16[896,384]{1,0:T(8,128)(2,1)} %get-tuple-element.32.refs_8_), channel_id=1, source_target_pairs={{0,16},{1,17},{2,18},{3,19},{4,20},{5,21},{6,22},{7,23},{8,24},{9,... | collective-permute-start | bytes 2064392 | tf_op jit(solution)/shard_map/ppermute | solution.py:314
  6.5 1.5 %collective-permute-start.7 = (bf16[896,384]{1,0:T(8,128)(2,1)}, bf16[896,384]{1,0:T(8,128)(2,1)S(1)}, u32[]{:S(2)}, u32[]{:S(2)}) collective-permute-start(bf16[896,384]{1,0:T(8,128)(2,1)} %get-tuple-element.32.refs_8_), channel_id=1, source_target_pairs={{0,8},{1,9},{2,10},{3,11},{4,12},{5,13},{6,14},{7,15},{8,0},{9,1},... | collective-permute-start | bytes 2064392 | tf_op jit(solution)/shard_map/ppermute | solution.py:314
  8.0 1.6 %collective-permute-start.2 = (bf16[16,7296]{1,0:T(8,128)(2,1)}, bf16[16,7296]{1,0:T(8,128)(2,1)S(1)}, u32[]{:S(2)}, u32[]{:S(2)}) collective-permute-start(bf16[16,7296]{1,0:T(8,128)(2,1)} %get-tuple-element.31.refs_3_), channel_id=1, source_target_pairs={{0,2},{1,3},{2,0},{3,1},{4,6},{5,7},{6,4},{7,5},{8,10},{9,11},{10,... | collective-permute-start | bytes 700424 | tf_op jit(solution)/shard_map/ppermute | solution.py:314
  9.6 2.6 %collective-permute-start.1 = (bf16[16,7296]{1,0:T(8,128)(2,1)}, bf16[16,7296]{1,0:T(8,128)(2,1)S(1)}, u32[]{:S(2)}, u32[]{:S(2)}) collective-permute-start(bf16[16,7296]{1,0:T(8,128)(2,1)} %get-tuple-element.31.refs_3_), channel_id=1, source_target_pairs={{0,4},{1,5},{2,6},{3,7},{4,0},{5,1},{6,2},{7,3},{8,12},{9,13},{10,... | collective-permute-start | bytes 700424 | tf_op jit(solution)/shard_map/ppermute | solution.py:314
  12.2 0.2 collective-permute-start
  12.4 6.6 %collective-permute-done.2.refs_2_ = bf16[16,7296]{1,0:T(8,128)(2,1)S(1)} collective-permute-done((bf16[16,7296]{1,0:T(8,128)(2,1)}, bf16[16,7296]{1,0:T(8,128)(2,1)S(1)}, u32[]{:S(2)}, u32[]{:S(2)}) %collective-permute-start.2) | collective-permute-done | bytes 233504 | tf_op jit(solution)/shard_map/ppermute | solution.py:314
  19.1 3.1 %collective-permute-done.8.all_ref.refs_10_ = bf16[896,384]{1,0:T(8,128)(2,1)S(1)} collective-permute-done((bf16[896,384]{1,0:T(8,128)(2,1)}, bf16[896,384]{1,0:T(8,128)(2,1)S(1)}, u32[]{:S(2)}, u32[]{:S(2)}) %collective-permute-start.8) | collective-permute-done | bytes 688160 | tf_op jit(solution)/shard_map/ppermute | solution.py:314
  22.2 1.8 %collective-permute-start.9 = (bf16[448,384]{1,0:T(8,128)(2,1)S(1)}, bf16[448,384]{1,0:T(8,128)(2,1)S(1)}, u32[]{:S(2)}, u32[]{:S(2)}) collective-permute-start(bf16[448,384]{1,0:T(8,128)(2,1)S(1)} %shard_map.129), channel_id=1, source_target_pairs={{0,8},{1,9},{2,10},{3,11},{4,12},{5,13},{6,14},{7,15},{8,0},{9,1},... | collective-permute-start | bytes 1032200 | tf_op jit(solution)/shard_map/ppermute | solution.py:314
  24.1 1.6 %collective-permute-start.10 = (bf16[448,384]{1,0:T(8,128)(2,1)S(1)}, bf16[448,384]{1,0:T(8,128)(2,1)S(1)}, u32[]{:S(2)}, u32[]{:S(2)}) collective-permute-start(bf16[448,384]{1,0:T(8,128)(2,1)S(1)} %shard_map.130), channel_id=1, source_target_pairs={{0,16},{1,17},{2,18},{3,19},{4,20},{5,21},{6,22},{7,23},{8,24},{9,... | collective-permute-start | bytes 1032200 | tf_op jit(solution)/shard_map/ppermute | solution.py:314
  25.7 3.7 %collective-permute-done.1.refs_1_ = bf16[16,7296]{1,0:T(8,128)(2,1)S(1)} collective-permute-done((bf16[16,7296]{1,0:T(8,128)(2,1)}, bf16[16,7296]{1,0:T(8,128)(2,1)S(1)}, u32[]{:S(2)}, u32[]{:S(2)}) %collective-permute-start.1) | collective-permute-done | bytes 233504 | tf_op jit(solution)/shard_map/ppermute | solution.py:314
  29.4 0.5 collective-permute-start.4
  29.9 0.1 collective-permute-start.3
  30.0 0.9 %collective-permute-done.5.refs_6_ = bf16[16,7296]{1,0:T(8,128)(2,1)S(1)} collective-permute-done((bf16[16,7296]{1,0:T(8,128)(2,1)S(1)}, bf16[16,7296]{1,0:T(8,128)(2,1)S(1)}, u32[]{:S(2)}, u32[]{:S(2)}) %collective-permute-start.5) | collective-permute-done | bytes 233504 | tf_op jit(solution)/shard_map/ppermute | solution.py:314
  30.9 0.5 collective-permute-start.11
  31.4 0.5 collective-permute-start.12
  31.9 0.9 %collective-permute-done.10.refs_12_ = bf16[448,384]{1,0:T(8,128)(2,1)S(1)} collective-permute-done((bf16[448,384]{1,0:T(8,128)(2,1)S(1)}, bf16[448,384]{1,0:T(8,128)(2,1)S(1)}, u32[]{:S(2)}, u32[]{:S(2)}) %collective-permute-start.10) | collective-permute-done | bytes 344096 | tf_op jit(solution)/shard_map/ppermute | solution.py:314
  32.8 1.7 %shard_map.131 = (bf16[64,3712]{1,0:T(8,128)(2,1)S(1)}, bf16[64,3712]{1,0:T(8,128)(2,1)S(1)}, bf16[128,384]{1,0:T(8,128)(2,1)S(1)}, bf16[2,128,896]{2,1,0:T(8,128)(2,1)S(1)}, bf16[128,1280]{1,0:T(8,128)(2,1)S(1)}) custom-call(s32[1,4]{1,0:T(1,128)S(1)} %bitcast.6, bf16[16,7296]{1,0:T(8,128)(2,1)S(1)} %collective-permute-done.refs_0_, ...), custom_call_target="tpu_custom_call" | custom-call | flops 587202560 | bytes 6455312 | tf_op jit(solution)/shard_map/pallas_call | solution.py:32
  34.5 0.1 collective-permute-start.13
  34.6 1.7 %collective-permute-start.18 = (bf16[128,1280]{1,0:T(8,128)(2,1)S(1)}, bf16[128,1280]{1,0:T(8,128)(2,1)S(1)}, u32[]{:S(2)}, u32[]{:S(2)}) collective-permute-start(bf16[128,1280]{1,0:T(8,128)(2,1)S(1)} %get-tuple-element.47), channel_id=1, source_target_pairs={{0,24},{1,25},{2,26},{3,27},{4,28},{5,29},{6,30},{7,31},{8,16},{9,... | collective-permute-start | bytes 983048 | tf_op jit(solution)/shard_map/ppermute | solution.py:314
  36.3 2.2 %collective-permute-done.11.refs_0_ = bf16[128,896]{1,0:T(8,128)(2,1)S(1)} collective-permute-done((bf16[128,896]{1,0:T(8,128)(2,1)S(1)}, bf16[128,896]{1,0:T(8,128)(2,1)S(1)}, u32[]{:S(2)}, u32[]{:S(2)}) %collective-permute-start.11) | collective-permute-done | bytes 229408 | tf_op jit(solution)/shard_map/ppermute | solution.py:314
  38.5 7.4 %collective-permute-done.12.refs_1_ = bf16[128,896]{1,0:T(8,128)(2,1)S(1)} collective-permute-done((bf16[128,896]{1,0:T(8,128)(2,1)S(1)}, bf16[128,896]{1,0:T(8,128)(2,1)S(1)}, u32[]{:S(2)}, u32[]{:S(2)}) %collective-permute-start.12) | collective-permute-done | bytes 229408 | tf_op jit(solution)/shard_map/ppermute | solution.py:314
  46.0 0.1 shard_map.134
  46.1 0.1 collective-permute-start.14
  46.2 4.7 %collective-permute-start.15 = (bf16[16,3712]{1,0:T(8,128)(2,1)S(1)}, bf16[16,3712]{1,0:T(8,128)(2,1)S(1)}, u32[]{:S(2)}, u32[]{:S(2)}) collective-permute-start(bf16[16,3712]{1,0:T(8,128)(2,1)S(1)} %get-tuple-element.40), channel_id=1, source_target_pairs={{0,4},{1,5},{2,6},{3,7},{4,0},{5,1},{6,2},{7,3},{8,12},{9,13},{10,... | collective-permute-start | bytes 356360 | tf_op jit(solution)/shard_map/ppermute | solution.py:314
  50.8 0.1 collective-permute-start.16
  50.9 0.1 collective-permute-start.21
  51.0 1.9 %collective-permute-done.14.refs_0_ = bf16[16,3712]{1,0:T(8,128)(2,1)S(1)} collective-permute-done((bf16[16,3712]{1,0:T(8,128)(2,1)S(1)}, bf16[16,3712]{1,0:T(8,128)(2,1)S(1)}, u32[]{:S(2)}, u32[]{:S(2)}) %collective-permute-start.14) | collective-permute-done | bytes 118816 | tf_op jit(solution)/shard_map/ppermute | solution.py:314
  53.0 1.3 %collective-permute-start.20 = (bf16[128,384]{1,0:T(8,128)(2,1)S(1)}, bf16[128,384]{1,0:T(8,128)(2,1)S(1)}, u32[]{:S(2)}, u32[]{:S(2)}) collective-permute-start(bf16[128,384]{1,0:T(8,128)(2,1)S(1)} %get-tuple-element.49.grads_ref), channel_id=1, source_target_pairs={{0,8},{1,9},{2,10},{3,11},{4,12},{5,13},{6,14},{7,15},{8,0},{9,1},... | collective-permute-start | bytes 294920 | tf_op jit(solution)/shard_map/ppermute | solution.py:314
  54.3 5.3 %collective-permute-done.15.refs_1_ = bf16[16,3712]{1,0:T(8,128)(2,1)S(1)} collective-permute-done((bf16[16,3712]{1,0:T(8,128)(2,1)S(1)}, bf16[16,3712]{1,0:T(8,128)(2,1)S(1)}, u32[]{:S(2)}, u32[]{:S(2)}) %collective-permute-start.15) | collective-permute-done | bytes 118816 | tf_op jit(solution)/shard_map/ppermute | solution.py:314
  59.6 1.4 %shard_map.135 = (bf16[128,3584]{1,0:T(8,128)(2,1)}, f32[8,128]{1,0:T(8,128)}) custom-call(s32[8,128]{1,0:T(8,128)S(1)} %bitcast.5, bf16[1,64,128]{2,1,0:T(8,128)(2,1)S(1)} %copy-done.4, bf16[16,3712]{1,0:T(8,128)(2,1)S(1)} %collective-permute-done.14.refs_0_, bf16[16,3712]{1,0:T(8,128)(2,1)S(1)} %collective-permute-done.15.refs_1_, ...), custom_call_target="tpu_custom_call" | custom-call | flops 58720256000 | bytes 1417216 | tf_op jit(solution)/shard_map/pallas_call | solution.py:32
  61.1 1.4 %shard_map.137 = (bf16[896,128]{1,0:T(8,128)(2,1)}, bf16[896,128]{1,0:T(8,128)(2,1)}, bf16[896,128]{1,0:T(8,128)(2,1)}) custom-call(bf16[2,128,896]{2,1,0:T(8,128)(2,1)S(1)} %get-tuple-element.45.here_ref, bf16[128,384]{1,0:T(8,128)(2,1)S(1)} %get-tuple-element.49.grads_ref, bf16[2,128,896]{2,1,0:T(8,128)(2,1)S(1)} %shard_map.133.near_ref, ...), custom_call_target="tpu_custom_call" | custom-call | flops 352321536 | bytes 2916352 | tf_op jit(solution)/shard_map/pallas_call | solution.py:32
  (32 shorter events, 0.2 us)
Async XLA Ops:
  3.5 18.7 %collective-permute-start.8 = (bf16[896,384]{1,0:T(8,128)(2,1)}, bf16[896,384]{1,0:T(8,128)(2,1)S(1)}, u32[]{:S(2)}, u32[]{:S(2)}) collective-permute-start(bf16[896,384]{1,0:T(8,128)(2,1)} %get-tuple-element.32.refs_8_), channel_id=1, source_target_pairs={{0,16},{1,17},{2,18},{3,19},{4,20},{5,21},{6,22},{7,23},{8,24},{9,... | collective-permute-start | bytes 2064392 | tf_op jit(solution)/shard_map/ppermute | solution.py:314
  6.5 17.5 %collective-permute-start.7 = (bf16[896,384]{1,0:T(8,128)(2,1)}, bf16[896,384]{1,0:T(8,128)(2,1)S(1)}, u32[]{:S(2)}, u32[]{:S(2)}) collective-permute-start(bf16[896,384]{1,0:T(8,128)(2,1)} %get-tuple-element.32.refs_8_), channel_id=1, source_target_pairs={{0,8},{1,9},{2,10},{3,11},{4,12},{5,13},{6,14},{7,15},{8,0},{9,1},... | collective-permute-start | bytes 2064392 | tf_op jit(solution)/shard_map/ppermute | solution.py:314
  8.0 11.0 %collective-permute-start.2 = (bf16[16,7296]{1,0:T(8,128)(2,1)}, bf16[16,7296]{1,0:T(8,128)(2,1)S(1)}, u32[]{:S(2)}, u32[]{:S(2)}) collective-permute-start(bf16[16,7296]{1,0:T(8,128)(2,1)} %get-tuple-element.31.refs_3_), channel_id=1, source_target_pairs={{0,2},{1,3},{2,0},{3,1},{4,6},{5,7},{6,4},{7,5},{8,10},{9,11},{10,... | collective-permute-start | bytes 700424 | tf_op jit(solution)/shard_map/ppermute | solution.py:314
  9.6 19.7 %collective-permute-start.1 = (bf16[16,7296]{1,0:T(8,128)(2,1)}, bf16[16,7296]{1,0:T(8,128)(2,1)S(1)}, u32[]{:S(2)}, u32[]{:S(2)}) collective-permute-start(bf16[16,7296]{1,0:T(8,128)(2,1)} %get-tuple-element.31.refs_3_), channel_id=1, source_target_pairs={{0,4},{1,5},{2,6},{3,7},{4,0},{5,1},{6,2},{7,3},{8,12},{9,13},{10,... | collective-permute-start | bytes 700424 | tf_op jit(solution)/shard_map/ppermute | solution.py:314
  12.2 17.2 %collective-permute-start = (bf16[16,7296]{1,0:T(8,128)(2,1)}, bf16[16,7296]{1,0:T(8,128)(2,1)S(1)}, u32[]{:S(2)}, u32[]{:S(2)}) collective-permute-start(bf16[16,7296]{1,0:T(8,128)(2,1)} %get-tuple-element.31.refs_3_), channel_id=1, source_target_pairs={{0,6},{1,7},{2,4},{3,5},{4,2},{5,3},{6,0},{7,1},{8,14},{9,15},{10,... | collective-permute-start | bytes 700424 | tf_op jit(solution)/shard_map/ppermute | solution.py:314
  19.1 10.8 %collective-permute-start.6 = (bf16[16,7296]{1,0:T(8,128)(2,1)}, bf16[16,7296]{1,0:T(8,128)(2,1)S(1)}, u32[]{:S(2)}, u32[]{:S(2)}) collective-permute-start(bf16[16,7296]{1,0:T(8,128)(2,1)} %get-tuple-element.31.refs_3_), channel_id=1, source_target_pairs={{0,1},{1,0},{2,3},{3,2},{4,5},{5,4},{6,7},{7,6},{8,9},{9,8},{10,11... | collective-permute-start | bytes 700424 | tf_op jit(solution)/shard_map/ppermute | solution.py:314
  22.2 7.7 %copy-start = (bf16[16,7296]{1,0:T(8,128)(2,1)S(1)}, bf16[16,7296]{1,0:T(8,128)(2,1)}, u32[]{:S(2)}) copy-start(bf16[16,7296]{1,0:T(8,128)(2,1)} %get-tuple-element.31.refs_3_) | copy-start | bytes 700420
  22.2 9.7 %collective-permute-start.9 = (bf16[448,384]{1,0:T(8,128)(2,1)S(1)}, bf16[448,384]{1,0:T(8,128)(2,1)S(1)}, u32[]{:S(2)}, u32[]{:S(2)}) collective-permute-start(bf16[448,384]{1,0:T(8,128)(2,1)S(1)} %shard_map.129), channel_id=1, source_target_pairs={{0,8},{1,9},{2,10},{3,11},{4,12},{5,13},{6,14},{7,15},{8,0},{9,1},... | collective-permute-start | bytes 1032200 | tf_op jit(solution)/shard_map/ppermute | solution.py:314
  24.1 8.7 %copy-start.1 = (bf16[896,384]{1,0:T(8,128)(2,1)S(1)}, bf16[896,384]{1,0:T(8,128)(2,1)}, u32[]{:S(2)}) copy-start(bf16[896,384]{1,0:T(8,128)(2,1)} %get-tuple-element.32.refs_8_) | copy-start | bytes 2064388
  24.1 8.7 %collective-permute-start.10 = (bf16[448,384]{1,0:T(8,128)(2,1)S(1)}, bf16[448,384]{1,0:T(8,128)(2,1)S(1)}, u32[]{:S(2)}, u32[]{:S(2)}) collective-permute-start(bf16[448,384]{1,0:T(8,128)(2,1)S(1)} %shard_map.130), channel_id=1, source_target_pairs={{0,16},{1,17},{2,18},{3,19},{4,20},{5,21},{6,22},{7,23},{8,24},{9,... | collective-permute-start | bytes 1032200 | tf_op jit(solution)/shard_map/ppermute | solution.py:314
  29.4 1.5 %collective-permute-start.5 = (bf16[16,7296]{1,0:T(8,128)(2,1)S(1)}, bf16[16,7296]{1,0:T(8,128)(2,1)S(1)}, u32[]{:S(2)}, u32[]{:S(2)}) collective-permute-start(bf16[16,7296]{1,0:T(8,128)(2,1)S(1)} %collective-permute-done.2.refs_2_), channel_id=1, source_target_pairs={{0,1},{1,0},{2,3},{3,2},{4,5},{5,4},{6,7},{7,6},{8,9},{9,8},{10,11... | collective-permute-start | bytes 700424 | tf_op jit(solution)/shard_map/ppermute | solution.py:314
  29.4 2.0 %collective-permute-start.4 = (bf16[16,7296]{1,0:T(8,128)(2,1)S(1)}, bf16[16,7296]{1,0:T(8,128)(2,1)S(1)}, u32[]{:S(2)}, u32[]{:S(2)}) collective-permute-start(bf16[16,7296]{1,0:T(8,128)(2,1)S(1)} %collective-permute-done.1.refs_1_), channel_id=1, source_target_pairs={{0,1},{1,0},{2,3},{3,2},{4,5},{5,4},{6,7},{7,6},{8,9},{9,8},{10,11... | collective-permute-start | bytes 700424 | tf_op jit(solution)/shard_map/ppermute | solution.py:314
  29.9 2.0 %collective-permute-start.3 = (bf16[16,7296]{1,0:T(8,128)(2,1)S(1)}, bf16[16,7296]{1,0:T(8,128)(2,1)S(1)}, u32[]{:S(2)}, u32[]{:S(2)}) collective-permute-start(bf16[16,7296]{1,0:T(8,128)(2,1)S(1)} %collective-permute-done.refs_0_), channel_id=1, source_target_pairs={{0,1},{1,0},{2,3},{3,2},{4,5},{5,4},{6,7},{7,6},{8,9},{9,8},{10,11... | collective-permute-start | bytes 700424 | tf_op jit(solution)/shard_map/ppermute | solution.py:314
  30.9 7.6 %collective-permute-start.11 = (bf16[128,896]{1,0:T(8,128)(2,1)S(1)}, bf16[128,896]{1,0:T(8,128)(2,1)S(1)}, u32[]{:S(2)}, u32[]{:S(2)}) collective-permute-start(bf16[128,896]{1,0:T(8,128)(2,1)S(1)} %get-tuple-element.35), channel_id=1, source_target_pairs={{0,8},{1,9},{2,10},{3,11},{4,12},{5,13},{6,14},{7,15},{8,0},{9,1},... | collective-permute-start | bytes 688136 | tf_op jit(solution)/shard_map/ppermute | solution.py:314
  31.4 1.4 %copy-start.3 = (s32[4,1]{0,1:T(1,128)S(1)}, s32[4,1]{0,1:T(1,128)}, u32[]{:S(2)}) copy-start(s32[4,1]{0,1:T(1,128)} %param.14) | copy-start | bytes 52
  31.4 14.5 %collective-permute-start.12 = (bf16[128,896]{1,0:T(8,128)(2,1)S(1)}, bf16[128,896]{1,0:T(8,128)(2,1)S(1)}, u32[]{:S(2)}, u32[]{:S(2)}) collective-permute-start(bf16[128,896]{1,0:T(8,128)(2,1)S(1)} %get-tuple-element.36), channel_id=1, source_target_pairs={{0,16},{1,17},{2,18},{3,19},{4,20},{5,21},{6,22},{7,23},{8,24},{9,... | collective-permute-start | bytes 688136 | tf_op jit(solution)/shard_map/ppermute | solution.py:314
  34.5 11.4 %collective-permute-start.13 = (bf16[64,3712]{1,0:T(8,128)(2,1)S(1)}, bf16[64,3712]{1,0:T(8,128)(2,1)S(1)}, u32[]{:S(2)}, u32[]{:S(2)}) collective-permute-start(bf16[64,3712]{1,0:T(8,128)(2,1)S(1)} %get-tuple-element.38), channel_id=1, source_target_pairs={{0,1},{1,0},{2,3},{3,2},{4,5},{5,4},{6,7},{7,6},{8,9},{9,8},{10,11... | collective-permute-start | bytes 1425416 | tf_op jit(solution)/shard_map/ppermute | solution.py:314
  34.6 16.3 %collective-permute-start.18 = (bf16[128,1280]{1,0:T(8,128)(2,1)S(1)}, bf16[128,1280]{1,0:T(8,128)(2,1)S(1)}, u32[]{:S(2)}, u32[]{:S(2)}) collective-permute-start(bf16[128,1280]{1,0:T(8,128)(2,1)S(1)} %get-tuple-element.47), channel_id=1, source_target_pairs={{0,24},{1,25},{2,26},{3,27},{4,28},{5,29},{6,30},{7,31},{8,16},{9,... | collective-permute-start | bytes 983048 | tf_op jit(solution)/shard_map/ppermute | solution.py:314
  46.1 6.9 %collective-permute-start.14 = (bf16[16,3712]{1,0:T(8,128)(2,1)S(1)}, bf16[16,3712]{1,0:T(8,128)(2,1)S(1)}, u32[]{:S(2)}, u32[]{:S(2)}) collective-permute-start(bf16[16,3712]{1,0:T(8,128)(2,1)S(1)} %get-tuple-element.39), channel_id=1, source_target_pairs={{0,6},{1,7},{2,4},{3,5},{4,2},{5,3},{6,0},{7,1},{8,14},{9,15},{10,... | collective-permute-start | bytes 356360 | tf_op jit(solution)/shard_map/ppermute | solution.py:314
  46.2 13.4 %collective-permute-start.15 = (bf16[16,3712]{1,0:T(8,128)(2,1)S(1)}, bf16[16,3712]{1,0:T(8,128)(2,1)S(1)}, u32[]{:S(2)}, u32[]{:S(2)}) collective-permute-start(bf16[16,3712]{1,0:T(8,128)(2,1)S(1)} %get-tuple-element.40), channel_id=1, source_target_pairs={{0,4},{1,5},{2,6},{3,7},{4,0},{5,1},{6,2},{7,3},{8,12},{9,13},{10,... | collective-permute-start | bytes 356360 | tf_op jit(solution)/shard_map/ppermute | solution.py:314
  50.8 8.8 %collective-permute-start.16 = (bf16[16,3712]{1,0:T(8,128)(2,1)S(1)}, bf16[16,3712]{1,0:T(8,128)(2,1)S(1)}, u32[]{:S(2)}, u32[]{:S(2)}) collective-permute-start(bf16[16,3712]{1,0:T(8,128)(2,1)S(1)} %get-tuple-element.41), channel_id=1, source_target_pairs={{0,2},{1,3},{2,0},{3,1},{4,6},{5,7},{6,4},{7,5},{8,10},{9,11},{10,... | collective-permute-start | bytes 356360 | tf_op jit(solution)/shard_map/ppermute | solution.py:314
  50.9 10.2 %collective-permute-start.17 = (bf16[2,128,896]{2,1,0:T(8,128)(2,1)S(1)}, bf16[2,128,896]{2,1,0:T(8,128)(2,1)S(1)}, u32[]{:S(2)}, u32[]{:S(2)}) collective-permute-start(bf16[2,128,896]{2,1,0:T(8,128)(2,1)S(1)} %shard_map.133.near_ref), channel_id=1, source_target_pairs={{0,1},{1,0},{2,3},{3,2},{4,5},{5,4},{6,7},{7,6},{8,9},{9,8},{10,11... | collective-permute-start | bytes 1376264 | tf_op jit(solution)/shard_map/ppermute | solution.py:314
  50.9 8.7 %copy-start.2 = (s32[128,8]{0,1:T(8,128)S(1)}, s32[128,8]{0,1:T(8,128)}, u32[]{:S(2)}) copy-start(s32[128,8]{0,1:T(8,128)} %param.11) | copy-start | bytes 12292
  50.9 8.7 %copy-start.4 = (bf16[1,64,128]{2,1,0:T(8,128)(2,1)S(1)}, bf16[1,64,128]{2,1,0:T(8,128)(2,1)}, u32[]{:S(2)}) copy-start(bf16[1,64,128]{2,1,0:T(8,128)(2,1)} %get-tuple-element.29.placed_ref) | copy-start | bytes 49156
  50.9 10.2 %collective-permute-start.21 = (bf16[128,384]{1,0:T(8,128)(2,1)S(1)}, bf16[128,384]{1,0:T(8,128)(2,1)S(1)}, u32[]{:S(2)}, u32[]{:S(2)}) collective-permute-start(bf16[128,384]{1,0:T(8,128)(2,1)S(1)} %get-tuple-element.49.grads_ref), channel_id=1, source_target_pairs={{0,16},{1,17},{2,18},{3,19},{4,20},{5,21},{6,22},{7,23},{8,24},{9,... | collective-permute-start | bytes 294920 | tf_op jit(solution)/shard_map/ppermute | solution.py:314
  53.0 8.2 %collective-permute-start.20 = (bf16[128,384]{1,0:T(8,128)(2,1)S(1)}, bf16[128,384]{1,0:T(8,128)(2,1)S(1)}, u32[]{:S(2)}, u32[]{:S(2)}) collective-permute-start(bf16[128,384]{1,0:T(8,128)(2,1)S(1)} %get-tuple-element.49.grads_ref), channel_id=1, source_target_pairs={{0,8},{1,9},{2,10},{3,11},{4,12},{5,13},{6,14},{7,15},{8,0},{9,1},... | collective-permute-start | bytes 294920 | tf_op jit(solution)/shard_map/ppermute | solution.py:314
  59.6 1.5 %collective-permute-start.19 = (bf16[1,128,896]{2,1,0:T(8,128)(2,1)S(1)}, bf16[1,128,896]{2,1,0:T(8,128)(2,1)S(1)}, u32[]{:S(2)}, u32[]{:S(2)}) collective-permute-start(bf16[1,128,896]{2,1,0:T(8,128)(2,1)S(1)} %shard_map.136), channel_id=1, source_target_pairs={{0,1},{1,0},{2,3},{3,2},{4,5},{5,4},{6,7},{7,6},{8,9},{9,8},{10,11... | collective-permute-start | bytes 688136 | tf_op jit(solution)/shard_map/ppermute | solution.py:314

commit v11 on v9

--- a/solution.py
+++ b/solution.py
@@ -352,7 +352,9 @@
     summed = call(sum_kernel, [shape((SLOT, model_dim + LANES))] * count, [own, send(other, 0, 1)])
     backs = [send(part, 0, CORES * j) if j else part for j, part in zip(order, summed)]
 
-    moved = [send(away[k - 1], k, 0) for k in range(1, rep)]
+    moved = [
+        send(part if k & (k - 1) else after(part, summed[-2]), k, 0) for k, part in enumerate(away, 1)
+    ]
     (own_rows,) = call(stack_kernel, [shape((rep - 1, 2 * rows, width))], moved)
     other_rows = send(own_rows, 0, 1)
     grad_gate, grad_up, grad_down = call(

time: 56.6 us -> 56.6 us (level)
  transfers between devices with their start and end apart: 19 -> 19, of which waited for: 11 -> 12; matrix products, arithmetic and copies ran while one was open for 0% -> 0% of each run, Pallas kernels for 3% -> 3%
where the time goes in v11:
time: 56.6 us; the launch traced here: 56.5 us
  waiting for transfers between devices  25.6 us (45%)
  starting transfers between devices  22.4 us (40%)
  Pallas kernels  7.71 us (14%)
  between operations  0.75 us (1%)
    ppermute x19, waiting for transfers between devices, send(): return lax.ppermute(array, ('rep', 'ep'), pairs)  25.6 us
    ppermute x19, starting transfers between devices, send(): return lax.ppermute(array, ('rep', 'ep'), pairs)  22.4 us
    pallas_call x8, Pallas kernels, call(): pl.pallas_call(kernel, out_shape=tuple(outs), in_specs=[HBM if n in store...  7.71 us
  transfers between devices with their start and end apart: 19, of which 12 were waited for; matrix products, arithmetic and copies ran while one was open for 0% of the time, Pallas kernels for 3%

profile of v11, /device:TPU:0, one launch (start us, length us, event | category | flops | bytes accessed | tf_op | source)
XLA Modules:
  0.0 56.5 jit_solution(15275034791420559708)
XLA Ops:
  0.6 2.9 %shard_map.128 = (bf16[16,7296]{1,0:T(8,128)(2,1)}, bf16[1,64,128]{2,1,0:T(8,128)(2,1)}, bf16[896,384]{1,0:T(8,128)(2,1)}) custom-call(s32[4]{0:T(128)} %live_ref.1, bf16[128,3584]{1,0:T(8,128)(2,1)} %tok_ref.1, bf16[128,3584]{1,0:T(8,128)(2,1)} %grad_ref.1, s32[8,128]{1,0:T(8,128)} %bitcast.4, bf16[8,128]{1,0:T(8,128)(2,1)} %bitcast.7, ...), custom_call_target="tpu_custom_call" | custom-call | bytes 3467280 | tf_op jit(solution)/shard_map/pallas_call | solution.py:32
  3.5 3.0 %collective-permute-start.8 = (bf16[896,384]{1,0:T(8,128)(2,1)}, bf16[896,384]{1,0:T(8,128)(2,1)S(1)}, u32[]{:S(2)}, u32[]{:S(2)}) collective-permute-start(bf16[896,384]{1,0:T(8,128)(2,1)} %get-tuple-element.30.refs_8_), channel_id=1, source_target_pairs={{0,16},{1,17},{2,18},{3,19},{4,20},{5,21},{6,22},{7,23},{8,24},{9,... | collective-permute-start | bytes 2064392 | tf_op jit(solution)/shard_map/ppermute | solution.py:289
  6.6 1.5 %collective-permute-start.7 = (bf16[896,384]{1,0:T(8,128)(2,1)}, bf16[896,384]{1,0:T(8,128)(2,1)S(1)}, u32[]{:S(2)}, u32[]{:S(2)}) collective-permute-start(bf16[896,384]{1,0:T(8,128)(2,1)} %get-tuple-element.30.refs_8_), channel_id=1, source_target_pairs={{0,8},{1,9},{2,10},{3,11},{4,12},{5,13},{6,14},{7,15},{8,0},{9,1},... | collective-permute-start | bytes 2064392 | tf_op jit(solution)/shard_map/ppermute | solution.py:289
  8.1 1.6 %collective-permute-start.2 = (bf16[16,7296]{1,0:T(8,128)(2,1)}, bf16[16,7296]{1,0:T(8,128)(2,1)S(1)}, u32[]{:S(2)}, u32[]{:S(2)}) collective-permute-start(bf16[16,7296]{1,0:T(8,128)(2,1)} %get-tuple-element.29.refs_3_), channel_id=1, source_target_pairs={{0,2},{1,3},{2,0},{3,1},{4,6},{5,7},{6,4},{7,5},{8,10},{9,11},{10,... | collective-permute-start | bytes 700424 | tf_op jit(solution)/shard_map/ppermute | solution.py:289
  9.6 2.6 %collective-permute-start.1 = (bf16[16,7296]{1,0:T(8,128)(2,1)}, bf16[16,7296]{1,0:T(8,128)(2,1)S(1)}, u32[]{:S(2)}, u32[]{:S(2)}) collective-permute-start(bf16[16,7296]{1,0:T(8,128)(2,1)} %get-tuple-element.29.refs_3_), channel_id=1, source_target_pairs={{0,4},{1,5},{2,6},{3,7},{4,0},{5,1},{6,2},{7,3},{8,12},{9,13},{10,... | collective-permute-start | bytes 700424 | tf_op jit(solution)/shard_map/ppermute | solution.py:289
  12.2 0.2 collective-permute-start
  12.4 6.6 %collective-permute-done.2.refs_2_ = bf16[16,7296]{1,0:T(8,128)(2,1)S(1)} collective-permute-done((bf16[16,7296]{1,0:T(8,128)(2,1)}, bf16[16,7296]{1,0:T(8,128)(2,1)S(1)}, u32[]{:S(2)}, u32[]{:S(2)}) %collective-permute-start.2) | collective-permute-done | bytes 233504 | tf_op jit(solution)/shard_map/ppermute | solution.py:289
  19.1 3.1 %collective-permute-done.8.all_ref.refs_10_ = bf16[896,384]{1,0:T(8,128)(2,1)S(1)} collective-permute-done((bf16[896,384]{1,0:T(8,128)(2,1)}, bf16[896,384]{1,0:T(8,128)(2,1)S(1)}, u32[]{:S(2)}, u32[]{:S(2)}) %collective-permute-start.8) | collective-permute-done | bytes 688160 | tf_op jit(solution)/shard_map/ppermute | solution.py:289
  22.3 1.8 %collective-permute-start.9 = (bf16[448,384]{1,0:T(8,128)(2,1)S(1)}, bf16[448,384]{1,0:T(8,128)(2,1)S(1)}, u32[]{:S(2)}, u32[]{:S(2)}) collective-permute-start(bf16[448,384]{1,0:T(8,128)(2,1)S(1)} %shard_map.129), channel_id=1, source_target_pairs={{0,8},{1,9},{2,10},{3,11},{4,12},{5,13},{6,14},{7,15},{8,0},{9,1},... | collective-permute-start | bytes 1032200 | tf_op jit(solution)/shard_map/ppermute | solution.py:289
  24.1 1.6 %collective-permute-start.10 = (bf16[448,384]{1,0:T(8,128)(2,1)S(1)}, bf16[448,384]{1,0:T(8,128)(2,1)S(1)}, u32[]{:S(2)}, u32[]{:S(2)}) collective-permute-start(bf16[448,384]{1,0:T(8,128)(2,1)S(1)} %shard_map.130), channel_id=1, source_target_pairs={{0,16},{1,17},{2,18},{3,19},{4,20},{5,21},{6,22},{7,23},{8,24},{9,... | collective-permute-start | bytes 1032200 | tf_op jit(solution)/shard_map/ppermute | solution.py:289
  25.7 3.7 %collective-permute-done.1.refs_1_ = bf16[16,7296]{1,0:T(8,128)(2,1)S(1)} collective-permute-done((bf16[16,7296]{1,0:T(8,128)(2,1)}, bf16[16,7296]{1,0:T(8,128)(2,1)S(1)}, u32[]{:S(2)}, u32[]{:S(2)}) %collective-permute-start.1) | collective-permute-done | bytes 233504 | tf_op jit(solution)/shard_map/ppermute | solution.py:289
  29.4 0.5 collective-permute-start.4
  30.0 0.9 %collective-permute-done.5.refs_6_ = bf16[16,7296]{1,0:T(8,128)(2,1)S(1)} collective-permute-done((bf16[16,7296]{1,0:T(8,128)(2,1)S(1)}, bf16[16,7296]{1,0:T(8,128)(2,1)S(1)}, u32[]{:S(2)}, u32[]{:S(2)}) %collective-permute-start.5) | collective-permute-done | bytes 233504 | tf_op jit(solution)/shard_map/ppermute | solution.py:289
  30.9 0.3 collective-permute-done.4.refs_5_
  31.2 0.3 collective-permute-done.3.refs_4_
  31.6 1.2 %collective-permute-done.10.refs_12_ = bf16[448,384]{1,0:T(8,128)(2,1)S(1)} collective-permute-done((bf16[448,384]{1,0:T(8,128)(2,1)S(1)}, bf16[448,384]{1,0:T(8,128)(2,1)S(1)}, u32[]{:S(2)}, u32[]{:S(2)}) %collective-permute-start.10) | collective-permute-done | bytes 344096 | tf_op jit(solution)/shard_map/ppermute | solution.py:289
  32.8 1.8 %shard_map.131 = (bf16[64,3712]{1,0:T(8,128)(2,1)S(1)}, bf16[64,3712]{1,0:T(8,128)(2,1)S(1)}, bf16[128,384]{1,0:T(8,128)(2,1)S(1)}, bf16[2,128,896]{2,1,0:T(8,12...) custom-call(s32[1,4]{1,0:T(1,128)S(1)} %bitcast.6, ...), custom_call_target="tpu_custom_call" | custom-call | flops 587202560 | bytes 7110672 | tf_op jit(solution)/shard_map/pallas_call | solution.py:32
  34.6 0.1 collective-permute-start.11
  34.7 1.6 %collective-permute-start.17 = (bf16[128,1280]{1,0:T(8,128)(2,1)S(1)}, bf16[128,1280]{1,0:T(8,128)(2,1)S(1)}, u32[]{:S(2)}, u32[]{:S(2)}) collective-permute-start(bf16[128,1280]{1,0:T(8,128)(2,1)S(1)} %get-tuple-element.45), channel_id=1, source_target_pairs={{0,24},{1,25},{2,26},{3,27},{4,28},{5,29},{6,30},{7,31},{8,16},{9,... | collective-permute-start | bytes 983048 | tf_op jit(solution)/shard_map/ppermute | solution.py:289
  36.2 0.3 collective-permute-done.11.got_ref
  36.5 0.1 shard_map.132
  36.6 1.3 %collective-permute-start.15 = (bf16[128,1280]{1,0:T(8,128)(2,1)S(1)}, bf16[128,1280]{1,0:T(8,128)(2,1)S(1)}, u32[]{:S(2)}, u32[]{:S(2)}) collective-permute-start(bf16[128,1280]{1,0:T(8,128)(2,1)S(1)} %get-tuple-element.42), channel_id=1, source_target_pairs={{0,8},{1,9},{2,10},{3,11},{4,12},{5,13},{6,14},{7,15},{8,0},{9,1},... | collective-permute-start | bytes 983048 | tf_op jit(solution)/shard_map/ppermute | solution.py:289
  37.9 0.8 %collective-permute-start.16 = (bf16[128,1280]{1,0:T(8,128)(2,1)S(1)}, bf16[128,1280]{1,0:T(8,128)(2,1)S(1)}, u32[]{:S(2)}, u32[]{:S(2)}) collective-permute-start(bf16[128,1280]{1,0:T(8,128)(2,1)S(1)} %get-tuple-element.44), channel_id=1, source_target_pairs={{0,16},{1,17},{2,18},{3,19},{4,20},{5,21},{6,22},{7,23},{8,24},{9,... | collective-permute-start | bytes 983048 | tf_op jit(solution)/shard_map/ppermute | solution.py:289
  38.7 3.6 %collective-permute-start.12 = (bf16[16,3712]{1,0:T(8,128)(2,1)S(1)}, bf16[16,3712]{1,0:T(8,128)(2,1)S(1)}, u32[]{:S(2)}, u32[]{:S(2)}) collective-permute-start(bf16[16,3712]{1,0:T(8,128)(2,1)S(1)} %get-tuple-element.33), channel_id=1, source_target_pairs={{0,6},{1,7},{2,4},{3,5},{4,2},{5,3},{6,0},{7,1},{8,14},{9,15},{10,... | collective-permute-start | bytes 356360 | tf_op jit(solution)/shard_map/ppermute | solution.py:289
  42.3 3.8 %collective-permute-done.17.refs_2_ = bf16[128,1280]{1,0:T(8,128)(2,1)S(1)} collective-permute-done((bf16[128,1280]{1,0:T(8,128)(2,1)S(1)}, bf16[128,1280]{1,0:T(8,128)(2,1)S(1)}, u32[]{:S(2)}, u32[]{:S(2)}) %collective-permute-start.17) | collective-permute-done | bytes 327712 | tf_op jit(solution)/shard_map/ppermute | solution.py:289
  46.2 2.1 %collective-permute-start.14 = (bf16[16,3712]{1,0:T(8,128)(2,1)S(1)}, bf16[16,3712]{1,0:T(8,128)(2,1)S(1)}, u32[]{:S(2)}, u32[]{:S(2)}) collective-permute-start(bf16[16,3712]{1,0:T(8,128)(2,1)S(1)} %get-tuple-element.35), channel_id=1, source_target_pairs={{0,2},{1,3},{2,0},{3,1},{4,6},{5,7},{6,4},{7,5},{8,10},{9,11},{10,... | collective-permute-start | bytes 356360 | tf_op jit(solution)/shard_map/ppermute | solution.py:289
  48.3 4.5 %collective-permute-done.15.refs_0_ = bf16[128,1280]{1,0:T(8,128)(2,1)S(1)} collective-permute-done((bf16[128,1280]{1,0:T(8,128)(2,1)S(1)}, bf16[128,1280]{1,0:T(8,128)(2,1)S(1)}, u32[]{:S(2)}, u32[]{:S(2)}) %collective-permute-start.15) | collective-permute-done | bytes 327712 | tf_op jit(solution)/shard_map/ppermute | solution.py:289
  52.9 0.1 collective-permute-start.18
  53.0 0.2 collective-permute-done.14.refs_2_
  53.2 1.4 %shard_map.133 = (bf16[128,3584]{1,0:T(8,128)(2,1)}, f32[8,128]{1,0:T(8,128)}) custom-call(s32[8,128]{1,0:T(8,128)S(1)} %bitcast.5, bf16[1,64,128]{2,1,0:T(8,128)(2,1)S(1)} %copy-done.4, bf16[16,3712]{1,0:T(8,128)(2,1)S(1)} %collective-permute-done.12.refs_0_, bf16[16,3712]{1,0:T(8,128)(2,1)S(1)} %collective-permute-done.13.refs_1_, ...), custom_call_target="tpu_custom_call" | custom-call | flops 58720256000 | bytes 1417216 | tf_op jit(solution)/shard_map/pallas_call | solution.py:32
  54.6 0.4 collective-permute-done.18.other_ref
  55.1 1.4 %shard_map.135 = (bf16[896,128]{1,0:T(8,128)(2,1)}, bf16[896,128]{1,0:T(8,128)(2,1)}, bf16[896,128]{1,0:T(8,128)(2,1)}) custom-call(bf16[2,128,896]{2,1,0:T(8,128)(2,1)S(1)} %get-tuple-element.39.here_ref, bf16[128,384]{1,0:T(8,128)(2,1)S(1)} %get-tuple-element.40.grads_ref, bf16[3,128,896]{2,1,0:T(8,128)(2,1)S(1)} %collective-permute-done.18.other_ref, ...), custom_call_target="tpu_custom_call" | custom-call | flops 352321536 | bytes 2916352 | tf_op jit(solution)/shard_map/pallas_call | solution.py:32
  (24 shorter events, 0.3 us)
Async XLA Ops:
  3.5 18.7 %collective-permute-start.8 = (bf16[896,384]{1,0:T(8,128)(2,1)}, bf16[896,384]{1,0:T(8,128)(2,1)S(1)}, u32[]{:S(2)}, u32[]{:S(2)}) collective-permute-start(bf16[896,384]{1,0:T(8,128)(2,1)} %get-tuple-element.30.refs_8_), channel_id=1, source_target_pairs={{0,16},{1,17},{2,18},{3,19},{4,20},{5,21},{6,22},{7,23},{8,24},{9,... | collective-permute-start | bytes 2064392 | tf_op jit(solution)/shard_map/ppermute | solution.py:289
  6.6 17.5 %collective-permute-start.7 = (bf16[896,384]{1,0:T(8,128)(2,1)}, bf16[896,384]{1,0:T(8,128)(2,1)S(1)}, u32[]{:S(2)}, u32[]{:S(2)}) collective-permute-start(bf16[896,384]{1,0:T(8,128)(2,1)} %get-tuple-element.30.refs_8_), channel_id=1, source_target_pairs={{0,8},{1,9},{2,10},{3,11},{4,12},{5,13},{6,14},{7,15},{8,0},{9,1},... | collective-permute-start | bytes 2064392 | tf_op jit(solution)/shard_map/ppermute | solution.py:289
  8.1 11.0 %collective-permute-start.2 = (bf16[16,7296]{1,0:T(8,128)(2,1)}, bf16[16,7296]{1,0:T(8,128)(2,1)S(1)}, u32[]{:S(2)}, u32[]{:S(2)}) collective-permute-start(bf16[16,7296]{1,0:T(8,128)(2,1)} %get-tuple-element.29.refs_3_), channel_id=1, source_target_pairs={{0,2},{1,3},{2,0},{3,1},{4,6},{5,7},{6,4},{7,5},{8,10},{9,11},{10,... | collective-permute-start | bytes 700424 | tf_op jit(solution)/shard_map/ppermute | solution.py:289
  9.6 19.7 %collective-permute-start.1 = (bf16[16,7296]{1,0:T(8,128)(2,1)}, bf16[16,7296]{1,0:T(8,128)(2,1)S(1)}, u32[]{:S(2)}, u32[]{:S(2)}) collective-permute-start(bf16[16,7296]{1,0:T(8,128)(2,1)} %get-tuple-element.29.refs_3_), channel_id=1, source_target_pairs={{0,4},{1,5},{2,6},{3,7},{4,0},{5,1},{6,2},{7,3},{8,12},{9,13},{10,... | collective-permute-start | bytes 700424 | tf_op jit(solution)/shard_map/ppermute | solution.py:289
  12.2 17.2 %collective-permute-start = (bf16[16,7296]{1,0:T(8,128)(2,1)}, bf16[16,7296]{1,0:T(8,128)(2,1)S(1)}, u32[]{:S(2)}, u32[]{:S(2)}) collective-permute-start(bf16[16,7296]{1,0:T(8,128)(2,1)} %get-tuple-element.29.refs_3_), channel_id=1, source_target_pairs={{0,6},{1,7},{2,4},{3,5},{4,2},{5,3},{6,0},{7,1},{8,14},{9,15},{10,... | collective-permute-start | bytes 700424 | tf_op jit(solution)/shard_map/ppermute | solution.py:289
  19.1 10.8 %collective-permute-start.6 = (bf16[16,7296]{1,0:T(8,128)(2,1)}, bf16[16,7296]{1,0:T(8,128)(2,1)S(1)}, u32[]{:S(2)}, u32[]{:S(2)}) collective-permute-start(bf16[16,7296]{1,0:T(8,128)(2,1)} %get-tuple-element.29.refs_3_), channel_id=1, source_target_pairs={{0,1},{1,0},{2,3},{3,2},{4,5},{5,4},{6,7},{7,6},{8,9},{9,8},{10,11... | collective-permute-start | bytes 700424 | tf_op jit(solution)/shard_map/ppermute | solution.py:289
  22.2 10.6 %copy-start = (bf16[896,384]{1,0:T(8,128)(2,1)S(1)}, bf16[896,384]{1,0:T(8,128)(2,1)}, u32[]{:S(2)}) copy-start(bf16[896,384]{1,0:T(8,128)(2,1)} %get-tuple-element.30.refs_8_) | copy-start | bytes 2064388
  22.2 10.6 %copy-start.1 = (bf16[16,7296]{1,0:T(8,128)(2,1)S(1)}, bf16[16,7296]{1,0:T(8,128)(2,1)}, u32[]{:S(2)}) copy-start(bf16[16,7296]{1,0:T(8,128)(2,1)} %get-tuple-element.29.refs_3_) | copy-start | bytes 700420
  22.3 9.3 %collective-permute-start.9 = (bf16[448,384]{1,0:T(8,128)(2,1)S(1)}, bf16[448,384]{1,0:T(8,128)(2,1)S(1)}, u32[]{:S(2)}, u32[]{:S(2)}) collective-permute-start(bf16[448,384]{1,0:T(8,128)(2,1)S(1)} %shard_map.129), channel_id=1, source_target_pairs={{0,8},{1,9},{2,10},{3,11},{4,12},{5,13},{6,14},{7,15},{8,0},{9,1},... | collective-permute-start | bytes 1032200 | tf_op jit(solution)/shard_map/ppermute | solution.py:289
  24.1 8.7 %copy-start.3 = (s32[4,1]{0,1:T(1,128)S(1)}, s32[4,1]{0,1:T(1,128)}, u32[]{:S(2)}) copy-start(s32[4,1]{0,1:T(1,128)} %param.14) | copy-start | bytes 52
  24.1 8.7 %collective-permute-start.10 = (bf16[448,384]{1,0:T(8,128)(2,1)S(1)}, bf16[448,384]{1,0:T(8,128)(2,1)S(1)}, u32[]{:S(2)}, u32[]{:S(2)}) collective-permute-start(bf16[448,384]{1,0:T(8,128)(2,1)S(1)} %shard_map.130), channel_id=1, source_target_pairs={{0,16},{1,17},{2,18},{3,19},{4,20},{5,21},{6,22},{7,23},{8,24},{9,... | collective-permute-start | bytes 1032200 | tf_op jit(solution)/shard_map/ppermute | solution.py:289
  29.4 1.5 %collective-permute-start.5 = (bf16[16,7296]{1,0:T(8,128)(2,1)S(1)}, bf16[16,7296]{1,0:T(8,128)(2,1)S(1)}, u32[]{:S(2)}, u32[]{:S(2)}) collective-permute-start(bf16[16,7296]{1,0:T(8,128)(2,1)S(1)} %collective-permute-done.2.refs_2_), channel_id=1, source_target_pairs={{0,1},{1,0},{2,3},{3,2},{4,5},{5,4},{6,7},{7,6},{8,9},{9,8},{10,11... | collective-permute-start | bytes 700424 | tf_op jit(solution)/shard_map/ppermute | solution.py:289
  29.4 1.8 %collective-permute-start.4 = (bf16[16,7296]{1,0:T(8,128)(2,1)S(1)}, bf16[16,7296]{1,0:T(8,128)(2,1)S(1)}, u32[]{:S(2)}, u32[]{:S(2)}) collective-permute-start(bf16[16,7296]{1,0:T(8,128)(2,1)S(1)} %collective-permute-done.1.refs_1_), channel_id=1, source_target_pairs={{0,1},{1,0},{2,3},{3,2},{4,5},{5,4},{6,7},{7,6},{8,9},{9,8},{10,11... | collective-permute-start | bytes 700424 | tf_op jit(solution)/shard_map/ppermute | solution.py:289
  29.9 1.6 %collective-permute-start.3 = (bf16[16,7296]{1,0:T(8,128)(2,1)S(1)}, bf16[16,7296]{1,0:T(8,128)(2,1)S(1)}, u32[]{:S(2)}, u32[]{:S(2)}) collective-permute-start(bf16[16,7296]{1,0:T(8,128)(2,1)S(1)} %collective-permute-done.refs_0_), channel_id=1, source_target_pairs={{0,1},{1,0},{2,3},{3,2},{4,5},{5,4},{6,7},{7,6},{8,9},{9,8},{10,11... | collective-permute-start | bytes 700424 | tf_op jit(solution)/shard_map/ppermute | solution.py:289
  34.6 1.9 %collective-permute-start.11 = (bf16[64,3712]{1,0:T(8,128)(2,1)S(1)}, bf16[64,3712]{1,0:T(8,128)(2,1)S(1)}, u32[]{:S(2)}, u32[]{:S(2)}) collective-permute-start(bf16[64,3712]{1,0:T(8,128)(2,1)S(1)} %get-tuple-element.32), channel_id=1, source_target_pairs={{0,1},{1,0},{2,3},{3,2},{4,5},{5,4},{6,7},{7,6},{8,9},{9,8},{10,11... | collective-permute-start | bytes 1425416 | tf_op jit(solution)/shard_map/ppermute | solution.py:289
  34.7 11.5 %collective-permute-start.17 = (bf16[128,1280]{1,0:T(8,128)(2,1)S(1)}, bf16[128,1280]{1,0:T(8,128)(2,1)S(1)}, u32[]{:S(2)}, u32[]{:S(2)}) collective-permute-start(bf16[128,1280]{1,0:T(8,128)(2,1)S(1)} %get-tuple-element.45), channel_id=1, source_target_pairs={{0,24},{1,25},{2,26},{3,27},{4,28},{5,29},{6,30},{7,31},{8,16},{9,... | collective-permute-start | bytes 983048 | tf_op jit(solution)/shard_map/ppermute | solution.py:289
  36.6 16.2 %collective-permute-start.15 = (bf16[128,1280]{1,0:T(8,128)(2,1)S(1)}, bf16[128,1280]{1,0:T(8,128)(2,1)S(1)}, u32[]{:S(2)}, u32[]{:S(2)}) collective-permute-start(bf16[128,1280]{1,0:T(8,128)(2,1)S(1)} %get-tuple-element.42), channel_id=1, source_target_pairs={{0,8},{1,9},{2,10},{3,11},{4,12},{5,13},{6,14},{7,15},{8,0},{9,1},... | collective-permute-start | bytes 983048 | tf_op jit(solution)/shard_map/ppermute | solution.py:289
  37.9 14.9 %collective-permute-start.16 = (bf16[128,1280]{1,0:T(8,128)(2,1)S(1)}, bf16[128,1280]{1,0:T(8,128)(2,1)S(1)}, u32[]{:S(2)}, u32[]{:S(2)}) collective-permute-start(bf16[128,1280]{1,0:T(8,128)(2,1)S(1)} %get-tuple-element.44), channel_id=1, source_target_pairs={{0,16},{1,17},{2,18},{3,19},{4,20},{5,21},{6,22},{7,23},{8,24},{9,... | collective-permute-start | bytes 983048 | tf_op jit(solution)/shard_map/ppermute | solution.py:289
  38.7 14.2 %collective-permute-start.12 = (bf16[16,3712]{1,0:T(8,128)(2,1)S(1)}, bf16[16,3712]{1,0:T(8,128)(2,1)S(1)}, u32[]{:S(2)}, u32[]{:S(2)}) collective-permute-start(bf16[16,3712]{1,0:T(8,128)(2,1)S(1)} %get-tuple-element.33), channel_id=1, source_target_pairs={{0,6},{1,7},{2,4},{3,5},{4,2},{5,3},{6,0},{7,1},{8,14},{9,15},{10,... | collective-permute-start | bytes 356360 | tf_op jit(solution)/shard_map/ppermute | solution.py:289
  42.3 10.9 %copy-start.2 = (s32[128,8]{0,1:T(8,128)S(1)}, s32[128,8]{0,1:T(8,128)}, u32[]{:S(2)}) copy-start(s32[128,8]{0,1:T(8,128)} %param.11) | copy-start | bytes 12292
  42.3 10.9 %copy-start.4 = (bf16[1,64,128]{2,1,0:T(8,128)(2,1)S(1)}, bf16[1,64,128]{2,1,0:T(8,128)(2,1)}, u32[]{:S(2)}) copy-start(bf16[1,64,128]{2,1,0:T(8,128)(2,1)} %get-tuple-element.27.placed_ref) | copy-start | bytes 49156
  42.3 10.6 %collective-permute-start.13 = (bf16[16,3712]{1,0:T(8,128)(2,1)S(1)}, bf16[16,3712]{1,0:T(8,128)(2,1)S(1)}, u32[]{:S(2)}, u32[]{:S(2)}) collective-permute-start(bf16[16,3712]{1,0:T(8,128)(2,1)S(1)} %get-tuple-element.34), channel_id=1, source_target_pairs={{0,4},{1,5},{2,6},{3,7},{4,0},{5,1},{6,2},{7,3},{8,12},{9,13},{10,... | collective-permute-start | bytes 356360 | tf_op jit(solution)/shard_map/ppermute | solution.py:289
  46.2 7.0 %collective-permute-start.14 = (bf16[16,3712]{1,0:T(8,128)(2,1)S(1)}, bf16[16,3712]{1,0:T(8,128)(2,1)S(1)}, u32[]{:S(2)}, u32[]{:S(2)}) collective-permute-start(bf16[16,3712]{1,0:T(8,128)(2,1)S(1)} %get-tuple-element.35), channel_id=1, source_target_pairs={{0,2},{1,3},{2,0},{3,1},{4,6},{5,7},{6,4},{7,5},{8,10},{9,11},{10,... | collective-permute-start | bytes 356360 | tf_op jit(solution)/shard_map/ppermute | solution.py:289
  52.9 2.2 %collective-permute-start.18 = (bf16[3,128,896]{2,1,0:T(8,128)(2,1)S(1)}, bf16[3,128,896]{2,1,0:T(8,128)(2,1)S(1)}, u32[]{:S(2)}, u32[]{:S(2)}) collective-permute-start(bf16[3,128,896]{2,1,0:T(8,128)(2,1)S(1)} %shard_map.134), channel_id=1, source_target_pairs={{0,1},{1,0},{2,3},{3,2},{4,5},{5,4},{6,7},{7,6},{8,9},{9,8},{10,11... | collective-permute-start | bytes 2064392 | tf_op jit(solution)/shard_map/ppermute | solution.py:289

commit v12 on v10

--- a/solution.py
+++ b/solution.py
@@ -386,7 +386,7 @@
         stack_kernel,
         [shape((len(near), 2 * rows, width))],
         moved,
-        flops=64000 * rows * width,
+        flops=32000 * rows * width,
     )
     near_other = send(near_rows, 0, 1)
     summed = call(
@@ -397,11 +397,10 @@
     )
     backs = [send(part, 0, CORES * j) if j else part for j, part in zip(order, summed)]
 
-    moved = [send(part, k, 0) for k, part in zip(far, away)]
-    ready = [after(moved[0], backs[0])] + moved[1:]
-    (far_rows,) = call(stack_kernel, [shape((len(far), 2 * rows, width))], ready)
+    moved = [send(after(part, summed[-2]), k, 0) for k, part in zip(far, away)]
+    (far_rows,) = call(stack_kernel, [shape((len(far), 2 * rows, width))], moved)
     far_other = send(far_rows, 0, 1)
-    late = after(grads, summed[0])
+    late = after(grads, near_other)
     near_grads = [send(late, k, 0) for k in near]
     grad_gate, grad_up, grad_down = call(
         functools.partial(weight_kernel, rep),

time: 62.7 us -> 58.4 us (0.931)
  waiting for transfers between devices: 32.1 us -> 26.9 us
  starting transfers between devices: 21.9 us -> 22.8 us
    ppermute x22, waiting for transfers between devices: 32.1 us -> 26.9 us  [send(): return lax.ppermute(array, ('rep', 'ep'), pairs)]
    ppermute x22, starting transfers between devices: 21.9 us -> 22.8 us  [send(): return lax.ppermute(array, ('rep', 'ep'), pairs)]
where the time goes in v12:
time: 58.4 us; the launch traced here: 58.2 us
  waiting for transfers between devices  26.9 us (46%)
  starting transfers between devices  22.8 us (39%)
  Pallas kernels  7.71 us (13%)
  between operations  0.79 us (1%)
    ppermute x22, waiting for transfers between devices, send(): return lax.ppermute(array, ('rep', 'ep'), pairs)  26.9 us
    ppermute x22, starting transfers between devices, send(): return lax.ppermute(array, ('rep', 'ep'), pairs)  22.8 us
    pallas_call x10, Pallas kernels, call(): pl.pallas_call(kernel, out_shape=tuple(outs), in_specs=[HBM if n in store...  7.71 us
  transfers between devices with their start and end apart: 22, of which 9 were waited for; matrix products, arithmetic and copies ran while one was open for 0% of the time, Pallas kernels for 6%

profile of v12, /device:TPU:0, one launch (start us, length us, event | category | flops | bytes accessed | tf_op | source)
XLA Modules:
  0.0 58.2 jit_solution(14104336287672033710)
XLA Ops:
  0.6 2.9 %shard_map.128 = (bf16[16,7296]{1,0:T(8,128)(2,1)}, bf16[1,64,128]{2,1,0:T(8,128)(2,1)}, bf16[896,384]{1,0:T(8,128)(2,1)}) custom-call(s32[4]{0:T(128)} %live_ref.1, bf16[128,3584]{1,0:T(8,128)(2,1)} %tok_ref.1, bf16[128,3584]{1,0:T(8,128)(2,1)} %grad_ref.1, s32[8,128]{1,0:T(8,128)} %bitcast.4, bf16[8,128]{1,0:T(8,128)(2,1)} %bitcast.7, ...), custom_call_target="tpu_custom_call" | custom-call | bytes 3467280 | tf_op jit(solution)/shard_map/pallas_call | solution.py:32
  3.5 3.0 %collective-permute-start.8 = (bf16[896,384]{1,0:T(8,128)(2,1)}, bf16[896,384]{1,0:T(8,128)(2,1)S(1)}, u32[]{:S(2)}, u32[]{:S(2)}) collective-permute-start(bf16[896,384]{1,0:T(8,128)(2,1)} %get-tuple-element.32.refs_8_), channel_id=1, source_target_pairs={{0,16},{1,17},{2,18},{3,19},{4,20},{5,21},{6,22},{7,23},{8,24},{9,... | collective-permute-start | bytes 2064392 | tf_op jit(solution)/shard_map/ppermute | solution.py:314
  6.5 1.5 %collective-permute-start.7 = (bf16[896,384]{1,0:T(8,128)(2,1)}, bf16[896,384]{1,0:T(8,128)(2,1)S(1)}, u32[]{:S(2)}, u32[]{:S(2)}) collective-permute-start(bf16[896,384]{1,0:T(8,128)(2,1)} %get-tuple-element.32.refs_8_), channel_id=1, source_target_pairs={{0,8},{1,9},{2,10},{3,11},{4,12},{5,13},{6,14},{7,15},{8,0},{9,1},... | collective-permute-start | bytes 2064392 | tf_op jit(solution)/shard_map/ppermute | solution.py:314
  8.0 1.6 %collective-permute-start.2 = (bf16[16,7296]{1,0:T(8,128)(2,1)}, bf16[16,7296]{1,0:T(8,128)(2,1)S(1)}, u32[]{:S(2)}, u32[]{:S(2)}) collective-permute-start(bf16[16,7296]{1,0:T(8,128)(2,1)} %get-tuple-element.31.refs_3_), channel_id=1, source_target_pairs={{0,2},{1,3},{2,0},{3,1},{4,6},{5,7},{6,4},{7,5},{8,10},{9,11},{10,... | collective-permute-start | bytes 700424 | tf_op jit(solution)/shard_map/ppermute | solution.py:314
  9.6 2.6 %collective-permute-start.1 = (bf16[16,7296]{1,0:T(8,128)(2,1)}, bf16[16,7296]{1,0:T(8,128)(2,1)S(1)}, u32[]{:S(2)}, u32[]{:S(2)}) collective-permute-start(bf16[16,7296]{1,0:T(8,128)(2,1)} %get-tuple-element.31.refs_3_), channel_id=1, source_target_pairs={{0,4},{1,5},{2,6},{3,7},{4,0},{5,1},{6,2},{7,3},{8,12},{9,13},{10,... | collective-permute-start | bytes 700424 | tf_op jit(solution)/shard_map/ppermute | solution.py:314
  12.2 0.2 collective-permute-start
  12.4 6.6 %collective-permute-done.2.refs_2_ = bf16[16,7296]{1,0:T(8,128)(2,1)S(1)} collective-permute-done((bf16[16,7296]{1,0:T(8,128)(2,1)}, bf16[16,7296]{1,0:T(8,128)(2,1)S(1)}, u32[]{:S(2)}, u32[]{:S(2)}) %collective-permute-start.2) | collective-permute-done | bytes 233504 | tf_op jit(solution)/shard_map/ppermute | solution.py:314
  19.1 3.1 %collective-permute-done.8.all_ref.refs_10_ = bf16[896,384]{1,0:T(8,128)(2,1)S(1)} collective-permute-done((bf16[896,384]{1,0:T(8,128)(2,1)}, bf16[896,384]{1,0:T(8,128)(2,1)S(1)}, u32[]{:S(2)}, u32[]{:S(2)}) %collective-permute-start.8) | collective-permute-done | bytes 688160 | tf_op jit(solution)/shard_map/ppermute | solution.py:314
  22.2 1.8 %collective-permute-start.9 = (bf16[448,384]{1,0:T(8,128)(2,1)S(1)}, bf16[448,384]{1,0:T(8,128)(2,1)S(1)}, u32[]{:S(2)}, u32[]{:S(2)}) collective-permute-start(bf16[448,384]{1,0:T(8,128)(2,1)S(1)} %shard_map.129), channel_id=1, source_target_pairs={{0,8},{1,9},{2,10},{3,11},{4,12},{5,13},{6,14},{7,15},{8,0},{9,1},... | collective-permute-start | bytes 1032200 | tf_op jit(solution)/shard_map/ppermute | solution.py:314
  24.1 1.6 %collective-permute-start.10 = (bf16[448,384]{1,0:T(8,128)(2,1)S(1)}, bf16[448,384]{1,0:T(8,128)(2,1)S(1)}, u32[]{:S(2)}, u32[]{:S(2)}) collective-permute-start(bf16[448,384]{1,0:T(8,128)(2,1)S(1)} %shard_map.130), channel_id=1, source_target_pairs={{0,16},{1,17},{2,18},{3,19},{4,20},{5,21},{6,22},{7,23},{8,24},{9,... | collective-permute-start | bytes 1032200 | tf_op jit(solution)/shard_map/ppermute | solution.py:314
  25.7 3.7 %collective-permute-done.1.refs_1_ = bf16[16,7296]{1,0:T(8,128)(2,1)S(1)} collective-permute-done((bf16[16,7296]{1,0:T(8,128)(2,1)}, bf16[16,7296]{1,0:T(8,128)(2,1)S(1)}, u32[]{:S(2)}, u32[]{:S(2)}) %collective-permute-start.1) | collective-permute-done | bytes 233504 | tf_op jit(solution)/shard_map/ppermute | solution.py:314
  29.4 0.5 collective-permute-start.4
  30.0 0.9 %collective-permute-done.5.refs_6_ = bf16[16,7296]{1,0:T(8,128)(2,1)S(1)} collective-permute-done((bf16[16,7296]{1,0:T(8,128)(2,1)S(1)}, bf16[16,7296]{1,0:T(8,128)(2,1)S(1)}, u32[]{:S(2)}, u32[]{:S(2)}) %collective-permute-start.5) | collective-permute-done | bytes 233504 | tf_op jit(solution)/shard_map/ppermute | solution.py:314
  30.9 0.5 collective-permute-start.11
  31.4 0.5 collective-permute-start.12
  31.9 0.9 %collective-permute-done.10.refs_12_ = bf16[448,384]{1,0:T(8,128)(2,1)S(1)} collective-permute-done((bf16[448,384]{1,0:T(8,128)(2,1)S(1)}, bf16[448,384]{1,0:T(8,128)(2,1)S(1)}, u32[]{:S(2)}, u32[]{:S(2)}) %collective-permute-start.10) | collective-permute-done | bytes 344096 | tf_op jit(solution)/shard_map/ppermute | solution.py:314
  32.8 1.7 %shard_map.131 = (bf16[64,3712]{1,0:T(8,128)(2,1)S(1)}, bf16[64,3712]{1,0:T(8,128)(2,1)S(1)}, bf16[128,384]{1,0:T(8,128)(2,1)S(1)}, bf16[2,128,896]{2,1,0:T(8,128)(2,1)S(1)}, bf16[128,1280]{1,0:T(8,128)(2,1)S(1)}) custom-call(s32[1,4]{1,0:T(1,128)S(1)} %bitcast.6, bf16[16,7296]{1,0:T(8,128)(2,1)S(1)} %collective-permute-done.refs_0_, ...), custom_call_target="tpu_custom_call" | custom-call | flops 587202560 | bytes 6455312 | tf_op jit(solution)/shard_map/pallas_call | solution.py:32
  34.5 0.1 collective-permute-start.13
  34.6 3.9 %collective-permute-done.11.refs_0_ = bf16[128,896]{1,0:T(8,128)(2,1)S(1)} collective-permute-done((bf16[128,896]{1,0:T(8,128)(2,1)S(1)}, bf16[128,896]{1,0:T(8,128)(2,1)S(1)}, u32[]{:S(2)}, u32[]{:S(2)}) %collective-permute-start.11) | collective-permute-done | bytes 229408 | tf_op jit(solution)/shard_map/ppermute | solution.py:314
  38.5 0.4 collective-permute-done.12.refs_1_
  39.0 0.1 shard_map.134
  39.1 1.4 %collective-permute-start.18 = (bf16[128,1280]{1,0:T(8,128)(2,1)S(1)}, bf16[128,1280]{1,0:T(8,128)(2,1)S(1)}, u32[]{:S(2)}, u32[]{:S(2)}) collective-permute-start(bf16[128,1280]{1,0:T(8,128)(2,1)S(1)} %get-tuple-element.48), channel_id=1, source_target_pairs={{0,24},{1,25},{2,26},{3,27},{4,28},{5,29},{6,30},{7,31},{8,16},{9,... | collective-permute-start | bytes 983048 | tf_op jit(solution)/shard_map/ppermute | solution.py:314
  40.5 2.6 %collective-permute-start.14 = (bf16[16,3712]{1,0:T(8,128)(2,1)S(1)}, bf16[16,3712]{1,0:T(8,128)(2,1)S(1)}, u32[]{:S(2)}, u32[]{:S(2)}) collective-permute-start(bf16[16,3712]{1,0:T(8,128)(2,1)S(1)} %get-tuple-element.39), channel_id=1, source_target_pairs={{0,6},{1,7},{2,4},{3,5},{4,2},{5,3},{6,0},{7,1},{8,14},{9,15},{10,... | collective-permute-start | bytes 356360 | tf_op jit(solution)/shard_map/ppermute | solution.py:314
  43.1 1.5 %collective-permute-start.15 = (bf16[16,3712]{1,0:T(8,128)(2,1)S(1)}, bf16[16,3712]{1,0:T(8,128)(2,1)S(1)}, u32[]{:S(2)}, u32[]{:S(2)}) collective-permute-start(bf16[16,3712]{1,0:T(8,128)(2,1)S(1)} %get-tuple-element.40), channel_id=1, source_target_pairs={{0,4},{1,5},{2,6},{3,7},{4,0},{5,1},{6,2},{7,3},{8,12},{9,13},{10,... | collective-permute-start | bytes 356360 | tf_op jit(solution)/shard_map/ppermute | solution.py:314
  44.6 0.3 collective-permute-start.16
  44.9 1.5 %collective-permute-start.21 = (bf16[128,384]{1,0:T(8,128)(2,1)S(1)}, bf16[128,384]{1,0:T(8,128)(2,1)S(1)}, u32[]{:S(2)}, u32[]{:S(2)}) collective-permute-start(bf16[128,384]{1,0:T(8,128)(2,1)S(1)} %get-tuple-element.49.grads_ref), channel_id=1, source_target_pairs={{0,16},{1,17},{2,18},{3,19},{4,20},{5,21},{6,22},{7,23},{8,24},{9,... | collective-permute-start | bytes 294920 | tf_op jit(solution)/shard_map/ppermute | solution.py:314
  46.4 3.9 %collective-permute-done.18.refs_0_.refs_2_ = bf16[128,1280]{1,0:T(8,128)(2,1)S(1)} collective-permute-done((bf16[128,1280]{1,0:T(8,128)(2,1)S(1)}, bf16[128,1280]{1,0:T(8,128)(2,1)S(1)}, u32[]{:S(2)}, u32[]{:S(2)}) %collective-permute-start.18) | collective-permute-done | bytes 327712 | tf_op jit(solution)/shard_map/ppermute | solution.py:314
  50.3 1.4 %collective-permute-start.20 = (bf16[128,384]{1,0:T(8,128)(2,1)S(1)}, bf16[128,384]{1,0:T(8,128)(2,1)S(1)}, u32[]{:S(2)}, u32[]{:S(2)}) collective-permute-start(bf16[128,384]{1,0:T(8,128)(2,1)S(1)} %get-tuple-element.49.grads_ref), channel_id=1, source_target_pairs={{0,8},{1,9},{2,10},{3,11},{4,12},{5,13},{6,14},{7,15},{8,0},{9,1},... | collective-permute-start | bytes 294920 | tf_op jit(solution)/shard_map/ppermute | solution.py:314
  51.7 0.1 collective-permute-start.19
  51.8 3.5 %collective-permute-done.15.refs_1_ = bf16[16,3712]{1,0:T(8,128)(2,1)S(1)} collective-permute-done((bf16[16,3712]{1,0:T(8,128)(2,1)S(1)}, bf16[16,3712]{1,0:T(8,128)(2,1)S(1)}, u32[]{:S(2)}, u32[]{:S(2)}) %collective-permute-start.15) | collective-permute-done | bytes 118816 | tf_op jit(solution)/shard_map/ppermute | solution.py:314
  55.3 1.4 %shard_map.135 = (bf16[128,3584]{1,0:T(8,128)(2,1)}, f32[8,128]{1,0:T(8,128)}) custom-call(s32[8,128]{1,0:T(8,128)S(1)} %bitcast.5, bf16[1,64,128]{2,1,0:T(8,128)(2,1)S(1)} %copy-done.4, bf16[16,3712]{1,0:T(8,128)(2,1)S(1)} %collective-permute-done.14.refs_0_, bf16[16,3712]{1,0:T(8,128)(2,1)S(1)} %collective-permute-done.15.refs_1_, ...), custom_call_target="tpu_custom_call" | custom-call | flops 58720256000 | bytes 1417216 | tf_op jit(solution)/shard_map/pallas_call | solution.py:32
  56.8 1.4 %shard_map.137 = (bf16[896,128]{1,0:T(8,128)(2,1)}, bf16[896,128]{1,0:T(8,128)(2,1)}, bf16[896,128]{1,0:T(8,128)(2,1)}) custom-call(bf16[2,128,896]{2,1,0:T(8,128)(2,1)S(1)} %get-tuple-element.45.here_ref, bf16[128,384]{1,0:T(8,128)(2,1)S(1)} %get-tuple-element.49.grads_ref, bf16[2,128,896]{2,1,0:T(8,128)(2,1)S(1)} %shard_map.133.near_ref, ...), custom_call_target="tpu_custom_call" | custom-call | flops 352321536 | bytes 2916352 | tf_op jit(solution)/shard_map/pallas_call | solution.py:32
  (32 shorter events, 0.4 us)
Async XLA Ops:
  3.5 18.7 %collective-permute-start.8 = (bf16[896,384]{1,0:T(8,128)(2,1)}, bf16[896,384]{1,0:T(8,128)(2,1)S(1)}, u32[]{:S(2)}, u32[]{:S(2)}) collective-permute-start(bf16[896,384]{1,0:T(8,128)(2,1)} %get-tuple-element.32.refs_8_), channel_id=1, source_target_pairs={{0,16},{1,17},{2,18},{3,19},{4,20},{5,21},{6,22},{7,23},{8,24},{9,... | collective-permute-start | bytes 2064392 | tf_op jit(solution)/shard_map/ppermute | solution.py:314
  6.5 17.5 %collective-permute-start.7 = (bf16[896,384]{1,0:T(8,128)(2,1)}, bf16[896,384]{1,0:T(8,128)(2,1)S(1)}, u32[]{:S(2)}, u32[]{:S(2)}) collective-permute-start(bf16[896,384]{1,0:T(8,128)(2,1)} %get-tuple-element.32.refs_8_), channel_id=1, source_target_pairs={{0,8},{1,9},{2,10},{3,11},{4,12},{5,13},{6,14},{7,15},{8,0},{9,1},... | collective-permute-start | bytes 2064392 | tf_op jit(solution)/shard_map/ppermute | solution.py:314
  8.0 11.0 %collective-permute-start.2 = (bf16[16,7296]{1,0:T(8,128)(2,1)}, bf16[16,7296]{1,0:T(8,128)(2,1)S(1)}, u32[]{:S(2)}, u32[]{:S(2)}) collective-permute-start(bf16[16,7296]{1,0:T(8,128)(2,1)} %get-tuple-element.31.refs_3_), channel_id=1, source_target_pairs={{0,2},{1,3},{2,0},{3,1},{4,6},{5,7},{6,4},{7,5},{8,10},{9,11},{10,... | collective-permute-start | bytes 700424 | tf_op jit(solution)/shard_map/ppermute | solution.py:314
  9.6 19.7 %collective-permute-start.1 = (bf16[16,7296]{1,0:T(8,128)(2,1)}, bf16[16,7296]{1,0:T(8,128)(2,1)S(1)}, u32[]{:S(2)}, u32[]{:S(2)}) collective-permute-start(bf16[16,7296]{1,0:T(8,128)(2,1)} %get-tuple-element.31.refs_3_), channel_id=1, source_target_pairs={{0,4},{1,5},{2,6},{3,7},{4,0},{5,1},{6,2},{7,3},{8,12},{9,13},{10,... | collective-permute-start | bytes 700424 | tf_op jit(solution)/shard_map/ppermute | solution.py:314
  12.2 17.2 %collective-permute-start = (bf16[16,7296]{1,0:T(8,128)(2,1)}, bf16[16,7296]{1,0:T(8,128)(2,1)S(1)}, u32[]{:S(2)}, u32[]{:S(2)}) collective-permute-start(bf16[16,7296]{1,0:T(8,128)(2,1)} %get-tuple-element.31.refs_3_), channel_id=1, source_target_pairs={{0,6},{1,7},{2,4},{3,5},{4,2},{5,3},{6,0},{7,1},{8,14},{9,15},{10,... | collective-permute-start | bytes 700424 | tf_op jit(solution)/shard_map/ppermute | solution.py:314
  19.1 10.8 %collective-permute-start.6 = (bf16[16,7296]{1,0:T(8,128)(2,1)}, bf16[16,7296]{1,0:T(8,128)(2,1)S(1)}, u32[]{:S(2)}, u32[]{:S(2)}) collective-permute-start(bf16[16,7296]{1,0:T(8,128)(2,1)} %get-tuple-element.31.refs_3_), channel_id=1, source_target_pairs={{0,1},{1,0},{2,3},{3,2},{4,5},{5,4},{6,7},{7,6},{8,9},{9,8},{10,11... | collective-permute-start | bytes 700424 | tf_op jit(solution)/shard_map/ppermute | solution.py:314
  22.2 7.7 %copy-start = (bf16[16,7296]{1,0:T(8,128)(2,1)S(1)}, bf16[16,7296]{1,0:T(8,128)(2,1)}, u32[]{:S(2)}) copy-start(bf16[16,7296]{1,0:T(8,128)(2,1)} %get-tuple-element.31.refs_3_) | copy-start | bytes 700420
  22.2 9.7 %collective-permute-start.9 = (bf16[448,384]{1,0:T(8,128)(2,1)S(1)}, bf16[448,384]{1,0:T(8,128)(2,1)S(1)}, u32[]{:S(2)}, u32[]{:S(2)}) collective-permute-start(bf16[448,384]{1,0:T(8,128)(2,1)S(1)} %shard_map.129), channel_id=1, source_target_pairs={{0,8},{1,9},{2,10},{3,11},{4,12},{5,13},{6,14},{7,15},{8,0},{9,1},... | collective-permute-start | bytes 1032200 | tf_op jit(solution)/shard_map/ppermute | solution.py:314
  24.1 8.7 %copy-start.1 = (bf16[896,384]{1,0:T(8,128)(2,1)S(1)}, bf16[896,384]{1,0:T(8,128)(2,1)}, u32[]{:S(2)}) copy-start(bf16[896,384]{1,0:T(8,128)(2,1)} %get-tuple-element.32.refs_8_) | copy-start | bytes 2064388
  24.1 8.7 %collective-permute-start.10 = (bf16[448,384]{1,0:T(8,128)(2,1)S(1)}, bf16[448,384]{1,0:T(8,128)(2,1)S(1)}, u32[]{:S(2)}, u32[]{:S(2)}) collective-permute-start(bf16[448,384]{1,0:T(8,128)(2,1)S(1)} %shard_map.130), channel_id=1, source_target_pairs={{0,16},{1,17},{2,18},{3,19},{4,20},{5,21},{6,22},{7,23},{8,24},{9,... | collective-permute-start | bytes 1032200 | tf_op jit(solution)/shard_map/ppermute | solution.py:314
  29.4 1.5 %collective-permute-start.5 = (bf16[16,7296]{1,0:T(8,128)(2,1)S(1)}, bf16[16,7296]{1,0:T(8,128)(2,1)S(1)}, u32[]{:S(2)}, u32[]{:S(2)}) collective-permute-start(bf16[16,7296]{1,0:T(8,128)(2,1)S(1)} %collective-permute-done.2.refs_2_), channel_id=1, source_target_pairs={{0,1},{1,0},{2,3},{3,2},{4,5},{5,4},{6,7},{7,6},{8,9},{9,8},{10,11... | collective-permute-start | bytes 700424 | tf_op jit(solution)/shard_map/ppermute | solution.py:314
  29.4 2.0 %collective-permute-start.4 = (bf16[16,7296]{1,0:T(8,128)(2,1)S(1)}, bf16[16,7296]{1,0:T(8,128)(2,1)S(1)}, u32[]{:S(2)}, u32[]{:S(2)}) collective-permute-start(bf16[16,7296]{1,0:T(8,128)(2,1)S(1)} %collective-permute-done.1.refs_1_), channel_id=1, source_target_pairs={{0,1},{1,0},{2,3},{3,2},{4,5},{5,4},{6,7},{7,6},{8,9},{9,8},{10,11... | collective-permute-start | bytes 700424 | tf_op jit(solution)/shard_map/ppermute | solution.py:314
  29.9 2.0 %collective-permute-start.3 = (bf16[16,7296]{1,0:T(8,128)(2,1)S(1)}, bf16[16,7296]{1,0:T(8,128)(2,1)S(1)}, u32[]{:S(2)}, u32[]{:S(2)}) collective-permute-start(bf16[16,7296]{1,0:T(8,128)(2,1)S(1)} %collective-permute-done.refs_0_), channel_id=1, source_target_pairs={{0,1},{1,0},{2,3},{3,2},{4,5},{5,4},{6,7},{7,6},{8,9},{9,8},{10,11... | collective-permute-start | bytes 700424 | tf_op jit(solution)/shard_map/ppermute | solution.py:314
  30.9 7.6 %collective-permute-start.11 = (bf16[128,896]{1,0:T(8,128)(2,1)S(1)}, bf16[128,896]{1,0:T(8,128)(2,1)S(1)}, u32[]{:S(2)}, u32[]{:S(2)}) collective-permute-start(bf16[128,896]{1,0:T(8,128)(2,1)S(1)} %get-tuple-element.35), channel_id=1, source_target_pairs={{0,8},{1,9},{2,10},{3,11},{4,12},{5,13},{6,14},{7,15},{8,0},{9,1},... | collective-permute-start | bytes 688136 | tf_op jit(solution)/shard_map/ppermute | solution.py:314
  31.4 1.4 %copy-start.3 = (s32[4,1]{0,1:T(1,128)S(1)}, s32[4,1]{0,1:T(1,128)}, u32[]{:S(2)}) copy-start(s32[4,1]{0,1:T(1,128)} %param.14) | copy-start | bytes 52
  31.4 7.5 %collective-permute-start.12 = (bf16[128,896]{1,0:T(8,128)(2,1)S(1)}, bf16[128,896]{1,0:T(8,128)(2,1)S(1)}, u32[]{:S(2)}, u32[]{:S(2)}) collective-permute-start(bf16[128,896]{1,0:T(8,128)(2,1)S(1)} %get-tuple-element.36), channel_id=1, source_target_pairs={{0,16},{1,17},{2,18},{3,19},{4,20},{5,21},{6,22},{7,23},{8,24},{9,... | collective-permute-start | bytes 688136 | tf_op jit(solution)/shard_map/ppermute | solution.py:314
  34.5 4.5 %collective-permute-start.13 = (bf16[64,3712]{1,0:T(8,128)(2,1)S(1)}, bf16[64,3712]{1,0:T(8,128)(2,1)S(1)}, u32[]{:S(2)}, u32[]{:S(2)}) collective-permute-start(bf16[64,3712]{1,0:T(8,128)(2,1)S(1)} %get-tuple-element.38), channel_id=1, source_target_pairs={{0,1},{1,0},{2,3},{3,2},{4,5},{5,4},{6,7},{7,6},{8,9},{9,8},{10,11... | collective-permute-start | bytes 1425416 | tf_op jit(solution)/shard_map/ppermute | solution.py:314
  38.9 6.0 %collective-permute-start.17 = (bf16[2,128,896]{2,1,0:T(8,128)(2,1)S(1)}, bf16[2,128,896]{2,1,0:T(8,128)(2,1)S(1)}, u32[]{:S(2)}, u32[]{:S(2)}) collective-permute-start(bf16[2,128,896]{2,1,0:T(8,128)(2,1)S(1)} %shard_map.133.near_ref), channel_id=1, source_target_pairs={{0,1},{1,0},{2,3},{3,2},{4,5},{5,4},{6,7},{7,6},{8,9},{9,8},{10,11... | collective-permute-start | bytes 1376264 | tf_op jit(solution)/shard_map/ppermute | solution.py:314
  39.1 11.2 %collective-permute-start.18 = (bf16[128,1280]{1,0:T(8,128)(2,1)S(1)}, bf16[128,1280]{1,0:T(8,128)(2,1)S(1)}, u32[]{:S(2)}, u32[]{:S(2)}) collective-permute-start(bf16[128,1280]{1,0:T(8,128)(2,1)S(1)} %get-tuple-element.48), channel_id=1, source_target_pairs={{0,24},{1,25},{2,26},{3,27},{4,28},{5,29},{6,30},{7,31},{8,16},{9,... | collective-permute-start | bytes 983048 | tf_op jit(solution)/shard_map/ppermute | solution.py:314
  40.5 11.2 %collective-permute-start.14 = (bf16[16,3712]{1,0:T(8,128)(2,1)S(1)}, bf16[16,3712]{1,0:T(8,128)(2,1)S(1)}, u32[]{:S(2)}, u32[]{:S(2)}) collective-permute-start(bf16[16,3712]{1,0:T(8,128)(2,1)S(1)} %get-tuple-element.39), channel_id=1, source_target_pairs={{0,6},{1,7},{2,4},{3,5},{4,2},{5,3},{6,0},{7,1},{8,14},{9,15},{10,... | collective-permute-start | bytes 356360 | tf_op jit(solution)/shard_map/ppermute | solution.py:314
  43.1 12.2 %collective-permute-start.15 = (bf16[16,3712]{1,0:T(8,128)(2,1)S(1)}, bf16[16,3712]{1,0:T(8,128)(2,1)S(1)}, u32[]{:S(2)}, u32[]{:S(2)}) collective-permute-start(bf16[16,3712]{1,0:T(8,128)(2,1)S(1)} %get-tuple-element.40), channel_id=1, source_target_pairs={{0,4},{1,5},{2,6},{3,7},{4,0},{5,1},{6,2},{7,3},{8,12},{9,13},{10,... | collective-permute-start | bytes 356360 | tf_op jit(solution)/shard_map/ppermute | solution.py:314
  44.6 10.7 %collective-permute-start.16 = (bf16[16,3712]{1,0:T(8,128)(2,1)S(1)}, bf16[16,3712]{1,0:T(8,128)(2,1)S(1)}, u32[]{:S(2)}, u32[]{:S(2)}) collective-permute-start(bf16[16,3712]{1,0:T(8,128)(2,1)S(1)} %get-tuple-element.41), channel_id=1, source_target_pairs={{0,2},{1,3},{2,0},{3,1},{4,6},{5,7},{6,4},{7,5},{8,10},{9,11},{10,... | collective-permute-start | bytes 356360 | tf_op jit(solution)/shard_map/ppermute | solution.py:314
  44.9 10.4 %copy-start.2 = (s32[128,8]{0,1:T(8,128)S(1)}, s32[128,8]{0,1:T(8,128)}, u32[]{:S(2)}) copy-start(s32[128,8]{0,1:T(8,128)} %param.11) | copy-start | bytes 12292
  44.9 10.4 %copy-start.4 = (bf16[1,64,128]{2,1,0:T(8,128)(2,1)S(1)}, bf16[1,64,128]{2,1,0:T(8,128)(2,1)}, u32[]{:S(2)}) copy-start(bf16[1,64,128]{2,1,0:T(8,128)(2,1)} %get-tuple-element.29.placed_ref) | copy-start | bytes 49156
  44.9 11.9 %collective-permute-start.21 = (bf16[128,384]{1,0:T(8,128)(2,1)S(1)}, bf16[128,384]{1,0:T(8,128)(2,1)S(1)}, u32[]{:S(2)}, u32[]{:S(2)}) collective-permute-start(bf16[128,384]{1,0:T(8,128)(2,1)S(1)} %get-tuple-element.49.grads_ref), channel_id=1, source_target_pairs={{0,16},{1,17},{2,18},{3,19},{4,20},{5,21},{6,22},{7,23},{8,24},{9,... | collective-permute-start | bytes 294920 | tf_op jit(solution)/shard_map/ppermute | solution.py:314
  50.3 6.5 %collective-permute-start.20 = (bf16[128,384]{1,0:T(8,128)(2,1)S(1)}, bf16[128,384]{1,0:T(8,128)(2,1)S(1)}, u32[]{:S(2)}, u32[]{:S(2)}) collective-permute-start(bf16[128,384]{1,0:T(8,128)(2,1)S(1)} %get-tuple-element.49.grads_ref), channel_id=1, source_target_pairs={{0,8},{1,9},{2,10},{3,11},{4,12},{5,13},{6,14},{7,15},{8,0},{9,1},... | collective-permute-start | bytes 294920 | tf_op jit(solution)/shard_map/ppermute | solution.py:314
  51.7 5.1 %collective-permute-start.19 = (bf16[1,128,896]{2,1,0:T(8,128)(2,1)S(1)}, bf16[1,128,896]{2,1,0:T(8,128)(2,1)S(1)}, u32[]{:S(2)}, u32[]{:S(2)}) collective-permute-start(bf16[1,128,896]{2,1,0:T(8,128)(2,1)S(1)} %shard_map.136), channel_id=1, source_target_pairs={{0,1},{1,0},{2,3},{3,2},{4,5},{5,4},{6,7},{7,6},{8,9},{9,8},{10,11... | collective-permute-start | bytes 688136 | tf_op jit(solution)/shard_map/ppermute | solution.py:314

commit v13 on v9

--- a/solution.py
+++ b/solution.py
@@ -127,6 +127,25 @@
         copy.wait()
 
 
+def columns_kernel(rep, count, *refs):
+    blocks, odd_ref, outs = refs[:count], refs[count], refs[count + 1 :]
+    rows, width = count * SLOT, odd_ref.shape[2]
+    for k in range(1, rep):
+        out = odd_ref.at[k // 2] if k % 2 else outs[k // 2 - 1]
+        for part in range(2):
+            n = 2 * k + part
+            for j in range(count):
+                start = part * rows + j * SLOT
+                out[start : start + SLOT] = blocks[j][:, n * width : (n + 1) * width]
+
+
+def split_kernel(all_ref, *outs):
+    rows = outs[0].shape[0]
+    for n, out in enumerate(outs):
+        start = n % 2 * rows
+        out[...] = all_ref[n // 2 + 1, start : start + rows]
+
+
 def half_kernel(start, all_ref, half_ref):
     half_ref[...] = all_ref[start : start + half_ref.shape[0]]
 
@@ -134,12 +153,12 @@
 def hidden_kernel(rep, count, spans, cap_ref, *refs):
     blocks, pieces = refs[: 2 * count], refs[2 * count : 2 * count + len(spans)]
     outs, cap, sem = refs[2 * count + len(spans) : -2], refs[-2], refs[-1]
-    own_ref, other_ref, grads_ref, here_ref, away_refs = *outs[:4], outs[4:]
+    own_refs, other_refs, grads_ref, here_ref = outs[:2], outs[2:4], outs[4], outs[5]
     cap_copy = pltpu.make_async_copy(cap_ref, cap, sem)
     cap_copy.start()
     width = here_ref.shape[2]
     units = pieces[0].shape[1] // 3
-    own_rows = count * SLOT
+    part_rows = count * SLOT // 2
     r = lax.axis_index("rep")
     e = lax.axis_index("ep")
     mine = e // SPLIT
@@ -152,9 +171,6 @@
             inputs[part].append(chosen)
             if k == 0:
                 here_ref[part] = chosen
-            else:
-                some = slice(part * own_rows, (part + 1) * own_rows)
-                away_refs[k - 1][some, :width] = chosen[:own_rows]
     sum_x, sum_d = 0.0, 0.0
     for (k, start, stop), piece in zip(spans, pieces):
         sum_x = sum_x + dot(inputs[0][k][:, start:stop], piece[:, : 2 * units])
@@ -187,23 +203,21 @@
     activated = pre_gate * sig
     hidden = activated * pre_up
     score = jnp.sum(hidden * back_hidden, axis=1, keepdims=True) * kept
-    lane = iota((2 * own_rows, LANES), 1)
+    lane = iota((4 * part_rows, LANES), 1)
     scores = jnp.where(lane == e % CORES, score, 0.0).astype(BF16)
     scaled = back_hidden * rate
     gate_grad = (scaled * pre_up * sig * (1.0 + pre_gate * (1.0 - sig))).astype(BF16)
     up_grad = (scaled * activated).astype(BF16)
     weighted = (hidden * rate).astype(BF16)
     grads_ref[...] = jnp.concatenate([gate_grad, up_grad, weighted], axis=1)
-    for ref in away_refs:
-        ref[:, width:] = grads_ref[...]
     pair = jnp.concatenate([gate_grad, up_grad], axis=1)
     for (k, start, stop), piece in zip(spans, pieces):
         back = dot(pair, piece[:, : 2 * units], ((1,), (1,))).astype(BF16)
         some = slice(k * width + start, k * width + stop)
-        own_ref[:, some] = back[:own_rows]
-        other_ref[:, some] = back[own_rows:]
-    own_ref[:, rep * width :] = scores[:own_rows]
-    other_ref[:, rep * width :] = scores[own_rows:]
+        for n, ref in enumerate(own_refs + other_refs):
+            ref[:, some] = back[n * part_rows : (n + 1) * part_rows]
+    for n, ref in enumerate(own_refs + other_refs):
+        ref[:, rep * width :] = scores[n * part_rows : (n + 1) * part_rows]
 
 
 def sum_kernel(own_ref, got_ref, *outs):
@@ -212,26 +226,28 @@
         out[...] = (own_ref[some].astype(F32) + got_ref[some].astype(F32)).astype(BF16)
 
 
-def stack_kernel(*refs):
-    for k, ref in enumerate(refs[:-1]):
-        refs[-1][k] = ref[:, : refs[-1].shape[2]]
-
-
-def weight_kernel(rep, here_ref, grads_ref, other_ref, *refs):
-    away, outs, held, sems = refs[: rep - 1], refs[rep - 1 : -4], refs[-4:-1], refs[-1]
+def stack_kernel(odd_ref, *refs):
+    out, count = refs[-1], len(refs) // 3
+    rows = out.shape[1] // 2
+    out[0] = odd_ref[0]
+    for n in range(count):
+        out[2 * n + 1] = refs[n][...]
+        out[2 * n + 2, :rows] = refs[count + 2 * n][...]
+        out[2 * n + 2, rows:] = refs[count + 2 * n + 1][...]
+
+
+def weight_kernel(rep, here_ref, own_ref, other_ref, *refs):
+    grads, outs, held, sems = refs[:-7], refs[-7:-4], refs[-4:-1], refs[-1]
     units = outs[0].shape[1]
-    width = here_ref.shape[2]
-    half = grads_ref.shape[0] // 2
+    half = own_ref.shape[1] // 2
     copies = []
     for part, columns in enumerate((slice(0, 2 * units), slice(2 * units, 3 * units))):
         some = slice(part * half, (part + 1) * half)
         rows = [here_ref[part]]
-        got = [grads_ref[:, columns]]
-        for k, ref in enumerate(away):
-            rows += [ref[some, :width], other_ref[k, some]]
-            got.append(ref[:, width + columns.start : width + columns.stop])
+        for k in range(rep - 1):
+            rows += [own_ref[k, some], other_ref[k, some]]
         rows = jnp.concatenate(rows, axis=0)
-        got = jnp.concatenate(got, axis=0)
+        got = jnp.concatenate([ref[:, columns] for ref in grads], axis=0)
         total = dot(got, rows, ((0,), (0,)))
         for n in range(total.shape[0] // units):
             held[2 * part + n][...] = total[n * units : (n + 1) * units].T.astype(BF16)
@@ -313,7 +329,7 @@
 
     half = width // 2
     whole = {0: weights}
-    halves = {}
+    halves, sent = {}, []
     for k in range(1, rep):
         low, high = k & -k, 1 << (k.bit_length() - 1)
         if low == high:
@@ -321,6 +337,7 @@
             for h in range(2):
                 kernel = functools.partial(half_kernel, h * half)
                 (halves[k, h],) = call(kernel, [shape((half, 3 * units))], [whole[k]])
+                sent.append(halves[k, h])
         else:
             halves[k, 0] = send(halves[k ^ low, 0], low, 0)
             halves[k, 1] = send(halves[k ^ high, 1], high, 0)
@@ -335,30 +352,48 @@
 
     order = [turned(n) for n in range(count)]
     blocks = [send(pays[j // CHIPS], 0, CORES * j) if j else pays[0] for j in order]
+    far = rep // 2
+    odd, *even = call(
+        functools.partial(columns_kernel, rep, count),
+        [shape((far, 2 * rows, width))] + [shape((2 * rows, width))] * (far - 1),
+        [after(blocks[0], *sent)] + blocks[1:],
+    )
+    odd = send(odd, 1, 0)
+    even = [send(part, 2 * k, 0) for k, part in enumerate(even, 1)]
     nearest = blocks[order.index(1)]
     ready = [after(b, nearest) if j == 0 else b for j, b in zip(order, blocks)]
     blocks = blocks + [send(block, 0, 1) for block in ready]
     results = call(
         functools.partial(hidden_kernel, rep, count, tuple(spans)),
-        [shape((rows, model_dim + LANES))] * 2
-        + [shape((2 * rows, 3 * units)), shape((2, 2 * rows, width))]
-        + [shape((2 * rows, width + 3 * units))] * (rep - 1),
+        [shape((rows // 2, model_dim + LANES))] * 4
+        + [shape((2 * rows, 3 * units)), shape((2, 2 * rows, width))],
         [caps] + blocks + pieces,
         stored=(0,),
         scratch=[pltpu.SMEM(caps.shape, jnp.int32), pltpu.SemaphoreType.DMA(())],
         flops=2 * 2 * rows * model_dim * 5 * units,
     )
-    own, other, grads, here, away = *results[:4], results[4:]
-    summed = call(sum_kernel, [shape((SLOT, model_dim + LANES))] * count, [own, send(other, 0, 1)])
+    own, other, grads, here = results[:2], results[2:4], results[4], results[5]
+    summed = []
+    for mine, theirs in zip(own, other):
+        summed += call(
+            sum_kernel,
+            [shape((SLOT, model_dim + LANES))] * (count // 2),
+            [mine, send(theirs, 0, 1)],
+            flops=2500 * rows * model_dim,
+        )
     backs = [send(part, 0, CORES * j) if j else part for j, part in zip(order, summed)]
 
-    moved = [send(away[k - 1], k, 0) for k in range(1, rep)]
-    (own_rows,) = call(stack_kernel, [shape((rep - 1, 2 * rows, width))], moved)
+    passed = call(
+        split_kernel, [shape((rows, width))] * (2 * far - 2), [after(odd, summed[-1])], flops=2 * rows * width
+    )
+    passed = [send(part, 2 * (n // 2 + 1), 0) for n, part in enumerate(passed)]
+    (own_rows,) = call(stack_kernel, [shape((rep - 1, 2 * rows, width))], [odd] + even + passed)
     other_rows = send(own_rows, 0, 1)
+    group_grads = [grads] + [send(grads, k, 0) for k in range(1, rep)]
     grad_gate, grad_up, grad_down = call(
         functools.partial(weight_kernel, rep),
         [shape((width, units))] * 3,
-        [here, grads, other_rows] + moved,
+        [here, own_rows, other_rows] + group_grads,
         kept=(0, 1, 2),
         scratch=[pltpu.VMEM((width, units), BF16)] * 3 + [pltpu.SemaphoreType.DMA((3,))],
         flops=2 * 2 * rep * rows * width * 3 * units,

time: 56.6 us -> 57.7 us (1.019)
  starting transfers between devices: 22.4 us -> 23.9 us
    ppermute x19 -> x24, starting transfers between devices: 22.4 us -> 23.9 us  [send(): return lax.ppermute(array, ('rep', 'ep'), pairs)]
    ppermute x19 -> x24, waiting for transfers between devices: 25.6 us -> 25.1 us  [send(): return lax.ppermute(array, ('rep', 'ep'), pairs)]
    pallas_call x8 -> x11, Pallas kernels: 7.71 us -> 7.76 us  [call(): pl.pallas_call(kernel, out_shape=tuple(outs), in_specs=[HBM if n in store...]
  transfers between devices with their start and end apart: 19 -> 24, of which waited for: 11 -> 12; matrix products, arithmetic and copies ran while one was open for 0% -> 0% of each run, Pallas kernels for 3% -> 6%
where the time goes in v13:
time: 57.7 us; the launch traced here: 57.5 us
  waiting for transfers between devices  25.1 us (44%)
  starting transfers between devices  23.9 us (41%)
  Pallas kernels  7.76 us (13%)
  between operations  0.76 us (1%)
    ppermute x24, waiting for transfers between devices, send(): return lax.ppermute(array, ('rep', 'ep'), pairs)  25.1 us
    ppermute x24, starting transfers between devices, send(): return lax.ppermute(array, ('rep', 'ep'), pairs)  23.9 us
    pallas_call x11, Pallas kernels, call(): pl.pallas_call(kernel, out_shape=tuple(outs), in_specs=[HBM if n in store...  7.76 us
  transfers between devices with their start and end apart: 24, of which 12 were waited for; matrix products, arithmetic and copies ran while one was open for 0% of the time, Pallas kernels for 6%

profile of v13, /device:TPU:0, one launch (start us, length us, event | category | flops | bytes accessed | tf_op | source)
XLA Modules:
  0.0 57.5 jit_solution(1910587283556111023)
XLA Ops:
  0.6 2.9 %shard_map.128 = (bf16[16,7296]{1,0:T(8,128)(2,1)}, bf16[1,64,128]{2,1,0:T(8,128)(2,1)}, bf16[896,384]{1,0:T(8,128)(2,1)}) custom-call(s32[4]{0:T(128)} %live_ref.1, bf16[128,3584]{1,0:T(8,128)(2,1)} %tok_ref.1, bf16[128,3584]{1,0:T(8,128)(2,1)} %grad_ref.1, s32[8,128]{1,0:T(8,128)} %bitcast.4, bf16[8,128]{1,0:T(8,128)(2,1)} %bitcast.7, ...), custom_call_target="tpu_custom_call" | custom-call | bytes 3467280 | tf_op jit(solution)/shard_map/pallas_call | solution.py:32
  3.5 3.0 %collective-permute-start.8 = (bf16[896,384]{1,0:T(8,128)(2,1)}, bf16[896,384]{1,0:T(8,128)(2,1)S(1)}, u32[]{:S(2)}, u32[]{:S(2)}) collective-permute-start(bf16[896,384]{1,0:T(8,128)(2,1)} %get-tuple-element.33.refs_8_), channel_id=1, source_target_pairs={{0,16},{1,17},{2,18},{3,19},{4,20},{5,21},{6,22},{7,23},{8,24},{9,... | collective-permute-start | bytes 2064392 | tf_op jit(solution)/shard_map/ppermute | solution.py:305
  6.5 1.5 %collective-permute-start.7 = (bf16[896,384]{1,0:T(8,128)(2,1)}, bf16[896,384]{1,0:T(8,128)(2,1)S(1)}, u32[]{:S(2)}, u32[]{:S(2)}) collective-permute-start(bf16[896,384]{1,0:T(8,128)(2,1)} %get-tuple-element.33.refs_8_), channel_id=1, source_target_pairs={{0,8},{1,9},{2,10},{3,11},{4,12},{5,13},{6,14},{7,15},{8,0},{9,1},... | collective-permute-start | bytes 2064392 | tf_op jit(solution)/shard_map/ppermute | solution.py:305
  8.0 1.6 %collective-permute-start.2 = (bf16[16,7296]{1,0:T(8,128)(2,1)}, bf16[16,7296]{1,0:T(8,128)(2,1)S(1)}, u32[]{:S(2)}, u32[]{:S(2)}) collective-permute-start(bf16[16,7296]{1,0:T(8,128)(2,1)} %get-tuple-element.32.refs_3_), channel_id=1, source_target_pairs={{0,2},{1,3},{2,0},{3,1},{4,6},{5,7},{6,4},{7,5},{8,10},{9,11},{10,... | collective-permute-start | bytes 700424 | tf_op jit(solution)/shard_map/ppermute | solution.py:305
  9.6 2.6 %collective-permute-start.1 = (bf16[16,7296]{1,0:T(8,128)(2,1)}, bf16[16,7296]{1,0:T(8,128)(2,1)S(1)}, u32[]{:S(2)}, u32[]{:S(2)}) collective-permute-start(bf16[16,7296]{1,0:T(8,128)(2,1)} %get-tuple-element.32.refs_3_), channel_id=1, source_target_pairs={{0,4},{1,5},{2,6},{3,7},{4,0},{5,1},{6,2},{7,3},{8,12},{9,13},{10,... | collective-permute-start | bytes 700424 | tf_op jit(solution)/shard_map/ppermute | solution.py:305
  12.2 0.2 collective-permute-start
  12.4 6.6 %collective-permute-done.2.refs_2_ = bf16[16,7296]{1,0:T(8,128)(2,1)S(1)} collective-permute-done((bf16[16,7296]{1,0:T(8,128)(2,1)}, bf16[16,7296]{1,0:T(8,128)(2,1)S(1)}, u32[]{:S(2)}, u32[]{:S(2)}) %collective-permute-start.2) | collective-permute-done | bytes 233504 | tf_op jit(solution)/shard_map/ppermute | solution.py:305
  19.1 3.1 %collective-permute-done.8.all_ref.refs_10_ = bf16[896,384]{1,0:T(8,128)(2,1)S(1)} collective-permute-done((bf16[896,384]{1,0:T(8,128)(2,1)}, bf16[896,384]{1,0:T(8,128)(2,1)S(1)}, u32[]{:S(2)}, u32[]{:S(2)}) %collective-permute-start.8) | collective-permute-done | bytes 688160 | tf_op jit(solution)/shard_map/ppermute | solution.py:305
  22.2 1.8 %collective-permute-start.9 = (bf16[448,384]{1,0:T(8,128)(2,1)S(1)}, bf16[448,384]{1,0:T(8,128)(2,1)S(1)}, u32[]{:S(2)}, u32[]{:S(2)}) collective-permute-start(bf16[448,384]{1,0:T(8,128)(2,1)S(1)} %shard_map.129), channel_id=1, source_target_pairs={{0,8},{1,9},{2,10},{3,11},{4,12},{5,13},{6,14},{7,15},{8,0},{9,1},... | collective-permute-start | bytes 1032200 | tf_op jit(solution)/shard_map/ppermute | solution.py:305
  24.1 1.6 %collective-permute-start.10 = (bf16[448,384]{1,0:T(8,128)(2,1)S(1)}, bf16[448,384]{1,0:T(8,128)(2,1)S(1)}, u32[]{:S(2)}, u32[]{:S(2)}) collective-permute-start(bf16[448,384]{1,0:T(8,128)(2,1)S(1)} %shard_map.130), channel_id=1, source_target_pairs={{0,16},{1,17},{2,18},{3,19},{4,20},{5,21},{6,22},{7,23},{8,24},{9,... | collective-permute-start | bytes 1032200 | tf_op jit(solution)/shard_map/ppermute | solution.py:305
  25.7 3.7 %collective-permute-done.1.refs_1_ = bf16[16,7296]{1,0:T(8,128)(2,1)S(1)} collective-permute-done((bf16[16,7296]{1,0:T(8,128)(2,1)}, bf16[16,7296]{1,0:T(8,128)(2,1)S(1)}, u32[]{:S(2)}, u32[]{:S(2)}) %collective-permute-start.1) | collective-permute-done | bytes 233504 | tf_op jit(solution)/shard_map/ppermute | solution.py:305
  29.4 0.5 collective-permute-start.4
  30.0 0.8 %collective-permute-done.5.refs_6_ = bf16[16,7296]{1,0:T(8,128)(2,1)S(1)} collective-permute-done((bf16[16,7296]{1,0:T(8,128)(2,1)S(1)}, bf16[16,7296]{1,0:T(8,128)(2,1)S(1)}, u32[]{:S(2)}, u32[]{:S(2)}) %collective-permute-start.5) | collective-permute-done | bytes 233504 | tf_op jit(solution)/shard_map/ppermute | solution.py:305
  30.9 0.5 collective-permute-start.16
  31.5 1.2 %collective-permute-done.10.refs_12_ = bf16[448,384]{1,0:T(8,128)(2,1)S(1)} collective-permute-done((bf16[448,384]{1,0:T(8,128)(2,1)S(1)}, bf16[448,384]{1,0:T(8,128)(2,1)S(1)}, u32[]{:S(2)}, u32[]{:S(2)}) %collective-permute-start.10) | collective-permute-done | bytes 344096 | tf_op jit(solution)/shard_map/ppermute | solution.py:305
  32.8 1.7 %shard_map.131 = (bf16[32,3712]{1,0:T(8,128)(2,1)S(1)}, bf16[32,3712]{1,0:T(8,128)(2,1)S(1)}, bf16[32,3712]{1,0:T(8,128)(2,1)S(1)}, bf16[32,3712]{1,0:T(8,128)(2...) custom-call(s32[1,4]{1,0:T(1,128)S(1)} %bitcast.6, ...), custom_call_target="tpu_custom_call" | custom-call | flops 587202560 | bytes 6127632 | tf_op jit(solution)/shard_map/pallas_call | solution.py:32
  34.6 0.5 collective-permute-start.14
  35.1 1.5 %collective-permute-start.17 = (bf16[128,896]{1,0:T(8,128)(2,1)S(1)}, bf16[128,896]{1,0:T(8,128)(2,1)S(1)}, u32[]{:S(2)}, u32[]{:S(2)}) collective-permute-start(bf16[128,896]{1,0:T(8,128)(2,1)S(1)} %get-tuple-element.47), channel_id=1, source_target_pairs={{0,16},{1,17},{2,18},{3,19},{4,20},{5,21},{6,22},{7,23},{8,24},{9,... | collective-permute-start | bytes 688136 | tf_op jit(solution)/shard_map/ppermute | solution.py:305
  36.7 3.7 %collective-permute-start.12 = (bf16[16,3712]{1,0:T(8,128)(2,1)S(1)}, bf16[16,3712]{1,0:T(8,128)(2,1)S(1)}, u32[]{:S(2)}, u32[]{:S(2)}) collective-permute-start(bf16[16,3712]{1,0:T(8,128)(2,1)S(1)} %get-tuple-element.36), channel_id=1, source_target_pairs={{0,6},{1,7},{2,4},{3,5},{4,2},{5,3},{6,0},{7,1},{8,14},{9,15},{10,... | collective-permute-start | bytes 356360 | tf_op jit(solution)/shard_map/ppermute | solution.py:305
  40.4 0.9 %collective-permute-start.15 = (bf16[16,3712]{1,0:T(8,128)(2,1)S(1)}, bf16[16,3712]{1,0:T(8,128)(2,1)S(1)}, u32[]{:S(2)}, u32[]{:S(2)}) collective-permute-start(bf16[16,3712]{1,0:T(8,128)(2,1)S(1)} %get-tuple-element.40), channel_id=1, source_target_pairs={{0,2},{1,3},{2,0},{3,1},{4,6},{5,7},{6,4},{7,5},{8,10},{9,11},{10,... | collective-permute-start | bytes 356360 | tf_op jit(solution)/shard_map/ppermute | solution.py:305
  41.3 2.1 %collective-permute-done.16.all_ref.odd_ref = bf16[2,128,896]{2,1,0:T(8,128)(2,1)S(1)} collective-permute-done((bf16[2,128,896]{2,1,0:T(8,128)(2,1)S(1)}, bf16[2,128,896]{2,1,0:T(8,128)(2,1)S(1)}, u32[]{:S(2)}, u32[]{:S(2)}) %collective-permute-start.16) | collective-permute-done | bytes 458784 | tf_op jit(solution)/shard_map/ppermute | solution.py:305
  43.4 0.6 collective-permute-start.18
  44.0 1.5 %collective-permute-start.19 = (bf16[64,896]{1,0:T(8,128)(2,1)S(1)}, bf16[64,896]{1,0:T(8,128)(2,1)S(1)}, u32[]{:S(2)}, u32[]{:S(2)}) collective-permute-start(bf16[64,896]{1,0:T(8,128)(2,1)S(1)} %get-tuple-element.50), channel_id=1, source_target_pairs={{0,16},{1,17},{2,18},{3,19},{4,20},{5,21},{6,22},{7,23},{8,24},{9,... | collective-permute-start | bytes 344072 | tf_op jit(solution)/shard_map/ppermute | solution.py:305
  45.5 3.6 %collective-permute-done.18.refs_1_ = bf16[64,896]{1,0:T(8,128)(2,1)S(1)} collective-permute-done((bf16[64,896]{1,0:T(8,128)(2,1)S(1)}, bf16[64,896]{1,0:T(8,128)(2,1)S(1)}, u32[]{:S(2)}, u32[]{:S(2)}) %collective-permute-start.18) | collective-permute-done | bytes 114720 | tf_op jit(solution)/shard_map/ppermute | solution.py:305
  49.1 0.5 collective-permute-start.23
  49.6 1.8 %collective-permute-done.19.refs_2_ = bf16[64,896]{1,0:T(8,128)(2,1)S(1)} collective-permute-done((bf16[64,896]{1,0:T(8,128)(2,1)S(1)}, bf16[64,896]{1,0:T(8,128)(2,1)S(1)}, u32[]{:S(2)}, u32[]{:S(2)}) %collective-permute-start.19) | collective-permute-done | bytes 114720 | tf_op jit(solution)/shard_map/ppermute | solution.py:305
  51.5 1.3 %collective-permute-start.21 = (bf16[128,384]{1,0:T(8,128)(2,1)S(1)}, bf16[128,384]{1,0:T(8,128)(2,1)S(1)}, u32[]{:S(2)}, u32[]{:S(2)}) collective-permute-start(bf16[128,384]{1,0:T(8,128)(2,1)S(1)} %get-tuple-element.51.refs_0_), channel_id=1, source_target_pairs={{0,8},{1,9},{2,10},{3,11},{4,12},{5,13},{6,14},{7,15},{8,0},{9,1},... | collective-permute-start | bytes 294920 | tf_op jit(solution)/shard_map/ppermute | solution.py:305
  52.8 1.4 %shard_map.134 = (bf16[128,3584]{1,0:T(8,128)(2,1)}, f32[8,128]{1,0:T(8,128)}) custom-call(s32[8,128]{1,0:T(8,128)S(1)} %bitcast.5, bf16[1,64,128]{2,1,0:T(8,128)(2,1)S(1)} %copy-done.4, bf16[16,3712]{1,0:T(8,128)(2,1)S(1)} %collective-permute-done.12.refs_0_, bf16[16,3712]{1,0:T(8,128)(2,1)S(1)} %collective-permute-done.13.refs_1_, ...), custom_call_target="tpu_custom_call" | custom-call | flops 58720256000 | bytes 1417216 | tf_op jit(solution)/shard_map/pallas_call | solution.py:32
  54.2 0.5 collective-permute-done.23.refs_3_
  54.7 1.3 %collective-permute-done.22.refs_2_ = bf16[128,384]{1,0:T(8,128)(2,1)S(1)} collective-permute-done((bf16[128,384]{1,0:T(8,128)(2,1)S(1)}, bf16[128,384]{1,0:T(8,128)(2,1)S(1)}, u32[]{:S(2)}, u32[]{:S(2)}) %collective-permute-start.22) | collective-permute-done | bytes 98336 | tf_op jit(solution)/shard_map/ppermute | solution.py:305
  56.0 0.1 collective-permute-done.21.refs_1_
  56.1 1.4 %shard_map.138 = (bf16[896,128]{1,0:T(8,128)(2,1)}, bf16[896,128]{1,0:T(8,128)(2,1)}, bf16[896,128]{1,0:T(8,128)(2,1)}) custom-call(bf16[2,128,896]{2,1,0:T(8,128)(2,1)S(1)} %get-tuple-element.44.here_ref, bf16[3,128,896]{2,1,0:T(8,128)(2,1)S(1)} %shard_map.137.own_ref, bf16[3,128,896]{2,1,0:T(8,128)(2,1)S(1)} %collective-permute-done.20.other_ref, ...), custom_call_target="tpu_custom_call" | custom-call | flops 352321536 | bytes 2916352 | tf_op jit(solution)/shard_map/pallas_call | solution.py:32
  (37 shorter events, 0.7 us)
Async XLA Ops:
  3.5 18.7 %collective-permute-start.8 = (bf16[896,384]{1,0:T(8,128)(2,1)}, bf16[896,384]{1,0:T(8,128)(2,1)S(1)}, u32[]{:S(2)}, u32[]{:S(2)}) collective-permute-start(bf16[896,384]{1,0:T(8,128)(2,1)} %get-tuple-element.33.refs_8_), channel_id=1, source_target_pairs={{0,16},{1,17},{2,18},{3,19},{4,20},{5,21},{6,22},{7,23},{8,24},{9,... | collective-permute-start | bytes 2064392 | tf_op jit(solution)/shard_map/ppermute | solution.py:305
  6.5 17.5 %collective-permute-start.7 = (bf16[896,384]{1,0:T(8,128)(2,1)}, bf16[896,384]{1,0:T(8,128)(2,1)S(1)}, u32[]{:S(2)}, u32[]{:S(2)}) collective-permute-start(bf16[896,384]{1,0:T(8,128)(2,1)} %get-tuple-element.33.refs_8_), channel_id=1, source_target_pairs={{0,8},{1,9},{2,10},{3,11},{4,12},{5,13},{6,14},{7,15},{8,0},{9,1},... | collective-permute-start | bytes 2064392 | tf_op jit(solution)/shard_map/ppermute | solution.py:305
  8.0 11.0 %collective-permute-start.2 = (bf16[16,7296]{1,0:T(8,128)(2,1)}, bf16[16,7296]{1,0:T(8,128)(2,1)S(1)}, u32[]{:S(2)}, u32[]{:S(2)}) collective-permute-start(bf16[16,7296]{1,0:T(8,128)(2,1)} %get-tuple-element.32.refs_3_), channel_id=1, source_target_pairs={{0,2},{1,3},{2,0},{3,1},{4,6},{5,7},{6,4},{7,5},{8,10},{9,11},{10,... | collective-permute-start | bytes 700424 | tf_op jit(solution)/shard_map/ppermute | solution.py:305
  9.6 19.7 %collective-permute-start.1 = (bf16[16,7296]{1,0:T(8,128)(2,1)}, bf16[16,7296]{1,0:T(8,128)(2,1)S(1)}, u32[]{:S(2)}, u32[]{:S(2)}) collective-permute-start(bf16[16,7296]{1,0:T(8,128)(2,1)} %get-tuple-element.32.refs_3_), channel_id=1, source_target_pairs={{0,4},{1,5},{2,6},{3,7},{4,0},{5,1},{6,2},{7,3},{8,12},{9,13},{10,... | collective-permute-start | bytes 700424 | tf_op jit(solution)/shard_map/ppermute | solution.py:305
  12.2 17.2 %collective-permute-start = (bf16[16,7296]{1,0:T(8,128)(2,1)}, bf16[16,7296]{1,0:T(8,128)(2,1)S(1)}, u32[]{:S(2)}, u32[]{:S(2)}) collective-permute-start(bf16[16,7296]{1,0:T(8,128)(2,1)} %get-tuple-element.32.refs_3_), channel_id=1, source_target_pairs={{0,6},{1,7},{2,4},{3,5},{4,2},{5,3},{6,0},{7,1},{8,14},{9,15},{10,... | collective-permute-start | bytes 700424 | tf_op jit(solution)/shard_map/ppermute | solution.py:305
  19.1 10.8 %collective-permute-start.6 = (bf16[16,7296]{1,0:T(8,128)(2,1)}, bf16[16,7296]{1,0:T(8,128)(2,1)S(1)}, u32[]{:S(2)}, u32[]{:S(2)}) collective-permute-start(bf16[16,7296]{1,0:T(8,128)(2,1)} %get-tuple-element.32.refs_3_), channel_id=1, source_target_pairs={{0,1},{1,0},{2,3},{3,2},{4,5},{5,4},{6,7},{7,6},{8,9},{9,8},{10,11... | collective-permute-start | bytes 700424 | tf_op jit(solution)/shard_map/ppermute | solution.py:305
  22.2 7.7 %copy-start = (bf16[16,7296]{1,0:T(8,128)(2,1)S(1)}, bf16[16,7296]{1,0:T(8,128)(2,1)}, u32[]{:S(2)}) copy-start(bf16[16,7296]{1,0:T(8,128)(2,1)} %get-tuple-element.32.refs_3_) | copy-start | bytes 700420
  22.2 9.3 %collective-permute-start.9 = (bf16[448,384]{1,0:T(8,128)(2,1)S(1)}, bf16[448,384]{1,0:T(8,128)(2,1)S(1)}, u32[]{:S(2)}, u32[]{:S(2)}) collective-permute-start(bf16[448,384]{1,0:T(8,128)(2,1)S(1)} %shard_map.129), channel_id=1, source_target_pairs={{0,8},{1,9},{2,10},{3,11},{4,12},{5,13},{6,14},{7,15},{8,0},{9,1},... | collective-permute-start | bytes 1032200 | tf_op jit(solution)/shard_map/ppermute | solution.py:305
  24.0 8.7 %copy-start.1 = (bf16[896,384]{1,0:T(8,128)(2,1)S(1)}, bf16[896,384]{1,0:T(8,128)(2,1)}, u32[]{:S(2)}) copy-start(bf16[896,384]{1,0:T(8,128)(2,1)} %get-tuple-element.33.refs_8_) | copy-start | bytes 2064388
  24.1 8.7 %collective-permute-start.10 = (bf16[448,384]{1,0:T(8,128)(2,1)S(1)}, bf16[448,384]{1,0:T(8,128)(2,1)S(1)}, u32[]{:S(2)}, u32[]{:S(2)}) collective-permute-start(bf16[448,384]{1,0:T(8,128)(2,1)S(1)} %shard_map.130), channel_id=1, source_target_pairs={{0,16},{1,17},{2,18},{3,19},{4,20},{5,21},{6,22},{7,23},{8,24},{9,... | collective-permute-start | bytes 1032200 | tf_op jit(solution)/shard_map/ppermute | solution.py:305
  29.4 1.5 %collective-permute-start.5 = (bf16[16,7296]{1,0:T(8,128)(2,1)S(1)}, bf16[16,7296]{1,0:T(8,128)(2,1)S(1)}, u32[]{:S(2)}, u32[]{:S(2)}) collective-permute-start(bf16[16,7296]{1,0:T(8,128)(2,1)S(1)} %collective-permute-done.2.refs_2_), channel_id=1, source_target_pairs={{0,1},{1,0},{2,3},{3,2},{4,5},{5,4},{6,7},{7,6},{8,9},{9,8},{10,11... | collective-permute-start | bytes 700424 | tf_op jit(solution)/shard_map/ppermute | solution.py:305
  29.4 2.0 %collective-permute-start.4 = (bf16[16,7296]{1,0:T(8,128)(2,1)S(1)}, bf16[16,7296]{1,0:T(8,128)(2,1)S(1)}, u32[]{:S(2)}, u32[]{:S(2)}) collective-permute-start(bf16[16,7296]{1,0:T(8,128)(2,1)S(1)} %collective-permute-done.1.refs_1_), channel_id=1, source_target_pairs={{0,1},{1,0},{2,3},{3,2},{4,5},{5,4},{6,7},{7,6},{8,9},{9,8},{10,11... | collective-permute-start | bytes 700424 | tf_op jit(solution)/shard_map/ppermute | solution.py:305
  29.9 1.6 %collective-permute-start.3 = (bf16[16,7296]{1,0:T(8,128)(2,1)S(1)}, bf16[16,7296]{1,0:T(8,128)(2,1)S(1)}, u32[]{:S(2)}, u32[]{:S(2)}) collective-permute-start(bf16[16,7296]{1,0:T(8,128)(2,1)S(1)} %collective-permute-done.refs_0_), channel_id=1, source_target_pairs={{0,1},{1,0},{2,3},{3,2},{4,5},{5,4},{6,7},{7,6},{8,9},{9,8},{10,11... | collective-permute-start | bytes 700424 | tf_op jit(solution)/shard_map/ppermute | solution.py:305
  30.9 1.9 %copy-start.3 = (s32[4,1]{0,1:T(1,128)S(1)}, s32[4,1]{0,1:T(1,128)}, u32[]{:S(2)}) copy-start(s32[4,1]{0,1:T(1,128)} %param.14) | copy-start | bytes 52
  30.9 12.6 %collective-permute-start.16 = (bf16[2,128,896]{2,1,0:T(8,128)(2,1)S(1)}, bf16[2,128,896]{2,1,0:T(8,128)(2,1)S(1)}, u32[]{:S(2)}, u32[]{:S(2)}) collective-permute-start(bf16[2,128,896]{2,1,0:T(8,128)(2,1)S(1)} %get-tuple-element.46), channel_id=1, source_target_pairs={{0,8},{1,9},{2,10},{3,11},{4,12},{5,13},{6,14},{7,15},{8,0},{9,1},... | collective-permute-start | bytes 1376264 | tf_op jit(solution)/shard_map/ppermute | solution.py:305
  34.5 2.1 %collective-permute-start.11 = (bf16[32,3712]{1,0:T(8,128)(2,1)S(1)}, bf16[32,3712]{1,0:T(8,128)(2,1)S(1)}, u32[]{:S(2)}, u32[]{:S(2)}) collective-permute-start(bf16[32,3712]{1,0:T(8,128)(2,1)S(1)} %get-tuple-element.35), channel_id=1, source_target_pairs={{0,1},{1,0},{2,3},{3,2},{4,5},{5,4},{6,7},{7,6},{8,9},{9,8},{10,11... | collective-permute-start | bytes 712712 | tf_op jit(solution)/shard_map/ppermute | solution.py:305
  34.6 5.7 %collective-permute-start.14 = (bf16[32,3712]{1,0:T(8,128)(2,1)S(1)}, bf16[32,3712]{1,0:T(8,128)(2,1)S(1)}, u32[]{:S(2)}, u32[]{:S(2)}) collective-permute-start(bf16[32,3712]{1,0:T(8,128)(2,1)S(1)} %get-tuple-element.39), channel_id=1, source_target_pairs={{0,1},{1,0},{2,3},{3,2},{4,5},{5,4},{6,7},{7,6},{8,9},{9,8},{10,11... | collective-permute-start | bytes 712712 | tf_op jit(solution)/shard_map/ppermute | solution.py:305
  35.1 8.9 %collective-permute-start.17 = (bf16[128,896]{1,0:T(8,128)(2,1)S(1)}, bf16[128,896]{1,0:T(8,128)(2,1)S(1)}, u32[]{:S(2)}, u32[]{:S(2)}) collective-permute-start(bf16[128,896]{1,0:T(8,128)(2,1)S(1)} %get-tuple-element.47), channel_id=1, source_target_pairs={{0,16},{1,17},{2,18},{3,19},{4,20},{5,21},{6,22},{7,23},{8,24},{9,... | collective-permute-start | bytes 688136 | tf_op jit(solution)/shard_map/ppermute | solution.py:305
  36.7 14.8 %collective-permute-start.12 = (bf16[16,3712]{1,0:T(8,128)(2,1)S(1)}, bf16[16,3712]{1,0:T(8,128)(2,1)S(1)}, u32[]{:S(2)}, u32[]{:S(2)}) collective-permute-start(bf16[16,3712]{1,0:T(8,128)(2,1)S(1)} %get-tuple-element.36), channel_id=1, source_target_pairs={{0,6},{1,7},{2,4},{3,5},{4,2},{5,3},{6,0},{7,1},{8,14},{9,15},{10,... | collective-permute-start | bytes 356360 | tf_op jit(solution)/shard_map/ppermute | solution.py:305
  40.4 12.4 %collective-permute-start.13 = (bf16[16,3712]{1,0:T(8,128)(2,1)S(1)}, bf16[16,3712]{1,0:T(8,128)(2,1)S(1)}, u32[]{:S(2)}, u32[]{:S(2)}) collective-permute-start(bf16[16,3712]{1,0:T(8,128)(2,1)S(1)} %get-tuple-element.37), channel_id=1, source_target_pairs={{0,4},{1,5},{2,6},{3,7},{4,0},{5,1},{6,2},{7,3},{8,12},{9,13},{10,... | collective-permute-start | bytes 356360 | tf_op jit(solution)/shard_map/ppermute | solution.py:305
  40.4 12.3 %collective-permute-start.15 = (bf16[16,3712]{1,0:T(8,128)(2,1)S(1)}, bf16[16,3712]{1,0:T(8,128)(2,1)S(1)}, u32[]{:S(2)}, u32[]{:S(2)}) collective-permute-start(bf16[16,3712]{1,0:T(8,128)(2,1)S(1)} %get-tuple-element.40), channel_id=1, source_target_pairs={{0,2},{1,3},{2,0},{3,1},{4,6},{5,7},{6,4},{7,5},{8,10},{9,11},{10,... | collective-permute-start | bytes 356360 | tf_op jit(solution)/shard_map/ppermute | solution.py:305
  43.4 5.7 %collective-permute-start.18 = (bf16[64,896]{1,0:T(8,128)(2,1)S(1)}, bf16[64,896]{1,0:T(8,128)(2,1)S(1)}, u32[]{:S(2)}, u32[]{:S(2)}) collective-permute-start(bf16[64,896]{1,0:T(8,128)(2,1)S(1)} %get-tuple-element.49), channel_id=1, source_target_pairs={{0,16},{1,17},{2,18},{3,19},{4,20},{5,21},{6,22},{7,23},{8,24},{9,... | collective-permute-start | bytes 344072 | tf_op jit(solution)/shard_map/ppermute | solution.py:305
  44.0 7.4 %collective-permute-start.19 = (bf16[64,896]{1,0:T(8,128)(2,1)S(1)}, bf16[64,896]{1,0:T(8,128)(2,1)S(1)}, u32[]{:S(2)}, u32[]{:S(2)}) collective-permute-start(bf16[64,896]{1,0:T(8,128)(2,1)S(1)} %get-tuple-element.50), channel_id=1, source_target_pairs={{0,16},{1,17},{2,18},{3,19},{4,20},{5,21},{6,22},{7,23},{8,24},{9,... | collective-permute-start | bytes 344072 | tf_op jit(solution)/shard_map/ppermute | solution.py:305
  49.1 3.6 %copy-start.2 = (s32[128,8]{0,1:T(8,128)S(1)}, s32[128,8]{0,1:T(8,128)}, u32[]{:S(2)}) copy-start(s32[128,8]{0,1:T(8,128)} %param.11) | copy-start | bytes 12292
  49.1 3.7 %copy-start.4 = (bf16[1,64,128]{2,1,0:T(8,128)(2,1)S(1)}, bf16[1,64,128]{2,1,0:T(8,128)(2,1)}, u32[]{:S(2)}) copy-start(bf16[1,64,128]{2,1,0:T(8,128)(2,1)} %get-tuple-element.30.placed_ref) | copy-start | bytes 49156
  49.1 5.6 %collective-permute-start.23 = (bf16[128,384]{1,0:T(8,128)(2,1)S(1)}, bf16[128,384]{1,0:T(8,128)(2,1)S(1)}, u32[]{:S(2)}, u32[]{:S(2)}) collective-permute-start(bf16[128,384]{1,0:T(8,128)(2,1)S(1)} %get-tuple-element.51.refs_0_), channel_id=1, source_target_pairs={{0,24},{1,25},{2,26},{3,27},{4,28},{5,29},{6,30},{7,31},{8,16},{9,... | collective-permute-start | bytes 294920 | tf_op jit(solution)/shard_map/ppermute | solution.py:305
  51.4 4.6 %collective-permute-start.22 = (bf16[128,384]{1,0:T(8,128)(2,1)S(1)}, bf16[128,384]{1,0:T(8,128)(2,1)S(1)}, u32[]{:S(2)}, u32[]{:S(2)}) collective-permute-start(bf16[128,384]{1,0:T(8,128)(2,1)S(1)} %get-tuple-element.51.refs_0_), channel_id=1, source_target_pairs={{0,16},{1,17},{2,18},{3,19},{4,20},{5,21},{6,22},{7,23},{8,24},{9,... | collective-permute-start | bytes 294920 | tf_op jit(solution)/shard_map/ppermute | solution.py:305
  51.5 4.7 %collective-permute-start.21 = (bf16[128,384]{1,0:T(8,128)(2,1)S(1)}, bf16[128,384]{1,0:T(8,128)(2,1)S(1)}, u32[]{:S(2)}, u32[]{:S(2)}) collective-permute-start(bf16[128,384]{1,0:T(8,128)(2,1)S(1)} %get-tuple-element.51.refs_0_), channel_id=1, source_target_pairs={{0,8},{1,9},{2,10},{3,11},{4,12},{5,13},{6,14},{7,15},{8,0},{9,1},... | collective-permute-start | bytes 294920 | tf_op jit(solution)/shard_map/ppermute | solution.py:305
  52.7 3.4 %collective-permute-start.20 = (bf16[3,128,896]{2,1,0:T(8,128)(2,1)S(1)}, bf16[3,128,896]{2,1,0:T(8,128)(2,1)S(1)}, u32[]{:S(2)}, u32[]{:S(2)}) collective-permute-start(bf16[3,128,896]{2,1,0:T(8,128)(2,1)S(1)} %shard_map.137.own_ref), channel_id=1, source_target_pairs={{0,1},{1,0},{2,3},{3,2},{4,5},{5,4},{6,7},{7,6},{8,9},{9,8},{10,11... | collective-permute-start | bytes 2064392 | tf_op jit(solution)/shard_map/ppermute | solution.py:305

commit v14 on v11

--- a/solution.py
+++ b/solution.py
@@ -217,7 +217,7 @@
         refs[-1][k] = ref[:, : refs[-1].shape[2]]
 
 
-def weight_kernel(rep, here_ref, grads_ref, other_ref, *refs):
+def weight_kernel(rep, here_ref, grads_ref, own_ref, other_ref, *refs):
     away, outs, held, sems = refs[: rep - 1], refs[rep - 1 : -4], refs[-4:-1], refs[-1]
     units = outs[0].shape[1]
     width = here_ref.shape[2]
@@ -225,14 +225,13 @@
     copies = []
     for part, columns in enumerate((slice(0, 2 * units), slice(2 * units, 3 * units))):
         some = slice(part * half, (part + 1) * half)
-        rows = [here_ref[part]]
-        got = [grads_ref[:, columns]]
-        for k, ref in enumerate(away):
-            rows += [ref[some, :width], other_ref[k, some]]
-            got.append(ref[:, width + columns.start : width + columns.stop])
-        rows = jnp.concatenate(rows, axis=0)
-        got = jnp.concatenate(got, axis=0)
-        total = dot(got, rows, ((0,), (0,)))
+        got = [ref[:, width + columns.start : width + columns.stop] for ref in away]
+        total = dot(grads_ref[:, columns], here_ref[part], ((0,), (0,)))
+        for core, ref in enumerate((own_ref, other_ref)):
+            mine = slice(core * half, (core + 1) * half)
+            chosen = jnp.concatenate([g[mine] for g in got], axis=0)
+            rows = ref[:, some].reshape(chosen.shape[0], width)
+            total = total + dot(chosen, rows, ((0,), (0,)))
         for n in range(total.shape[0] // units):
             held[2 * part + n][...] = total[n * units : (n + 1) * units].T.astype(BF16)
             copies += fetch([(held[2 * part + n], outs[2 * part + n])], sems, 2 * part + n)
@@ -242,8 +241,9 @@
 
 def token_kernel(rep, flight, ids_ref, placed_ref, *refs):
     backs, rest = refs[: flight * CHIPS], refs[flight * CHIPS :]
-    out_ref, weight_ref, blocks, ids, sems = rest
+    out_ref, weight_ref, blocks, joined_out, ids, sems = rest
     (ids_copy,) = fetch([(ids_ref, ids)], sems)
+    copies = []
     r = lax.axis_index("rep")
     mine = lax.axis_index("ep") // SPLIT
     spacing = EXPERTS // flight
@@ -257,9 +257,15 @@
         for w in range(flight):
             some = joined[w][:, k * width : (k + 1) * width]
             total = total + dot(placed_ref[w], some, ((0,), (0,)))
-        blocks[jnp.bitwise_xor(r, k)] = total.astype(BF16)
-    for b in range(rep):
-        out_ref[:, b * width : (b + 1) * width] = blocks[b]
+        group = jnp.bitwise_xor(r, k)
+        blocks[group] = total.astype(BF16)
+        if width % LANES == 0:
+            some = pl.ds(pl.multiple_of(group * width, LANES), width)
+            copies += fetch([(blocks.at[group], out_ref.at[:, some])], sems, k + 1)
+    if width % LANES:
+        for b in range(rep):
+            joined_out[:, b * width : (b + 1) * width] = blocks[b]
+        copies += fetch([(joined_out, out_ref)], sems, 1)
     result = jnp.zeros(weight_ref.shape, F32)
     ids_copy.wait()
     for w in range(flight):
@@ -268,6 +274,8 @@
         match = ids[...] == jnp.bitwise_xor(mine, w) * spacing
         result = result + jnp.where(match, score, 0.0)
     weight_ref[...] = result
+    for copy in copies:
+        copy.wait()
 
 
 def local(
@@ -360,7 +368,7 @@
     grad_gate, grad_up, grad_down = call(
         functools.partial(weight_kernel, rep),
         [shape((width, units))] * 3,
-        [here, grads, other_rows] + moved,
+        [here, grads, own_rows, other_rows] + moved,
         kept=(0, 1, 2),
         scratch=[pltpu.VMEM((width, units), BF16)] * 3 + [pltpu.SemaphoreType.DMA((3,))],
         flops=2 * 2 * rep * rows * width * 3 * units,
@@ -370,10 +378,12 @@
         [shape((tok_count, model_dim)), shape(ids_rows.shape, F32)],
         [ids_rows, placed] + backs,
         stored=(0,),
+        kept=(0,),
         scratch=[
             pltpu.VMEM((rep, tok_count, width), BF16),
+            pltpu.VMEM((tok_count, model_dim), BF16),
             pltpu.VMEM(ids_rows.shape, jnp.int32),
-            pltpu.SemaphoreType.DMA((1,)),
+            pltpu.SemaphoreType.DMA((rep + 1,)),
         ],
         flops=1000 * 2 * tok_count * CHIPS * SLOT * model_dim,
     )

time: 56.6 us -> 56.8 us (level)
  transfers between devices with their start and end apart: 19 -> 19, of which waited for: 12 -> 12; matrix products, arithmetic and copies ran while one was open for 0% -> 0% of each run, Pallas kernels for 3% -> 4%
where the time goes in v14:
time: 56.8 us; the launch traced here: 56.7 us
  waiting for transfers between devices  25.2 us (44%)
  starting transfers between devices  22.4 us (39%)
  Pallas kernels  8.25 us (15%)
  between operations  0.75 us (1%)
    ppermute x19, waiting for transfers between devices, send(): return lax.ppermute(array, ('rep', 'ep'), pairs)  25.2 us
    ppermute x19, starting transfers between devices, send(): return lax.ppermute(array, ('rep', 'ep'), pairs)  22.4 us
    pallas_call x8, Pallas kernels, call(): pl.pallas_call(kernel, out_shape=tuple(outs), in_specs=[HBM if n in store...  8.25 us
  transfers between devices with their start and end apart: 19, of which 12 were waited for; matrix products, arithmetic and copies ran while one was open for 0% of the time, Pallas kernels for 4%

profile of v14, /device:TPU:0, one launch (start us, length us, event | category | flops | bytes accessed | tf_op | source)
XLA Modules:
  0.0 56.7 jit_solution(13510459028474798862)
XLA Ops:
  0.6 2.9 %shard_map.128 = (bf16[16,7296]{1,0:T(8,128)(2,1)}, bf16[1,64,128]{2,1,0:T(8,128)(2,1)}, bf16[896,384]{1,0:T(8,128)(2,1)}) custom-call(s32[4]{0:T(128)} %live_ref.1, bf16[128,3584]{1,0:T(8,128)(2,1)} %tok_ref.1, bf16[128,3584]{1,0:T(8,128)(2,1)} %grad_ref.1, s32[8,128]{1,0:T(8,128)} %bitcast.4, bf16[8,128]{1,0:T(8,128)(2,1)} %bitcast.7, ...), custom_call_target="tpu_custom_call" | custom-call | bytes 3467280 | tf_op jit(solution)/shard_map/pallas_call | solution.py:32
  3.5 3.0 %collective-permute-start.8 = (bf16[896,384]{1,0:T(8,128)(2,1)}, bf16[896,384]{1,0:T(8,128)(2,1)S(1)}, u32[]{:S(2)}, u32[]{:S(2)}) collective-permute-start(bf16[896,384]{1,0:T(8,128)(2,1)} %get-tuple-element.30.refs_8_), channel_id=1, source_target_pairs={{0,16},{1,17},{2,18},{3,19},{4,20},{5,21},{6,22},{7,23},{8,24},{9,... | collective-permute-start | bytes 2064392 | tf_op jit(solution)/shard_map/ppermute | solution.py:297
  6.6 1.5 %collective-permute-start.7 = (bf16[896,384]{1,0:T(8,128)(2,1)}, bf16[896,384]{1,0:T(8,128)(2,1)S(1)}, u32[]{:S(2)}, u32[]{:S(2)}) collective-permute-start(bf16[896,384]{1,0:T(8,128)(2,1)} %get-tuple-element.30.refs_8_), channel_id=1, source_target_pairs={{0,8},{1,9},{2,10},{3,11},{4,12},{5,13},{6,14},{7,15},{8,0},{9,1},... | collective-permute-start | bytes 2064392 | tf_op jit(solution)/shard_map/ppermute | solution.py:297
  8.1 1.6 %collective-permute-start.2 = (bf16[16,7296]{1,0:T(8,128)(2,1)}, bf16[16,7296]{1,0:T(8,128)(2,1)S(1)}, u32[]{:S(2)}, u32[]{:S(2)}) collective-permute-start(bf16[16,7296]{1,0:T(8,128)(2,1)} %get-tuple-element.29.refs_3_), channel_id=1, source_target_pairs={{0,2},{1,3},{2,0},{3,1},{4,6},{5,7},{6,4},{7,5},{8,10},{9,11},{10,... | collective-permute-start | bytes 700424 | tf_op jit(solution)/shard_map/ppermute | solution.py:297
  9.6 2.6 %collective-permute-start.1 = (bf16[16,7296]{1,0:T(8,128)(2,1)}, bf16[16,7296]{1,0:T(8,128)(2,1)S(1)}, u32[]{:S(2)}, u32[]{:S(2)}) collective-permute-start(bf16[16,7296]{1,0:T(8,128)(2,1)} %get-tuple-element.29.refs_3_), channel_id=1, source_target_pairs={{0,4},{1,5},{2,6},{3,7},{4,0},{5,1},{6,2},{7,3},{8,12},{9,13},{10,... | collective-permute-start | bytes 700424 | tf_op jit(solution)/shard_map/ppermute | solution.py:297
  12.2 0.2 collective-permute-start
  12.4 6.6 %collective-permute-done.2.refs_2_ = bf16[16,7296]{1,0:T(8,128)(2,1)S(1)} collective-permute-done((bf16[16,7296]{1,0:T(8,128)(2,1)}, bf16[16,7296]{1,0:T(8,128)(2,1)S(1)}, u32[]{:S(2)}, u32[]{:S(2)}) %collective-permute-start.2) | collective-permute-done | bytes 233504 | tf_op jit(solution)/shard_map/ppermute | solution.py:297
  19.1 3.1 %collective-permute-done.8.all_ref.refs_10_ = bf16[896,384]{1,0:T(8,128)(2,1)S(1)} collective-permute-done((bf16[896,384]{1,0:T(8,128)(2,1)}, bf16[896,384]{1,0:T(8,128)(2,1)S(1)}, u32[]{:S(2)}, u32[]{:S(2)}) %collective-permute-start.8) | collective-permute-done | bytes 688160 | tf_op jit(solution)/shard_map/ppermute | solution.py:297
  22.3 1.8 %collective-permute-start.9 = (bf16[448,384]{1,0:T(8,128)(2,1)S(1)}, bf16[448,384]{1,0:T(8,128)(2,1)S(1)}, u32[]{:S(2)}, u32[]{:S(2)}) collective-permute-start(bf16[448,384]{1,0:T(8,128)(2,1)S(1)} %shard_map.129), channel_id=1, source_target_pairs={{0,8},{1,9},{2,10},{3,11},{4,12},{5,13},{6,14},{7,15},{8,0},{9,1},... | collective-permute-start | bytes 1032200 | tf_op jit(solution)/shard_map/ppermute | solution.py:297
  24.1 1.6 %collective-permute-start.10 = (bf16[448,384]{1,0:T(8,128)(2,1)S(1)}, bf16[448,384]{1,0:T(8,128)(2,1)S(1)}, u32[]{:S(2)}, u32[]{:S(2)}) collective-permute-start(bf16[448,384]{1,0:T(8,128)(2,1)S(1)} %shard_map.130), channel_id=1, source_target_pairs={{0,16},{1,17},{2,18},{3,19},{4,20},{5,21},{6,22},{7,23},{8,24},{9,... | collective-permute-start | bytes 1032200 | tf_op jit(solution)/shard_map/ppermute | solution.py:297
  25.7 3.7 %collective-permute-done.1.refs_1_ = bf16[16,7296]{1,0:T(8,128)(2,1)S(1)} collective-permute-done((bf16[16,7296]{1,0:T(8,128)(2,1)}, bf16[16,7296]{1,0:T(8,128)(2,1)S(1)}, u32[]{:S(2)}, u32[]{:S(2)}) %collective-permute-start.1) | collective-permute-done | bytes 233504 | tf_op jit(solution)/shard_map/ppermute | solution.py:297
  29.4 0.5 collective-permute-start.4
  30.0 0.9 %collective-permute-done.5.refs_6_ = bf16[16,7296]{1,0:T(8,128)(2,1)S(1)} collective-permute-done((bf16[16,7296]{1,0:T(8,128)(2,1)S(1)}, bf16[16,7296]{1,0:T(8,128)(2,1)S(1)}, u32[]{:S(2)}, u32[]{:S(2)}) %collective-permute-start.5) | collective-permute-done | bytes 233504 | tf_op jit(solution)/shard_map/ppermute | solution.py:297
  30.9 0.3 collective-permute-done.4.refs_5_
  31.2 0.3 collective-permute-done.3.refs_4_
  31.6 1.2 %collective-permute-done.10.refs_12_ = bf16[448,384]{1,0:T(8,128)(2,1)S(1)} collective-permute-done((bf16[448,384]{1,0:T(8,128)(2,1)S(1)}, bf16[448,384]{1,0:T(8,128)(2,1)S(1)}, u32[]{:S(2)}, u32[]{:S(2)}) %collective-permute-start.10) | collective-permute-done | bytes 344096 | tf_op jit(solution)/shard_map/ppermute | solution.py:297
  32.8 1.8 %shard_map.131 = (bf16[64,3712]{1,0:T(8,128)(2,1)S(1)}, bf16[64,3712]{1,0:T(8,128)(2,1)S(1)}, bf16[128,384]{1,0:T(8,128)(2,1)S(1)}, bf16[2,128,896]{2,1,0:T(8,12...) custom-call(s32[1,4]{1,0:T(1,128)S(1)} %bitcast.6, ...), custom_call_target="tpu_custom_call" | custom-call | flops 587202560 | bytes 7110672 | tf_op jit(solution)/shard_map/pallas_call | solution.py:32
  34.6 0.1 collective-permute-start.11
  34.7 1.6 %collective-permute-start.17 = (bf16[128,1280]{1,0:T(8,128)(2,1)S(1)}, bf16[128,1280]{1,0:T(8,128)(2,1)S(1)}, u32[]{:S(2)}, u32[]{:S(2)}) collective-permute-start(bf16[128,1280]{1,0:T(8,128)(2,1)S(1)} %get-tuple-element.45), channel_id=1, source_target_pairs={{0,24},{1,25},{2,26},{3,27},{4,28},{5,29},{6,30},{7,31},{8,16},{9,... | collective-permute-start | bytes 983048 | tf_op jit(solution)/shard_map/ppermute | solution.py:297
  36.2 0.3 collective-permute-done.11.got_ref
  36.5 0.1 shard_map.132
  36.6 1.3 %collective-permute-start.15 = (bf16[128,1280]{1,0:T(8,128)(2,1)S(1)}, bf16[128,1280]{1,0:T(8,128)(2,1)S(1)}, u32[]{:S(2)}, u32[]{:S(2)}) collective-permute-start(bf16[128,1280]{1,0:T(8,128)(2,1)S(1)} %get-tuple-element.42), channel_id=1, source_target_pairs={{0,8},{1,9},{2,10},{3,11},{4,12},{5,13},{6,14},{7,15},{8,0},{9,1},... | collective-permute-start | bytes 983048 | tf_op jit(solution)/shard_map/ppermute | solution.py:297
  37.9 0.8 %collective-permute-start.16 = (bf16[128,1280]{1,0:T(8,128)(2,1)S(1)}, bf16[128,1280]{1,0:T(8,128)(2,1)S(1)}, u32[]{:S(2)}, u32[]{:S(2)}) collective-permute-start(bf16[128,1280]{1,0:T(8,128)(2,1)S(1)} %get-tuple-element.44), channel_id=1, source_target_pairs={{0,16},{1,17},{2,18},{3,19},{4,20},{5,21},{6,22},{7,23},{8,24},{9,... | collective-permute-start | bytes 983048 | tf_op jit(solution)/shard_map/ppermute | solution.py:297
  38.7 3.6 %collective-permute-start.12 = (bf16[16,3712]{1,0:T(8,128)(2,1)S(1)}, bf16[16,3712]{1,0:T(8,128)(2,1)S(1)}, u32[]{:S(2)}, u32[]{:S(2)}) collective-permute-start(bf16[16,3712]{1,0:T(8,128)(2,1)S(1)} %get-tuple-element.33), channel_id=1, source_target_pairs={{0,6},{1,7},{2,4},{3,5},{4,2},{5,3},{6,0},{7,1},{8,14},{9,15},{10,... | collective-permute-start | bytes 356360 | tf_op jit(solution)/shard_map/ppermute | solution.py:297
  42.3 3.8 %collective-permute-done.17.refs_2_ = bf16[128,1280]{1,0:T(8,128)(2,1)S(1)} collective-permute-done((bf16[128,1280]{1,0:T(8,128)(2,1)S(1)}, bf16[128,1280]{1,0:T(8,128)(2,1)S(1)}, u32[]{:S(2)}, u32[]{:S(2)}) %collective-permute-start.17) | collective-permute-done | bytes 327712 | tf_op jit(solution)/shard_map/ppermute | solution.py:297
  46.2 2.1 %collective-permute-start.14 = (bf16[16,3712]{1,0:T(8,128)(2,1)S(1)}, bf16[16,3712]{1,0:T(8,128)(2,1)S(1)}, u32[]{:S(2)}, u32[]{:S(2)}) collective-permute-start(bf16[16,3712]{1,0:T(8,128)(2,1)S(1)} %get-tuple-element.35), channel_id=1, source_target_pairs={{0,2},{1,3},{2,0},{3,1},{4,6},{5,7},{6,4},{7,5},{8,10},{9,11},{10,... | collective-permute-start | bytes 356360 | tf_op jit(solution)/shard_map/ppermute | solution.py:297
  48.3 4.5 %collective-permute-done.15.refs_0_ = bf16[128,1280]{1,0:T(8,128)(2,1)S(1)} collective-permute-done((bf16[128,1280]{1,0:T(8,128)(2,1)S(1)}, bf16[128,1280]{1,0:T(8,128)(2,1)S(1)}, u32[]{:S(2)}, u32[]{:S(2)}) %collective-permute-start.15) | collective-permute-done | bytes 327712 | tf_op jit(solution)/shard_map/ppermute | solution.py:297
  52.9 0.1 collective-permute-start.18
  53.0 0.2 collective-permute-done.14.refs_2_
  53.2 1.8 %shard_map.133 = (bf16[128,3584]{1,0:T(8,128)(2,1)}, f32[8,128]{1,0:T(8,128)}) custom-call(s32[8,128]{1,0:T(8,128)S(1)} %bitcast.5, bf16[1,64,128]{2,1,0:T(8,128)(2,1)S(1)} %copy-done.4, bf16[16,3712]{1,0:T(8,128)(2,1)S(1)} %collective-permute-done.12.refs_0_, bf16[16,3712]{1,0:T(8,128)(2,1)S(1)} %collective-permute-done.13.refs_1_, ...), custom_call_target="tpu_custom_call" | custom-call | flops 58720256000 | bytes 1417216 | tf_op jit(solution)/shard_map/pallas_call | solution.py:32
  55.0 0.1 collective-permute-done.18.other_ref
  55.1 1.6 %shard_map.135 = (bf16[896,128]{1,0:T(8,128)(2,1)}, bf16[896,128]{1,0:T(8,128)(2,1)}, bf16[896,128]{1,0:T(8,128)(2,1)}) custom-call(bf16[2,128,896]{2,1,0:T(8,128)(2,1)S(1)} %get-tuple-element.39.here_ref, bf16[128,384]{1,0:T(8,128)(2,1)S(1)} %get-tuple-element.40.grads_ref, bf16[3,128,896]{2,1,0:T(8,128)(2,1)S(1)} %shard_map.134.own_ref, ...), custom_call_target="tpu_custom_call" | custom-call | flops 352321536 | bytes 3604480 | tf_op jit(solution)/shard_map/pallas_call | solution.py:32
  (24 shorter events, 0.3 us)
Async XLA Ops:
  3.5 18.7 %collective-permute-start.8 = (bf16[896,384]{1,0:T(8,128)(2,1)}, bf16[896,384]{1,0:T(8,128)(2,1)S(1)}, u32[]{:S(2)}, u32[]{:S(2)}) collective-permute-start(bf16[896,384]{1,0:T(8,128)(2,1)} %get-tuple-element.30.refs_8_), channel_id=1, source_target_pairs={{0,16},{1,17},{2,18},{3,19},{4,20},{5,21},{6,22},{7,23},{8,24},{9,... | collective-permute-start | bytes 2064392 | tf_op jit(solution)/shard_map/ppermute | solution.py:297
  6.6 17.5 %collective-permute-start.7 = (bf16[896,384]{1,0:T(8,128)(2,1)}, bf16[896,384]{1,0:T(8,128)(2,1)S(1)}, u32[]{:S(2)}, u32[]{:S(2)}) collective-permute-start(bf16[896,384]{1,0:T(8,128)(2,1)} %get-tuple-element.30.refs_8_), channel_id=1, source_target_pairs={{0,8},{1,9},{2,10},{3,11},{4,12},{5,13},{6,14},{7,15},{8,0},{9,1},... | collective-permute-start | bytes 2064392 | tf_op jit(solution)/shard_map/ppermute | solution.py:297
  8.1 11.0 %collective-permute-start.2 = (bf16[16,7296]{1,0:T(8,128)(2,1)}, bf16[16,7296]{1,0:T(8,128)(2,1)S(1)}, u32[]{:S(2)}, u32[]{:S(2)}) collective-permute-start(bf16[16,7296]{1,0:T(8,128)(2,1)} %get-tuple-element.29.refs_3_), channel_id=1, source_target_pairs={{0,2},{1,3},{2,0},{3,1},{4,6},{5,7},{6,4},{7,5},{8,10},{9,11},{10,... | collective-permute-start | bytes 700424 | tf_op jit(solution)/shard_map/ppermute | solution.py:297
  9.6 19.7 %collective-permute-start.1 = (bf16[16,7296]{1,0:T(8,128)(2,1)}, bf16[16,7296]{1,0:T(8,128)(2,1)S(1)}, u32[]{:S(2)}, u32[]{:S(2)}) collective-permute-start(bf16[16,7296]{1,0:T(8,128)(2,1)} %get-tuple-element.29.refs_3_), channel_id=1, source_target_pairs={{0,4},{1,5},{2,6},{3,7},{4,0},{5,1},{6,2},{7,3},{8,12},{9,13},{10,... | collective-permute-start | bytes 700424 | tf_op jit(solution)/shard_map/ppermute | solution.py:297
  12.2 17.2 %collective-permute-start = (bf16[16,7296]{1,0:T(8,128)(2,1)}, bf16[16,7296]{1,0:T(8,128)(2,1)S(1)}, u32[]{:S(2)}, u32[]{:S(2)}) collective-permute-start(bf16[16,7296]{1,0:T(8,128)(2,1)} %get-tuple-element.29.refs_3_), channel_id=1, source_target_pairs={{0,6},{1,7},{2,4},{3,5},{4,2},{5,3},{6,0},{7,1},{8,14},{9,15},{10,... | collective-permute-start | bytes 700424 | tf_op jit(solution)/shard_map/ppermute | solution.py:297
  19.1 10.8 %collective-permute-start.6 = (bf16[16,7296]{1,0:T(8,128)(2,1)}, bf16[16,7296]{1,0:T(8,128)(2,1)S(1)}, u32[]{:S(2)}, u32[]{:S(2)}) collective-permute-start(bf16[16,7296]{1,0:T(8,128)(2,1)} %get-tuple-element.29.refs_3_), channel_id=1, source_target_pairs={{0,1},{1,0},{2,3},{3,2},{4,5},{5,4},{6,7},{7,6},{8,9},{9,8},{10,11... | collective-permute-start | bytes 700424 | tf_op jit(solution)/shard_map/ppermute | solution.py:297
  22.2 10.6 %copy-start = (bf16[896,384]{1,0:T(8,128)(2,1)S(1)}, bf16[896,384]{1,0:T(8,128)(2,1)}, u32[]{:S(2)}) copy-start(bf16[896,384]{1,0:T(8,128)(2,1)} %get-tuple-element.30.refs_8_) | copy-start | bytes 2064388
  22.2 10.6 %copy-start.1 = (bf16[16,7296]{1,0:T(8,128)(2,1)S(1)}, bf16[16,7296]{1,0:T(8,128)(2,1)}, u32[]{:S(2)}) copy-start(bf16[16,7296]{1,0:T(8,128)(2,1)} %get-tuple-element.29.refs_3_) | copy-start | bytes 700420
  22.3 9.3 %collective-permute-start.9 = (bf16[448,384]{1,0:T(8,128)(2,1)S(1)}, bf16[448,384]{1,0:T(8,128)(2,1)S(1)}, u32[]{:S(2)}, u32[]{:S(2)}) collective-permute-start(bf16[448,384]{1,0:T(8,128)(2,1)S(1)} %shard_map.129), channel_id=1, source_target_pairs={{0,8},{1,9},{2,10},{3,11},{4,12},{5,13},{6,14},{7,15},{8,0},{9,1},... | collective-permute-start | bytes 1032200 | tf_op jit(solution)/shard_map/ppermute | solution.py:297
  24.1 8.7 %copy-start.3 = (s32[4,1]{0,1:T(1,128)S(1)}, s32[4,1]{0,1:T(1,128)}, u32[]{:S(2)}) copy-start(s32[4,1]{0,1:T(1,128)} %param.14) | copy-start | bytes 52
  24.1 8.7 %collective-permute-start.10 = (bf16[448,384]{1,0:T(8,128)(2,1)S(1)}, bf16[448,384]{1,0:T(8,128)(2,1)S(1)}, u32[]{:S(2)}, u32[]{:S(2)}) collective-permute-start(bf16[448,384]{1,0:T(8,128)(2,1)S(1)} %shard_map.130), channel_id=1, source_target_pairs={{0,16},{1,17},{2,18},{3,19},{4,20},{5,21},{6,22},{7,23},{8,24},{9,... | collective-permute-start | bytes 1032200 | tf_op jit(solution)/shard_map/ppermute | solution.py:297
  29.4 1.5 %collective-permute-start.5 = (bf16[16,7296]{1,0:T(8,128)(2,1)S(1)}, bf16[16,7296]{1,0:T(8,128)(2,1)S(1)}, u32[]{:S(2)}, u32[]{:S(2)}) collective-permute-start(bf16[16,7296]{1,0:T(8,128)(2,1)S(1)} %collective-permute-done.2.refs_2_), channel_id=1, source_target_pairs={{0,1},{1,0},{2,3},{3,2},{4,5},{5,4},{6,7},{7,6},{8,9},{9,8},{10,11... | collective-permute-start | bytes 700424 | tf_op jit(solution)/shard_map/ppermute | solution.py:297
  29.4 1.8 %collective-permute-start.4 = (bf16[16,7296]{1,0:T(8,128)(2,1)S(1)}, bf16[16,7296]{1,0:T(8,128)(2,1)S(1)}, u32[]{:S(2)}, u32[]{:S(2)}) collective-permute-start(bf16[16,7296]{1,0:T(8,128)(2,1)S(1)} %collective-permute-done.1.refs_1_), channel_id=1, source_target_pairs={{0,1},{1,0},{2,3},{3,2},{4,5},{5,4},{6,7},{7,6},{8,9},{9,8},{10,11... | collective-permute-start | bytes 700424 | tf_op jit(solution)/shard_map/ppermute | solution.py:297
  29.9 1.6 %collective-permute-start.3 = (bf16[16,7296]{1,0:T(8,128)(2,1)S(1)}, bf16[16,7296]{1,0:T(8,128)(2,1)S(1)}, u32[]{:S(2)}, u32[]{:S(2)}) collective-permute-start(bf16[16,7296]{1,0:T(8,128)(2,1)S(1)} %collective-permute-done.refs_0_), channel_id=1, source_target_pairs={{0,1},{1,0},{2,3},{3,2},{4,5},{5,4},{6,7},{7,6},{8,9},{9,8},{10,11... | collective-permute-start | bytes 700424 | tf_op jit(solution)/shard_map/ppermute | solution.py:297
  34.6 1.9 %collective-permute-start.11 = (bf16[64,3712]{1,0:T(8,128)(2,1)S(1)}, bf16[64,3712]{1,0:T(8,128)(2,1)S(1)}, u32[]{:S(2)}, u32[]{:S(2)}) collective-permute-start(bf16[64,3712]{1,0:T(8,128)(2,1)S(1)} %get-tuple-element.32), channel_id=1, source_target_pairs={{0,1},{1,0},{2,3},{3,2},{4,5},{5,4},{6,7},{7,6},{8,9},{9,8},{10,11... | collective-permute-start | bytes 1425416 | tf_op jit(solution)/shard_map/ppermute | solution.py:297
  34.7 11.5 %collective-permute-start.17 = (bf16[128,1280]{1,0:T(8,128)(2,1)S(1)}, bf16[128,1280]{1,0:T(8,128)(2,1)S(1)}, u32[]{:S(2)}, u32[]{:S(2)}) collective-permute-start(bf16[128,1280]{1,0:T(8,128)(2,1)S(1)} %get-tuple-element.45), channel_id=1, source_target_pairs={{0,24},{1,25},{2,26},{3,27},{4,28},{5,29},{6,30},{7,31},{8,16},{9,... | collective-permute-start | bytes 983048 | tf_op jit(solution)/shard_map/ppermute | solution.py:297
  36.6 16.2 %collective-permute-start.15 = (bf16[128,1280]{1,0:T(8,128)(2,1)S(1)}, bf16[128,1280]{1,0:T(8,128)(2,1)S(1)}, u32[]{:S(2)}, u32[]{:S(2)}) collective-permute-start(bf16[128,1280]{1,0:T(8,128)(2,1)S(1)} %get-tuple-element.42), channel_id=1, source_target_pairs={{0,8},{1,9},{2,10},{3,11},{4,12},{5,13},{6,14},{7,15},{8,0},{9,1},... | collective-permute-start | bytes 983048 | tf_op jit(solution)/shard_map/ppermute | solution.py:297
  37.9 14.9 %collective-permute-start.16 = (bf16[128,1280]{1,0:T(8,128)(2,1)S(1)}, bf16[128,1280]{1,0:T(8,128)(2,1)S(1)}, u32[]{:S(2)}, u32[]{:S(2)}) collective-permute-start(bf16[128,1280]{1,0:T(8,128)(2,1)S(1)} %get-tuple-element.44), channel_id=1, source_target_pairs={{0,16},{1,17},{2,18},{3,19},{4,20},{5,21},{6,22},{7,23},{8,24},{9,... | collective-permute-start | bytes 983048 | tf_op jit(solution)/shard_map/ppermute | solution.py:297
  38.7 14.2 %collective-permute-start.12 = (bf16[16,3712]{1,0:T(8,128)(2,1)S(1)}, bf16[16,3712]{1,0:T(8,128)(2,1)S(1)}, u32[]{:S(2)}, u32[]{:S(2)}) collective-permute-start(bf16[16,3712]{1,0:T(8,128)(2,1)S(1)} %get-tuple-element.33), channel_id=1, source_target_pairs={{0,6},{1,7},{2,4},{3,5},{4,2},{5,3},{6,0},{7,1},{8,14},{9,15},{10,... | collective-permute-start | bytes 356360 | tf_op jit(solution)/shard_map/ppermute | solution.py:297
  42.3 10.9 %copy-start.2 = (s32[128,8]{0,1:T(8,128)S(1)}, s32[128,8]{0,1:T(8,128)}, u32[]{:S(2)}) copy-start(s32[128,8]{0,1:T(8,128)} %param.11) | copy-start | bytes 12292
  42.3 10.9 %copy-start.4 = (bf16[1,64,128]{2,1,0:T(8,128)(2,1)S(1)}, bf16[1,64,128]{2,1,0:T(8,128)(2,1)}, u32[]{:S(2)}) copy-start(bf16[1,64,128]{2,1,0:T(8,128)(2,1)} %get-tuple-element.27.placed_ref) | copy-start | bytes 49156
  42.3 10.6 %collective-permute-start.13 = (bf16[16,3712]{1,0:T(8,128)(2,1)S(1)}, bf16[16,3712]{1,0:T(8,128)(2,1)S(1)}, u32[]{:S(2)}, u32[]{:S(2)}) collective-permute-start(bf16[16,3712]{1,0:T(8,128)(2,1)S(1)} %get-tuple-element.34), channel_id=1, source_target_pairs={{0,4},{1,5},{2,6},{3,7},{4,0},{5,1},{6,2},{7,3},{8,12},{9,13},{10,... | collective-permute-start | bytes 356360 | tf_op jit(solution)/shard_map/ppermute | solution.py:297
  46.2 7.0 %collective-permute-start.14 = (bf16[16,3712]{1,0:T(8,128)(2,1)S(1)}, bf16[16,3712]{1,0:T(8,128)(2,1)S(1)}, u32[]{:S(2)}, u32[]{:S(2)}) collective-permute-start(bf16[16,3712]{1,0:T(8,128)(2,1)S(1)} %get-tuple-element.35), channel_id=1, source_target_pairs={{0,2},{1,3},{2,0},{3,1},{4,6},{5,7},{6,4},{7,5},{8,10},{9,11},{10,... | collective-permute-start | bytes 356360 | tf_op jit(solution)/shard_map/ppermute | solution.py:297
  52.9 2.2 %collective-permute-start.18 = (bf16[3,128,896]{2,1,0:T(8,128)(2,1)S(1)}, bf16[3,128,896]{2,1,0:T(8,128)(2,1)S(1)}, u32[]{:S(2)}, u32[]{:S(2)}) collective-permute-start(bf16[3,128,896]{2,1,0:T(8,128)(2,1)S(1)} %shard_map.134.own_ref), channel_id=1, source_target_pairs={{0,1},{1,0},{2,3},{3,2},{4,5},{5,4},{6,7},{7,6},{8,9},{9,8},{10,11... | collective-permute-start | bytes 2064392 | tf_op jit(solution)/shard_map/ppermute | solution.py:297

commit v15 on v13

--- a/solution.py
+++ b/solution.py
@@ -389,7 +389,12 @@
     passed = [send(part, 2 * (n // 2 + 1), 0) for n, part in enumerate(passed)]
     (own_rows,) = call(stack_kernel, [shape((rep - 1, 2 * rows, width))], [odd] + even + passed)
     other_rows = send(own_rows, 0, 1)
-    group_grads = [grads] + [send(grads, k, 0) for k in range(1, rep)]
+    group_grads = [grads]
+    bit = 1
+    while bit < rep:
+        array = group_grads[0] if bit == 1 else jnp.concatenate(group_grads, axis=0)
+        group_grads.append(send(array, bit, 0))
+        bit *= 2
     grad_gate, grad_up, grad_down = call(
         functools.partial(weight_kernel, rep),
         [shape((width, units))] * 3,

time: 57.7 us -> 59.5 us (1.031)
  starting transfers between devices: 23.9 us -> 25.7 us
    ppermute x24 -> x23, starting transfers between devices: 23.9 us -> 25.7 us  [send(): return lax.ppermute(array, ('rep', 'ep'), pairs)]
    ppermute x24 -> x23, waiting for transfers between devices: 25.1 us -> 25 us  [send(): return lax.ppermute(array, ('rep', 'ep'), pairs)]
  transfers between devices with their start and end apart: 24 -> 23, of which waited for: 12 -> 10; matrix products, arithmetic and copies ran while one was open for 0% -> 0% of each run, Pallas kernels for 6% -> 6%
where the time goes in v15:
time: 59.5 us; the launch traced here: 59.3 us
  starting transfers between devices  25.7 us (43%)
  waiting for transfers between devices  25 us (42%)
  Pallas kernels  7.75 us (13%)
  between operations  0.81 us (1%)
    ppermute x23, starting transfers between devices, send(): return lax.ppermute(array, ('rep', 'ep'), pairs)  25.7 us
    ppermute x23, waiting for transfers between devices, send(): return lax.ppermute(array, ('rep', 'ep'), pairs)  25 us
    pallas_call x11, Pallas kernels, call(): pl.pallas_call(kernel, out_shape=tuple(outs), in_specs=[HBM if n in store...  7.75 us
  transfers between devices with their start and end apart: 23, of which 10 were waited for; matrix products, arithmetic and copies ran while one was open for 0% of the time, Pallas kernels for 6%

profile of v15, /device:TPU:0, one launch (start us, length us, event | category | flops | bytes accessed | tf_op | source)
XLA Modules:
  0.0 59.3 jit_solution(5119376769173442546)
XLA Ops:
  0.6 2.9 %shard_map.128 = (bf16[16,7296]{1,0:T(8,128)(2,1)}, bf16[1,64,128]{2,1,0:T(8,128)(2,1)}, bf16[896,384]{1,0:T(8,128)(2,1)}) custom-call(s32[4]{0:T(128)} %live_ref.1, bf16[128,3584]{1,0:T(8,128)(2,1)} %tok_ref.1, bf16[128,3584]{1,0:T(8,128)(2,1)} %grad_ref.1, s32[8,128]{1,0:T(8,128)} %bitcast.4, bf16[8,128]{1,0:T(8,128)(2,1)} %bitcast.7, ...), custom_call_target="tpu_custom_call" | custom-call | bytes 3467280 | tf_op jit(solution)/shard_map/pallas_call | solution.py:32
  3.5 3.0 %collective-permute-start.8 = (bf16[896,384]{1,0:T(8,128)(2,1)}, bf16[896,384]{1,0:T(8,128)(2,1)S(1)}, u32[]{:S(2)}, u32[]{:S(2)}) collective-permute-start(bf16[896,384]{1,0:T(8,128)(2,1)} %get-tuple-element.33.refs_8_), channel_id=1, source_target_pairs={{0,16},{1,17},{2,18},{3,19},{4,20},{5,21},{6,22},{7,23},{8,24},{9,... | collective-permute-start | bytes 2064392 | tf_op jit(solution)/shard_map/ppermute | solution.py:305
  6.5 1.5 %collective-permute-start.7 = (bf16[896,384]{1,0:T(8,128)(2,1)}, bf16[896,384]{1,0:T(8,128)(2,1)S(1)}, u32[]{:S(2)}, u32[]{:S(2)}) collective-permute-start(bf16[896,384]{1,0:T(8,128)(2,1)} %get-tuple-element.33.refs_8_), channel_id=1, source_target_pairs={{0,8},{1,9},{2,10},{3,11},{4,12},{5,13},{6,14},{7,15},{8,0},{9,1},... | collective-permute-start | bytes 2064392 | tf_op jit(solution)/shard_map/ppermute | solution.py:305
  8.0 1.6 %collective-permute-start.2 = (bf16[16,7296]{1,0:T(8,128)(2,1)}, bf16[16,7296]{1,0:T(8,128)(2,1)S(1)}, u32[]{:S(2)}, u32[]{:S(2)}) collective-permute-start(bf16[16,7296]{1,0:T(8,128)(2,1)} %get-tuple-element.32.refs_3_), channel_id=1, source_target_pairs={{0,2},{1,3},{2,0},{3,1},{4,6},{5,7},{6,4},{7,5},{8,10},{9,11},{10,... | collective-permute-start | bytes 700424 | tf_op jit(solution)/shard_map/ppermute | solution.py:305
  9.6 2.6 %collective-permute-start.1 = (bf16[16,7296]{1,0:T(8,128)(2,1)}, bf16[16,7296]{1,0:T(8,128)(2,1)S(1)}, u32[]{:S(2)}, u32[]{:S(2)}) collective-permute-start(bf16[16,7296]{1,0:T(8,128)(2,1)} %get-tuple-element.32.refs_3_), channel_id=1, source_target_pairs={{0,4},{1,5},{2,6},{3,7},{4,0},{5,1},{6,2},{7,3},{8,12},{9,13},{10,... | collective-permute-start | bytes 700424 | tf_op jit(solution)/shard_map/ppermute | solution.py:305
  12.2 0.2 collective-permute-start
  12.4 6.6 %collective-permute-done.2.refs_2_ = bf16[16,7296]{1,0:T(8,128)(2,1)S(1)} collective-permute-done((bf16[16,7296]{1,0:T(8,128)(2,1)}, bf16[16,7296]{1,0:T(8,128)(2,1)S(1)}, u32[]{:S(2)}, u32[]{:S(2)}) %collective-permute-start.2) | collective-permute-done | bytes 233504 | tf_op jit(solution)/shard_map/ppermute | solution.py:305
  19.1 3.1 %collective-permute-done.8.all_ref.refs_10_ = bf16[896,384]{1,0:T(8,128)(2,1)S(1)} collective-permute-done((bf16[896,384]{1,0:T(8,128)(2,1)}, bf16[896,384]{1,0:T(8,128)(2,1)S(1)}, u32[]{:S(2)}, u32[]{:S(2)}) %collective-permute-start.8) | collective-permute-done | bytes 688160 | tf_op jit(solution)/shard_map/ppermute | solution.py:305
  22.2 1.8 %collective-permute-start.9 = (bf16[448,384]{1,0:T(8,128)(2,1)S(1)}, bf16[448,384]{1,0:T(8,128)(2,1)S(1)}, u32[]{:S(2)}, u32[]{:S(2)}) collective-permute-start(bf16[448,384]{1,0:T(8,128)(2,1)S(1)} %shard_map.129), channel_id=1, source_target_pairs={{0,8},{1,9},{2,10},{3,11},{4,12},{5,13},{6,14},{7,15},{8,0},{9,1},... | collective-permute-start | bytes 1032200 | tf_op jit(solution)/shard_map/ppermute | solution.py:305
  24.1 1.6 %collective-permute-start.10 = (bf16[448,384]{1,0:T(8,128)(2,1)S(1)}, bf16[448,384]{1,0:T(8,128)(2,1)S(1)}, u32[]{:S(2)}, u32[]{:S(2)}) collective-permute-start(bf16[448,384]{1,0:T(8,128)(2,1)S(1)} %shard_map.130), channel_id=1, source_target_pairs={{0,16},{1,17},{2,18},{3,19},{4,20},{5,21},{6,22},{7,23},{8,24},{9,... | collective-permute-start | bytes 1032200 | tf_op jit(solution)/shard_map/ppermute | solution.py:305
  25.6 3.7 %collective-permute-done.1.refs_1_ = bf16[16,7296]{1,0:T(8,128)(2,1)S(1)} collective-permute-done((bf16[16,7296]{1,0:T(8,128)(2,1)}, bf16[16,7296]{1,0:T(8,128)(2,1)S(1)}, u32[]{:S(2)}, u32[]{:S(2)}) %collective-permute-start.1) | collective-permute-done | bytes 233504 | tf_op jit(solution)/shard_map/ppermute | solution.py:305
  29.4 0.5 collective-permute-start.4
  30.0 0.8 %collective-permute-done.5.refs_6_ = bf16[16,7296]{1,0:T(8,128)(2,1)S(1)} collective-permute-done((bf16[16,7296]{1,0:T(8,128)(2,1)S(1)}, bf16[16,7296]{1,0:T(8,128)(2,1)S(1)}, u32[]{:S(2)}, u32[]{:S(2)}) %collective-permute-start.5) | collective-permute-done | bytes 233504 | tf_op jit(solution)/shard_map/ppermute | solution.py:305
  30.9 0.5 collective-permute-start.16
  31.4 0.1 collective-permute-done.3.refs_4_
  31.5 1.2 %collective-permute-done.10.refs_12_ = bf16[448,384]{1,0:T(8,128)(2,1)S(1)} collective-permute-done((bf16[448,384]{1,0:T(8,128)(2,1)S(1)}, bf16[448,384]{1,0:T(8,128)(2,1)S(1)}, u32[]{:S(2)}, u32[]{:S(2)}) %collective-permute-start.10) | collective-permute-done | bytes 344096 | tf_op jit(solution)/shard_map/ppermute | solution.py:305
  32.8 1.7 %shard_map.131 = (bf16[32,3712]{1,0:T(8,128)(2,1)S(1)}, bf16[32,3712]{1,0:T(8,128)(2,1)S(1)}, bf16[32,3712]{1,0:T(8,128)(2,1)S(1)}, bf16[32,3712]{1,0:T(8,128)(2...) custom-call(s32[1,4]{1,0:T(1,128)S(1)} %bitcast.6, ...), custom_call_target="tpu_custom_call" | custom-call | flops 587202560 | bytes 6127632 | tf_op jit(solution)/shard_map/pallas_call | solution.py:32
  34.6 0.5 collective-permute-start.14
  35.1 1.5 %collective-permute-start.17 = (bf16[128,896]{1,0:T(8,128)(2,1)S(1)}, bf16[128,896]{1,0:T(8,128)(2,1)S(1)}, u32[]{:S(2)}, u32[]{:S(2)}) collective-permute-start(bf16[128,896]{1,0:T(8,128)(2,1)S(1)} %get-tuple-element.47), channel_id=1, source_target_pairs={{0,16},{1,17},{2,18},{3,19},{4,20},{5,21},{6,22},{7,23},{8,24},{9,... | collective-permute-start | bytes 688136 | tf_op jit(solution)/shard_map/ppermute | solution.py:305
  36.6 0.5 collective-permute-start.21
  37.2 4.2 %collective-permute-start.12 = (bf16[16,3712]{1,0:T(8,128)(2,1)S(1)}, bf16[16,3712]{1,0:T(8,128)(2,1)S(1)}, u32[]{:S(2)}, u32[]{:S(2)}) collective-permute-start(bf16[16,3712]{1,0:T(8,128)(2,1)S(1)} %get-tuple-element.36), channel_id=1, source_target_pairs={{0,6},{1,7},{2,4},{3,5},{4,2},{5,3},{6,0},{7,1},{8,14},{9,15},{10,... | collective-permute-start | bytes 356360 | tf_op jit(solution)/shard_map/ppermute | solution.py:305
  41.5 2.7 %collective-permute-done.16.all_ref.odd_ref = bf16[2,128,896]{2,1,0:T(8,128)(2,1)S(1)} collective-permute-done((bf16[2,128,896]{2,1,0:T(8,128)(2,1)S(1)}, bf16[2,128,896]{2,1,0:T(8,128)(2,1)S(1)}, u32[]{:S(2)}, u32[]{:S(2)}) %collective-permute-start.16) | collective-permute-done | bytes 458784 | tf_op jit(solution)/shard_map/ppermute | solution.py:305
  44.2 2.8 %collective-permute-start.15 = (bf16[16,3712]{1,0:T(8,128)(2,1)S(1)}, bf16[16,3712]{1,0:T(8,128)(2,1)S(1)}, u32[]{:S(2)}, u32[]{:S(2)}) collective-permute-start(bf16[16,3712]{1,0:T(8,128)(2,1)S(1)} %get-tuple-element.40), channel_id=1, source_target_pairs={{0,2},{1,3},{2,0},{3,1},{4,6},{5,7},{6,4},{7,5},{8,10},{9,11},{10,... | collective-permute-start | bytes 356360 | tf_op jit(solution)/shard_map/ppermute | solution.py:305
  47.0 0.6 collective-permute-start.18
  47.6 1.5 %collective-permute-start.19 = (bf16[64,896]{1,0:T(8,128)(2,1)S(1)}, bf16[64,896]{1,0:T(8,128)(2,1)S(1)}, u32[]{:S(2)}, u32[]{:S(2)}) collective-permute-start(bf16[64,896]{1,0:T(8,128)(2,1)S(1)} %get-tuple-element.50), channel_id=1, source_target_pairs={{0,16},{1,17},{2,18},{3,19},{4,20},{5,21},{6,22},{7,23},{8,24},{9,... | collective-permute-start | bytes 344072 | tf_op jit(solution)/shard_map/ppermute | solution.py:305
  49.2 3.1 %collective-permute-done.18.refs_1_ = bf16[64,896]{1,0:T(8,128)(2,1)S(1)} collective-permute-done((bf16[64,896]{1,0:T(8,128)(2,1)S(1)}, bf16[64,896]{1,0:T(8,128)(2,1)S(1)}, u32[]{:S(2)}, u32[]{:S(2)}) %collective-permute-start.18) | collective-permute-done | bytes 114720 | tf_op jit(solution)/shard_map/ppermute | solution.py:305
  52.2 0.5 collective-permute-start.22
  52.8 2.0 %collective-permute-done.19.refs_2_ = bf16[64,896]{1,0:T(8,128)(2,1)S(1)} collective-permute-done((bf16[64,896]{1,0:T(8,128)(2,1)S(1)}, bf16[64,896]{1,0:T(8,128)(2,1)S(1)}, u32[]{:S(2)}, u32[]{:S(2)}) %collective-permute-start.19) | collective-permute-done | bytes 114720 | tf_op jit(solution)/shard_map/ppermute | solution.py:305
  54.8 0.1 collective-permute-start.20
  54.9 1.4 %shard_map.134 = (bf16[128,3584]{1,0:T(8,128)(2,1)}, f32[8,128]{1,0:T(8,128)}) custom-call(s32[8,128]{1,0:T(8,128)S(1)} %bitcast.5, bf16[1,64,128]{2,1,0:T(8,128)(2,1)S(1)} %copy-done.4, bf16[16,3712]{1,0:T(8,128)(2,1)S(1)} %collective-permute-done.12.refs_0_, bf16[16,3712]{1,0:T(8,128)(2,1)S(1)} %collective-permute-done.13.refs_1_, ...), custom_call_target="tpu_custom_call" | custom-call | flops 58720256000 | bytes 1417216 | tf_op jit(solution)/shard_map/pallas_call | solution.py:32
  56.3 1.6 %collective-permute-done.22.refs_2_ = bf16[256,384]{1,0:T(8,128)(2,1)S(1)} collective-permute-done((bf16[256,384]{1,0:T(8,128)(2,1)S(1)}, bf16[256,384]{1,0:T(8,128)(2,1)S(1)}, u32[]{:S(2)}, u32[]{:S(2)}) %collective-permute-start.22) | collective-permute-done | bytes 196640 | tf_op jit(solution)/shard_map/ppermute | solution.py:305
  57.9 1.4 %shard_map.138 = (bf16[896,128]{1,0:T(8,128)(2,1)}, bf16[896,128]{1,0:T(8,128)(2,1)}, bf16[896,128]{1,0:T(8,128)(2,1)}) custom-call(bf16[2,128,896]{2,1,0:T(8,128)(2,1)S(1)} %get-tuple-element.44.here_ref, bf16[3,128,896]{2,1,0:T(8,128)(2,1)S(1)} %shard_map.137.own_ref, bf16[3,128,896]{2,1,0:T(8,128)(2,1)S(1)} %collective-permute-done.20.other_ref, ...), custom_call_target="tpu_custom_call" | custom-call | flops 352321536 | bytes 2916352 | tf_op jit(solution)/shard_map/pallas_call | solution.py:32
  (36 shorter events, 0.6 us)
Async XLA Ops:
  3.5 18.7 %collective-permute-start.8 = (bf16[896,384]{1,0:T(8,128)(2,1)}, bf16[896,384]{1,0:T(8,128)(2,1)S(1)}, u32[]{:S(2)}, u32[]{:S(2)}) collective-permute-start(bf16[896,384]{1,0:T(8,128)(2,1)} %get-tuple-element.33.refs_8_), channel_id=1, source_target_pairs={{0,16},{1,17},{2,18},{3,19},{4,20},{5,21},{6,22},{7,23},{8,24},{9,... | collective-permute-start | bytes 2064392 | tf_op jit(solution)/shard_map/ppermute | solution.py:305
  6.5 17.5 %collective-permute-start.7 = (bf16[896,384]{1,0:T(8,128)(2,1)}, bf16[896,384]{1,0:T(8,128)(2,1)S(1)}, u32[]{:S(2)}, u32[]{:S(2)}) collective-permute-start(bf16[896,384]{1,0:T(8,128)(2,1)} %get-tuple-element.33.refs_8_), channel_id=1, source_target_pairs={{0,8},{1,9},{2,10},{3,11},{4,12},{5,13},{6,14},{7,15},{8,0},{9,1},... | collective-permute-start | bytes 2064392 | tf_op jit(solution)/shard_map/ppermute | solution.py:305
  8.0 11.0 %collective-permute-start.2 = (bf16[16,7296]{1,0:T(8,128)(2,1)}, bf16[16,7296]{1,0:T(8,128)(2,1)S(1)}, u32[]{:S(2)}, u32[]{:S(2)}) collective-permute-start(bf16[16,7296]{1,0:T(8,128)(2,1)} %get-tuple-element.32.refs_3_), channel_id=1, source_target_pairs={{0,2},{1,3},{2,0},{3,1},{4,6},{5,7},{6,4},{7,5},{8,10},{9,11},{10,... | collective-permute-start | bytes 700424 | tf_op jit(solution)/shard_map/ppermute | solution.py:305
  9.6 19.7 %collective-permute-start.1 = (bf16[16,7296]{1,0:T(8,128)(2,1)}, bf16[16,7296]{1,0:T(8,128)(2,1)S(1)}, u32[]{:S(2)}, u32[]{:S(2)}) collective-permute-start(bf16[16,7296]{1,0:T(8,128)(2,1)} %get-tuple-element.32.refs_3_), channel_id=1, source_target_pairs={{0,4},{1,5},{2,6},{3,7},{4,0},{5,1},{6,2},{7,3},{8,12},{9,13},{10,... | collective-permute-start | bytes 700424 | tf_op jit(solution)/shard_map/ppermute | solution.py:305
  12.2 17.2 %collective-permute-start = (bf16[16,7296]{1,0:T(8,128)(2,1)}, bf16[16,7296]{1,0:T(8,128)(2,1)S(1)}, u32[]{:S(2)}, u32[]{:S(2)}) collective-permute-start(bf16[16,7296]{1,0:T(8,128)(2,1)} %get-tuple-element.32.refs_3_), channel_id=1, source_target_pairs={{0,6},{1,7},{2,4},{3,5},{4,2},{5,3},{6,0},{7,1},{8,14},{9,15},{10,... | collective-permute-start | bytes 700424 | tf_op jit(solution)/shard_map/ppermute | solution.py:305
  19.1 10.8 %collective-permute-start.6 = (bf16[16,7296]{1,0:T(8,128)(2,1)}, bf16[16,7296]{1,0:T(8,128)(2,1)S(1)}, u32[]{:S(2)}, u32[]{:S(2)}) collective-permute-start(bf16[16,7296]{1,0:T(8,128)(2,1)} %get-tuple-element.32.refs_3_), channel_id=1, source_target_pairs={{0,1},{1,0},{2,3},{3,2},{4,5},{5,4},{6,7},{7,6},{8,9},{9,8},{10,11... | collective-permute-start | bytes 700424 | tf_op jit(solution)/shard_map/ppermute | solution.py:305
  22.2 7.7 %copy-start = (bf16[16,7296]{1,0:T(8,128)(2,1)S(1)}, bf16[16,7296]{1,0:T(8,128)(2,1)}, u32[]{:S(2)}) copy-start(bf16[16,7296]{1,0:T(8,128)(2,1)} %get-tuple-element.32.refs_3_) | copy-start | bytes 700420
  22.2 9.3 %collective-permute-start.9 = (bf16[448,384]{1,0:T(8,128)(2,1)S(1)}, bf16[448,384]{1,0:T(8,128)(2,1)S(1)}, u32[]{:S(2)}, u32[]{:S(2)}) collective-permute-start(bf16[448,384]{1,0:T(8,128)(2,1)S(1)} %shard_map.129), channel_id=1, source_target_pairs={{0,8},{1,9},{2,10},{3,11},{4,12},{5,13},{6,14},{7,15},{8,0},{9,1},... | collective-permute-start | bytes 1032200 | tf_op jit(solution)/shard_map/ppermute | solution.py:305
  24.0 8.7 %copy-start.1 = (bf16[896,384]{1,0:T(8,128)(2,1)S(1)}, bf16[896,384]{1,0:T(8,128)(2,1)}, u32[]{:S(2)}) copy-start(bf16[896,384]{1,0:T(8,128)(2,1)} %get-tuple-element.33.refs_8_) | copy-start | bytes 2064388
  24.1 8.7 %collective-permute-start.10 = (bf16[448,384]{1,0:T(8,128)(2,1)S(1)}, bf16[448,384]{1,0:T(8,128)(2,1)S(1)}, u32[]{:S(2)}, u32[]{:S(2)}) collective-permute-start(bf16[448,384]{1,0:T(8,128)(2,1)S(1)} %shard_map.130), channel_id=1, source_target_pairs={{0,16},{1,17},{2,18},{3,19},{4,20},{5,21},{6,22},{7,23},{8,24},{9,... | collective-permute-start | bytes 1032200 | tf_op jit(solution)/shard_map/ppermute | solution.py:305
  29.4 1.5 %collective-permute-start.5 = (bf16[16,7296]{1,0:T(8,128)(2,1)S(1)}, bf16[16,7296]{1,0:T(8,128)(2,1)S(1)}, u32[]{:S(2)}, u32[]{:S(2)}) collective-permute-start(bf16[16,7296]{1,0:T(8,128)(2,1)S(1)} %collective-permute-done.2.refs_2_), channel_id=1, source_target_pairs={{0,1},{1,0},{2,3},{3,2},{4,5},{5,4},{6,7},{7,6},{8,9},{9,8},{10,11... | collective-permute-start | bytes 700424 | tf_op jit(solution)/shard_map/ppermute | solution.py:305
  29.4 2.0 %collective-permute-start.4 = (bf16[16,7296]{1,0:T(8,128)(2,1)S(1)}, bf16[16,7296]{1,0:T(8,128)(2,1)S(1)}, u32[]{:S(2)}, u32[]{:S(2)}) collective-permute-start(bf16[16,7296]{1,0:T(8,128)(2,1)S(1)} %collective-permute-done.1.refs_1_), channel_id=1, source_target_pairs={{0,1},{1,0},{2,3},{3,2},{4,5},{5,4},{6,7},{7,6},{8,9},{9,8},{10,11... | collective-permute-start | bytes 700424 | tf_op jit(solution)/shard_map/ppermute | solution.py:305
  29.9 1.6 %collective-permute-start.3 = (bf16[16,7296]{1,0:T(8,128)(2,1)S(1)}, bf16[16,7296]{1,0:T(8,128)(2,1)S(1)}, u32[]{:S(2)}, u32[]{:S(2)}) collective-permute-start(bf16[16,7296]{1,0:T(8,128)(2,1)S(1)} %collective-permute-done.refs_0_), channel_id=1, source_target_pairs={{0,1},{1,0},{2,3},{3,2},{4,5},{5,4},{6,7},{7,6},{8,9},{9,8},{10,11... | collective-permute-start | bytes 700424 | tf_op jit(solution)/shard_map/ppermute | solution.py:305
  30.9 1.9 %copy-start.3 = (s32[4,1]{0,1:T(1,128)S(1)}, s32[4,1]{0,1:T(1,128)}, u32[]{:S(2)}) copy-start(s32[4,1]{0,1:T(1,128)} %param.14) | copy-start | bytes 52
  30.9 13.4 %collective-permute-start.16 = (bf16[2,128,896]{2,1,0:T(8,128)(2,1)S(1)}, bf16[2,128,896]{2,1,0:T(8,128)(2,1)S(1)}, u32[]{:S(2)}, u32[]{:S(2)}) collective-permute-start(bf16[2,128,896]{2,1,0:T(8,128)(2,1)S(1)} %get-tuple-element.46), channel_id=1, source_target_pairs={{0,8},{1,9},{2,10},{3,11},{4,12},{5,13},{6,14},{7,15},{8,0},{9,1},... | collective-permute-start | bytes 1376264 | tf_op jit(solution)/shard_map/ppermute | solution.py:305
  34.5 2.6 %collective-permute-start.11 = (bf16[32,3712]{1,0:T(8,128)(2,1)S(1)}, bf16[32,3712]{1,0:T(8,128)(2,1)S(1)}, u32[]{:S(2)}, u32[]{:S(2)}) collective-permute-start(bf16[32,3712]{1,0:T(8,128)(2,1)S(1)} %get-tuple-element.35), channel_id=1, source_target_pairs={{0,1},{1,0},{2,3},{3,2},{4,5},{5,4},{6,7},{7,6},{8,9},{9,8},{10,11... | collective-permute-start | bytes 712712 | tf_op jit(solution)/shard_map/ppermute | solution.py:305
  34.6 6.9 %collective-permute-start.14 = (bf16[32,3712]{1,0:T(8,128)(2,1)S(1)}, bf16[32,3712]{1,0:T(8,128)(2,1)S(1)}, u32[]{:S(2)}, u32[]{:S(2)}) collective-permute-start(bf16[32,3712]{1,0:T(8,128)(2,1)S(1)} %get-tuple-element.39), channel_id=1, source_target_pairs={{0,1},{1,0},{2,3},{3,2},{4,5},{5,4},{6,7},{7,6},{8,9},{9,8},{10,11... | collective-permute-start | bytes 712712 | tf_op jit(solution)/shard_map/ppermute | solution.py:305
  35.1 11.9 %collective-permute-start.17 = (bf16[128,896]{1,0:T(8,128)(2,1)S(1)}, bf16[128,896]{1,0:T(8,128)(2,1)S(1)}, u32[]{:S(2)}, u32[]{:S(2)}) collective-permute-start(bf16[128,896]{1,0:T(8,128)(2,1)S(1)} %get-tuple-element.47), channel_id=1, source_target_pairs={{0,16},{1,17},{2,18},{3,19},{4,20},{5,21},{6,22},{7,23},{8,24},{9,... | collective-permute-start | bytes 688136 | tf_op jit(solution)/shard_map/ppermute | solution.py:305
  36.6 11.0 %collective-permute-start.21 = (bf16[128,384]{1,0:T(8,128)(2,1)S(1)}, bf16[128,384]{1,0:T(8,128)(2,1)S(1)}, u32[]{:S(2)}, u32[]{:S(2)}) collective-permute-start(bf16[128,384]{1,0:T(8,128)(2,1)S(1)} %get-tuple-element.51.refs_0_), channel_id=1, source_target_pairs={{0,8},{1,9},{2,10},{3,11},{4,12},{5,13},{6,14},{7,15},{8,0},{9,1},... | collective-permute-start | bytes 294920 | tf_op jit(solution)/shard_map/ppermute | solution.py:305
  37.2 17.6 %collective-permute-start.12 = (bf16[16,3712]{1,0:T(8,128)(2,1)S(1)}, bf16[16,3712]{1,0:T(8,128)(2,1)S(1)}, u32[]{:S(2)}, u32[]{:S(2)}) collective-permute-start(bf16[16,3712]{1,0:T(8,128)(2,1)S(1)} %get-tuple-element.36), channel_id=1, source_target_pairs={{0,6},{1,7},{2,4},{3,5},{4,2},{5,3},{6,0},{7,1},{8,14},{9,15},{10,... | collective-permute-start | bytes 356360 | tf_op jit(solution)/shard_map/ppermute | solution.py:305
  41.5 13.4 %collective-permute-start.13 = (bf16[16,3712]{1,0:T(8,128)(2,1)S(1)}, bf16[16,3712]{1,0:T(8,128)(2,1)S(1)}, u32[]{:S(2)}, u32[]{:S(2)}) collective-permute-start(bf16[16,3712]{1,0:T(8,128)(2,1)S(1)} %get-tuple-element.37), channel_id=1, source_target_pairs={{0,4},{1,5},{2,6},{3,7},{4,0},{5,1},{6,2},{7,3},{8,12},{9,13},{10,... | collective-permute-start | bytes 356360 | tf_op jit(solution)/shard_map/ppermute | solution.py:305
  44.2 10.6 %collective-permute-start.15 = (bf16[16,3712]{1,0:T(8,128)(2,1)S(1)}, bf16[16,3712]{1,0:T(8,128)(2,1)S(1)}, u32[]{:S(2)}, u32[]{:S(2)}) collective-permute-start(bf16[16,3712]{1,0:T(8,128)(2,1)S(1)} %get-tuple-element.40), channel_id=1, source_target_pairs={{0,2},{1,3},{2,0},{3,1},{4,6},{5,7},{6,4},{7,5},{8,10},{9,11},{10,... | collective-permute-start | bytes 356360 | tf_op jit(solution)/shard_map/ppermute | solution.py:305
  47.0 5.2 %collective-permute-start.18 = (bf16[64,896]{1,0:T(8,128)(2,1)S(1)}, bf16[64,896]{1,0:T(8,128)(2,1)S(1)}, u32[]{:S(2)}, u32[]{:S(2)}) collective-permute-start(bf16[64,896]{1,0:T(8,128)(2,1)S(1)} %get-tuple-element.49), channel_id=1, source_target_pairs={{0,16},{1,17},{2,18},{3,19},{4,20},{5,21},{6,22},{7,23},{8,24},{9,... | collective-permute-start | bytes 344072 | tf_op jit(solution)/shard_map/ppermute | solution.py:305
  47.6 7.1 %collective-permute-start.19 = (bf16[64,896]{1,0:T(8,128)(2,1)S(1)}, bf16[64,896]{1,0:T(8,128)(2,1)S(1)}, u32[]{:S(2)}, u32[]{:S(2)}) collective-permute-start(bf16[64,896]{1,0:T(8,128)(2,1)S(1)} %get-tuple-element.50), channel_id=1, source_target_pairs={{0,16},{1,17},{2,18},{3,19},{4,20},{5,21},{6,22},{7,23},{8,24},{9,... | collective-permute-start | bytes 344072 | tf_op jit(solution)/shard_map/ppermute | solution.py:305
  49.2 5.7 %copy-start.2 = (s32[128,8]{0,1:T(8,128)S(1)}, s32[128,8]{0,1:T(8,128)}, u32[]{:S(2)}) copy-start(s32[128,8]{0,1:T(8,128)} %param.11) | copy-start | bytes 12292
  49.2 5.7 %copy-start.4 = (bf16[1,64,128]{2,1,0:T(8,128)(2,1)S(1)}, bf16[1,64,128]{2,1,0:T(8,128)(2,1)}, u32[]{:S(2)}) copy-start(bf16[1,64,128]{2,1,0:T(8,128)(2,1)} %get-tuple-element.30.placed_ref) | copy-start | bytes 49156
  52.2 5.7 %collective-permute-start.22 = (bf16[256,384]{1,0:T(8,128)(2,1)S(1)}, bf16[256,384]{1,0:T(8,128)(2,1)S(1)}, u32[]{:S(2)}, u32[]{:S(2)}) collective-permute-start(bf16[256,384]{1,0:T(8,128)(2,1)S(1)} %pad_maximum_fusion), channel_id=1, source_target_pairs={{0,16},{1,17},{2,18},{3,19},{4,20},{5,21},{6,22},{7,23},{8,24},{9,... | collective-permute-start | bytes 589832 | tf_op jit(solution)/shard_map/ppermute | solution.py:305
  54.8 3.2 %collective-permute-start.20 = (bf16[3,128,896]{2,1,0:T(8,128)(2,1)S(1)}, bf16[3,128,896]{2,1,0:T(8,128)(2,1)S(1)}, u32[]{:S(2)}, u32[]{:S(2)}) collective-permute-start(bf16[3,128,896]{2,1,0:T(8,128)(2,1)S(1)} %shard_map.137.own_ref), channel_id=1, source_target_pairs={{0,1},{1,0},{2,3},{3,2},{4,5},{5,4},{6,7},{7,6},{8,9},{9,8},{10,11... | collective-permute-start | bytes 2064392 | tf_op jit(solution)/shard_map/ppermute | solution.py:305

commit v16 on v9

--- a/solution.py
+++ b/solution.py
@@ -217,7 +217,7 @@
         refs[-1][k] = ref[:, : refs[-1].shape[2]]
 
 
-def weight_kernel(rep, here_ref, grads_ref, other_ref, *refs):
+def weight_kernel(rep, here_ref, grads_ref, near_ref, far_ref, *refs):
     away, outs, held, sems = refs[: rep - 1], refs[rep - 1 : -4], refs[-4:-1], refs[-1]
     units = outs[0].shape[1]
     width = here_ref.shape[2]
@@ -227,8 +227,9 @@
         some = slice(part * half, (part + 1) * half)
         rows = [here_ref[part]]
         got = [grads_ref[:, columns]]
-        for k, ref in enumerate(away):
-            rows += [ref[some, :width], other_ref[k, some]]
+        others = [ref[k, some] for ref in (near_ref, far_ref) for k in range(ref.shape[0])]
+        for other, ref in zip(others, away):
+            rows += [ref[some, :width], other]
             got.append(ref[:, width + columns.start : width + columns.stop])
         rows = jnp.concatenate(rows, axis=0)
         got = jnp.concatenate(got, axis=0)
@@ -352,13 +353,19 @@
     summed = call(sum_kernel, [shape((SLOT, model_dim + LANES))] * count, [own, send(other, 0, 1)])
     backs = [send(part, 0, CORES * j) if j else part for j, part in zip(order, summed)]
 
-    moved = [send(away[k - 1], k, 0) for k in range(1, rep)]
-    (own_rows,) = call(stack_kernel, [shape((rep - 1, 2 * rows, width))], moved)
-    other_rows = send(own_rows, 0, 1)
+    near = [k for k in range(1, rep) if k & (k - 1) == 0]
+    far = [k for k in range(1, rep) if k & (k - 1)]
+    near_moved = [send(away[k - 1], k, 0) for k in near]
+    (stacked,) = call(stack_kernel, [shape((len(near), 2 * rows, width))], near_moved)
+    near_other = send(stacked, 0, 1)
+    far_moved = [send(after(away[k - 1], summed[-2]), k, 0) for k in far]
+    ready = [after(far_moved[0], stacked)] + far_moved[1:]
+    (stacked,) = call(stack_kernel, [shape((len(far), 2 * rows, width))], ready)
+    far_other = send(stacked, 0, 1)
     grad_gate, grad_up, grad_down = call(
         functools.partial(weight_kernel, rep),
         [shape((width, units))] * 3,
-        [here, grads, other_rows] + moved,
+        [here, grads, near_other, far_other] + near_moved + far_moved,
         kept=(0, 1, 2),
         scratch=[pltpu.VMEM((width, units), BF16)] * 3 + [pltpu.SemaphoreType.DMA((3,))],
         flops=2 * 2 * rep * rows * width * 3 * units,

time: 56.6 us -> 56 us (0.989)
  waiting for transfers between devices: 25.6 us -> 24.8 us
    ppermute x19 -> x20, waiting for transfers between devices: 25.6 us -> 24.8 us  [send(): return lax.ppermute(array, ('rep', 'ep'), pairs)]
    ppermute x19 -> x20, starting transfers between devices: 22.4 us -> 22.5 us  [send(): return lax.ppermute(array, ('rep', 'ep'), pairs)]
    pallas_call x8 -> x9, Pallas kernels: 7.71 us -> 7.7 us  [call(): pl.pallas_call(kernel, out_shape=tuple(outs), in_specs=[HBM if n in store...]
  transfers between devices with their start and end apart: 19 -> 20, of which waited for: 11 -> 10; matrix products, arithmetic and copies ran while one was open for 0% -> 0% of each run, Pallas kernels for 3% -> 3%
where the time goes in v16:
time: 56 us; the launch traced here: 55.8 us
  waiting for transfers between devices  24.8 us (44%)
  starting transfers between devices  22.5 us (40%)
  Pallas kernels  7.7 us (14%)
  between operations  0.82 us (1%)
    ppermute x20, waiting for transfers between devices, send(): return lax.ppermute(array, ('rep', 'ep'), pairs)  24.8 us
    ppermute x20, starting transfers between devices, send(): return lax.ppermute(array, ('rep', 'ep'), pairs)  22.5 us
    pallas_call x9, Pallas kernels, call(): pl.pallas_call(kernel, out_shape=tuple(outs), in_specs=[HBM if n in store...  7.7 us
  transfers between devices with their start and end apart: 20, of which 10 were waited for; matrix products, arithmetic and copies ran while one was open for 0% of the time, Pallas kernels for 3%

profile of v16, /device:TPU:0, one launch (start us, length us, event | category | flops | bytes accessed | tf_op | source)
XLA Modules:
  0.0 55.8 jit_solution(17388012265351221616)
XLA Ops:
  0.6 2.9 %shard_map.128 = (bf16[16,7296]{1,0:T(8,128)(2,1)}, bf16[1,64,128]{2,1,0:T(8,128)(2,1)}, bf16[896,384]{1,0:T(8,128)(2,1)}) custom-call(s32[4]{0:T(128)} %live_ref.1, bf16[128,3584]{1,0:T(8,128)(2,1)} %tok_ref.1, bf16[128,3584]{1,0:T(8,128)(2,1)} %grad_ref.1, s32[8,128]{1,0:T(8,128)} %bitcast.4, bf16[8,128]{1,0:T(8,128)(2,1)} %bitcast.7, ...), custom_call_target="tpu_custom_call" | custom-call | bytes 3467280 | tf_op jit(solution)/shard_map/pallas_call | solution.py:32
  3.5 3.0 %collective-permute-start.8 = (bf16[896,384]{1,0:T(8,128)(2,1)}, bf16[896,384]{1,0:T(8,128)(2,1)S(1)}, u32[]{:S(2)}, u32[]{:S(2)}) collective-permute-start(bf16[896,384]{1,0:T(8,128)(2,1)} %get-tuple-element.30.refs_8_), channel_id=1, source_target_pairs={{0,16},{1,17},{2,18},{3,19},{4,20},{5,21},{6,22},{7,23},{8,24},{9,... | collective-permute-start | bytes 2064392 | tf_op jit(solution)/shard_map/ppermute | solution.py:290
  6.5 1.5 %collective-permute-start.7 = (bf16[896,384]{1,0:T(8,128)(2,1)}, bf16[896,384]{1,0:T(8,128)(2,1)S(1)}, u32[]{:S(2)}, u32[]{:S(2)}) collective-permute-start(bf16[896,384]{1,0:T(8,128)(2,1)} %get-tuple-element.30.refs_8_), channel_id=1, source_target_pairs={{0,8},{1,9},{2,10},{3,11},{4,12},{5,13},{6,14},{7,15},{8,0},{9,1},... | collective-permute-start | bytes 2064392 | tf_op jit(solution)/shard_map/ppermute | solution.py:290
  8.0 1.6 %collective-permute-start.2 = (bf16[16,7296]{1,0:T(8,128)(2,1)}, bf16[16,7296]{1,0:T(8,128)(2,1)S(1)}, u32[]{:S(2)}, u32[]{:S(2)}) collective-permute-start(bf16[16,7296]{1,0:T(8,128)(2,1)} %get-tuple-element.29.refs_3_), channel_id=1, source_target_pairs={{0,2},{1,3},{2,0},{3,1},{4,6},{5,7},{6,4},{7,5},{8,10},{9,11},{10,... | collective-permute-start | bytes 700424 | tf_op jit(solution)/shard_map/ppermute | solution.py:290
  9.6 2.6 %collective-permute-start.1 = (bf16[16,7296]{1,0:T(8,128)(2,1)}, bf16[16,7296]{1,0:T(8,128)(2,1)S(1)}, u32[]{:S(2)}, u32[]{:S(2)}) collective-permute-start(bf16[16,7296]{1,0:T(8,128)(2,1)} %get-tuple-element.29.refs_3_), channel_id=1, source_target_pairs={{0,4},{1,5},{2,6},{3,7},{4,0},{5,1},{6,2},{7,3},{8,12},{9,13},{10,... | collective-permute-start | bytes 700424 | tf_op jit(solution)/shard_map/ppermute | solution.py:290
  12.2 0.2 collective-permute-start
  12.4 6.6 %collective-permute-done.2.refs_2_ = bf16[16,7296]{1,0:T(8,128)(2,1)S(1)} collective-permute-done((bf16[16,7296]{1,0:T(8,128)(2,1)}, bf16[16,7296]{1,0:T(8,128)(2,1)S(1)}, u32[]{:S(2)}, u32[]{:S(2)}) %collective-permute-start.2) | collective-permute-done | bytes 233504 | tf_op jit(solution)/shard_map/ppermute | solution.py:290
  19.1 3.1 %collective-permute-done.8.all_ref.refs_10_ = bf16[896,384]{1,0:T(8,128)(2,1)S(1)} collective-permute-done((bf16[896,384]{1,0:T(8,128)(2,1)}, bf16[896,384]{1,0:T(8,128)(2,1)S(1)}, u32[]{:S(2)}, u32[]{:S(2)}) %collective-permute-start.8) | collective-permute-done | bytes 688160 | tf_op jit(solution)/shard_map/ppermute | solution.py:290
  22.2 1.8 %collective-permute-start.9 = (bf16[448,384]{1,0:T(8,128)(2,1)S(1)}, bf16[448,384]{1,0:T(8,128)(2,1)S(1)}, u32[]{:S(2)}, u32[]{:S(2)}) collective-permute-start(bf16[448,384]{1,0:T(8,128)(2,1)S(1)} %shard_map.129), channel_id=1, source_target_pairs={{0,8},{1,9},{2,10},{3,11},{4,12},{5,13},{6,14},{7,15},{8,0},{9,1},... | collective-permute-start | bytes 1032200 | tf_op jit(solution)/shard_map/ppermute | solution.py:290
  24.1 1.6 %collective-permute-start.10 = (bf16[448,384]{1,0:T(8,128)(2,1)S(1)}, bf16[448,384]{1,0:T(8,128)(2,1)S(1)}, u32[]{:S(2)}, u32[]{:S(2)}) collective-permute-start(bf16[448,384]{1,0:T(8,128)(2,1)S(1)} %shard_map.130), channel_id=1, source_target_pairs={{0,16},{1,17},{2,18},{3,19},{4,20},{5,21},{6,22},{7,23},{8,24},{9,... | collective-permute-start | bytes 1032200 | tf_op jit(solution)/shard_map/ppermute | solution.py:290
  25.7 3.7 %collective-permute-done.1.refs_1_ = bf16[16,7296]{1,0:T(8,128)(2,1)S(1)} collective-permute-done((bf16[16,7296]{1,0:T(8,128)(2,1)}, bf16[16,7296]{1,0:T(8,128)(2,1)S(1)}, u32[]{:S(2)}, u32[]{:S(2)}) %collective-permute-start.1) | collective-permute-done | bytes 233504 | tf_op jit(solution)/shard_map/ppermute | solution.py:290
  29.4 0.5 collective-permute-start.4
  29.9 0.1 collective-permute-start.3
  30.0 0.9 %collective-permute-done.5.refs_6_ = bf16[16,7296]{1,0:T(8,128)(2,1)S(1)} collective-permute-done((bf16[16,7296]{1,0:T(8,128)(2,1)S(1)}, bf16[16,7296]{1,0:T(8,128)(2,1)S(1)}, u32[]{:S(2)}, u32[]{:S(2)}) %collective-permute-start.5) | collective-permute-done | bytes 233504 | tf_op jit(solution)/shard_map/ppermute | solution.py:290
  30.9 0.3 collective-permute-done.4.refs_5_
  31.2 0.3 collective-permute-done.3.refs_4_
  31.6 1.2 %collective-permute-done.10.refs_12_ = bf16[448,384]{1,0:T(8,128)(2,1)S(1)} collective-permute-done((bf16[448,384]{1,0:T(8,128)(2,1)S(1)}, bf16[448,384]{1,0:T(8,128)(2,1)S(1)}, u32[]{:S(2)}, u32[]{:S(2)}) %collective-permute-start.10) | collective-permute-done | bytes 344096 | tf_op jit(solution)/shard_map/ppermute | solution.py:290
  32.8 1.8 %shard_map.131 = (bf16[64,3712]{1,0:T(8,128)(2,1)S(1)}, bf16[64,3712]{1,0:T(8,128)(2,1)S(1)}, bf16[128,384]{1,0:T(8,128)(2,1)S(1)}, bf16[2,128,896]{2,1,0:T(8,12...) custom-call(s32[1,4]{1,0:T(1,128)S(1)} %bitcast.6, ...), custom_call_target="tpu_custom_call" | custom-call | flops 587202560 | bytes 7110672 | tf_op jit(solution)/shard_map/pallas_call | solution.py:32
  34.6 0.1 collective-permute-start.11
  34.6 1.1 %collective-permute-start.15 = (bf16[128,1280]{1,0:T(8,128)(2,1)S(1)}, bf16[128,1280]{1,0:T(8,128)(2,1)S(1)}, u32[]{:S(2)}, u32[]{:S(2)}) collective-permute-start(bf16[128,1280]{1,0:T(8,128)(2,1)S(1)} %get-tuple-element.41), channel_id=1, source_target_pairs={{0,8},{1,9},{2,10},{3,11},{4,12},{5,13},{6,14},{7,15},{8,0},{9,1},... | collective-permute-start | bytes 983048 | tf_op jit(solution)/shard_map/ppermute | solution.py:290
  35.8 1.0 %collective-permute-start.16 = (bf16[128,1280]{1,0:T(8,128)(2,1)S(1)}, bf16[128,1280]{1,0:T(8,128)(2,1)S(1)}, u32[]{:S(2)}, u32[]{:S(2)}) collective-permute-start(bf16[128,1280]{1,0:T(8,128)(2,1)S(1)} %get-tuple-element.42), channel_id=1, source_target_pairs={{0,16},{1,17},{2,18},{3,19},{4,20},{5,21},{6,22},{7,23},{8,24},{9,... | collective-permute-start | bytes 983048 | tf_op jit(solution)/shard_map/ppermute | solution.py:290
  36.8 0.1 shard_map.132
  36.9 1.5 %collective-permute-start.18 = (bf16[128,1280]{1,0:T(8,128)(2,1)S(1)}, bf16[128,1280]{1,0:T(8,128)(2,1)S(1)}, u32[]{:S(2)}, u32[]{:S(2)}) collective-permute-start(bf16[128,1280]{1,0:T(8,128)(2,1)S(1)} %get-tuple-element.44), channel_id=1, source_target_pairs={{0,24},{1,25},{2,26},{3,27},{4,28},{5,29},{6,30},{7,31},{8,16},{9,... | collective-permute-start | bytes 983048 | tf_op jit(solution)/shard_map/ppermute | solution.py:290
  38.4 3.6 %collective-permute-start.12 = (bf16[16,3712]{1,0:T(8,128)(2,1)S(1)}, bf16[16,3712]{1,0:T(8,128)(2,1)S(1)}, u32[]{:S(2)}, u32[]{:S(2)}) collective-permute-start(bf16[16,3712]{1,0:T(8,128)(2,1)S(1)} %get-tuple-element.33), channel_id=1, source_target_pairs={{0,6},{1,7},{2,4},{3,5},{4,2},{5,3},{6,0},{7,1},{8,14},{9,15},{10,... | collective-permute-start | bytes 356360 | tf_op jit(solution)/shard_map/ppermute | solution.py:290
  42.0 3.2 %collective-permute-done.15.refs_0_ = bf16[128,1280]{1,0:T(8,128)(2,1)S(1)} collective-permute-done((bf16[128,1280]{1,0:T(8,128)(2,1)S(1)}, bf16[128,1280]{1,0:T(8,128)(2,1)S(1)}, u32[]{:S(2)}, u32[]{:S(2)}) %collective-permute-start.15) | collective-permute-done | bytes 327712 | tf_op jit(solution)/shard_map/ppermute | solution.py:290
  45.2 2.1 %collective-permute-start.14 = (bf16[16,3712]{1,0:T(8,128)(2,1)S(1)}, bf16[16,3712]{1,0:T(8,128)(2,1)S(1)}, u32[]{:S(2)}, u32[]{:S(2)}) collective-permute-start(bf16[16,3712]{1,0:T(8,128)(2,1)S(1)} %get-tuple-element.35), channel_id=1, source_target_pairs={{0,2},{1,3},{2,0},{3,1},{4,6},{5,7},{6,4},{7,5},{8,10},{9,11},{10,... | collective-permute-start | bytes 356360 | tf_op jit(solution)/shard_map/ppermute | solution.py:290
  47.4 3.8 %collective-permute-done.16.refs_1_ = bf16[128,1280]{1,0:T(8,128)(2,1)S(1)} collective-permute-done((bf16[128,1280]{1,0:T(8,128)(2,1)S(1)}, bf16[128,1280]{1,0:T(8,128)(2,1)S(1)}, u32[]{:S(2)}, u32[]{:S(2)}) %collective-permute-start.16) | collective-permute-done | bytes 327712 | tf_op jit(solution)/shard_map/ppermute | solution.py:290
  51.2 0.1 collective-permute-start.17
  51.3 1.5 %collective-permute-done.18.refs_0_.refs_2_ = bf16[128,1280]{1,0:T(8,128)(2,1)S(1)} collective-permute-done((bf16[128,1280]{1,0:T(8,128)(2,1)S(1)}, bf16[128,1280]{1,0:T(8,128)(2,1)S(1)}, u32[]{:S(2)}, u32[]{:S(2)}) %collective-permute-start.18) | collective-permute-done | bytes 327712 | tf_op jit(solution)/shard_map/ppermute | solution.py:290
  52.8 0.1 collective-permute-start.19
  52.9 1.4 %shard_map.133 = (bf16[128,3584]{1,0:T(8,128)(2,1)}, f32[8,128]{1,0:T(8,128)}) custom-call(s32[8,128]{1,0:T(8,128)S(1)} %bitcast.5, bf16[1,64,128]{2,1,0:T(8,128)(2,1)S(1)} %copy-done.4, bf16[16,3712]{1,0:T(8,128)(2,1)S(1)} %collective-permute-done.12.refs_0_, bf16[16,3712]{1,0:T(8,128)(2,1)S(1)} %collective-permute-done.13.refs_1_, ...), custom_call_target="tpu_custom_call" | custom-call | flops 58720256000 | bytes 1417216 | tf_op jit(solution)/shard_map/pallas_call | solution.py:32
  54.4 1.4 %shard_map.136 = (bf16[896,128]{1,0:T(8,128)(2,1)}, bf16[896,128]{1,0:T(8,128)(2,1)}, bf16[896,128]{1,0:T(8,128)(2,1)}) custom-call(bf16[2,128,896]{2,1,0:T(8,128)(2,1)S(1)} %get-tuple-element.39.here_ref, bf16[128,384]{1,0:T(8,128)(2,1)S(1)} %get-tuple-element.40.grads_ref, bf16[2,128,896]{2,1,0:T(8,128)(2,1)S(1)} %collective-permute-done.17.near_ref, ...), custom_call_target="tpu_custom_call" | custom-call | flops 352321536 | bytes 2916352 | tf_op jit(solution)/shard_map/pallas_call | solution.py:32
  (27 shorter events, 0.2 us)
Async XLA Ops:
  3.5 18.7 %collective-permute-start.8 = (bf16[896,384]{1,0:T(8,128)(2,1)}, bf16[896,384]{1,0:T(8,128)(2,1)S(1)}, u32[]{:S(2)}, u32[]{:S(2)}) collective-permute-start(bf16[896,384]{1,0:T(8,128)(2,1)} %get-tuple-element.30.refs_8_), channel_id=1, source_target_pairs={{0,16},{1,17},{2,18},{3,19},{4,20},{5,21},{6,22},{7,23},{8,24},{9,... | collective-permute-start | bytes 2064392 | tf_op jit(solution)/shard_map/ppermute | solution.py:290
  6.5 17.5 %collective-permute-start.7 = (bf16[896,384]{1,0:T(8,128)(2,1)}, bf16[896,384]{1,0:T(8,128)(2,1)S(1)}, u32[]{:S(2)}, u32[]{:S(2)}) collective-permute-start(bf16[896,384]{1,0:T(8,128)(2,1)} %get-tuple-element.30.refs_8_), channel_id=1, source_target_pairs={{0,8},{1,9},{2,10},{3,11},{4,12},{5,13},{6,14},{7,15},{8,0},{9,1},... | collective-permute-start | bytes 2064392 | tf_op jit(solution)/shard_map/ppermute | solution.py:290
  8.0 11.0 %collective-permute-start.2 = (bf16[16,7296]{1,0:T(8,128)(2,1)}, bf16[16,7296]{1,0:T(8,128)(2,1)S(1)}, u32[]{:S(2)}, u32[]{:S(2)}) collective-permute-start(bf16[16,7296]{1,0:T(8,128)(2,1)} %get-tuple-element.29.refs_3_), channel_id=1, source_target_pairs={{0,2},{1,3},{2,0},{3,1},{4,6},{5,7},{6,4},{7,5},{8,10},{9,11},{10,... | collective-permute-start | bytes 700424 | tf_op jit(solution)/shard_map/ppermute | solution.py:290
  9.6 19.7 %collective-permute-start.1 = (bf16[16,7296]{1,0:T(8,128)(2,1)}, bf16[16,7296]{1,0:T(8,128)(2,1)S(1)}, u32[]{:S(2)}, u32[]{:S(2)}) collective-permute-start(bf16[16,7296]{1,0:T(8,128)(2,1)} %get-tuple-element.29.refs_3_), channel_id=1, source_target_pairs={{0,4},{1,5},{2,6},{3,7},{4,0},{5,1},{6,2},{7,3},{8,12},{9,13},{10,... | collective-permute-start | bytes 700424 | tf_op jit(solution)/shard_map/ppermute | solution.py:290
  12.2 17.2 %collective-permute-start = (bf16[16,7296]{1,0:T(8,128)(2,1)}, bf16[16,7296]{1,0:T(8,128)(2,1)S(1)}, u32[]{:S(2)}, u32[]{:S(2)}) collective-permute-start(bf16[16,7296]{1,0:T(8,128)(2,1)} %get-tuple-element.29.refs_3_), channel_id=1, source_target_pairs={{0,6},{1,7},{2,4},{3,5},{4,2},{5,3},{6,0},{7,1},{8,14},{9,15},{10,... | collective-permute-start | bytes 700424 | tf_op jit(solution)/shard_map/ppermute | solution.py:290
  19.1 10.8 %collective-permute-start.6 = (bf16[16,7296]{1,0:T(8,128)(2,1)}, bf16[16,7296]{1,0:T(8,128)(2,1)S(1)}, u32[]{:S(2)}, u32[]{:S(2)}) collective-permute-start(bf16[16,7296]{1,0:T(8,128)(2,1)} %get-tuple-element.29.refs_3_), channel_id=1, source_target_pairs={{0,1},{1,0},{2,3},{3,2},{4,5},{5,4},{6,7},{7,6},{8,9},{9,8},{10,11... | collective-permute-start | bytes 700424 | tf_op jit(solution)/shard_map/ppermute | solution.py:290
  22.2 10.6 %copy-start = (bf16[896,384]{1,0:T(8,128)(2,1)S(1)}, bf16[896,384]{1,0:T(8,128)(2,1)}, u32[]{:S(2)}) copy-start(bf16[896,384]{1,0:T(8,128)(2,1)} %get-tuple-element.30.refs_8_) | copy-start | bytes 2064388
  22.2 10.6 %copy-start.1 = (bf16[16,7296]{1,0:T(8,128)(2,1)S(1)}, bf16[16,7296]{1,0:T(8,128)(2,1)}, u32[]{:S(2)}) copy-start(bf16[16,7296]{1,0:T(8,128)(2,1)} %get-tuple-element.29.refs_3_) | copy-start | bytes 700420
  22.2 9.3 %collective-permute-start.9 = (bf16[448,384]{1,0:T(8,128)(2,1)S(1)}, bf16[448,384]{1,0:T(8,128)(2,1)S(1)}, u32[]{:S(2)}, u32[]{:S(2)}) collective-permute-start(bf16[448,384]{1,0:T(8,128)(2,1)S(1)} %shard_map.129), channel_id=1, source_target_pairs={{0,8},{1,9},{2,10},{3,11},{4,12},{5,13},{6,14},{7,15},{8,0},{9,1},... | collective-permute-start | bytes 1032200 | tf_op jit(solution)/shard_map/ppermute | solution.py:290
  24.1 8.7 %copy-start.3 = (s32[4,1]{0,1:T(1,128)S(1)}, s32[4,1]{0,1:T(1,128)}, u32[]{:S(2)}) copy-start(s32[4,1]{0,1:T(1,128)} %param.14) | copy-start | bytes 52
  24.1 8.7 %collective-permute-start.10 = (bf16[448,384]{1,0:T(8,128)(2,1)S(1)}, bf16[448,384]{1,0:T(8,128)(2,1)S(1)}, u32[]{:S(2)}, u32[]{:S(2)}) collective-permute-start(bf16[448,384]{1,0:T(8,128)(2,1)S(1)} %shard_map.130), channel_id=1, source_target_pairs={{0,16},{1,17},{2,18},{3,19},{4,20},{5,21},{6,22},{7,23},{8,24},{9,... | collective-permute-start | bytes 1032200 | tf_op jit(solution)/shard_map/ppermute | solution.py:290
  29.4 1.5 %collective-permute-start.5 = (bf16[16,7296]{1,0:T(8,128)(2,1)S(1)}, bf16[16,7296]{1,0:T(8,128)(2,1)S(1)}, u32[]{:S(2)}, u32[]{:S(2)}) collective-permute-start(bf16[16,7296]{1,0:T(8,128)(2,1)S(1)} %collective-permute-done.2.refs_2_), channel_id=1, source_target_pairs={{0,1},{1,0},{2,3},{3,2},{4,5},{5,4},{6,7},{7,6},{8,9},{9,8},{10,11... | collective-permute-start | bytes 700424 | tf_op jit(solution)/shard_map/ppermute | solution.py:290
  29.4 1.8 %collective-permute-start.4 = (bf16[16,7296]{1,0:T(8,128)(2,1)S(1)}, bf16[16,7296]{1,0:T(8,128)(2,1)S(1)}, u32[]{:S(2)}, u32[]{:S(2)}) collective-permute-start(bf16[16,7296]{1,0:T(8,128)(2,1)S(1)} %collective-permute-done.1.refs_1_), channel_id=1, source_target_pairs={{0,1},{1,0},{2,3},{3,2},{4,5},{5,4},{6,7},{7,6},{8,9},{9,8},{10,11... | collective-permute-start | bytes 700424 | tf_op jit(solution)/shard_map/ppermute | solution.py:290
  29.9 1.6 %collective-permute-start.3 = (bf16[16,7296]{1,0:T(8,128)(2,1)S(1)}, bf16[16,7296]{1,0:T(8,128)(2,1)S(1)}, u32[]{:S(2)}, u32[]{:S(2)}) collective-permute-start(bf16[16,7296]{1,0:T(8,128)(2,1)S(1)} %collective-permute-done.refs_0_), channel_id=1, source_target_pairs={{0,1},{1,0},{2,3},{3,2},{4,5},{5,4},{6,7},{7,6},{8,9},{9,8},{10,11... | collective-permute-start | bytes 700424 | tf_op jit(solution)/shard_map/ppermute | solution.py:290
  34.6 2.2 %collective-permute-start.11 = (bf16[64,3712]{1,0:T(8,128)(2,1)S(1)}, bf16[64,3712]{1,0:T(8,128)(2,1)S(1)}, u32[]{:S(2)}, u32[]{:S(2)}) collective-permute-start(bf16[64,3712]{1,0:T(8,128)(2,1)S(1)} %get-tuple-element.32), channel_id=1, source_target_pairs={{0,1},{1,0},{2,3},{3,2},{4,5},{5,4},{6,7},{7,6},{8,9},{9,8},{10,11... | collective-permute-start | bytes 1425416 | tf_op jit(solution)/shard_map/ppermute | solution.py:290
  34.6 10.6 %collective-permute-start.15 = (bf16[128,1280]{1,0:T(8,128)(2,1)S(1)}, bf16[128,1280]{1,0:T(8,128)(2,1)S(1)}, u32[]{:S(2)}, u32[]{:S(2)}) collective-permute-start(bf16[128,1280]{1,0:T(8,128)(2,1)S(1)} %get-tuple-element.41), channel_id=1, source_target_pairs={{0,8},{1,9},{2,10},{3,11},{4,12},{5,13},{6,14},{7,15},{8,0},{9,1},... | collective-permute-start | bytes 983048 | tf_op jit(solution)/shard_map/ppermute | solution.py:290
  35.8 15.3 %collective-permute-start.16 = (bf16[128,1280]{1,0:T(8,128)(2,1)S(1)}, bf16[128,1280]{1,0:T(8,128)(2,1)S(1)}, u32[]{:S(2)}, u32[]{:S(2)}) collective-permute-start(bf16[128,1280]{1,0:T(8,128)(2,1)S(1)} %get-tuple-element.42), channel_id=1, source_target_pairs={{0,16},{1,17},{2,18},{3,19},{4,20},{5,21},{6,22},{7,23},{8,24},{9,... | collective-permute-start | bytes 983048 | tf_op jit(solution)/shard_map/ppermute | solution.py:290
  36.9 15.9 %collective-permute-start.18 = (bf16[128,1280]{1,0:T(8,128)(2,1)S(1)}, bf16[128,1280]{1,0:T(8,128)(2,1)S(1)}, u32[]{:S(2)}, u32[]{:S(2)}) collective-permute-start(bf16[128,1280]{1,0:T(8,128)(2,1)S(1)} %get-tuple-element.44), channel_id=1, source_target_pairs={{0,24},{1,25},{2,26},{3,27},{4,28},{5,29},{6,30},{7,31},{8,16},{9,... | collective-permute-start | bytes 983048 | tf_op jit(solution)/shard_map/ppermute | solution.py:290
  38.4 14.5 %collective-permute-start.12 = (bf16[16,3712]{1,0:T(8,128)(2,1)S(1)}, bf16[16,3712]{1,0:T(8,128)(2,1)S(1)}, u32[]{:S(2)}, u32[]{:S(2)}) collective-permute-start(bf16[16,3712]{1,0:T(8,128)(2,1)S(1)} %get-tuple-element.33), channel_id=1, source_target_pairs={{0,6},{1,7},{2,4},{3,5},{4,2},{5,3},{6,0},{7,1},{8,14},{9,15},{10,... | collective-permute-start | bytes 356360 | tf_op jit(solution)/shard_map/ppermute | solution.py:290
  42.0 10.9 %collective-permute-start.13 = (bf16[16,3712]{1,0:T(8,128)(2,1)S(1)}, bf16[16,3712]{1,0:T(8,128)(2,1)S(1)}, u32[]{:S(2)}, u32[]{:S(2)}) collective-permute-start(bf16[16,3712]{1,0:T(8,128)(2,1)S(1)} %get-tuple-element.34), channel_id=1, source_target_pairs={{0,4},{1,5},{2,6},{3,7},{4,0},{5,1},{6,2},{7,3},{8,12},{9,13},{10,... | collective-permute-start | bytes 356360 | tf_op jit(solution)/shard_map/ppermute | solution.py:290
  45.2 7.7 %collective-permute-start.14 = (bf16[16,3712]{1,0:T(8,128)(2,1)S(1)}, bf16[16,3712]{1,0:T(8,128)(2,1)S(1)}, u32[]{:S(2)}, u32[]{:S(2)}) collective-permute-start(bf16[16,3712]{1,0:T(8,128)(2,1)S(1)} %get-tuple-element.35), channel_id=1, source_target_pairs={{0,2},{1,3},{2,0},{3,1},{4,6},{5,7},{6,4},{7,5},{8,10},{9,11},{10,... | collective-permute-start | bytes 356360 | tf_op jit(solution)/shard_map/ppermute | solution.py:290
  51.2 1.7 %copy-start.2 = (s32[128,8]{0,1:T(8,128)S(1)}, s32[128,8]{0,1:T(8,128)}, u32[]{:S(2)}) copy-start(s32[128,8]{0,1:T(8,128)} %param.11) | copy-start | bytes 12292
  51.2 1.7 %copy-start.4 = (bf16[1,64,128]{2,1,0:T(8,128)(2,1)S(1)}, bf16[1,64,128]{2,1,0:T(8,128)(2,1)}, u32[]{:S(2)}) copy-start(bf16[1,64,128]{2,1,0:T(8,128)(2,1)} %get-tuple-element.27.placed_ref) | copy-start | bytes 49156
  51.2 3.2 %collective-permute-start.17 = (bf16[2,128,896]{2,1,0:T(8,128)(2,1)S(1)}, bf16[2,128,896]{2,1,0:T(8,128)(2,1)S(1)}, u32[]{:S(2)}, u32[]{:S(2)}) collective-permute-start(bf16[2,128,896]{2,1,0:T(8,128)(2,1)S(1)} %shard_map.134), channel_id=1, source_target_pairs={{0,1},{1,0},{2,3},{3,2},{4,5},{5,4},{6,7},{7,6},{8,9},{9,8},{10,11... | collective-permute-start | bytes 1376264 | tf_op jit(solution)/shard_map/ppermute | solution.py:290
  52.8 1.6 %collective-permute-start.19 = (bf16[1,128,896]{2,1,0:T(8,128)(2,1)S(1)}, bf16[1,128,896]{2,1,0:T(8,128)(2,1)S(1)}, u32[]{:S(2)}, u32[]{:S(2)}) collective-permute-start(bf16[1,128,896]{2,1,0:T(8,128)(2,1)S(1)} %shard_map.135), channel_id=1, source_target_pairs={{0,1},{1,0},{2,3},{3,2},{4,5},{5,4},{6,7},{7,6},{8,9},{9,8},{10,11... | collective-permute-start | bytes 688136 | tf_op jit(solution)/shard_map/ppermute | solution.py:290

commit v17 on v16

--- a/solution.py
+++ b/solution.py
@@ -358,18 +358,6 @@
     near_moved = [send(away[k - 1], k, 0) for k in near]
     (stacked,) = call(stack_kernel, [shape((len(near), 2 * rows, width))], near_moved)
     near_other = send(stacked, 0, 1)
-    far_moved = [send(after(away[k - 1], summed[-2]), k, 0) for k in far]
-    ready = [after(far_moved[0], stacked)] + far_moved[1:]
-    (stacked,) = call(stack_kernel, [shape((len(far), 2 * rows, width))], ready)
-    far_other = send(stacked, 0, 1)
-    grad_gate, grad_up, grad_down = call(
-        functools.partial(weight_kernel, rep),
-        [shape((width, units))] * 3,
-        [here, grads, near_other, far_other] + near_moved + far_moved,
-        kept=(0, 1, 2),
-        scratch=[pltpu.VMEM((width, units), BF16)] * 3 + [pltpu.SemaphoreType.DMA((3,))],
-        flops=2 * 2 * rep * rows * width * 3 * units,
-    )
     grad_tokens, grad_weight = call(
         functools.partial(token_kernel, rep, flight),
         [shape((tok_count, model_dim)), shape(ids_rows.shape, F32)],
@@ -380,7 +368,19 @@
             pltpu.VMEM(ids_rows.shape, jnp.int32),
             pltpu.SemaphoreType.DMA((1,)),
         ],
-        flops=1000 * 2 * tok_count * CHIPS * SLOT * model_dim,
+        flops=40 * 2 * tok_count * CHIPS * SLOT * model_dim,
+    )
+    far_moved = [send(after(away[k - 1], summed[-2]), k, 0) for k in far]
+    ready = [after(far_moved[0], stacked, grad_weight)] + far_moved[1:]
+    (stacked,) = call(stack_kernel, [shape((len(far), 2 * rows, width))], ready)
+    far_other = send(stacked, 0, 1)
+    grad_gate, grad_up, grad_down = call(
+        functools.partial(weight_kernel, rep),
+        [shape((width, units))] * 3,
+        [here, grads, near_other, far_other] + near_moved + far_moved,
+        kept=(0, 1, 2),
+        scratch=[pltpu.VMEM((width, units), BF16)] * 3 + [pltpu.SemaphoreType.DMA((3,))],
+        flops=2 * 2 * rep * rows * width * 3 * units,
     )
     return grad_tokens, grad_weight.T, grad_gate, grad_up, grad_down
 

time: 56 us -> 58.1 us (1.038)
  waiting for transfers between devices: 24.8 us -> 28.3 us
  starting transfers between devices: 22.5 us -> 21.2 us
    ppermute x20, waiting for transfers between devices: 24.8 us -> 28.3 us  [send(): return lax.ppermute(array, ('rep', 'ep'), pairs)]
    ppermute x20, starting transfers between devices: 22.5 us -> 21.2 us  [send(): return lax.ppermute(array, ('rep', 'ep'), pairs)]
  transfers between devices with their start and end apart: 20 -> 20, of which waited for: 10 -> 11; matrix products, arithmetic and copies ran while one was open for 0% -> 0% of each run, Pallas kernels for 3% -> 3%
where the time goes in v17:
time: 58.1 us; the launch traced here: 57.9 us
  waiting for transfers between devices  28.3 us (49%)
  starting transfers between devices  21.2 us (36%)
  Pallas kernels  7.69 us (13%)
  between operations  0.77 us (1%)
    ppermute x20, waiting for transfers between devices, send(): return lax.ppermute(array, ('rep', 'ep'), pairs)  28.3 us
    ppermute x20, starting transfers between devices, send(): return lax.ppermute(array, ('rep', 'ep'), pairs)  21.2 us
    pallas_call x9, Pallas kernels, call(): pl.pallas_call(kernel, out_shape=tuple(outs), in_specs=[HBM if n in store...  7.69 us
  transfers between devices with their start and end apart: 20, of which 11 were waited for; matrix products, arithmetic and copies ran while one was open for 0% of the time, Pallas kernels for 3%

profile of v17, /device:TPU:0, one launch (start us, length us, event | category | flops | bytes accessed | tf_op | source)
XLA Modules:
  0.0 57.9 jit_solution(2463432323971365207)
XLA Ops:
  0.6 2.9 %shard_map.128 = (bf16[16,7296]{1,0:T(8,128)(2,1)}, bf16[1,64,128]{2,1,0:T(8,128)(2,1)}, bf16[896,384]{1,0:T(8,128)(2,1)}) custom-call(s32[4]{0:T(128)} %live_ref.1, bf16[128,3584]{1,0:T(8,128)(2,1)} %tok_ref.1, bf16[128,3584]{1,0:T(8,128)(2,1)} %grad_ref.1, s32[8,128]{1,0:T(8,128)} %bitcast.4, bf16[8,128]{1,0:T(8,128)(2,1)} %bitcast.7, ...), custom_call_target="tpu_custom_call" | custom-call | bytes 3467280 | tf_op jit(solution)/shard_map/pallas_call | solution.py:32
  3.5 3.0 %collective-permute-start.8 = (bf16[896,384]{1,0:T(8,128)(2,1)}, bf16[896,384]{1,0:T(8,128)(2,1)S(1)}, u32[]{:S(2)}, u32[]{:S(2)}) collective-permute-start(bf16[896,384]{1,0:T(8,128)(2,1)} %get-tuple-element.30.refs_8_), channel_id=1, source_target_pairs={{0,16},{1,17},{2,18},{3,19},{4,20},{5,21},{6,22},{7,23},{8,24},{9,... | collective-permute-start | bytes 2064392 | tf_op jit(solution)/shard_map/ppermute | solution.py:290
  6.5 1.5 %collective-permute-start.7 = (bf16[896,384]{1,0:T(8,128)(2,1)}, bf16[896,384]{1,0:T(8,128)(2,1)S(1)}, u32[]{:S(2)}, u32[]{:S(2)}) collective-permute-start(bf16[896,384]{1,0:T(8,128)(2,1)} %get-tuple-element.30.refs_8_), channel_id=1, source_target_pairs={{0,8},{1,9},{2,10},{3,11},{4,12},{5,13},{6,14},{7,15},{8,0},{9,1},... | collective-permute-start | bytes 2064392 | tf_op jit(solution)/shard_map/ppermute | solution.py:290
  8.0 1.6 %collective-permute-start.2 = (bf16[16,7296]{1,0:T(8,128)(2,1)}, bf16[16,7296]{1,0:T(8,128)(2,1)S(1)}, u32[]{:S(2)}, u32[]{:S(2)}) collective-permute-start(bf16[16,7296]{1,0:T(8,128)(2,1)} %get-tuple-element.29.refs_3_), channel_id=1, source_target_pairs={{0,2},{1,3},{2,0},{3,1},{4,6},{5,7},{6,4},{7,5},{8,10},{9,11},{10,... | collective-permute-start | bytes 700424 | tf_op jit(solution)/shard_map/ppermute | solution.py:290
  9.6 2.6 %collective-permute-start.1 = (bf16[16,7296]{1,0:T(8,128)(2,1)}, bf16[16,7296]{1,0:T(8,128)(2,1)S(1)}, u32[]{:S(2)}, u32[]{:S(2)}) collective-permute-start(bf16[16,7296]{1,0:T(8,128)(2,1)} %get-tuple-element.29.refs_3_), channel_id=1, source_target_pairs={{0,4},{1,5},{2,6},{3,7},{4,0},{5,1},{6,2},{7,3},{8,12},{9,13},{10,... | collective-permute-start | bytes 700424 | tf_op jit(solution)/shard_map/ppermute | solution.py:290
  12.2 0.2 collective-permute-start
  12.4 6.6 %collective-permute-done.2.refs_2_ = bf16[16,7296]{1,0:T(8,128)(2,1)S(1)} collective-permute-done((bf16[16,7296]{1,0:T(8,128)(2,1)}, bf16[16,7296]{1,0:T(8,128)(2,1)S(1)}, u32[]{:S(2)}, u32[]{:S(2)}) %collective-permute-start.2) | collective-permute-done | bytes 233504 | tf_op jit(solution)/shard_map/ppermute | solution.py:290
  19.1 3.1 %collective-permute-done.8.all_ref.refs_10_ = bf16[896,384]{1,0:T(8,128)(2,1)S(1)} collective-permute-done((bf16[896,384]{1,0:T(8,128)(2,1)}, bf16[896,384]{1,0:T(8,128)(2,1)S(1)}, u32[]{:S(2)}, u32[]{:S(2)}) %collective-permute-start.8) | collective-permute-done | bytes 688160 | tf_op jit(solution)/shard_map/ppermute | solution.py:290
  22.2 1.8 %collective-permute-start.9 = (bf16[448,384]{1,0:T(8,128)(2,1)S(1)}, bf16[448,384]{1,0:T(8,128)(2,1)S(1)}, u32[]{:S(2)}, u32[]{:S(2)}) collective-permute-start(bf16[448,384]{1,0:T(8,128)(2,1)S(1)} %shard_map.129), channel_id=1, source_target_pairs={{0,8},{1,9},{2,10},{3,11},{4,12},{5,13},{6,14},{7,15},{8,0},{9,1},... | collective-permute-start | bytes 1032200 | tf_op jit(solution)/shard_map/ppermute | solution.py:290
  24.1 1.6 %collective-permute-start.10 = (bf16[448,384]{1,0:T(8,128)(2,1)S(1)}, bf16[448,384]{1,0:T(8,128)(2,1)S(1)}, u32[]{:S(2)}, u32[]{:S(2)}) collective-permute-start(bf16[448,384]{1,0:T(8,128)(2,1)S(1)} %shard_map.130), channel_id=1, source_target_pairs={{0,16},{1,17},{2,18},{3,19},{4,20},{5,21},{6,22},{7,23},{8,24},{9,... | collective-permute-start | bytes 1032200 | tf_op jit(solution)/shard_map/ppermute | solution.py:290
  25.7 3.7 %collective-permute-done.1.refs_1_ = bf16[16,7296]{1,0:T(8,128)(2,1)S(1)} collective-permute-done((bf16[16,7296]{1,0:T(8,128)(2,1)}, bf16[16,7296]{1,0:T(8,128)(2,1)S(1)}, u32[]{:S(2)}, u32[]{:S(2)}) %collective-permute-start.1) | collective-permute-done | bytes 233504 | tf_op jit(solution)/shard_map/ppermute | solution.py:290
  29.4 0.5 collective-permute-start.4
  30.0 0.9 %collective-permute-done.5.refs_6_ = bf16[16,7296]{1,0:T(8,128)(2,1)S(1)} collective-permute-done((bf16[16,7296]{1,0:T(8,128)(2,1)S(1)}, bf16[16,7296]{1,0:T(8,128)(2,1)S(1)}, u32[]{:S(2)}, u32[]{:S(2)}) %collective-permute-start.5) | collective-permute-done | bytes 233504 | tf_op jit(solution)/shard_map/ppermute | solution.py:290
  30.9 0.3 collective-permute-done.4.refs_5_
  31.2 0.3 collective-permute-done.3.refs_4_
  31.6 1.2 %collective-permute-done.10.refs_12_ = bf16[448,384]{1,0:T(8,128)(2,1)S(1)} collective-permute-done((bf16[448,384]{1,0:T(8,128)(2,1)S(1)}, bf16[448,384]{1,0:T(8,128)(2,1)S(1)}, u32[]{:S(2)}, u32[]{:S(2)}) %collective-permute-start.10) | collective-permute-done | bytes 344096 | tf_op jit(solution)/shard_map/ppermute | solution.py:290
  32.8 1.8 %shard_map.131 = (bf16[64,3712]{1,0:T(8,128)(2,1)S(1)}, bf16[64,3712]{1,0:T(8,128)(2,1)S(1)}, bf16[128,384]{1,0:T(8,128)(2,1)S(1)}, bf16[2,128,896]{2,1,0:T(8,12...) custom-call(s32[1,4]{1,0:T(1,128)S(1)} %bitcast.6, ...), custom_call_target="tpu_custom_call" | custom-call | flops 587202560 | bytes 7110672 | tf_op jit(solution)/shard_map/pallas_call | solution.py:32
  34.6 0.1 collective-permute-start.11
  34.6 1.1 %collective-permute-start.15 = (bf16[128,1280]{1,0:T(8,128)(2,1)S(1)}, bf16[128,1280]{1,0:T(8,128)(2,1)S(1)}, u32[]{:S(2)}, u32[]{:S(2)}) collective-permute-start(bf16[128,1280]{1,0:T(8,128)(2,1)S(1)} %get-tuple-element.41), channel_id=1, source_target_pairs={{0,8},{1,9},{2,10},{3,11},{4,12},{5,13},{6,14},{7,15},{8,0},{9,1},... | collective-permute-start | bytes 983048 | tf_op jit(solution)/shard_map/ppermute | solution.py:290
  35.8 1.0 %collective-permute-start.16 = (bf16[128,1280]{1,0:T(8,128)(2,1)S(1)}, bf16[128,1280]{1,0:T(8,128)(2,1)S(1)}, u32[]{:S(2)}, u32[]{:S(2)}) collective-permute-start(bf16[128,1280]{1,0:T(8,128)(2,1)S(1)} %get-tuple-element.42), channel_id=1, source_target_pairs={{0,16},{1,17},{2,18},{3,19},{4,20},{5,21},{6,22},{7,23},{8,24},{9,... | collective-permute-start | bytes 983048 | tf_op jit(solution)/shard_map/ppermute | solution.py:290
  36.8 0.1 shard_map.132
  36.9 3.7 %collective-permute-start.12 = (bf16[16,3712]{1,0:T(8,128)(2,1)S(1)}, bf16[16,3712]{1,0:T(8,128)(2,1)S(1)}, u32[]{:S(2)}, u32[]{:S(2)}) collective-permute-start(bf16[16,3712]{1,0:T(8,128)(2,1)S(1)} %get-tuple-element.33), channel_id=1, source_target_pairs={{0,6},{1,7},{2,4},{3,5},{4,2},{5,3},{6,0},{7,1},{8,14},{9,15},{10,... | collective-permute-start | bytes 356360 | tf_op jit(solution)/shard_map/ppermute | solution.py:290
  40.6 0.8 %collective-permute-start.14 = (bf16[16,3712]{1,0:T(8,128)(2,1)S(1)}, bf16[16,3712]{1,0:T(8,128)(2,1)S(1)}, u32[]{:S(2)}, u32[]{:S(2)}) collective-permute-start(bf16[16,3712]{1,0:T(8,128)(2,1)S(1)} %get-tuple-element.35), channel_id=1, source_target_pairs={{0,2},{1,3},{2,0},{3,1},{4,6},{5,7},{6,4},{7,5},{8,10},{9,11},{10,... | collective-permute-start | bytes 356360 | tf_op jit(solution)/shard_map/ppermute | solution.py:290
  41.4 3.4 %collective-permute-done.15.refs_0_ = bf16[128,1280]{1,0:T(8,128)(2,1)S(1)} collective-permute-done((bf16[128,1280]{1,0:T(8,128)(2,1)S(1)}, bf16[128,1280]{1,0:T(8,128)(2,1)S(1)}, u32[]{:S(2)}, u32[]{:S(2)}) %collective-permute-start.15) | collective-permute-done | bytes 327712 | tf_op jit(solution)/shard_map/ppermute | solution.py:290
  44.8 1.5 %collective-permute-start.18 = (bf16[128,1280]{1,0:T(8,128)(2,1)S(1)}, bf16[128,1280]{1,0:T(8,128)(2,1)S(1)}, u32[]{:S(2)}, u32[]{:S(2)}) collective-permute-start(bf16[128,1280]{1,0:T(8,128)(2,1)S(1)} %get-tuple-element.44), channel_id=1, source_target_pairs={{0,24},{1,25},{2,26},{3,27},{4,28},{5,29},{6,30},{7,31},{8,16},{9,... | collective-permute-start | bytes 983048 | tf_op jit(solution)/shard_map/ppermute | solution.py:290
  46.3 0.1 collective-permute-start.17
  46.4 4.7 %collective-permute-done.13.refs_1_ = bf16[16,3712]{1,0:T(8,128)(2,1)S(1)} collective-permute-done((bf16[16,3712]{1,0:T(8,128)(2,1)S(1)}, bf16[16,3712]{1,0:T(8,128)(2,1)S(1)}, u32[]{:S(2)}, u32[]{:S(2)}) %collective-permute-start.13) | collective-permute-done | bytes 118816 | tf_op jit(solution)/shard_map/ppermute | solution.py:290
  51.1 1.4 %shard_map.133 = (bf16[128,3584]{1,0:T(8,128)(2,1)}, f32[8,128]{1,0:T(8,128)}) custom-call(s32[8,128]{1,0:T(8,128)S(1)} %bitcast.5, bf16[1,64,128]{2,1,0:T(8,128)(2,1)S(1)} %copy-done.4, bf16[16,3712]{1,0:T(8,128)(2,1)S(1)} %collective-permute-done.12.refs_0_, bf16[16,3712]{1,0:T(8,128)(2,1)S(1)} %collective-permute-done.13.refs_1_, ...), custom_call_target="tpu_custom_call" | custom-call | flops 2348810240 | bytes 1417216 | tf_op jit(solution)/shard_map/pallas_call | solution.py:32
  52.5 2.4 %collective-permute-done.18.refs_0_.refs_2_ = bf16[128,1280]{1,0:T(8,128)(2,1)S(1)} collective-permute-done((bf16[128,1280]{1,0:T(8,128)(2,1)S(1)}, bf16[128,1280]{1,0:T(8,128)(2,1)S(1)}, u32[]{:S(2)}, u32[]{:S(2)}) %collective-permute-start.18) | collective-permute-done | bytes 327712 | tf_op jit(solution)/shard_map/ppermute | solution.py:290
  55.0 0.1 collective-permute-start.19
  55.1 1.5 %collective-permute-done.19.far_ref = bf16[1,128,896]{2,1,0:T(8,128)(2,1)S(1)} collective-permute-done((bf16[1,128,896]{2,1,0:T(8,128)(2,1)S(1)}, bf16[1,128,896]{2,1,0:T(8,128)(2,1)S(1)}, u32[]{:S(2)}, u32[]{:S(2)}) %collective-permute-start.19) | collective-permute-done | bytes 229408 | tf_op jit(solution)/shard_map/ppermute | solution.py:290
  56.5 1.4 %shard_map.136 = (bf16[896,128]{1,0:T(8,128)(2,1)}, bf16[896,128]{1,0:T(8,128)(2,1)}, bf16[896,128]{1,0:T(8,128)(2,1)}) custom-call(bf16[2,128,896]{2,1,0:T(8,128)(2,1)S(1)} %get-tuple-element.39.here_ref, bf16[128,384]{1,0:T(8,128)(2,1)S(1)} %get-tuple-element.40.grads_ref, bf16[2,128,896]{2,1,0:T(8,128)(2,1)S(1)} %collective-permute-done.17.near_ref, ...), custom_call_target="tpu_custom_call" | custom-call | flops 352321536 | bytes 2916352 | tf_op jit(solution)/shard_map/pallas_call | solution.py:32
  (27 shorter events, 0.3 us)
Async XLA Ops:
  3.5 18.7 %collective-permute-start.8 = (bf16[896,384]{1,0:T(8,128)(2,1)}, bf16[896,384]{1,0:T(8,128)(2,1)S(1)}, u32[]{:S(2)}, u32[]{:S(2)}) collective-permute-start(bf16[896,384]{1,0:T(8,128)(2,1)} %get-tuple-element.30.refs_8_), channel_id=1, source_target_pairs={{0,16},{1,17},{2,18},{3,19},{4,20},{5,21},{6,22},{7,23},{8,24},{9,... | collective-permute-start | bytes 2064392 | tf_op jit(solution)/shard_map/ppermute | solution.py:290
  6.5 17.5 %collective-permute-start.7 = (bf16[896,384]{1,0:T(8,128)(2,1)}, bf16[896,384]{1,0:T(8,128)(2,1)S(1)}, u32[]{:S(2)}, u32[]{:S(2)}) collective-permute-start(bf16[896,384]{1,0:T(8,128)(2,1)} %get-tuple-element.30.refs_8_), channel_id=1, source_target_pairs={{0,8},{1,9},{2,10},{3,11},{4,12},{5,13},{6,14},{7,15},{8,0},{9,1},... | collective-permute-start | bytes 2064392 | tf_op jit(solution)/shard_map/ppermute | solution.py:290
  8.0 11.0 %collective-permute-start.2 = (bf16[16,7296]{1,0:T(8,128)(2,1)}, bf16[16,7296]{1,0:T(8,128)(2,1)S(1)}, u32[]{:S(2)}, u32[]{:S(2)}) collective-permute-start(bf16[16,7296]{1,0:T(8,128)(2,1)} %get-tuple-element.29.refs_3_), channel_id=1, source_target_pairs={{0,2},{1,3},{2,0},{3,1},{4,6},{5,7},{6,4},{7,5},{8,10},{9,11},{10,... | collective-permute-start | bytes 700424 | tf_op jit(solution)/shard_map/ppermute | solution.py:290
  9.6 19.7 %collective-permute-start.1 = (bf16[16,7296]{1,0:T(8,128)(2,1)}, bf16[16,7296]{1,0:T(8,128)(2,1)S(1)}, u32[]{:S(2)}, u32[]{:S(2)}) collective-permute-start(bf16[16,7296]{1,0:T(8,128)(2,1)} %get-tuple-element.29.refs_3_), channel_id=1, source_target_pairs={{0,4},{1,5},{2,6},{3,7},{4,0},{5,1},{6,2},{7,3},{8,12},{9,13},{10,... | collective-permute-start | bytes 700424 | tf_op jit(solution)/shard_map/ppermute | solution.py:290
  12.2 17.2 %collective-permute-start = (bf16[16,7296]{1,0:T(8,128)(2,1)}, bf16[16,7296]{1,0:T(8,128)(2,1)S(1)}, u32[]{:S(2)}, u32[]{:S(2)}) collective-permute-start(bf16[16,7296]{1,0:T(8,128)(2,1)} %get-tuple-element.29.refs_3_), channel_id=1, source_target_pairs={{0,6},{1,7},{2,4},{3,5},{4,2},{5,3},{6,0},{7,1},{8,14},{9,15},{10,... | collective-permute-start | bytes 700424 | tf_op jit(solution)/shard_map/ppermute | solution.py:290
  19.1 10.8 %collective-permute-start.6 = (bf16[16,7296]{1,0:T(8,128)(2,1)}, bf16[16,7296]{1,0:T(8,128)(2,1)S(1)}, u32[]{:S(2)}, u32[]{:S(2)}) collective-permute-start(bf16[16,7296]{1,0:T(8,128)(2,1)} %get-tuple-element.29.refs_3_), channel_id=1, source_target_pairs={{0,1},{1,0},{2,3},{3,2},{4,5},{5,4},{6,7},{7,6},{8,9},{9,8},{10,11... | collective-permute-start | bytes 700424 | tf_op jit(solution)/shard_map/ppermute | solution.py:290
  22.2 10.6 %copy-start = (bf16[896,384]{1,0:T(8,128)(2,1)S(1)}, bf16[896,384]{1,0:T(8,128)(2,1)}, u32[]{:S(2)}) copy-start(bf16[896,384]{1,0:T(8,128)(2,1)} %get-tuple-element.30.refs_8_) | copy-start | bytes 2064388
  22.2 10.6 %copy-start.1 = (bf16[16,7296]{1,0:T(8,128)(2,1)S(1)}, bf16[16,7296]{1,0:T(8,128)(2,1)}, u32[]{:S(2)}) copy-start(bf16[16,7296]{1,0:T(8,128)(2,1)} %get-tuple-element.29.refs_3_) | copy-start | bytes 700420
  22.2 9.3 %collective-permute-start.9 = (bf16[448,384]{1,0:T(8,128)(2,1)S(1)}, bf16[448,384]{1,0:T(8,128)(2,1)S(1)}, u32[]{:S(2)}, u32[]{:S(2)}) collective-permute-start(bf16[448,384]{1,0:T(8,128)(2,1)S(1)} %shard_map.129), channel_id=1, source_target_pairs={{0,8},{1,9},{2,10},{3,11},{4,12},{5,13},{6,14},{7,15},{8,0},{9,1},... | collective-permute-start | bytes 1032200 | tf_op jit(solution)/shard_map/ppermute | solution.py:290
  24.1 8.7 %copy-start.3 = (s32[4,1]{0,1:T(1,128)S(1)}, s32[4,1]{0,1:T(1,128)}, u32[]{:S(2)}) copy-start(s32[4,1]{0,1:T(1,128)} %param.14) | copy-start | bytes 52
  24.1 8.7 %collective-permute-start.10 = (bf16[448,384]{1,0:T(8,128)(2,1)S(1)}, bf16[448,384]{1,0:T(8,128)(2,1)S(1)}, u32[]{:S(2)}, u32[]{:S(2)}) collective-permute-start(bf16[448,384]{1,0:T(8,128)(2,1)S(1)} %shard_map.130), channel_id=1, source_target_pairs={{0,16},{1,17},{2,18},{3,19},{4,20},{5,21},{6,22},{7,23},{8,24},{9,... | collective-permute-start | bytes 1032200 | tf_op jit(solution)/shard_map/ppermute | solution.py:290
  29.4 1.5 %collective-permute-start.5 = (bf16[16,7296]{1,0:T(8,128)(2,1)S(1)}, bf16[16,7296]{1,0:T(8,128)(2,1)S(1)}, u32[]{:S(2)}, u32[]{:S(2)}) collective-permute-start(bf16[16,7296]{1,0:T(8,128)(2,1)S(1)} %collective-permute-done.2.refs_2_), channel_id=1, source_target_pairs={{0,1},{1,0},{2,3},{3,2},{4,5},{5,4},{6,7},{7,6},{8,9},{9,8},{10,11... | collective-permute-start | bytes 700424 | tf_op jit(solution)/shard_map/ppermute | solution.py:290
  29.4 1.8 %collective-permute-start.4 = (bf16[16,7296]{1,0:T(8,128)(2,1)S(1)}, bf16[16,7296]{1,0:T(8,128)(2,1)S(1)}, u32[]{:S(2)}, u32[]{:S(2)}) collective-permute-start(bf16[16,7296]{1,0:T(8,128)(2,1)S(1)} %collective-permute-done.1.refs_1_), channel_id=1, source_target_pairs={{0,1},{1,0},{2,3},{3,2},{4,5},{5,4},{6,7},{7,6},{8,9},{9,8},{10,11... | collective-permute-start | bytes 700424 | tf_op jit(solution)/shard_map/ppermute | solution.py:290
  29.9 1.6 %collective-permute-start.3 = (bf16[16,7296]{1,0:T(8,128)(2,1)S(1)}, bf16[16,7296]{1,0:T(8,128)(2,1)S(1)}, u32[]{:S(2)}, u32[]{:S(2)}) collective-permute-start(bf16[16,7296]{1,0:T(8,128)(2,1)S(1)} %collective-permute-done.refs_0_), channel_id=1, source_target_pairs={{0,1},{1,0},{2,3},{3,2},{4,5},{5,4},{6,7},{7,6},{8,9},{9,8},{10,11... | collective-permute-start | bytes 700424 | tf_op jit(solution)/shard_map/ppermute | solution.py:290
  34.6 2.2 %collective-permute-start.11 = (bf16[64,3712]{1,0:T(8,128)(2,1)S(1)}, bf16[64,3712]{1,0:T(8,128)(2,1)S(1)}, u32[]{:S(2)}, u32[]{:S(2)}) collective-permute-start(bf16[64,3712]{1,0:T(8,128)(2,1)S(1)} %get-tuple-element.32), channel_id=1, source_target_pairs={{0,1},{1,0},{2,3},{3,2},{4,5},{5,4},{6,7},{7,6},{8,9},{9,8},{10,11... | collective-permute-start | bytes 1425416 | tf_op jit(solution)/shard_map/ppermute | solution.py:290
  34.6 10.1 %collective-permute-start.15 = (bf16[128,1280]{1,0:T(8,128)(2,1)S(1)}, bf16[128,1280]{1,0:T(8,128)(2,1)S(1)}, u32[]{:S(2)}, u32[]{:S(2)}) collective-permute-start(bf16[128,1280]{1,0:T(8,128)(2,1)S(1)} %get-tuple-element.41), channel_id=1, source_target_pairs={{0,8},{1,9},{2,10},{3,11},{4,12},{5,13},{6,14},{7,15},{8,0},{9,1},... | collective-permute-start | bytes 983048 | tf_op jit(solution)/shard_map/ppermute | solution.py:290
  35.8 10.5 %collective-permute-start.16 = (bf16[128,1280]{1,0:T(8,128)(2,1)S(1)}, bf16[128,1280]{1,0:T(8,128)(2,1)S(1)}, u32[]{:S(2)}, u32[]{:S(2)}) collective-permute-start(bf16[128,1280]{1,0:T(8,128)(2,1)S(1)} %get-tuple-element.42), channel_id=1, source_target_pairs={{0,16},{1,17},{2,18},{3,19},{4,20},{5,21},{6,22},{7,23},{8,24},{9,... | collective-permute-start | bytes 983048 | tf_op jit(solution)/shard_map/ppermute | solution.py:290
  36.9 9.5 %collective-permute-start.12 = (bf16[16,3712]{1,0:T(8,128)(2,1)S(1)}, bf16[16,3712]{1,0:T(8,128)(2,1)S(1)}, u32[]{:S(2)}, u32[]{:S(2)}) collective-permute-start(bf16[16,3712]{1,0:T(8,128)(2,1)S(1)} %get-tuple-element.33), channel_id=1, source_target_pairs={{0,6},{1,7},{2,4},{3,5},{4,2},{5,3},{6,0},{7,1},{8,14},{9,15},{10,... | collective-permute-start | bytes 356360 | tf_op jit(solution)/shard_map/ppermute | solution.py:290
  40.6 10.5 %collective-permute-start.13 = (bf16[16,3712]{1,0:T(8,128)(2,1)S(1)}, bf16[16,3712]{1,0:T(8,128)(2,1)S(1)}, u32[]{:S(2)}, u32[]{:S(2)}) collective-permute-start(bf16[16,3712]{1,0:T(8,128)(2,1)S(1)} %get-tuple-element.34), channel_id=1, source_target_pairs={{0,4},{1,5},{2,6},{3,7},{4,0},{5,1},{6,2},{7,3},{8,12},{9,13},{10,... | collective-permute-start | bytes 356360 | tf_op jit(solution)/shard_map/ppermute | solution.py:290
  40.6 10.5 %collective-permute-start.14 = (bf16[16,3712]{1,0:T(8,128)(2,1)S(1)}, bf16[16,3712]{1,0:T(8,128)(2,1)S(1)}, u32[]{:S(2)}, u32[]{:S(2)}) collective-permute-start(bf16[16,3712]{1,0:T(8,128)(2,1)S(1)} %get-tuple-element.35), channel_id=1, source_target_pairs={{0,2},{1,3},{2,0},{3,1},{4,6},{5,7},{6,4},{7,5},{8,10},{9,11},{10,... | collective-permute-start | bytes 356360 | tf_op jit(solution)/shard_map/ppermute | solution.py:290
  41.4 9.7 %copy-start.2 = (s32[128,8]{0,1:T(8,128)S(1)}, s32[128,8]{0,1:T(8,128)}, u32[]{:S(2)}) copy-start(s32[128,8]{0,1:T(8,128)} %param.11) | copy-start | bytes 12292
  41.4 9.7 %copy-start.4 = (bf16[1,64,128]{2,1,0:T(8,128)(2,1)S(1)}, bf16[1,64,128]{2,1,0:T(8,128)(2,1)}, u32[]{:S(2)}) copy-start(bf16[1,64,128]{2,1,0:T(8,128)(2,1)} %get-tuple-element.27.placed_ref) | copy-start | bytes 49156
  44.8 10.2 %collective-permute-start.18 = (bf16[128,1280]{1,0:T(8,128)(2,1)S(1)}, bf16[128,1280]{1,0:T(8,128)(2,1)S(1)}, u32[]{:S(2)}, u32[]{:S(2)}) collective-permute-start(bf16[128,1280]{1,0:T(8,128)(2,1)S(1)} %get-tuple-element.44), channel_id=1, source_target_pairs={{0,24},{1,25},{2,26},{3,27},{4,28},{5,29},{6,30},{7,31},{8,16},{9,... | collective-permute-start | bytes 983048 | tf_op jit(solution)/shard_map/ppermute | solution.py:290
  46.3 8.7 %collective-permute-start.17 = (bf16[2,128,896]{2,1,0:T(8,128)(2,1)S(1)}, bf16[2,128,896]{2,1,0:T(8,128)(2,1)S(1)}, u32[]{:S(2)}, u32[]{:S(2)}) collective-permute-start(bf16[2,128,896]{2,1,0:T(8,128)(2,1)S(1)} %shard_map.134), channel_id=1, source_target_pairs={{0,1},{1,0},{2,3},{3,2},{4,5},{5,4},{6,7},{7,6},{8,9},{9,8},{10,11... | collective-permute-start | bytes 1376264 | tf_op jit(solution)/shard_map/ppermute | solution.py:290
  55.0 1.6 %collective-permute-start.19 = (bf16[1,128,896]{2,1,0:T(8,128)(2,1)S(1)}, bf16[1,128,896]{2,1,0:T(8,128)(2,1)S(1)}, u32[]{:S(2)}, u32[]{:S(2)}) collective-permute-start(bf16[1,128,896]{2,1,0:T(8,128)(2,1)S(1)} %shard_map.135), channel_id=1, source_target_pairs={{0,1},{1,0},{2,3},{3,2},{4,5},{5,4},{6,7},{7,6},{8,9},{9,8},{10,11... | collective-permute-start | bytes 688136 | tf_op jit(solution)/shard_map/ppermute | solution.py:290

commit v18 on v16

--- a/solution.py
+++ b/solution.py
@@ -312,7 +312,7 @@
     )
     pays, placed, weights = packed[:flight], packed[flight], packed[flight + 1]
 
-    half = width // 2
+    half = width // 2 if width % LANES else -(-width // (2 * LANES)) * LANES
     whole = {0: weights}
     halves = {}
     for k in range(1, rep):
@@ -321,7 +321,8 @@
             whole[k] = send(weights, k, 0)
             for h in range(2):
                 kernel = functools.partial(half_kernel, h * half)
-                (halves[k, h],) = call(kernel, [shape((half, 3 * units))], [whole[k]])
+                size = width - half if h else half
+                (halves[k, h],) = call(kernel, [shape((size, 3 * units))], [whole[k]])
         else:
             halves[k, 0] = send(halves[k ^ low, 0], low, 0)
             halves[k, 1] = send(halves[k ^ high, 1], high, 0)

time: 56 us -> 56.5 us (level)
  starting transfers between devices: 22.5 us -> 23.7 us
  waiting for transfers between devices: 24.8 us -> 24.2 us
    ppermute x20, starting transfers between devices: 22.5 us -> 23.7 us  [send(): return lax.ppermute(array, ('rep', 'ep'), pairs)]
    ppermute x20, waiting for transfers between devices: 24.8 us -> 24.2 us  [send(): return lax.ppermute(array, ('rep', 'ep'), pairs)]
where the time goes in v18:
time: 56.5 us; the launch traced here: 56.3 us
  waiting for transfers between devices  24.2 us (43%)
  starting transfers between devices  23.7 us (42%)
  Pallas kernels  7.59 us (13%)
  between operations  0.79 us (1%)
    ppermute x20, waiting for transfers between devices, send(): return lax.ppermute(array, ('rep', 'ep'), pairs)  24.2 us
    ppermute x20, starting transfers between devices, send(): return lax.ppermute(array, ('rep', 'ep'), pairs)  23.7 us
    pallas_call x9, Pallas kernels, call(): pl.pallas_call(kernel, out_shape=tuple(outs), in_specs=[HBM if n in store...  7.59 us
  transfers between devices with their start and end apart: 20, of which 10 were waited for; matrix products, arithmetic and copies ran while one was open for 0% of the time, Pallas kernels for 3%

profile of v18, /device:TPU:0, one launch (start us, length us, event | category | flops | bytes accessed | tf_op | source)
XLA Modules:
  0.0 56.3 jit_solution(11329703925245723691)
XLA Ops:
  0.6 2.9 %shard_map.128 = (bf16[16,7296]{1,0:T(8,128)(2,1)}, bf16[1,64,128]{2,1,0:T(8,128)(2,1)}, bf16[896,384]{1,0:T(8,128)(2,1)}) custom-call(s32[4]{0:T(128)} %live_ref.1, bf16[128,3584]{1,0:T(8,128)(2,1)} %tok_ref.1, bf16[128,3584]{1,0:T(8,128)(2,1)} %grad_ref.1, s32[8,128]{1,0:T(8,128)} %bitcast.4, bf16[8,128]{1,0:T(8,128)(2,1)} %bitcast.7, ...), custom_call_target="tpu_custom_call" | custom-call | bytes 3467280 | tf_op jit(solution)/shard_map/pallas_call | solution.py:32
  3.5 3.0 %collective-permute-start.8 = (bf16[896,384]{1,0:T(8,128)(2,1)}, bf16[896,384]{1,0:T(8,128)(2,1)S(1)}, u32[]{:S(2)}, u32[]{:S(2)}) collective-permute-start(bf16[896,384]{1,0:T(8,128)(2,1)} %get-tuple-element.30.refs_8_), channel_id=1, source_target_pairs={{0,16},{1,17},{2,18},{3,19},{4,20},{5,21},{6,22},{7,23},{8,24},{9,... | collective-permute-start | bytes 2064392 | tf_op jit(solution)/shard_map/ppermute | solution.py:290
  6.5 1.5 %collective-permute-start.7 = (bf16[896,384]{1,0:T(8,128)(2,1)}, bf16[896,384]{1,0:T(8,128)(2,1)S(1)}, u32[]{:S(2)}, u32[]{:S(2)}) collective-permute-start(bf16[896,384]{1,0:T(8,128)(2,1)} %get-tuple-element.30.refs_8_), channel_id=1, source_target_pairs={{0,8},{1,9},{2,10},{3,11},{4,12},{5,13},{6,14},{7,15},{8,0},{9,1},... | collective-permute-start | bytes 2064392 | tf_op jit(solution)/shard_map/ppermute | solution.py:290
  8.0 1.6 %collective-permute-start.2 = (bf16[16,7296]{1,0:T(8,128)(2,1)}, bf16[16,7296]{1,0:T(8,128)(2,1)S(1)}, u32[]{:S(2)}, u32[]{:S(2)}) collective-permute-start(bf16[16,7296]{1,0:T(8,128)(2,1)} %get-tuple-element.29.refs_3_), channel_id=1, source_target_pairs={{0,2},{1,3},{2,0},{3,1},{4,6},{5,7},{6,4},{7,5},{8,10},{9,11},{10,... | collective-permute-start | bytes 700424 | tf_op jit(solution)/shard_map/ppermute | solution.py:290
  9.6 2.6 %collective-permute-start.1 = (bf16[16,7296]{1,0:T(8,128)(2,1)}, bf16[16,7296]{1,0:T(8,128)(2,1)S(1)}, u32[]{:S(2)}, u32[]{:S(2)}) collective-permute-start(bf16[16,7296]{1,0:T(8,128)(2,1)} %get-tuple-element.29.refs_3_), channel_id=1, source_target_pairs={{0,4},{1,5},{2,6},{3,7},{4,0},{5,1},{6,2},{7,3},{8,12},{9,13},{10,... | collective-permute-start | bytes 700424 | tf_op jit(solution)/shard_map/ppermute | solution.py:290
  12.2 0.2 collective-permute-start
  12.4 6.6 %collective-permute-done.2.refs_2_ = bf16[16,7296]{1,0:T(8,128)(2,1)S(1)} collective-permute-done((bf16[16,7296]{1,0:T(8,128)(2,1)}, bf16[16,7296]{1,0:T(8,128)(2,1)S(1)}, u32[]{:S(2)}, u32[]{:S(2)}) %collective-permute-start.2) | collective-permute-done | bytes 233504 | tf_op jit(solution)/shard_map/ppermute | solution.py:290
  19.1 3.1 %collective-permute-done.8.all_ref.refs_10_ = bf16[896,384]{1,0:T(8,128)(2,1)S(1)} collective-permute-done((bf16[896,384]{1,0:T(8,128)(2,1)}, bf16[896,384]{1,0:T(8,128)(2,1)S(1)}, u32[]{:S(2)}, u32[]{:S(2)}) %collective-permute-start.8) | collective-permute-done | bytes 688160 | tf_op jit(solution)/shard_map/ppermute | solution.py:290
  22.3 1.8 %collective-permute-start.9 = (bf16[512,384]{1,0:T(8,128)(2,1)S(1)}, bf16[512,384]{1,0:T(8,128)(2,1)S(1)}, u32[]{:S(2)}, u32[]{:S(2)}) collective-permute-start(bf16[512,384]{1,0:T(8,128)(2,1)S(1)} %shard_map.129), channel_id=1, source_target_pairs={{0,8},{1,9},{2,10},{3,11},{4,12},{5,13},{6,14},{7,15},{8,0},{9,1},... | collective-permute-start | bytes 1179656 | tf_op jit(solution)/shard_map/ppermute | solution.py:290
  24.1 1.6 %collective-permute-start.10 = (bf16[384,384]{1,0:T(8,128)(2,1)S(1)}, bf16[384,384]{1,0:T(8,128)(2,1)S(1)}, u32[]{:S(2)}, u32[]{:S(2)}) collective-permute-start(bf16[384,384]{1,0:T(8,128)(2,1)S(1)} %shard_map.130), channel_id=1, source_target_pairs={{0,16},{1,17},{2,18},{3,19},{4,20},{5,21},{6,22},{7,23},{8,24},{9,... | collective-permute-start | bytes 884744 | tf_op jit(solution)/shard_map/ppermute | solution.py:290
  25.7 3.7 %collective-permute-done.1.refs_1_ = bf16[16,7296]{1,0:T(8,128)(2,1)S(1)} collective-permute-done((bf16[16,7296]{1,0:T(8,128)(2,1)}, bf16[16,7296]{1,0:T(8,128)(2,1)S(1)}, u32[]{:S(2)}, u32[]{:S(2)}) %collective-permute-start.1) | collective-permute-done | bytes 233504 | tf_op jit(solution)/shard_map/ppermute | solution.py:290
  29.4 0.5 collective-permute-start.4
  29.9 0.1 collective-permute-start.3
  30.0 0.9 %collective-permute-done.5.refs_6_ = bf16[16,7296]{1,0:T(8,128)(2,1)S(1)} collective-permute-done((bf16[16,7296]{1,0:T(8,128)(2,1)S(1)}, bf16[16,7296]{1,0:T(8,128)(2,1)S(1)}, u32[]{:S(2)}, u32[]{:S(2)}) %collective-permute-start.5) | collective-permute-done | bytes 233504 | tf_op jit(solution)/shard_map/ppermute | solution.py:290
  30.9 0.3 collective-permute-done.4.refs_5_
  31.2 0.3 collective-permute-done.3.refs_4_
  31.5 0.2 collective-permute-done.10.refs_12_
  31.7 0.9 %collective-permute-done.9.refs_11_ = bf16[512,384]{1,0:T(8,128)(2,1)S(1)} collective-permute-done((bf16[512,384]{1,0:T(8,128)(2,1)S(1)}, bf16[512,384]{1,0:T(8,128)(2,1)S(1)}, u32[]{:S(2)}, u32[]{:S(2)}) %collective-permute-start.9) | collective-permute-done | bytes 393248 | tf_op jit(solution)/shard_map/ppermute | solution.py:290
  32.6 1.7 %shard_map.131 = (bf16[64,3712]{1,0:T(8,128)(2,1)S(1)}, bf16[64,3712]{1,0:T(8,128)(2,1)S(1)}, bf16[128,384]{1,0:T(8,128)(2,1)S(1)}, bf16[2,128,896]{2,1,0:T(8,12...) custom-call(s32[1,4]{1,0:T(1,128)S(1)} %bitcast.6, ...), custom_call_target="tpu_custom_call" | custom-call | flops 587202560 | bytes 7110672 | tf_op jit(solution)/shard_map/pallas_call | solution.py:32
  34.3 0.1 collective-permute-start.11
  34.4 1.5 %collective-permute-start.15 = (bf16[128,1280]{1,0:T(8,128)(2,1)S(1)}, bf16[128,1280]{1,0:T(8,128)(2,1)S(1)}, u32[]{:S(2)}, u32[]{:S(2)}) collective-permute-start(bf16[128,1280]{1,0:T(8,128)(2,1)S(1)} %get-tuple-element.41), channel_id=1, source_target_pairs={{0,8},{1,9},{2,10},{3,11},{4,12},{5,13},{6,14},{7,15},{8,0},{9,1},... | collective-permute-start | bytes 983048 | tf_op jit(solution)/shard_map/ppermute | solution.py:290
  35.8 1.5 %collective-permute-start.16 = (bf16[128,1280]{1,0:T(8,128)(2,1)S(1)}, bf16[128,1280]{1,0:T(8,128)(2,1)S(1)}, u32[]{:S(2)}, u32[]{:S(2)}) collective-permute-start(bf16[128,1280]{1,0:T(8,128)(2,1)S(1)} %get-tuple-element.42), channel_id=1, source_target_pairs={{0,16},{1,17},{2,18},{3,19},{4,20},{5,21},{6,22},{7,23},{8,24},{9,... | collective-permute-start | bytes 983048 | tf_op jit(solution)/shard_map/ppermute | solution.py:290
  37.4 0.1 shard_map.132
  37.5 1.3 %collective-permute-start.18 = (bf16[128,1280]{1,0:T(8,128)(2,1)S(1)}, bf16[128,1280]{1,0:T(8,128)(2,1)S(1)}, u32[]{:S(2)}, u32[]{:S(2)}) collective-permute-start(bf16[128,1280]{1,0:T(8,128)(2,1)S(1)} %get-tuple-element.44), channel_id=1, source_target_pairs={{0,24},{1,25},{2,26},{3,27},{4,28},{5,29},{6,30},{7,31},{8,16},{9,... | collective-permute-start | bytes 983048 | tf_op jit(solution)/shard_map/ppermute | solution.py:290
  38.7 3.6 %collective-permute-start.12 = (bf16[16,3712]{1,0:T(8,128)(2,1)S(1)}, bf16[16,3712]{1,0:T(8,128)(2,1)S(1)}, u32[]{:S(2)}, u32[]{:S(2)}) collective-permute-start(bf16[16,3712]{1,0:T(8,128)(2,1)S(1)} %get-tuple-element.33), channel_id=1, source_target_pairs={{0,6},{1,7},{2,4},{3,5},{4,2},{5,3},{6,0},{7,1},{8,14},{9,15},{10,... | collective-permute-start | bytes 356360 | tf_op jit(solution)/shard_map/ppermute | solution.py:290
  42.3 2.6 %collective-permute-done.15.refs_0_ = bf16[128,1280]{1,0:T(8,128)(2,1)S(1)} collective-permute-done((bf16[128,1280]{1,0:T(8,128)(2,1)S(1)}, bf16[128,1280]{1,0:T(8,128)(2,1)S(1)}, u32[]{:S(2)}, u32[]{:S(2)}) %collective-permute-start.15) | collective-permute-done | bytes 327712 | tf_op jit(solution)/shard_map/ppermute | solution.py:290
  44.9 2.3 %collective-permute-start.14 = (bf16[16,3712]{1,0:T(8,128)(2,1)S(1)}, bf16[16,3712]{1,0:T(8,128)(2,1)S(1)}, u32[]{:S(2)}, u32[]{:S(2)}) collective-permute-start(bf16[16,3712]{1,0:T(8,128)(2,1)S(1)} %get-tuple-element.35), channel_id=1, source_target_pairs={{0,2},{1,3},{2,0},{3,1},{4,6},{5,7},{6,4},{7,5},{8,10},{9,11},{10,... | collective-permute-start | bytes 356360 | tf_op jit(solution)/shard_map/ppermute | solution.py:290
  47.3 5.4 %collective-permute-done.16.refs_1_ = bf16[128,1280]{1,0:T(8,128)(2,1)S(1)} collective-permute-done((bf16[128,1280]{1,0:T(8,128)(2,1)S(1)}, bf16[128,1280]{1,0:T(8,128)(2,1)S(1)}, u32[]{:S(2)}, u32[]{:S(2)}) %collective-permute-start.16) | collective-permute-done | bytes 327712 | tf_op jit(solution)/shard_map/ppermute | solution.py:290
  52.7 0.1 collective-permute-start.17
  52.8 0.6 collective-permute-start.19
  53.4 1.4 %shard_map.133 = (bf16[128,3584]{1,0:T(8,128)(2,1)}, f32[8,128]{1,0:T(8,128)}) custom-call(s32[8,128]{1,0:T(8,128)S(1)} %bitcast.5, bf16[1,64,128]{2,1,0:T(8,128)(2,1)S(1)} %copy-done.4, bf16[16,3712]{1,0:T(8,128)(2,1)S(1)} %collective-permute-done.12.refs_0_, bf16[16,3712]{1,0:T(8,128)(2,1)S(1)} %collective-permute-done.13.refs_1_, ...), custom_call_target="tpu_custom_call" | custom-call | flops 58720256000 | bytes 1417216 | tf_op jit(solution)/shard_map/pallas_call | solution.py:32
  54.9 1.4 %shard_map.136 = (bf16[896,128]{1,0:T(8,128)(2,1)}, bf16[896,128]{1,0:T(8,128)(2,1)}, bf16[896,128]{1,0:T(8,128)(2,1)}) custom-call(bf16[2,128,896]{2,1,0:T(8,128)(2,1)S(1)} %get-tuple-element.39.here_ref, bf16[128,384]{1,0:T(8,128)(2,1)S(1)} %get-tuple-element.40.grads_ref, bf16[2,128,896]{2,1,0:T(8,128)(2,1)S(1)} %collective-permute-done.17.near_ref, ...), custom_call_target="tpu_custom_call" | custom-call | flops 352321536 | bytes 2916352 | tf_op jit(solution)/shard_map/pallas_call | solution.py:32
  (27 shorter events, 0.2 us)
Async XLA Ops:
  3.5 18.7 %collective-permute-start.8 = (bf16[896,384]{1,0:T(8,128)(2,1)}, bf16[896,384]{1,0:T(8,128)(2,1)S(1)}, u32[]{:S(2)}, u32[]{:S(2)}) collective-permute-start(bf16[896,384]{1,0:T(8,128)(2,1)} %get-tuple-element.30.refs_8_), channel_id=1, source_target_pairs={{0,16},{1,17},{2,18},{3,19},{4,20},{5,21},{6,22},{7,23},{8,24},{9,... | collective-permute-start | bytes 2064392 | tf_op jit(solution)/shard_map/ppermute | solution.py:290
  6.5 17.5 %collective-permute-start.7 = (bf16[896,384]{1,0:T(8,128)(2,1)}, bf16[896,384]{1,0:T(8,128)(2,1)S(1)}, u32[]{:S(2)}, u32[]{:S(2)}) collective-permute-start(bf16[896,384]{1,0:T(8,128)(2,1)} %get-tuple-element.30.refs_8_), channel_id=1, source_target_pairs={{0,8},{1,9},{2,10},{3,11},{4,12},{5,13},{6,14},{7,15},{8,0},{9,1},... | collective-permute-start | bytes 2064392 | tf_op jit(solution)/shard_map/ppermute | solution.py:290
  8.0 11.0 %collective-permute-start.2 = (bf16[16,7296]{1,0:T(8,128)(2,1)}, bf16[16,7296]{1,0:T(8,128)(2,1)S(1)}, u32[]{:S(2)}, u32[]{:S(2)}) collective-permute-start(bf16[16,7296]{1,0:T(8,128)(2,1)} %get-tuple-element.29.refs_3_), channel_id=1, source_target_pairs={{0,2},{1,3},{2,0},{3,1},{4,6},{5,7},{6,4},{7,5},{8,10},{9,11},{10,... | collective-permute-start | bytes 700424 | tf_op jit(solution)/shard_map/ppermute | solution.py:290
  9.6 19.7 %collective-permute-start.1 = (bf16[16,7296]{1,0:T(8,128)(2,1)}, bf16[16,7296]{1,0:T(8,128)(2,1)S(1)}, u32[]{:S(2)}, u32[]{:S(2)}) collective-permute-start(bf16[16,7296]{1,0:T(8,128)(2,1)} %get-tuple-element.29.refs_3_), channel_id=1, source_target_pairs={{0,4},{1,5},{2,6},{3,7},{4,0},{5,1},{6,2},{7,3},{8,12},{9,13},{10,... | collective-permute-start | bytes 700424 | tf_op jit(solution)/shard_map/ppermute | solution.py:290
  12.2 17.2 %collective-permute-start = (bf16[16,7296]{1,0:T(8,128)(2,1)}, bf16[16,7296]{1,0:T(8,128)(2,1)S(1)}, u32[]{:S(2)}, u32[]{:S(2)}) collective-permute-start(bf16[16,7296]{1,0:T(8,128)(2,1)} %get-tuple-element.29.refs_3_), channel_id=1, source_target_pairs={{0,6},{1,7},{2,4},{3,5},{4,2},{5,3},{6,0},{7,1},{8,14},{9,15},{10,... | collective-permute-start | bytes 700424 | tf_op jit(solution)/shard_map/ppermute | solution.py:290
  19.1 10.8 %collective-permute-start.6 = (bf16[16,7296]{1,0:T(8,128)(2,1)}, bf16[16,7296]{1,0:T(8,128)(2,1)S(1)}, u32[]{:S(2)}, u32[]{:S(2)}) collective-permute-start(bf16[16,7296]{1,0:T(8,128)(2,1)} %get-tuple-element.29.refs_3_), channel_id=1, source_target_pairs={{0,1},{1,0},{2,3},{3,2},{4,5},{5,4},{6,7},{7,6},{8,9},{9,8},{10,11... | collective-permute-start | bytes 700424 | tf_op jit(solution)/shard_map/ppermute | solution.py:290
  22.2 10.4 %copy-start = (bf16[896,384]{1,0:T(8,128)(2,1)S(1)}, bf16[896,384]{1,0:T(8,128)(2,1)}, u32[]{:S(2)}) copy-start(bf16[896,384]{1,0:T(8,128)(2,1)} %get-tuple-element.30.refs_8_) | copy-start | bytes 2064388
  22.2 10.4 %copy-start.1 = (bf16[16,7296]{1,0:T(8,128)(2,1)S(1)}, bf16[16,7296]{1,0:T(8,128)(2,1)}, u32[]{:S(2)}) copy-start(bf16[16,7296]{1,0:T(8,128)(2,1)} %get-tuple-element.29.refs_3_) | copy-start | bytes 700420
  22.3 10.4 %collective-permute-start.9 = (bf16[512,384]{1,0:T(8,128)(2,1)S(1)}, bf16[512,384]{1,0:T(8,128)(2,1)S(1)}, u32[]{:S(2)}, u32[]{:S(2)}) collective-permute-start(bf16[512,384]{1,0:T(8,128)(2,1)S(1)} %shard_map.129), channel_id=1, source_target_pairs={{0,8},{1,9},{2,10},{3,11},{4,12},{5,13},{6,14},{7,15},{8,0},{9,1},... | collective-permute-start | bytes 1179656 | tf_op jit(solution)/shard_map/ppermute | solution.py:290
  24.1 8.6 %copy-start.3 = (s32[4,1]{0,1:T(1,128)S(1)}, s32[4,1]{0,1:T(1,128)}, u32[]{:S(2)}) copy-start(s32[4,1]{0,1:T(1,128)} %param.14) | copy-start | bytes 52
  24.1 7.7 %collective-permute-start.10 = (bf16[384,384]{1,0:T(8,128)(2,1)S(1)}, bf16[384,384]{1,0:T(8,128)(2,1)S(1)}, u32[]{:S(2)}, u32[]{:S(2)}) collective-permute-start(bf16[384,384]{1,0:T(8,128)(2,1)S(1)} %shard_map.130), channel_id=1, source_target_pairs={{0,16},{1,17},{2,18},{3,19},{4,20},{5,21},{6,22},{7,23},{8,24},{9,... | collective-permute-start | bytes 884744 | tf_op jit(solution)/shard_map/ppermute | solution.py:290
  29.4 1.5 %collective-permute-start.5 = (bf16[16,7296]{1,0:T(8,128)(2,1)S(1)}, bf16[16,7296]{1,0:T(8,128)(2,1)S(1)}, u32[]{:S(2)}, u32[]{:S(2)}) collective-permute-start(bf16[16,7296]{1,0:T(8,128)(2,1)S(1)} %collective-permute-done.2.refs_2_), channel_id=1, source_target_pairs={{0,1},{1,0},{2,3},{3,2},{4,5},{5,4},{6,7},{7,6},{8,9},{9,8},{10,11... | collective-permute-start | bytes 700424 | tf_op jit(solution)/shard_map/ppermute | solution.py:290
  29.4 1.8 %collective-permute-start.4 = (bf16[16,7296]{1,0:T(8,128)(2,1)S(1)}, bf16[16,7296]{1,0:T(8,128)(2,1)S(1)}, u32[]{:S(2)}, u32[]{:S(2)}) collective-permute-start(bf16[16,7296]{1,0:T(8,128)(2,1)S(1)} %collective-permute-done.1.refs_1_), channel_id=1, source_target_pairs={{0,1},{1,0},{2,3},{3,2},{4,5},{5,4},{6,7},{7,6},{8,9},{9,8},{10,11... | collective-permute-start | bytes 700424 | tf_op jit(solution)/shard_map/ppermute | solution.py:290
  29.9 1.6 %collective-permute-start.3 = (bf16[16,7296]{1,0:T(8,128)(2,1)S(1)}, bf16[16,7296]{1,0:T(8,128)(2,1)S(1)}, u32[]{:S(2)}, u32[]{:S(2)}) collective-permute-start(bf16[16,7296]{1,0:T(8,128)(2,1)S(1)} %collective-permute-done.refs_0_), channel_id=1, source_target_pairs={{0,1},{1,0},{2,3},{3,2},{4,5},{5,4},{6,7},{7,6},{8,9},{9,8},{10,11... | collective-permute-start | bytes 700424 | tf_op jit(solution)/shard_map/ppermute | solution.py:290
  34.3 3.1 %collective-permute-start.11 = (bf16[64,3712]{1,0:T(8,128)(2,1)S(1)}, bf16[64,3712]{1,0:T(8,128)(2,1)S(1)}, u32[]{:S(2)}, u32[]{:S(2)}) collective-permute-start(bf16[64,3712]{1,0:T(8,128)(2,1)S(1)} %get-tuple-element.32), channel_id=1, source_target_pairs={{0,1},{1,0},{2,3},{3,2},{4,5},{5,4},{6,7},{7,6},{8,9},{9,8},{10,11... | collective-permute-start | bytes 1425416 | tf_op jit(solution)/shard_map/ppermute | solution.py:290
  34.4 10.6 %collective-permute-start.15 = (bf16[128,1280]{1,0:T(8,128)(2,1)S(1)}, bf16[128,1280]{1,0:T(8,128)(2,1)S(1)}, u32[]{:S(2)}, u32[]{:S(2)}) collective-permute-start(bf16[128,1280]{1,0:T(8,128)(2,1)S(1)} %get-tuple-element.41), channel_id=1, source_target_pairs={{0,8},{1,9},{2,10},{3,11},{4,12},{5,13},{6,14},{7,15},{8,0},{9,1},... | collective-permute-start | bytes 983048 | tf_op jit(solution)/shard_map/ppermute | solution.py:290
  35.8 16.8 %collective-permute-start.16 = (bf16[128,1280]{1,0:T(8,128)(2,1)S(1)}, bf16[128,1280]{1,0:T(8,128)(2,1)S(1)}, u32[]{:S(2)}, u32[]{:S(2)}) collective-permute-start(bf16[128,1280]{1,0:T(8,128)(2,1)S(1)} %get-tuple-element.42), channel_id=1, source_target_pairs={{0,16},{1,17},{2,18},{3,19},{4,20},{5,21},{6,22},{7,23},{8,24},{9,... | collective-permute-start | bytes 983048 | tf_op jit(solution)/shard_map/ppermute | solution.py:290
  37.5 15.3 %collective-permute-start.18 = (bf16[128,1280]{1,0:T(8,128)(2,1)S(1)}, bf16[128,1280]{1,0:T(8,128)(2,1)S(1)}, u32[]{:S(2)}, u32[]{:S(2)}) collective-permute-start(bf16[128,1280]{1,0:T(8,128)(2,1)S(1)} %get-tuple-element.44), channel_id=1, source_target_pairs={{0,24},{1,25},{2,26},{3,27},{4,28},{5,29},{6,30},{7,31},{8,16},{9,... | collective-permute-start | bytes 983048 | tf_op jit(solution)/shard_map/ppermute | solution.py:290
  38.7 14.6 %collective-permute-start.12 = (bf16[16,3712]{1,0:T(8,128)(2,1)S(1)}, bf16[16,3712]{1,0:T(8,128)(2,1)S(1)}, u32[]{:S(2)}, u32[]{:S(2)}) collective-permute-start(bf16[16,3712]{1,0:T(8,128)(2,1)S(1)} %get-tuple-element.33), channel_id=1, source_target_pairs={{0,6},{1,7},{2,4},{3,5},{4,2},{5,3},{6,0},{7,1},{8,14},{9,15},{10,... | collective-permute-start | bytes 356360 | tf_op jit(solution)/shard_map/ppermute | solution.py:290
  42.3 11.0 %collective-permute-start.13 = (bf16[16,3712]{1,0:T(8,128)(2,1)S(1)}, bf16[16,3712]{1,0:T(8,128)(2,1)S(1)}, u32[]{:S(2)}, u32[]{:S(2)}) collective-permute-start(bf16[16,3712]{1,0:T(8,128)(2,1)S(1)} %get-tuple-element.34), channel_id=1, source_target_pairs={{0,4},{1,5},{2,6},{3,7},{4,0},{5,1},{6,2},{7,3},{8,12},{9,13},{10,... | collective-permute-start | bytes 356360 | tf_op jit(solution)/shard_map/ppermute | solution.py:290
  44.9 8.4 %collective-permute-start.14 = (bf16[16,3712]{1,0:T(8,128)(2,1)S(1)}, bf16[16,3712]{1,0:T(8,128)(2,1)S(1)}, u32[]{:S(2)}, u32[]{:S(2)}) collective-permute-start(bf16[16,3712]{1,0:T(8,128)(2,1)S(1)} %get-tuple-element.35), channel_id=1, source_target_pairs={{0,2},{1,3},{2,0},{3,1},{4,6},{5,7},{6,4},{7,5},{8,10},{9,11},{10,... | collective-permute-start | bytes 356360 | tf_op jit(solution)/shard_map/ppermute | solution.py:290
  52.7 0.7 %copy-start.2 = (s32[128,8]{0,1:T(8,128)S(1)}, s32[128,8]{0,1:T(8,128)}, u32[]{:S(2)}) copy-start(s32[128,8]{0,1:T(8,128)} %param.11) | copy-start | bytes 12292
  52.7 0.7 %copy-start.4 = (bf16[1,64,128]{2,1,0:T(8,128)(2,1)S(1)}, bf16[1,64,128]{2,1,0:T(8,128)(2,1)}, u32[]{:S(2)}) copy-start(bf16[1,64,128]{2,1,0:T(8,128)(2,1)} %get-tuple-element.27.placed_ref) | copy-start | bytes 49156
  52.7 2.2 %collective-permute-start.17 = (bf16[2,128,896]{2,1,0:T(8,128)(2,1)S(1)}, bf16[2,128,896]{2,1,0:T(8,128)(2,1)S(1)}, u32[]{:S(2)}, u32[]{:S(2)}) collective-permute-start(bf16[2,128,896]{2,1,0:T(8,128)(2,1)S(1)} %shard_map.134), channel_id=1, source_target_pairs={{0,1},{1,0},{2,3},{3,2},{4,5},{5,4},{6,7},{7,6},{8,9},{9,8},{10,11... | collective-permute-start | bytes 1376264 | tf_op jit(solution)/shard_map/ppermute | solution.py:290
  52.8 2.1 %collective-permute-start.19 = (bf16[1,128,896]{2,1,0:T(8,128)(2,1)S(1)}, bf16[1,128,896]{2,1,0:T(8,128)(2,1)S(1)}, u32[]{:S(2)}, u32[]{:S(2)}) collective-permute-start(bf16[1,128,896]{2,1,0:T(8,128)(2,1)S(1)} %shard_map.135), channel_id=1, source_target_pairs={{0,1},{1,0},{2,3},{3,2},{4,5},{5,4},{6,7},{7,6},{8,9},{9,8},{10,11... | collective-permute-start | bytes 688136 | tf_op jit(solution)/shard_map/ppermute | solution.py:290

commit v19 on v16

--- a/solution.py
+++ b/solution.py
@@ -16,7 +16,7 @@
 LANES = 128
 F32 = jnp.float32
 BF16 = jnp.bfloat16
-PARTS = 4
+PARTS = 2
 HBM = pl.BlockSpec(memory_space=pltpu.HBM)
 VMEM = pl.BlockSpec(memory_space=pltpu.VMEM)
 

time: 56 us -> 55.9 us (level)
  no operation moved by 1% of the time
where the time goes in v19:
time: 55.9 us; the launch traced here: 55.8 us
  waiting for transfers between devices  24.8 us (44%)
  starting transfers between devices  22.4 us (40%)
  Pallas kernels  7.68 us (14%)
  between operations  0.82 us (1%)
    ppermute x20, waiting for transfers between devices, send(): return lax.ppermute(array, ('rep', 'ep'), pairs)  24.8 us
    ppermute x20, starting transfers between devices, send(): return lax.ppermute(array, ('rep', 'ep'), pairs)  22.4 us
    pallas_call x9, Pallas kernels, call(): pl.pallas_call(kernel, out_shape=tuple(outs), in_specs=[HBM if n in store...  7.68 us
  transfers between devices with their start and end apart: 20, of which 10 were waited for; matrix products, arithmetic and copies ran while one was open for 0% of the time, Pallas kernels for 3%

profile of v19, /device:TPU:0, one launch (start us, length us, event | category | flops | bytes accessed | tf_op | source)
XLA Modules:
  0.0 55.8 jit_solution(8692681558395898318)
XLA Ops:
  0.6 2.8 %shard_map.128 = (bf16[16,7296]{1,0:T(8,128)(2,1)}, bf16[1,64,128]{2,1,0:T(8,128)(2,1)}, bf16[896,384]{1,0:T(8,128)(2,1)}) custom-call(s32[4]{0:T(128)} %live_ref.1, bf16[128,3584]{1,0:T(8,128)(2,1)} %tok_ref.1, bf16[128,3584]{1,0:T(8,128)(2,1)} %grad_ref.1, s32[8,128]{1,0:T(8,128)} %bitcast.4, bf16[8,128]{1,0:T(8,128)(2,1)} %bitcast.7, ...), custom_call_target="tpu_custom_call" | custom-call | bytes 3467280 | tf_op jit(solution)/shard_map/pallas_call | solution.py:32
  3.5 3.0 %collective-permute-start.8 = (bf16[896,384]{1,0:T(8,128)(2,1)}, bf16[896,384]{1,0:T(8,128)(2,1)S(1)}, u32[]{:S(2)}, u32[]{:S(2)}) collective-permute-start(bf16[896,384]{1,0:T(8,128)(2,1)} %get-tuple-element.30.refs_8_), channel_id=1, source_target_pairs={{0,16},{1,17},{2,18},{3,19},{4,20},{5,21},{6,22},{7,23},{8,24},{9,... | collective-permute-start | bytes 2064392 | tf_op jit(solution)/shard_map/ppermute | solution.py:290
  6.5 1.5 %collective-permute-start.7 = (bf16[896,384]{1,0:T(8,128)(2,1)}, bf16[896,384]{1,0:T(8,128)(2,1)S(1)}, u32[]{:S(2)}, u32[]{:S(2)}) collective-permute-start(bf16[896,384]{1,0:T(8,128)(2,1)} %get-tuple-element.30.refs_8_), channel_id=1, source_target_pairs={{0,8},{1,9},{2,10},{3,11},{4,12},{5,13},{6,14},{7,15},{8,0},{9,1},... | collective-permute-start | bytes 2064392 | tf_op jit(solution)/shard_map/ppermute | solution.py:290
  8.0 1.6 %collective-permute-start.2 = (bf16[16,7296]{1,0:T(8,128)(2,1)}, bf16[16,7296]{1,0:T(8,128)(2,1)S(1)}, u32[]{:S(2)}, u32[]{:S(2)}) collective-permute-start(bf16[16,7296]{1,0:T(8,128)(2,1)} %get-tuple-element.29.refs_3_), channel_id=1, source_target_pairs={{0,2},{1,3},{2,0},{3,1},{4,6},{5,7},{6,4},{7,5},{8,10},{9,11},{10,... | collective-permute-start | bytes 700424 | tf_op jit(solution)/shard_map/ppermute | solution.py:290
  9.6 2.6 %collective-permute-start.1 = (bf16[16,7296]{1,0:T(8,128)(2,1)}, bf16[16,7296]{1,0:T(8,128)(2,1)S(1)}, u32[]{:S(2)}, u32[]{:S(2)}) collective-permute-start(bf16[16,7296]{1,0:T(8,128)(2,1)} %get-tuple-element.29.refs_3_), channel_id=1, source_target_pairs={{0,4},{1,5},{2,6},{3,7},{4,0},{5,1},{6,2},{7,3},{8,12},{9,13},{10,... | collective-permute-start | bytes 700424 | tf_op jit(solution)/shard_map/ppermute | solution.py:290
  12.2 0.2 collective-permute-start
  12.4 6.6 %collective-permute-done.2.refs_2_ = bf16[16,7296]{1,0:T(8,128)(2,1)S(1)} collective-permute-done((bf16[16,7296]{1,0:T(8,128)(2,1)}, bf16[16,7296]{1,0:T(8,128)(2,1)S(1)}, u32[]{:S(2)}, u32[]{:S(2)}) %collective-permute-start.2) | collective-permute-done | bytes 233504 | tf_op jit(solution)/shard_map/ppermute | solution.py:290
  19.1 3.1 %collective-permute-done.8.all_ref.refs_10_ = bf16[896,384]{1,0:T(8,128)(2,1)S(1)} collective-permute-done((bf16[896,384]{1,0:T(8,128)(2,1)}, bf16[896,384]{1,0:T(8,128)(2,1)S(1)}, u32[]{:S(2)}, u32[]{:S(2)}) %collective-permute-start.8) | collective-permute-done | bytes 688160 | tf_op jit(solution)/shard_map/ppermute | solution.py:290
  22.2 1.8 %collective-permute-start.9 = (bf16[448,384]{1,0:T(8,128)(2,1)S(1)}, bf16[448,384]{1,0:T(8,128)(2,1)S(1)}, u32[]{:S(2)}, u32[]{:S(2)}) collective-permute-start(bf16[448,384]{1,0:T(8,128)(2,1)S(1)} %shard_map.129), channel_id=1, source_target_pairs={{0,8},{1,9},{2,10},{3,11},{4,12},{5,13},{6,14},{7,15},{8,0},{9,1},... | collective-permute-start | bytes 1032200 | tf_op jit(solution)/shard_map/ppermute | solution.py:290
  24.1 1.6 %collective-permute-start.10 = (bf16[448,384]{1,0:T(8,128)(2,1)S(1)}, bf16[448,384]{1,0:T(8,128)(2,1)S(1)}, u32[]{:S(2)}, u32[]{:S(2)}) collective-permute-start(bf16[448,384]{1,0:T(8,128)(2,1)S(1)} %shard_map.130), channel_id=1, source_target_pairs={{0,16},{1,17},{2,18},{3,19},{4,20},{5,21},{6,22},{7,23},{8,24},{9,... | collective-permute-start | bytes 1032200 | tf_op jit(solution)/shard_map/ppermute | solution.py:290
  25.6 3.7 %collective-permute-done.1.refs_1_ = bf16[16,7296]{1,0:T(8,128)(2,1)S(1)} collective-permute-done((bf16[16,7296]{1,0:T(8,128)(2,1)}, bf16[16,7296]{1,0:T(8,128)(2,1)S(1)}, u32[]{:S(2)}, u32[]{:S(2)}) %collective-permute-start.1) | collective-permute-done | bytes 233504 | tf_op jit(solution)/shard_map/ppermute | solution.py:290
  29.3 0.5 collective-permute-start.4
  29.9 0.1 collective-permute-start.3
  29.9 0.9 %collective-permute-done.5.refs_6_ = bf16[16,7296]{1,0:T(8,128)(2,1)S(1)} collective-permute-done((bf16[16,7296]{1,0:T(8,128)(2,1)S(1)}, bf16[16,7296]{1,0:T(8,128)(2,1)S(1)}, u32[]{:S(2)}, u32[]{:S(2)}) %collective-permute-start.5) | collective-permute-done | bytes 233504 | tf_op jit(solution)/shard_map/ppermute | solution.py:290
  30.8 0.3 collective-permute-done.4.refs_5_
  31.2 0.3 collective-permute-done.3.refs_4_
  31.5 1.2 %collective-permute-done.10.refs_12_ = bf16[448,384]{1,0:T(8,128)(2,1)S(1)} collective-permute-done((bf16[448,384]{1,0:T(8,128)(2,1)S(1)}, bf16[448,384]{1,0:T(8,128)(2,1)S(1)}, u32[]{:S(2)}, u32[]{:S(2)}) %collective-permute-start.10) | collective-permute-done | bytes 344096 | tf_op jit(solution)/shard_map/ppermute | solution.py:290
  32.8 1.8 %shard_map.131 = (bf16[64,3712]{1,0:T(8,128)(2,1)S(1)}, bf16[64,3712]{1,0:T(8,128)(2,1)S(1)}, bf16[128,384]{1,0:T(8,128)(2,1)S(1)}, bf16[2,128,896]{2,1,0:T(8,12...) custom-call(s32[1,4]{1,0:T(1,128)S(1)} %bitcast.6, ...), custom_call_target="tpu_custom_call" | custom-call | flops 587202560 | bytes 7110672 | tf_op jit(solution)/shard_map/pallas_call | solution.py:32
  34.6 0.1 collective-permute-start.11
  34.6 1.1 %collective-permute-start.15 = (bf16[128,1280]{1,0:T(8,128)(2,1)S(1)}, bf16[128,1280]{1,0:T(8,128)(2,1)S(1)}, u32[]{:S(2)}, u32[]{:S(2)}) collective-permute-start(bf16[128,1280]{1,0:T(8,128)(2,1)S(1)} %get-tuple-element.41), channel_id=1, source_target_pairs={{0,8},{1,9},{2,10},{3,11},{4,12},{5,13},{6,14},{7,15},{8,0},{9,1},... | collective-permute-start | bytes 983048 | tf_op jit(solution)/shard_map/ppermute | solution.py:290
  35.8 1.0 %collective-permute-start.16 = (bf16[128,1280]{1,0:T(8,128)(2,1)S(1)}, bf16[128,1280]{1,0:T(8,128)(2,1)S(1)}, u32[]{:S(2)}, u32[]{:S(2)}) collective-permute-start(bf16[128,1280]{1,0:T(8,128)(2,1)S(1)} %get-tuple-element.42), channel_id=1, source_target_pairs={{0,16},{1,17},{2,18},{3,19},{4,20},{5,21},{6,22},{7,23},{8,24},{9,... | collective-permute-start | bytes 983048 | tf_op jit(solution)/shard_map/ppermute | solution.py:290
  36.8 0.1 shard_map.132
  36.9 1.5 %collective-permute-start.18 = (bf16[128,1280]{1,0:T(8,128)(2,1)S(1)}, bf16[128,1280]{1,0:T(8,128)(2,1)S(1)}, u32[]{:S(2)}, u32[]{:S(2)}) collective-permute-start(bf16[128,1280]{1,0:T(8,128)(2,1)S(1)} %get-tuple-element.44), channel_id=1, source_target_pairs={{0,24},{1,25},{2,26},{3,27},{4,28},{5,29},{6,30},{7,31},{8,16},{9,... | collective-permute-start | bytes 983048 | tf_op jit(solution)/shard_map/ppermute | solution.py:290
  38.4 3.6 %collective-permute-start.12 = (bf16[16,3712]{1,0:T(8,128)(2,1)S(1)}, bf16[16,3712]{1,0:T(8,128)(2,1)S(1)}, u32[]{:S(2)}, u32[]{:S(2)}) collective-permute-start(bf16[16,3712]{1,0:T(8,128)(2,1)S(1)} %get-tuple-element.33), channel_id=1, source_target_pairs={{0,6},{1,7},{2,4},{3,5},{4,2},{5,3},{6,0},{7,1},{8,14},{9,15},{10,... | collective-permute-start | bytes 356360 | tf_op jit(solution)/shard_map/ppermute | solution.py:290
  42.0 3.2 %collective-permute-done.15.refs_0_ = bf16[128,1280]{1,0:T(8,128)(2,1)S(1)} collective-permute-done((bf16[128,1280]{1,0:T(8,128)(2,1)S(1)}, bf16[128,1280]{1,0:T(8,128)(2,1)S(1)}, u32[]{:S(2)}, u32[]{:S(2)}) %collective-permute-start.15) | collective-permute-done | bytes 327712 | tf_op jit(solution)/shard_map/ppermute | solution.py:290
  45.2 2.1 %collective-permute-start.14 = (bf16[16,3712]{1,0:T(8,128)(2,1)S(1)}, bf16[16,3712]{1,0:T(8,128)(2,1)S(1)}, u32[]{:S(2)}, u32[]{:S(2)}) collective-permute-start(bf16[16,3712]{1,0:T(8,128)(2,1)S(1)} %get-tuple-element.35), channel_id=1, source_target_pairs={{0,2},{1,3},{2,0},{3,1},{4,6},{5,7},{6,4},{7,5},{8,10},{9,11},{10,... | collective-permute-start | bytes 356360 | tf_op jit(solution)/shard_map/ppermute | solution.py:290
  47.3 3.8 %collective-permute-done.16.refs_1_ = bf16[128,1280]{1,0:T(8,128)(2,1)S(1)} collective-permute-done((bf16[128,1280]{1,0:T(8,128)(2,1)S(1)}, bf16[128,1280]{1,0:T(8,128)(2,1)S(1)}, u32[]{:S(2)}, u32[]{:S(2)}) %collective-permute-start.16) | collective-permute-done | bytes 327712 | tf_op jit(solution)/shard_map/ppermute | solution.py:290
  51.2 0.1 collective-permute-start.17
  51.2 1.5 %collective-permute-done.18.refs_0_.refs_2_ = bf16[128,1280]{1,0:T(8,128)(2,1)S(1)} collective-permute-done((bf16[128,1280]{1,0:T(8,128)(2,1)S(1)}, bf16[128,1280]{1,0:T(8,128)(2,1)S(1)}, u32[]{:S(2)}, u32[]{:S(2)}) %collective-permute-start.18) | collective-permute-done | bytes 327712 | tf_op jit(solution)/shard_map/ppermute | solution.py:290
  52.8 0.1 collective-permute-start.19
  52.9 1.4 %shard_map.133 = (bf16[128,3584]{1,0:T(8,128)(2,1)}, f32[8,128]{1,0:T(8,128)}) custom-call(s32[8,128]{1,0:T(8,128)S(1)} %bitcast.5, bf16[1,64,128]{2,1,0:T(8,128)(2,1)S(1)} %copy-done.4, bf16[16,3712]{1,0:T(8,128)(2,1)S(1)} %collective-permute-done.12.refs_0_, bf16[16,3712]{1,0:T(8,128)(2,1)S(1)} %collective-permute-done.13.refs_1_, ...), custom_call_target="tpu_custom_call" | custom-call | flops 58720256000 | bytes 1417216 | tf_op jit(solution)/shard_map/pallas_call | solution.py:32
  54.4 1.4 %shard_map.136 = (bf16[896,128]{1,0:T(8,128)(2,1)}, bf16[896,128]{1,0:T(8,128)(2,1)}, bf16[896,128]{1,0:T(8,128)(2,1)}) custom-call(bf16[2,128,896]{2,1,0:T(8,128)(2,1)S(1)} %get-tuple-element.39.here_ref, bf16[128,384]{1,0:T(8,128)(2,1)S(1)} %get-tuple-element.40.grads_ref, bf16[2,128,896]{2,1,0:T(8,128)(2,1)S(1)} %collective-permute-done.17.near_ref, ...), custom_call_target="tpu_custom_call" | custom-call | flops 352321536 | bytes 2916352 | tf_op jit(solution)/shard_map/pallas_call | solution.py:32
  (27 shorter events, 0.2 us)
Async XLA Ops:
  3.5 18.7 %collective-permute-start.8 = (bf16[896,384]{1,0:T(8,128)(2,1)}, bf16[896,384]{1,0:T(8,128)(2,1)S(1)}, u32[]{:S(2)}, u32[]{:S(2)}) collective-permute-start(bf16[896,384]{1,0:T(8,128)(2,1)} %get-tuple-element.30.refs_8_), channel_id=1, source_target_pairs={{0,16},{1,17},{2,18},{3,19},{4,20},{5,21},{6,22},{7,23},{8,24},{9,... | collective-permute-start | bytes 2064392 | tf_op jit(solution)/shard_map/ppermute | solution.py:290
  6.5 17.5 %collective-permute-start.7 = (bf16[896,384]{1,0:T(8,128)(2,1)}, bf16[896,384]{1,0:T(8,128)(2,1)S(1)}, u32[]{:S(2)}, u32[]{:S(2)}) collective-permute-start(bf16[896,384]{1,0:T(8,128)(2,1)} %get-tuple-element.30.refs_8_), channel_id=1, source_target_pairs={{0,8},{1,9},{2,10},{3,11},{4,12},{5,13},{6,14},{7,15},{8,0},{9,1},... | collective-permute-start | bytes 2064392 | tf_op jit(solution)/shard_map/ppermute | solution.py:290
  8.0 11.0 %collective-permute-start.2 = (bf16[16,7296]{1,0:T(8,128)(2,1)}, bf16[16,7296]{1,0:T(8,128)(2,1)S(1)}, u32[]{:S(2)}, u32[]{:S(2)}) collective-permute-start(bf16[16,7296]{1,0:T(8,128)(2,1)} %get-tuple-element.29.refs_3_), channel_id=1, source_target_pairs={{0,2},{1,3},{2,0},{3,1},{4,6},{5,7},{6,4},{7,5},{8,10},{9,11},{10,... | collective-permute-start | bytes 700424 | tf_op jit(solution)/shard_map/ppermute | solution.py:290
  9.6 19.7 %collective-permute-start.1 = (bf16[16,7296]{1,0:T(8,128)(2,1)}, bf16[16,7296]{1,0:T(8,128)(2,1)S(1)}, u32[]{:S(2)}, u32[]{:S(2)}) collective-permute-start(bf16[16,7296]{1,0:T(8,128)(2,1)} %get-tuple-element.29.refs_3_), channel_id=1, source_target_pairs={{0,4},{1,5},{2,6},{3,7},{4,0},{5,1},{6,2},{7,3},{8,12},{9,13},{10,... | collective-permute-start | bytes 700424 | tf_op jit(solution)/shard_map/ppermute | solution.py:290
  12.2 17.2 %collective-permute-start = (bf16[16,7296]{1,0:T(8,128)(2,1)}, bf16[16,7296]{1,0:T(8,128)(2,1)S(1)}, u32[]{:S(2)}, u32[]{:S(2)}) collective-permute-start(bf16[16,7296]{1,0:T(8,128)(2,1)} %get-tuple-element.29.refs_3_), channel_id=1, source_target_pairs={{0,6},{1,7},{2,4},{3,5},{4,2},{5,3},{6,0},{7,1},{8,14},{9,15},{10,... | collective-permute-start | bytes 700424 | tf_op jit(solution)/shard_map/ppermute | solution.py:290
  19.1 10.8 %collective-permute-start.6 = (bf16[16,7296]{1,0:T(8,128)(2,1)}, bf16[16,7296]{1,0:T(8,128)(2,1)S(1)}, u32[]{:S(2)}, u32[]{:S(2)}) collective-permute-start(bf16[16,7296]{1,0:T(8,128)(2,1)} %get-tuple-element.29.refs_3_), channel_id=1, source_target_pairs={{0,1},{1,0},{2,3},{3,2},{4,5},{5,4},{6,7},{7,6},{8,9},{9,8},{10,11... | collective-permute-start | bytes 700424 | tf_op jit(solution)/shard_map/ppermute | solution.py:290
  22.2 10.6 %copy-start = (bf16[896,384]{1,0:T(8,128)(2,1)S(1)}, bf16[896,384]{1,0:T(8,128)(2,1)}, u32[]{:S(2)}) copy-start(bf16[896,384]{1,0:T(8,128)(2,1)} %get-tuple-element.30.refs_8_) | copy-start | bytes 2064388
  22.2 10.6 %copy-start.1 = (bf16[16,7296]{1,0:T(8,128)(2,1)S(1)}, bf16[16,7296]{1,0:T(8,128)(2,1)}, u32[]{:S(2)}) copy-start(bf16[16,7296]{1,0:T(8,128)(2,1)} %get-tuple-element.29.refs_3_) | copy-start | bytes 700420
  22.2 9.3 %collective-permute-start.9 = (bf16[448,384]{1,0:T(8,128)(2,1)S(1)}, bf16[448,384]{1,0:T(8,128)(2,1)S(1)}, u32[]{:S(2)}, u32[]{:S(2)}) collective-permute-start(bf16[448,384]{1,0:T(8,128)(2,1)S(1)} %shard_map.129), channel_id=1, source_target_pairs={{0,8},{1,9},{2,10},{3,11},{4,12},{5,13},{6,14},{7,15},{8,0},{9,1},... | collective-permute-start | bytes 1032200 | tf_op jit(solution)/shard_map/ppermute | solution.py:290
  24.0 8.7 %copy-start.3 = (s32[4,1]{0,1:T(1,128)S(1)}, s32[4,1]{0,1:T(1,128)}, u32[]{:S(2)}) copy-start(s32[4,1]{0,1:T(1,128)} %param.14) | copy-start | bytes 52
  24.1 8.7 %collective-permute-start.10 = (bf16[448,384]{1,0:T(8,128)(2,1)S(1)}, bf16[448,384]{1,0:T(8,128)(2,1)S(1)}, u32[]{:S(2)}, u32[]{:S(2)}) collective-permute-start(bf16[448,384]{1,0:T(8,128)(2,1)S(1)} %shard_map.130), channel_id=1, source_target_pairs={{0,16},{1,17},{2,18},{3,19},{4,20},{5,21},{6,22},{7,23},{8,24},{9,... | collective-permute-start | bytes 1032200 | tf_op jit(solution)/shard_map/ppermute | solution.py:290
  29.3 1.5 %collective-permute-start.5 = (bf16[16,7296]{1,0:T(8,128)(2,1)S(1)}, bf16[16,7296]{1,0:T(8,128)(2,1)S(1)}, u32[]{:S(2)}, u32[]{:S(2)}) collective-permute-start(bf16[16,7296]{1,0:T(8,128)(2,1)S(1)} %collective-permute-done.2.refs_2_), channel_id=1, source_target_pairs={{0,1},{1,0},{2,3},{3,2},{4,5},{5,4},{6,7},{7,6},{8,9},{9,8},{10,11... | collective-permute-start | bytes 700424 | tf_op jit(solution)/shard_map/ppermute | solution.py:290
  29.3 1.8 %collective-permute-start.4 = (bf16[16,7296]{1,0:T(8,128)(2,1)S(1)}, bf16[16,7296]{1,0:T(8,128)(2,1)S(1)}, u32[]{:S(2)}, u32[]{:S(2)}) collective-permute-start(bf16[16,7296]{1,0:T(8,128)(2,1)S(1)} %collective-permute-done.1.refs_1_), channel_id=1, source_target_pairs={{0,1},{1,0},{2,3},{3,2},{4,5},{5,4},{6,7},{7,6},{8,9},{9,8},{10,11... | collective-permute-start | bytes 700424 | tf_op jit(solution)/shard_map/ppermute | solution.py:290
  29.9 1.6 %collective-permute-start.3 = (bf16[16,7296]{1,0:T(8,128)(2,1)S(1)}, bf16[16,7296]{1,0:T(8,128)(2,1)S(1)}, u32[]{:S(2)}, u32[]{:S(2)}) collective-permute-start(bf16[16,7296]{1,0:T(8,128)(2,1)S(1)} %collective-permute-done.refs_0_), channel_id=1, source_target_pairs={{0,1},{1,0},{2,3},{3,2},{4,5},{5,4},{6,7},{7,6},{8,9},{9,8},{10,11... | collective-permute-start | bytes 700424 | tf_op jit(solution)/shard_map/ppermute | solution.py:290
  34.6 2.2 %collective-permute-start.11 = (bf16[64,3712]{1,0:T(8,128)(2,1)S(1)}, bf16[64,3712]{1,0:T(8,128)(2,1)S(1)}, u32[]{:S(2)}, u32[]{:S(2)}) collective-permute-start(bf16[64,3712]{1,0:T(8,128)(2,1)S(1)} %get-tuple-element.32), channel_id=1, source_target_pairs={{0,1},{1,0},{2,3},{3,2},{4,5},{5,4},{6,7},{7,6},{8,9},{9,8},{10,11... | collective-permute-start | bytes 1425416 | tf_op jit(solution)/shard_map/ppermute | solution.py:290
  34.6 10.6 %collective-permute-start.15 = (bf16[128,1280]{1,0:T(8,128)(2,1)S(1)}, bf16[128,1280]{1,0:T(8,128)(2,1)S(1)}, u32[]{:S(2)}, u32[]{:S(2)}) collective-permute-start(bf16[128,1280]{1,0:T(8,128)(2,1)S(1)} %get-tuple-element.41), channel_id=1, source_target_pairs={{0,8},{1,9},{2,10},{3,11},{4,12},{5,13},{6,14},{7,15},{8,0},{9,1},... | collective-permute-start | bytes 983048 | tf_op jit(solution)/shard_map/ppermute | solution.py:290
  35.8 15.3 %collective-permute-start.16 = (bf16[128,1280]{1,0:T(8,128)(2,1)S(1)}, bf16[128,1280]{1,0:T(8,128)(2,1)S(1)}, u32[]{:S(2)}, u32[]{:S(2)}) collective-permute-start(bf16[128,1280]{1,0:T(8,128)(2,1)S(1)} %get-tuple-element.42), channel_id=1, source_target_pairs={{0,16},{1,17},{2,18},{3,19},{4,20},{5,21},{6,22},{7,23},{8,24},{9,... | collective-permute-start | bytes 983048 | tf_op jit(solution)/shard_map/ppermute | solution.py:290
  36.9 15.9 %collective-permute-start.18 = (bf16[128,1280]{1,0:T(8,128)(2,1)S(1)}, bf16[128,1280]{1,0:T(8,128)(2,1)S(1)}, u32[]{:S(2)}, u32[]{:S(2)}) collective-permute-start(bf16[128,1280]{1,0:T(8,128)(2,1)S(1)} %get-tuple-element.44), channel_id=1, source_target_pairs={{0,24},{1,25},{2,26},{3,27},{4,28},{5,29},{6,30},{7,31},{8,16},{9,... | collective-permute-start | bytes 983048 | tf_op jit(solution)/shard_map/ppermute | solution.py:290
  38.4 14.5 %collective-permute-start.12 = (bf16[16,3712]{1,0:T(8,128)(2,1)S(1)}, bf16[16,3712]{1,0:T(8,128)(2,1)S(1)}, u32[]{:S(2)}, u32[]{:S(2)}) collective-permute-start(bf16[16,3712]{1,0:T(8,128)(2,1)S(1)} %get-tuple-element.33), channel_id=1, source_target_pairs={{0,6},{1,7},{2,4},{3,5},{4,2},{5,3},{6,0},{7,1},{8,14},{9,15},{10,... | collective-permute-start | bytes 356360 | tf_op jit(solution)/shard_map/ppermute | solution.py:290
  42.0 10.9 %collective-permute-start.13 = (bf16[16,3712]{1,0:T(8,128)(2,1)S(1)}, bf16[16,3712]{1,0:T(8,128)(2,1)S(1)}, u32[]{:S(2)}, u32[]{:S(2)}) collective-permute-start(bf16[16,3712]{1,0:T(8,128)(2,1)S(1)} %get-tuple-element.34), channel_id=1, source_target_pairs={{0,4},{1,5},{2,6},{3,7},{4,0},{5,1},{6,2},{7,3},{8,12},{9,13},{10,... | collective-permute-start | bytes 356360 | tf_op jit(solution)/shard_map/ppermute | solution.py:290
  45.2 7.7 %collective-permute-start.14 = (bf16[16,3712]{1,0:T(8,128)(2,1)S(1)}, bf16[16,3712]{1,0:T(8,128)(2,1)S(1)}, u32[]{:S(2)}, u32[]{:S(2)}) collective-permute-start(bf16[16,3712]{1,0:T(8,128)(2,1)S(1)} %get-tuple-element.35), channel_id=1, source_target_pairs={{0,2},{1,3},{2,0},{3,1},{4,6},{5,7},{6,4},{7,5},{8,10},{9,11},{10,... | collective-permute-start | bytes 356360 | tf_op jit(solution)/shard_map/ppermute | solution.py:290
  51.1 1.7 %copy-start.2 = (s32[128,8]{0,1:T(8,128)S(1)}, s32[128,8]{0,1:T(8,128)}, u32[]{:S(2)}) copy-start(s32[128,8]{0,1:T(8,128)} %param.11) | copy-start | bytes 12292
  51.2 1.7 %copy-start.4 = (bf16[1,64,128]{2,1,0:T(8,128)(2,1)S(1)}, bf16[1,64,128]{2,1,0:T(8,128)(2,1)}, u32[]{:S(2)}) copy-start(bf16[1,64,128]{2,1,0:T(8,128)(2,1)} %get-tuple-element.27.placed_ref) | copy-start | bytes 49156
  51.2 3.2 %collective-permute-start.17 = (bf16[2,128,896]{2,1,0:T(8,128)(2,1)S(1)}, bf16[2,128,896]{2,1,0:T(8,128)(2,1)S(1)}, u32[]{:S(2)}, u32[]{:S(2)}) collective-permute-start(bf16[2,128,896]{2,1,0:T(8,128)(2,1)S(1)} %shard_map.134), channel_id=1, source_target_pairs={{0,1},{1,0},{2,3},{3,2},{4,5},{5,4},{6,7},{7,6},{8,9},{9,8},{10,11... | collective-permute-start | bytes 1376264 | tf_op jit(solution)/shard_map/ppermute | solution.py:290
  52.8 1.6 %collective-permute-start.19 = (bf16[1,128,896]{2,1,0:T(8,128)(2,1)S(1)}, bf16[1,128,896]{2,1,0:T(8,128)(2,1)S(1)}, u32[]{:S(2)}, u32[]{:S(2)}) collective-permute-start(bf16[1,128,896]{2,1,0:T(8,128)(2,1)S(1)} %shard_map.135), channel_id=1, source_target_pairs={{0,1},{1,0},{2,3},{3,2},{4,5},{5,4},{6,7},{7,6},{8,9},{9,8},{10,11... | collective-permute-start | bytes 688136 | tf_op jit(solution)/shard_map/ppermute | solution.py:290
